TPU v7x, 32 devices: a whole 2x2x4 slice. The times are simulated.
32 devices in a mesh: box: 8 (over z, y), dir: 4 (over x, core).
Axes of the slice: x: 2, y: 2, z: 4, core: 2. Of those that a mesh axis runs over, the one named last changes fastest.
Arguments:
- coarse_field: float32 [512, 2, 4, 2048], P('box', None, None, 'dir'), may hold values from -6 to 6
- trans_table: float32 [316, 2, 2048], P(None, None, 'dir'), may hold values from -1.5 to 1.5
- partner_ids: int32 [512, 30], P('box'), may hold values from 0 to 511, as said below
- partner_types: int32 [512, 30], P('box'), may hold values from 0 to 315
- partner_count: int32 [512], P('box'), may hold values from 15 to 30
- child_count: int32 [512], P('box'), may hold values from 1 to 7, as said below
- child_octant: int32 [2048], P('box'), may hold values from 0 to 7
- dir_angles: float32 [2, 2048], replicated, may hold values from -3.140625 to 3.140625
- stencil_ids: int32 [2048, 4], replicated, may hold values from 0 to 511, as said below
- stencil_weights: float32 [2048, 4], replicated, may hold values from -1.8 to 1.8
Outputs:
- fine_field: float32 [2048, 2, 4, 512], P(('box', 'dir'))
Inputs may be any that keep to these rules, and one draw needn't show every extreme that they name: `partner_ids`: coarse box b sits on a grid whose z coordinate takes the two highest bits of b (the higher one as its bit 1) and whose x and y coordinates take the lower bits in turn (x from bit 0, y from bit 1, x from bit 2, and so on); the slots of b name distinct boxes that are children of neighbours of b's parent and not adjacent to b. `child_count`: each aligned block of 64 coarse boxes has exactly 256 children in all. stencil_ids[c, s] lies within 2 of c // 4, counted circularly over 512 directions.
All inputs are finite; a program needn't handle non-finite values.
Results may differ from a plain program's by a relative error of at most 0.0003.
Values sent between devices are 32-bit elements; how exact they have to be, the bound alone decides.
No kernel may reach another device: no remote copies, remote signals or barrier semaphores. Data moves between devices by JAX's collectives and lax.ppermute only.
A program may use at most 64 MiB of HBM per device.

v0:
```python
import collections
import functools

import jax
import jax.numpy as jnp
from jax import lax
from jax.experimental import pallas as pl
from jax.experimental.pallas import tpu as pltpu
from jax.sharding import Mesh
from jax.sharding import PartitionSpec as P

wave_scale = 3.0
planes = 4
lanes = 128
half = 4
rim = 2


plan_fields = ["rows", "slots", "fine_rows", "stride", "kinds", "parent", "octant", "order", "turns"]
Plan = collections.namedtuple("Plan", plan_fields + ["together", "fixed", "group"])


def up(size, step):
    return -(-size // step) * step


def edge_bits(rows):
    bits = rows.bit_length() - 1
    return bits, [place for place in range(2, bits) if place % 2 == bits % 2]


def near_edge(block, ring):
    rows = block.shape[0]
    bits, fixed = edge_bits(rows)
    tail = block.shape[1:]
    picked = block.reshape((2,) * bits + tail)
    for place in fixed:
        picked = lax.dynamic_index_in_dim(picked, 1 - ring, axis=bits - 1 - place, keepdims=True)
    return picked.reshape((rows >> len(fixed),) + tail)


def edge_rank(local, rows):
    bits, fixed = edge_bits(rows)
    rank = jnp.zeros_like(local)
    taken = 0
    for place in range(bits):
        if place not in fixed:
            rank = rank + (local // 2**place % 2) * 2**taken
            taken += 1
    return rank


def split(value):
    high = value.astype(jnp.bfloat16)
    low = (value - high.astype(jnp.float32)).astype(jnp.bfloat16)
    return high, low


def three_pass(left, right, dims):
    dot = functools.partial(
        lax.dot_general, dimension_numbers=(dims, ((), ())), preferred_element_type=jnp.float32
    )
    return dot(left[0], right[0]) + (dot(left[0], right[1]) + dot(left[1], right[0]))


def pack_kernel(source_count, field, *refs):
    notes, (out, whole) = refs[:-2], refs[-2:]
    rows = field.shape[0]
    stride = 2 * source_count

    def row_step(row, unused):
        both = jnp.concatenate([field[row, 0], field[row, 1]], axis=0)
        for block in range(half):
            whole[block, pl.ds(pl.multiple_of(row * stride, stride), stride), :] = both[
                :, block * lanes : (block + 1) * lanes
            ]
        return unused

    lax.fori_loop(0, rows, row_step, 0, unroll=8)
    for source in range(source_count):
        for part in range(2):
            for block in range(half):
                out[source, pl.ds(part * half + block, rows, stride=2 * half), :] = whole[
                    block, pl.ds(part * source_count + source, rows, stride=stride), :
                ]
        for note in notes:
            out[source, rows * 2 * half :, :] = note[...]


def pack(field, notes):
    rows, _, source_count, width = field.shape
    length = rows * 2 * half + sum(note.shape[0] for note in notes)
    whole = pl.BlockSpec(memory_space=pltpu.VMEM)
    return pl.pallas_call(
        functools.partial(pack_kernel, source_count),
        out_shape=pltpu.HBM((source_count, length, lanes), jnp.float32),
        in_specs=[whole] * (1 + len(notes)),
        out_specs=whole,
        scratch_shapes=[pltpu.VMEM((half, rows * 2 * source_count, lanes), jnp.float32)],
        name="pack_sources",
    )(field, *notes)


def tile(start):
    return pl.ds(pl.multiple_of(start, 2 * half), 2 * half)


def fine_kernel(plan, size, edge_size, zed, meta, main, *refs):
    edges = refs[: planes if edge_size else 0]
    refs = refs[len(edges) :]
    table, phases, high, low, out, field, moved, shifted, ready, sems = refs
    rows, slots, fine_rows = plan.rows, plan.slots, plan.fine_rows
    own = zed[0]

    def fill(value, place):
        field[place, 0] = value
        field[place, 1] = pltpu.roll(value, half, 0)

    for plane in range(planes):

        def main_step(row, unused, plane=plane):
            fill(main[plane, tile(row * 2 * half), :], plane * size + row)
            return unused

        lax.fori_loop(0, size, main_step, 0, unroll=8)
    for step, edge in enumerate(edges):

        def edge_step(row, unused, step=step, edge=edge):
            fill(edge[tile(row * 2 * half), :], planes * size + (own ^ step) * edge_size + row)
            return unused

        lax.fori_loop(0, edge_size, edge_step, 0, unroll=8)
    blank = jnp.zeros((2 * half, lanes), jnp.float32)
    field[planes * (size + edge_size), 0] = blank
    field[planes * (size + edge_size), 1] = blank

    sub = lax.broadcasted_iota(jnp.int32, (2 * half, lanes), 0)
    dest_count = out.shape[1]
    dest_rows = fine_rows // dest_count

    def plane_step(plane, unused):
        base = (own ^ plane) * plan.stride

        def boxes_step(step, unused):
            boxes = [meta[base + plan.order + step * plan.together + each] for each in range(plan.together)]
            turns = meta[base + plan.turns + step]

            def work(slot_count):
                places = [base + box * slots for box in boxes]
                sums = [[blank, blank] for box in boxes]
                for slot in range(slot_count):
                    for each in range(plan.together):
                        value = field[meta[places[each] + slot]]
                        factor = table[meta[places[each] + plan.kinds + slot]]
                        sums[each][0] += factor * value[0]
                        sums[each][1] += factor * value[1]
                for each in range(plan.together):
                    straight, crossed = sums[each]
                    total = jnp.where(
                        sub < half,
                        straight + pltpu.roll(straight, half, 0),
                        pltpu.roll(crossed, half, 0) - crossed,
                    )
                    moved[boxes[each], 0] = total
                    moved[boxes[each], 1] = pltpu.roll(total, half, 0)

            for turn in range((slots - plan.fixed) // plan.group + 1):
                pl.when(turns == turn)(functools.partial(work, plan.fixed + turn * plan.group))
            return unused

        lax.fori_loop(0, rows // plan.together, boxes_step, 0)

        def fine_step(fine, unused):
            value = moved[meta[base + plan.parent + fine]]
            phase = phases[meta[base + plan.octant + fine]]
            shifted[tile(fine * 2 * half), :] = value[0] * phase[0] + value[1] * phase[1]
            return unused

        lax.fori_loop(0, fine_rows, fine_step, 0, unroll=16)
        width = ready.shape[3]
        left = jnp.concatenate(
            [
                jnp.concatenate(
                    [
                        shifted[pl.ds(part * half + block, fine_rows, stride=2 * half), :]
                        for block in range(half)
                    ],
                    axis=1,
                )
                for part in range(2)
            ],
            axis=0,
        )
        result = three_pass(split(left), (high[...], low[...]), ((1,), (0,)))
        for part in range(2):
            for dest in range(dest_count):
                start = part * fine_rows + dest * dest_rows
                ready[plane, dest, part * dest_rows : (part + 1) * dest_rows, :] = result[
                    start : start + dest_rows, :width
                ]
        spill = result[:fine_rows, width:] + pltpu.roll(result[fine_rows:, width:], half, 1)
        spill = spill.T[: 2 * half]
        for dest in range(dest_count):
            ready[plane, dest, 2 * dest_rows :, :] = jnp.concatenate(
                [
                    spill[:, dest * dest_rows : (dest + 1) * dest_rows],
                    jnp.zeros((2 * half, width - dest_rows), jnp.float32),
                ],
                axis=1,
            )
        pltpu.make_async_copy(ready.at[plane], out.at[plane], sems.at[plane]).start()
        return unused

    lax.fori_loop(0, planes, plane_step, 0)
    for plane in range(planes):
        pltpu.make_async_copy(ready.at[plane], out.at[plane], sems.at[plane]).wait()


def join_kernel(source_count, parts, out, whole):
    dest_rows = out.shape[0]
    dirs = parts.shape[0] // source_count
    over = jnp.concatenate(
        [parts[index, 2 * dest_rows :, :lanes] for index in range(parts.shape[0])], axis=0
    ).T[:dest_rows]
    lane = lax.broadcasted_iota(jnp.int32, (dest_rows, lanes), 1)
    for source in range(source_count):
        for part in range(2):
            turned = []
            for index in range(dirs):
                first = (source * dirs + index) * 2 * half + part * half
                turned.append(pltpu.roll(over, (lanes - rim - first) % lanes, 1))
            for index in range(dirs):
                fix = jnp.where(lane < rim, turned[index - 1], 0.0) + jnp.where(
                    lane >= lanes - rim, turned[(index + 1) % dirs], 0.0
                )
                whole[
                    index, pl.ds(part * source_count + source, dest_rows, stride=2 * source_count), :
                ] = parts[source * dirs + index, part * dest_rows : (part + 1) * dest_rows, :] + fix

    def row_step(row, unused):
        start = pl.multiple_of(row * 2 * source_count, 2 * source_count)
        both = jnp.concatenate(
            [whole[index, pl.ds(start, 2 * source_count), :] for index in range(dirs)], axis=1
        )
        out[row, 0] = both[:source_count]
        out[row, 1] = both[source_count:]
        return unused

    lax.fori_loop(0, dest_rows, row_step, 0, unroll=8)


def per_device(
    coarse_field,
    trans_table,
    partner_ids,
    partner_types,
    partner_count,
    child_count,
    child_octant,
    dir_angles,
    stencil_ids,
    stencil_weights,
):
    rows, _, source_count, kc_dev = coarse_field.shape
    slots = partner_ids.shape[1]
    type_count = trans_table.shape[0]
    fine_rows = child_octant.shape[0]
    ring_count = lax.axis_size("ring")
    dir_count = lax.axis_size("dir")
    zed = lax.axis_index("zed")
    ring = lax.axis_index("ring")
    dir_index = lax.axis_index("dir")
    fine_count = stencil_ids.shape[0] // 4
    kf_dev = fine_count // dir_count
    kc_pad = up(kc_dev, half * lanes)
    kf_pad = up(kf_dev, lanes)
    pad_dirs = kc_pad - kc_dev
    assert source_count == planes and kc_pad == half * lanes
    dest_rows = fine_rows // dir_count

    field = jnp.pad(coarse_field, ((0, 0), (0, 0), (0, 0), (0, pad_dirs)))
    edge_rows = 0
    if ring_count == 2:
        edges = lax.ppermute(near_edge(field, ring), "ring", [(0, 1), (1, 0)])
        edge_rows = edges.shape[0]
    arrived = lax.all_to_all(pack(field, []), "zed", split_axis=0, concat_axis=0, tiled=True)

    plane_of = partner_ids // (ring_count * rows)
    ring_of = partner_ids // rows % ring_count
    local = partner_ids % rows
    live = jnp.arange(slots, dtype=jnp.int32)[None, :] < partner_count[:, None]
    if ring_count == 2:
        size = rows
        place = jnp.where(
            ring_of == ring,
            plane_of * rows + local,
            planes * rows + plane_of * edge_rows + edge_rank(local, rows),
        )
    else:
        size = ring_count * rows
        place = partner_ids
    field_rows = planes * (size + edge_rows)
    place = jnp.where(live, place, field_rows)
    together = 4
    fixed = slots // 2
    group = 5 if (slots - fixed) % 5 == 0 else 1
    index = jnp.arange(rows, dtype=jnp.int32)
    before = (partner_count[None, :] > partner_count[:, None]) | (
        (partner_count[None, :] == partner_count[:, None]) & (index[None, :] < index[:, None])
    )
    rank = jnp.sum(before.astype(jnp.int32), axis=1)
    at_rank = rank[None, :] == index[:, None]
    order = jnp.sum(jnp.where(at_rank, index[None, :], 0), axis=1)
    first = rank[None, :] == index[: rows // together, None] * together
    longest = jnp.sum(jnp.where(first, partner_count[None, :], 0), axis=1)
    turns = jnp.maximum((longest - fixed + group - 1) // group, 0)
    bounds = jnp.sum(jnp.where(index[None, :] <= index[:, None], child_count[None, :], 0), axis=1)
    parent = jnp.sum(
        (bounds[None, :] <= jnp.arange(fine_rows, dtype=jnp.int32)[:, None]).astype(jnp.int32), axis=1
    )
    lists = [
        place.reshape(-1),
        partner_types.reshape(-1),
        parent,
        child_octant,
        order,
        turns,
    ]
    offsets = [sum(one.shape[0] for one in lists[:count]) for count in range(len(lists) + 1)]
    stride = up(offsets[-1], 8 * lanes)
    plan = Plan(rows, slots, fine_rows, stride, *offsets[1:-1], together, fixed, group)
    meta = jnp.pad(jnp.concatenate(lists), (0, stride - offsets[-1])).astype(jnp.float32)
    meta = meta.reshape(stride // lanes, lanes)

    if ring_count == 2:
        notes = pack(edges, [meta])
    else:
        notes = jnp.broadcast_to(meta[None], (planes,) + meta.shape)
    received = []
    for step in range(planes):
        note = lax.dynamic_index_in_dim(notes, zed ^ step, axis=0, keepdims=False)
        if step:
            note = lax.ppermute(note, "zed", [(plane, plane ^ step) for plane in range(planes)])
        received.append(note)
    edge_part = edge_rows * 2 * half
    meta = jnp.concatenate([note[edge_part:] for note in received]).astype(jnp.int32).reshape(-1)
    if ring_count == 2:
        pieces = [arrived] + received
    else:
        pieces = [lax.all_gather(arrived, "ring", axis=1, tiled=True)]

    def blocks(table):
        return jnp.pad(table, ((0, 0), (0, pad_dirs))).reshape(-1, half, lanes)

    def doubled(table, sign):
        return jnp.concatenate([blocks(table), sign * blocks(table)], axis=1)

    table = jnp.pad(trans_table, ((0, 0), (0, 0), (0, pad_dirs))).reshape(-1, 2 * half, lanes)
    angles = lax.dynamic_slice_in_dim(dir_angles, dir_index * kc_dev, kc_dev, axis=1)
    octants = jnp.arange(8, dtype=jnp.int32)
    sign_x = 1.0 - 2.0 * (octants % 2).astype(jnp.float32)
    sign_y = 1.0 - 2.0 * (octants // 2 % 2).astype(jnp.float32)
    sign_z = 1.0 - 2.0 * (octants // 4).astype(jnp.float32)
    unit_x = jnp.sin(angles[0]) * jnp.cos(angles[1])
    unit_y = jnp.sin(angles[0]) * jnp.sin(angles[1])
    unit_z = jnp.cos(angles[0])
    phase = wave_scale * (
        sign_x[:, None] * unit_x[None, :] + sign_y[:, None] * unit_y[None, :] + sign_z[:, None] * unit_z[None, :]
    )
    phases = jnp.concatenate(
        [doubled(jnp.cos(phase), 1.0), doubled(jnp.sin(phase), -1.0)], axis=1
    ).reshape(-1, 2, 2 * half, lanes)

    ids = lax.dynamic_slice_in_dim(stencil_ids, dir_index * kc_dev, kc_dev, axis=0).T
    weights = lax.dynamic_slice_in_dim(stencil_weights, dir_index * kc_dev, kc_dev, axis=0).T

    def interp(targets):
        matrix = jnp.zeros((targets.shape[0], kc_dev), jnp.float32)
        for point in range(ids.shape[0]):
            matrix = matrix + jnp.where(
                ids[point][None, :] == targets[:, None], weights[point][None, :], 0.0
            )
        return jnp.pad(matrix, ((0, 0), (0, pad_dirs)))

    first_fine = dir_index * kf_dev
    own = jnp.arange(kf_dev, dtype=jnp.int32)
    outside = jnp.concatenate(
        [jnp.arange(-rim, 0, dtype=jnp.int32), jnp.arange(kf_dev, kf_dev + rim, dtype=jnp.int32)]
    )
    matrix = jnp.pad(interp(first_fine + own), ((0, kf_pad - kf_dev), (0, 0)))
    spill = interp((first_fine + outside) % fine_count)
    matrices = jnp.concatenate([matrix, jnp.pad(spill, ((0, lanes - half), (0, 0)))], axis=0).T
    rounded = lax.reduce_precision(matrices, 8, 7)
    high = rounded.astype(jnp.bfloat16)
    low = (matrices - rounded).astype(jnp.bfloat16)

    whole = pl.BlockSpec(memory_space=pltpu.VMEM)
    message = (2 * dest_rows + 2 * half, kf_pad)
    local_fine = pl.pallas_call(
        functools.partial(fine_kernel, plan, size, edge_rows),
        out_shape=pltpu.HBM((planes, dir_count) + message, jnp.float32),
        in_specs=[pl.BlockSpec(memory_space=pltpu.SMEM)] * 2 + [whole] * (len(pieces) + 4),
        out_specs=pl.BlockSpec(memory_space=pltpu.HBM),
        scratch_shapes=[
            pltpu.VMEM((field_rows + 1, 2, 2 * half, lanes), jnp.float32),
            pltpu.VMEM((rows, 2, 2 * half, lanes), jnp.float32),
            pltpu.VMEM((fine_rows * 2 * half, lanes), jnp.float32),
            pltpu.VMEM((planes, dir_count) + message, jnp.float32),
            pltpu.SemaphoreType.DMA((planes,)),
        ],
        compiler_params=pltpu.CompilerParams(vmem_limit_bytes=48 * 2**20),
        name="translate_and_interpolate",
    )(zed.reshape(1), meta, *pieces, table, phases, high, low)

    parts = lax.all_to_all(
        local_fine.reshape((planes * dir_count,) + message),
        ("zed", "dir"),
        split_axis=0,
        concat_axis=0,
        tiled=True,
    )
    result = (dest_rows, 2, source_count, fine_count)
    if kf_dev == lanes and planes * dir_count * 2 * half == lanes and dest_rows <= lanes:
        return pl.pallas_call(
            functools.partial(join_kernel, source_count),
            out_shape=jax.ShapeDtypeStruct(result, jnp.float32),
            in_specs=[whole],
            out_specs=whole,
            scratch_shapes=[pltpu.VMEM((dir_count, dest_rows * 2 * source_count, lanes), jnp.float32)],
            name="join_parts",
        )(parts)
    parts = parts.reshape((planes, dir_count) + message)
    main = parts[:, :, : 2 * dest_rows, :kf_dev].reshape(planes, dir_count, 2, dest_rows, kf_dev)
    over = parts[:, :, 2 * dest_rows :, :dest_rows].reshape(planes, dir_count, 2, 2 * rim, dest_rows)
    low = jnp.roll(over[:, :, :, :rim], -1, axis=1)
    high = jnp.roll(over[:, :, :, rim:], 1, axis=1)
    middle = jnp.zeros((planes, dir_count, 2, kf_dev - 2 * rim, dest_rows), jnp.float32)
    fix = jnp.concatenate([high, middle, low], axis=3)
    total = main.transpose(3, 2, 0, 1, 4) + fix.transpose(4, 2, 0, 1, 3)
    return total.reshape(result)


def solution(mesh):
    boxes, dirs = mesh.shape["box"], mesh.shape["dir"]
    fine_mesh = Mesh(mesh.devices.reshape(planes, boxes // planes, dirs), ("zed", "ring", "dir"))
    box = ("zed", "ring")
    placed = (
        P(box, None, None, "dir"),
        P(None, None, "dir"),
        P(box, None),
        P(box, None),
        P(box),
        P(box),
        P(box),
        P(),
        P(),
        P(),
    )
    return jax.shard_map(
        per_device,
        mesh=fine_mesh,
        in_specs=placed,
        out_specs=P(("zed", "ring", "dir"), None, None, None),
        check_vma=False,
    )
```

profile of v0, /device:TPU:0, one launch (start us, length us, event | category | flops | bytes accessed | tf_op | source)
XLA Modules:
  0.0 108.4 jit_solution(16720394442363816576)
XLA Ops:
  0.0 1.7 %constant_dynamic-slice_fusion.1 = f32[2,1,2,1,2,2,2,4,512]{8,7,6,5,4,3,2,1,0:T(4,128)} fusion(f32[2,2,2,2,2,2,2,4,512]{8,7,6,5,4,3,2,1,0:T(4,128)} %bitcast.44, s32[]{:T(128)S(6)} %select_n.165), kind=kLoop, calls=%fused_computation.92 | loop fusion | bytes 524292 | tf_op jit(solution)/shard_map/jit(dynamic_index_in_dim)/dynamic_slice | solution.py:38
  1.7 3.0 %collective-permute-start = (f32[16,2,4,512]{3,2,1,0:T(4,128)}, f32[16,2,4,512]{3,2,1,0:T(4,128)}, u32[]{:S(2)}, u32[]{:S(2)}) collective-permute-start(f32[16,2,4,512]{3,2,1,0:T(4,128)} %bitcast.2), channel_id=1, source_target_pairs={{0,4},{4,0},{1,5},{5,1},{2,6},{6,2},{3,7},{7,3},{8,12},{12,8},{9,1... | collective-permute-start | bytes 786440 | tf_op jit(solution)/shard_map/ppermute | solution.py:284
  4.6 2.6 %pack_sources.3 = f32[4,512,128]{2,1,0:T(8,128)} custom-call(f32[64,2,4,512]{3,2,1,0:T(4,128)} %field.1), custom_call_target="tpu_custom_call" | custom-call | tf_op jit(solution)/shard_map/pack_sources/pallas_call | solution.py:94
  7.2 5.0 %all-to-all-start = ((f32[4,512,128]{2,1,0:T(8,128)}), f32[4,512,128]{2,1,0:T(8,128)S(1)}, u32[]{:S(2)}, u32[]{:S(2)}) async-start(f32[4,512,128]{2,1,0:T(8,128)} %pack_sources.3), calls=%async_computation | async-start | bytes 2097152 | tf_op jit(solution)/shard_map/all_to_all | solution.py:286
  12.3 0.2 convert_reduce_fusion.1
  12.8 0.2 select_reduce_fusion.2
  13.1 0.7 dynamic-slice_bitcast_fusion.5
  14.0 0.1 reshape.186
  14.4 0.9 cosine_multiply_fusion
  15.4 0.2 fusion.29
  15.7 0.6 select_add_fusion
  16.3 0.6 select_add_fusion.1
  16.9 0.6 convert_bitcast_fusion.refs_0_
  17.5 2.3 %reshape.189.refs_4_ = f32[316,8,128]{2,1,0:T(8,128)S(1)} reshape(f32[316,2,512]{2,1,0:T(2,128)} %param.11) | data formatting | bytes 2588672 | tf_op jit(solution)/shard_map/reshape | solution.py:358
  20.0 1.8 %pack_sources.2 = f32[4,168,128]{2,1,0:T(8,128)} custom-call(f32[16,2,4,512]{3,2,1,0:T(4,128)} %collective-permute-done.field, f32[40,128]{1,0:T(8,128)} %convert_bitcast_fusion.refs_0_), custom_call_target="tpu_custom_call" | custom-call | tf_op jit(solution)/shard_map/pack_sources/pallas_call | solution.py:94
  21.8 1.0 dynamic-slice_bitcast_fusion.3
  22.8 3.9 %collective-permute-start.3 = (f32[168,128]{1,0:T(8,128)S(1)}, f32[168,128]{1,0:T(8,128)S(1)}, u32[]{:S(2)}, u32[]{:S(2)}) collective-permute-start(f32[168,128]{1,0:T(8,128)S(1)} %get-tuple-element.8), channel_id=1, source_target_pairs={{0,24},{8,16},{16,8},{24,0},{1,25},{9,17},{17,9},{25,1},{2,26},{10... | collective-permute-start | bytes 258056 | tf_op jit(solution)/shard_map/ppermute | solution.py:343
  26.7 0.6 collective-permute-start.1
  27.3 0.7 dynamic-slice_bitcast_fusion.4
  28.1 8.6 %collective-permute-done.3.refs_3_ = f32[168,128]{1,0:T(8,128)S(1)} collective-permute-done((f32[168,128]{1,0:T(8,128)S(1)}, f32[168,128]{1,0:T(8,128)S(1)}, u32[]{:S(2)}, u32[]{:S(2)}) %collective-permute-start.3) | collective-permute-done | bytes 86048 | tf_op jit(solution)/shard_map/ppermute | solution.py:343
  36.6 8.4 %collective-permute-done.2.refs_2_ = f32[168,128]{1,0:T(8,128)S(1)} collective-permute-done((f32[168,128]{1,0:T(8,128)S(1)}, f32[168,128]{1,0:T(8,128)S(1)}, u32[]{:S(2)}, u32[]{:S(2)}) %collective-permute-start.2) | collective-permute-done | bytes 86048 | tf_op jit(solution)/shard_map/ppermute | solution.py:343
  45.1 27.6 %translate_and_interpolate.1 = f32[4,4,136,128]{3,2,1,0:T(8,128)} custom-call(s32[1]{0:T(128)} %bitcast.zed, s32[20480]{0:T(1024)S(1)} %fusion.2.meta, f32[4,512,128]{2,1,0:T(8,128)S(1)} %all-to-all-done.main, f32[168,128]{1,0:T(8,128)S(1)} %get-tuple-element.7.refs_0_, f32[168,128]{1,0:T(8,128)S(1)} %collective-permute-done.1.refs_1_, ...), custom_call_target="tpu_custom_call" | custom-call | tf_op jit(solution)/shard_map/translate_and_interpolate/pallas_call | solution.py:399
  72.8 32.9 %all_to_all.10.parts = f32[16,136,128]{2,1,0:T(8,128)} all-to-all(f32[16,136,128]{2,1,0:T(8,128)} %bitcast.43), channel_id=1, replica_groups=mesh['zed'=4,'ring'=2,'dir'=4] {'zed','dir'}, dimensions={0} | all-to-all | bytes 2228224 | tf_op jit(solution)/shard_map/all_to_all | solution.py:415
  105.6 2.8 %join_parts.1 = f32[64,2,4,512]{3,2,1,0:T(4,128)} custom-call(f32[16,136,128]{2,1,0:T(8,128)} %all_to_all.10.parts), custom_call_target="tpu_custom_call" | custom-call | tf_op jit(solution)/shard_map/join_parts/pallas_call | solution.py:424
  (41 shorter events, 1.1 us)
Async XLA Ops:
  0.0 13.0 %copy-start = (s32[2048,4]{0,1:T(4,128)S(1)}, s32[2048,4]{0,1:T(4,128)}, u32[]{:S(2)}) copy-start(s32[2048,4]{0,1:T(4,128)} %param.18) | copy-start | bytes 98308
  1.7 18.3 %collective-permute-start = (f32[16,2,4,512]{3,2,1,0:T(4,128)}, f32[16,2,4,512]{3,2,1,0:T(4,128)}, u32[]{:S(2)}, u32[]{:S(2)}) collective-permute-start(f32[16,2,4,512]{3,2,1,0:T(4,128)} %bitcast.2), channel_id=1, source_target_pairs={{0,4},{4,0},{1,5},{5,1},{2,6},{6,2},{3,7},{7,3},{8,12},{12,8},{9,1... | collective-permute-start | bytes 786440 | tf_op jit(solution)/shard_map/ppermute | solution.py:284
  7.2 5.1 %copy-start.3 = (s32[64]{0:T(128)S(1)}, s32[64]{0:T(128)}, u32[]{:S(2)}) copy-start(s32[64]{0:T(128)} %param.14) | copy-start | bytes 772
  7.2 5.4 %copy-start.5 = (s32[64]{0:T(128)S(1)}, s32[64]{0:T(128)}, u32[]{:S(2)}) copy-start(s32[64]{0:T(128)} %param.15) | copy-start | bytes 772
  7.2 6.6 %copy-start.2 = (s32[64,30]{0,1:T(8,128)S(1)}, s32[64,30]{0,1:T(8,128)}, u32[]{:S(2)}) copy-start(s32[64,30]{0,1:T(8,128)} %param.12) | copy-start | bytes 23044
  7.2 6.9 %copy-start.1 = (s32[64,30]{0,1:T(8,128)S(1)}, s32[64,30]{0,1:T(8,128)}, u32[]{:S(2)}) copy-start(s32[64,30]{0,1:T(8,128)} %param.13) | copy-start | bytes 23044
  7.2 8.1 %copy-start.4 = (s32[256]{0:T(256)S(1)}, s32[256]{0:T(256)}, u32[]{:S(2)}) copy-start(s32[256]{0:T(256)} %param.16) | copy-start | bytes 3076
  7.2 37.9 %all-to-all-start = ((f32[4,512,128]{2,1,0:T(8,128)}), f32[4,512,128]{2,1,0:T(8,128)S(1)}, u32[]{:S(2)}, u32[]{:S(2)}) async-start(f32[4,512,128]{2,1,0:T(8,128)} %pack_sources.3), calls=%async_computation | async-start | bytes 2097152 | tf_op jit(solution)/shard_map/all_to_all | solution.py:286
  22.8 13.8 %collective-permute-start.3 = (f32[168,128]{1,0:T(8,128)S(1)}, f32[168,128]{1,0:T(8,128)S(1)}, u32[]{:S(2)}, u32[]{:S(2)}) collective-permute-start(f32[168,128]{1,0:T(8,128)S(1)} %get-tuple-element.8), channel_id=1, source_target_pairs={{0,24},{8,16},{16,8},{24,0},{1,25},{9,17},{17,9},{25,1},{2,26},{10... | collective-permute-start | bytes 258056 | tf_op jit(solution)/shard_map/ppermute | solution.py:343
  26.7 18.4 %collective-permute-start.2 = (f32[168,128]{1,0:T(8,128)S(1)}, f32[168,128]{1,0:T(8,128)S(1)}, u32[]{:S(2)}, u32[]{:S(2)}) collective-permute-start(f32[168,128]{1,0:T(8,128)S(1)} %get-tuple-element.9), channel_id=1, source_target_pairs={{0,16},{8,24},{16,0},{24,8},{1,17},{9,25},{17,1},{25,9},{2,18},{10... | collective-permute-start | bytes 258056 | tf_op jit(solution)/shard_map/ppermute | solution.py:343
  26.7 18.4 %collective-permute-start.1 = (f32[168,128]{1,0:T(8,128)S(1)}, f32[168,128]{1,0:T(8,128)S(1)}, u32[]{:S(2)}, u32[]{:S(2)}) collective-permute-start(f32[168,128]{1,0:T(8,128)S(1)} %get-tuple-element.10), channel_id=1, source_target_pairs={{0,8},{8,0},{16,24},{24,16},{1,9},{9,1},{17,25},{25,17},{2,10},{10... | collective-permute-start | bytes 258056 | tf_op jit(solution)/shard_map/ppermute | solution.py:343
where the time goes:
time: 109 us; the launch traced here: 108 us
  Pallas kernels  34.8 us (32%)
  blocking collectives  32.9 us (30%)
  waiting for transfers between devices  17 us (16%)
  starting transfers between devices  12.5 us (11%)
  local copies, waits for them, and re-layouts  7.04 us (6%)
  other arithmetic  3.94 us (4%)
    all_to_all x1, blocking collectives, per_device(): lax.all_to_all(local_fine.reshape((planes * dir_count,) + message), ('zed...  32.9 us
    pallas_call x1, Pallas kernels, per_device(): pl.pallas_call(functools.partial(fine_kernel, plan, size, edge_rows), out...  27.6 us
    ppermute x3, waiting for transfers between devices, per_device(): lax.ppermute(note, 'zed', [(plane, plane ^ step) for plane in range(plane...  17 us
    all_to_all x1, starting transfers between devices, per_device(): lax.all_to_all(pack(field, []), 'zed', split_axis=0, concat_axis=0, tiled...  5.01 us
    ppermute x3, starting transfers between devices, per_device(): lax.ppermute(note, 'zed', [(plane, plane ^ step) for plane in range(plane...  4.53 us
    pallas_call x2, Pallas kernels, pack(): pl.pallas_call(functools.partial(pack_kernel, source_count), out_shape=pl...  4.37 us
    ppermute x1, starting transfers between devices, per_device(): edges = lax.ppermute(near_edge(field, ring), 'ring', [(0, 1), (1, 0)])  2.97 us
    pallas_call x1, Pallas kernels, per_device(): pl.pallas_call(functools.partial(join_kernel, source_count), out_shape=ja...  2.8 us
  transfers between devices with their start and end apart: 5, of which 2 were waited for; matrix products, arithmetic and copies ran while one was open for 9% of the time, Pallas kernels for 4%

commit v1 on v0

--- a/solution.py
+++ b/solution.py
@@ -109,31 +109,34 @@
     edges = refs[: planes if edge_size else 0]
     refs = refs[len(edges) :]
     table, phases, high, low, out, field, moved, shifted, ready, sems = refs
-    rows, slots, fine_rows = plan.rows, plan.slots, plan.fine_rows
+    rows, fine_rows = plan.rows, plan.fine_rows
     own = zed[0]
 
-    def fill(value, place):
-        field[place, 0] = value
-        field[place, 1] = pltpu.roll(value, half, 0)
+    def both(start):
+        return pl.ds(pl.multiple_of(start, 4 * half), 4 * half)
+
+    def with_turned(value):
+        return jnp.concatenate([value, pltpu.roll(value, half, 0)], axis=0)
 
     for plane in range(planes):
 
         def main_step(row, unused, plane=plane):
-            fill(main[plane, tile(row * 2 * half), :], plane * size + row)
+            value = main[plane, tile(row * 2 * half), :]
+            field[both((plane * size + row) * 4 * half), :] = with_turned(value)
             return unused
 
         lax.fori_loop(0, size, main_step, 0, unroll=8)
     for step, edge in enumerate(edges):
-
-        def edge_step(row, unused, step=step, edge=edge):
-            fill(edge[tile(row * 2 * half), :], planes * size + (own ^ step) * edge_size + row)
+        first = planes * size + (own ^ step) * edge_size
+
+        def edge_step(row, unused, first=first, edge=edge):
+            field[both((first + row) * 4 * half), :] = with_turned(edge[tile(row * 2 * half), :])
             return unused
 
         lax.fori_loop(0, edge_size, edge_step, 0, unroll=8)
+    field[both(planes * (size + edge_size) * 4 * half), :] = jnp.zeros((4 * half, lanes), jnp.float32)
+
     blank = jnp.zeros((2 * half, lanes), jnp.float32)
-    field[planes * (size + edge_size), 0] = blank
-    field[planes * (size + edge_size), 1] = blank
-
     sub = lax.broadcasted_iota(jnp.int32, (2 * half, lanes), 0)
     dest_count = out.shape[1]
     dest_rows = fine_rows // dest_count
@@ -142,18 +145,19 @@
         base = (own ^ plane) * plan.stride
 
         def boxes_step(step, unused):
-            boxes = [meta[base + plan.order + step * plan.together + each] for each in range(plan.together)]
-            turns = meta[base + plan.turns + step]
+            ranks = [step * plan.together + each for each in range(plan.together)]
+            boxes = [meta[base + plan.order, rank] for rank in ranks]
+            turns = meta[base + plan.order, plan.turns + step]
 
             def work(slot_count):
-                places = [base + box * slots for box in boxes]
+                places = [base + box for box in boxes]
                 sums = [[blank, blank] for box in boxes]
                 for slot in range(slot_count):
                     for each in range(plan.together):
-                        value = field[meta[places[each] + slot]]
-                        factor = table[meta[places[each] + plan.kinds + slot]]
-                        sums[each][0] += factor * value[0]
-                        sums[each][1] += factor * value[1]
+                        value = field[both(meta[places[each], slot]), :]
+                        factor = table[tile(meta[places[each], plan.kinds + slot]), :]
+                        sums[each][0] += factor * value[: 2 * half]
+                        sums[each][1] += factor * value[2 * half :]
                 for each in range(plan.together):
                     straight, crossed = sums[each]
                     total = jnp.where(
@@ -161,22 +165,23 @@
                         straight + pltpu.roll(straight, half, 0),
                         pltpu.roll(crossed, half, 0) - crossed,
                     )
-                    moved[boxes[each], 0] = total
-                    moved[boxes[each], 1] = pltpu.roll(total, half, 0)
-
-            for turn in range((slots - plan.fixed) // plan.group + 1):
+                    moved[both(boxes[each] * 4 * half), :] = with_turned(total)
+
+            for turn in range((plan.slots - plan.fixed) // plan.group + 1):
                 pl.when(turns == turn)(functools.partial(work, plan.fixed + turn * plan.group))
             return unused
 
         lax.fori_loop(0, rows // plan.together, boxes_step, 0)
 
-        def fine_step(fine, unused):
-            value = moved[meta[base + plan.parent + fine]]
-            phase = phases[meta[base + plan.octant + fine]]
-            shifted[tile(fine * 2 * half), :] = value[0] * phase[0] + value[1] * phase[1]
+        def fine_step(block, unused):
+            for each in range(lanes):
+                value = moved[both(meta[base + plan.parent + block, each]), :]
+                phase = phases[both(meta[base + plan.octant + block, each]), :]
+                value = value * phase
+                shifted[tile((block * lanes + each) * 2 * half), :] = value[: 2 * half] + value[2 * half :]
             return unused
 
-        lax.fori_loop(0, fine_rows, fine_step, 0, unroll=16)
+        lax.fori_loop(0, fine_rows // lanes, fine_step, 0)
         width = ready.shape[3]
         left = jnp.concatenate(
             [
@@ -279,11 +284,13 @@
     dest_rows = fine_rows // dir_count
 
     field = jnp.pad(coarse_field, ((0, 0), (0, 0), (0, 0), (0, pad_dirs)))
+    packed = pack(field, [])
     edge_rows = 0
     if ring_count == 2:
+        packed, field = lax.optimization_barrier((packed, field))
         edges = lax.ppermute(near_edge(field, ring), "ring", [(0, 1), (1, 0)])
         edge_rows = edges.shape[0]
-    arrived = lax.all_to_all(pack(field, []), "zed", split_axis=0, concat_axis=0, tiled=True)
+    arrived = lax.all_to_all(packed, "zed", split_axis=0, concat_axis=0, tiled=True)
 
     plane_of = partner_ids // (ring_count * rows)
     ring_of = partner_ids // rows % ring_count
@@ -318,19 +325,24 @@
     parent = jnp.sum(
         (bounds[None, :] <= jnp.arange(fine_rows, dtype=jnp.int32)[:, None]).astype(jnp.int32), axis=1
     )
+    def across(one, width=lanes):
+        return jnp.pad(one, ((0, 0), (0, width - one.shape[1])))
+
+    kinds_at = up(slots, lanes // 2)
+    turns_at = lanes // 2
+    assert 2 * kinds_at <= lanes and rows <= turns_at and fine_rows % lanes == 0
     lists = [
-        place.reshape(-1),
-        partner_types.reshape(-1),
-        parent,
-        child_octant,
-        order,
-        turns,
+        jnp.concatenate(
+            [across(place * 4 * half, kinds_at), across(partner_types * 2 * half, lanes - kinds_at)], axis=1
+        ),
+        (parent * 4 * half).reshape(-1, lanes),
+        (child_octant * 4 * half).reshape(-1, lanes),
+        across(jnp.concatenate([across(order[None], turns_at), turns[None]], axis=1)),
     ]
     offsets = [sum(one.shape[0] for one in lists[:count]) for count in range(len(lists) + 1)]
-    stride = up(offsets[-1], 8 * lanes)
-    plan = Plan(rows, slots, fine_rows, stride, *offsets[1:-1], together, fixed, group)
-    meta = jnp.pad(jnp.concatenate(lists), (0, stride - offsets[-1])).astype(jnp.float32)
-    meta = meta.reshape(stride // lanes, lanes)
+    stride = up(offsets[-1], 8)
+    plan = Plan(rows, slots, fine_rows, stride, kinds_at, *offsets[1:-1], turns_at, together, fixed, group)
+    meta = jnp.pad(jnp.concatenate(lists), ((0, stride - offsets[-1]), (0, 0))).astype(jnp.float32)
 
     if ring_count == 2:
         notes = pack(edges, [meta])
@@ -343,7 +355,7 @@
             note = lax.ppermute(note, "zed", [(plane, plane ^ step) for plane in range(planes)])
         received.append(note)
     edge_part = edge_rows * 2 * half
-    meta = jnp.concatenate([note[edge_part:] for note in received]).astype(jnp.int32).reshape(-1)
+    meta = jnp.concatenate([note[edge_part:] for note in received]).astype(jnp.int32)
     if ring_count == 2:
         pieces = [arrived] + received
     else:
@@ -355,7 +367,7 @@
     def doubled(table, sign):
         return jnp.concatenate([blocks(table), sign * blocks(table)], axis=1)
 
-    table = jnp.pad(trans_table, ((0, 0), (0, 0), (0, pad_dirs))).reshape(-1, 2 * half, lanes)
+    table = jnp.pad(trans_table, ((0, 0), (0, 0), (0, pad_dirs))).reshape(-1, lanes)
     angles = lax.dynamic_slice_in_dim(dir_angles, dir_index * kc_dev, kc_dev, axis=1)
     octants = jnp.arange(8, dtype=jnp.int32)
     sign_x = 1.0 - 2.0 * (octants % 2).astype(jnp.float32)
@@ -369,7 +381,7 @@
     )
     phases = jnp.concatenate(
         [doubled(jnp.cos(phase), 1.0), doubled(jnp.sin(phase), -1.0)], axis=1
-    ).reshape(-1, 2, 2 * half, lanes)
+    ).reshape(-1, lanes)
 
     ids = lax.dynamic_slice_in_dim(stencil_ids, dir_index * kc_dev, kc_dev, axis=0).T
     weights = lax.dynamic_slice_in_dim(stencil_weights, dir_index * kc_dev, kc_dev, axis=0).T
@@ -402,8 +414,8 @@
         in_specs=[pl.BlockSpec(memory_space=pltpu.SMEM)] * 2 + [whole] * (len(pieces) + 4),
         out_specs=pl.BlockSpec(memory_space=pltpu.HBM),
         scratch_shapes=[
-            pltpu.VMEM((field_rows + 1, 2, 2 * half, lanes), jnp.float32),
-            pltpu.VMEM((rows, 2, 2 * half, lanes), jnp.float32),
+            pltpu.VMEM(((field_rows + 1) * 4 * half, lanes), jnp.float32),
+            pltpu.VMEM((rows * 4 * half, lanes), jnp.float32),
             pltpu.VMEM((fine_rows * 2 * half, lanes), jnp.float32),
             pltpu.VMEM((planes, dir_count) + message, jnp.float32),
             pltpu.SemaphoreType.DMA((planes,)),
@@ -427,6 +439,7 @@
             in_specs=[whole],
             out_specs=whole,
             scratch_shapes=[pltpu.VMEM((dir_count, dest_rows * 2 * source_count, lanes), jnp.float32)],
+            compiler_params=pltpu.CompilerParams(vmem_limit_bytes=24 * 2**20),
             name="join_parts",
         )(parts)
     parts = parts.reshape((planes, dir_count) + message)

time: 109 us -> 102 us (0.936)
  Pallas kernels: 34.8 us -> 30.3 us
  waiting for transfers between devices: 17 us -> 15.6 us
    pallas_call x1, Pallas kernels: 27.6 us -> 24.4 us  [per_device(): pl.pallas_call(functools.partial(fine_kernel, plan, size, edge_rows), out...]
    ppermute x3, waiting for transfers between devices: 17 us -> 15.6 us  [per_device(): lax.ppermute(note, 'zed', [(plane, plane ^ step) for plane in range(plane...]
    ppermute x1, starting transfers between devices: 2.97 us -> 1.52 us  [per_device(): edges = lax.ppermute(near_edge(field, ring), 'ring', [(0, 1), (1, 0)])]
    all_to_all x1, starting transfers between devices: 5.01 us -> 6.46 us  [per_device(): lax.all_to_all(packed, 'zed', split_axis=0, concat_axis=0, tiled=True)]
    pallas_call x1, Pallas kernels: 2.8 us -> 1.55 us  [per_device(): pl.pallas_call(functools.partial(join_kernel, source_count), out_shape=ja...]
    reshape x3 -> x1, local copies, waits for them, and re-layouts: 2.58 us -> 2.31 us  [per_device(): jnp.pad(trans_table, ((0, 0), (0, 0), (0, pad_dirs))).reshape(-1, lanes)]
  transfers between devices with their start and end apart: 5 -> 5, of which waited for: 2 -> 2; matrix products, arithmetic and copies ran while one was open for 9% -> 11% of each run, Pallas kernels for 4% -> 2%
where the time goes in v1:
time: 102 us
  blocking collectives  32.3 us (32%)
  Pallas kernels  30.3 us (30%)
  waiting for transfers between devices  15.6 us (15%)
  starting transfers between devices  12.5 us (12%)
  local copies, waits for them, and re-layouts  6.77 us (7%)
  other arithmetic  4.19 us (4%)
    all_to_all x1, blocking collectives, per_device(): lax.all_to_all(local_fine.reshape((planes * dir_count,) + message), ('zed...  32.3 us
    pallas_call x1, Pallas kernels, per_device(): pl.pallas_call(functools.partial(fine_kernel, plan, size, edge_rows), out...  24.4 us
    ppermute x3, waiting for transfers between devices, per_device(): lax.ppermute(note, 'zed', [(plane, plane ^ step) for plane in range(plane...  15.6 us
    all_to_all x1, starting transfers between devices, per_device(): lax.all_to_all(packed, 'zed', split_axis=0, concat_axis=0, tiled=True)  6.46 us
    ppermute x3, starting transfers between devices, per_device(): lax.ppermute(note, 'zed', [(plane, plane ^ step) for plane in range(plane...  4.53 us
    pallas_call x2, Pallas kernels, pack(): pl.pallas_call(functools.partial(pack_kernel, source_count), out_shape=pl...  4.38 us
    reshape x1, local copies, waits for them, and re-layouts, per_device(): jnp.pad(trans_table, ((0, 0), (0, 0), (0, pad_dirs))).reshape(-1, lanes)  2.31 us
  transfers between devices with their start and end apart: 5, of which 2 were waited for; matrix products, arithmetic and copies ran while one was open for 11% of the time, Pallas kernels for 2%

profile of v1, /device:TPU:0, one launch (start us, length us, event | category | flops | bytes accessed | tf_op | source)
XLA Modules:
  0.0 101.9 jit_solution(13491484320386032658)
XLA Ops:
  0.0 2.6 %pack_sources.2 = f32[4,512,128]{2,1,0:T(8,128)} custom-call(f32[64,2,4,512]{3,2,1,0:T(4,128)} %field.1), custom_call_target="tpu_custom_call" | custom-call | tf_op jit(solution)/shard_map/pack_sources/pallas_call | solution.py:94
  2.6 6.5 %all-to-all-start = ((f32[4,512,128]{2,1,0:T(8,128)}), f32[4,512,128]{2,1,0:T(8,128)S(1)}, u32[]{:S(2)}, u32[]{:S(2)}) async-start(f32[4,512,128]{2,1,0:T(8,128)} %pack_sources.2), calls=%async_computation | async-start | bytes 2097152 | tf_op jit(solution)/shard_map/all_to_all | solution.py:293
  9.1 1.7 %constant_dynamic-slice_fusion.1 = f32[2,1,2,1,2,2,2,4,512]{8,7,6,5,4,3,2,1,0:T(4,128)} fusion(f32[2,2,2,2,2,2,2,4,512]{8,7,6,5,4,3,2,1,0:T(4,128)} %bitcast.53, s32[]{:T(128)S(6)} %select_n.172), kind=kLoop, calls=%fused_computation.97 | loop fusion | bytes 524292 | tf_op jit(solution)/shard_map/jit(dynamic_index_in_dim)/dynamic_slice | solution.py:38
  10.7 1.5 %collective-permute-start = (f32[16,2,4,512]{3,2,1,0:T(4,128)}, f32[16,2,4,512]{3,2,1,0:T(4,128)}, u32[]{:S(2)}, u32[]{:S(2)}) collective-permute-start(f32[16,2,4,512]{3,2,1,0:T(4,128)} %bitcast.2), channel_id=1, source_target_pairs={{0,4},{4,0},{1,5},{5,1},{2,6},{6,2},{3,7},{7,3},{8,12},{12,8},{9,1... | collective-permute-start | bytes 786440 | tf_op jit(solution)/shard_map/ppermute | solution.py:291
  12.3 0.2 convert_reduce_fusion.1
  12.8 0.2 select_reduce_fusion.2
  13.1 0.7 dynamic-slice_bitcast_fusion.5
  14.1 0.9 cosine_multiply_fusion
  15.1 0.2 fusion.13
  15.3 0.2 fusion.31
  15.5 0.6 select_add_fusion
  16.2 0.6 select_add_fusion.1
  16.8 0.6 pad_convert_fusion.refs_0_
  17.4 2.3 %reshape.229.refs_4_ = f32[2528,128]{1,0:T(8,128)S(1)} reshape(f32[316,2,512]{2,1,0:T(2,128)} %param.11) | data formatting | bytes 2588672 | tf_op jit(solution)/shard_map/reshape | solution.py:370
  19.8 1.8 %pack_sources.3 = f32[4,200,128]{2,1,0:T(8,128)} custom-call(f32[16,2,4,512]{3,2,1,0:T(4,128)} %collective-permute-done.field, f32[72,128]{1,0:T(8,128)} %pad_convert_fusion.refs_0_), custom_call_target="tpu_custom_call" | custom-call | tf_op jit(solution)/shard_map/pack_sources/pallas_call | solution.py:94
  21.6 1.1 %dynamic-slice_bitcast_fusion.3 = (f32[200,128]{1,0:T(8,128)S(1)}, f32[200,128]{1,0:T(8,128)S(1)}, f32[200,128]{1,0:T(8,128)S(1)}, f32[200,128]{1,0:T(8,128)S(1)}) fusion(f32[4,200,128]{2,1,0:T(8,128)} %pack_sources.3, s32[]{:T(128)S(6)} %select_n.190, s32[]{:T(128)S(6)} %select_n.193, s32[]{:T(128)S(6)} %select_n.192, s32[]{:T(128)S(6)} %select_n.191), kind=kLoop, calls=%fused_computation.12 | loop fusion | bytes 819216 | tf_op jit(solution)/shard_map/jit(dynamic_index_in_dim)/squeeze | solution.py:353
  22.7 3.9 %collective-permute-start.3 = (f32[200,128]{1,0:T(8,128)S(1)}, f32[200,128]{1,0:T(8,128)S(1)}, u32[]{:S(2)}, u32[]{:S(2)}) collective-permute-start(f32[200,128]{1,0:T(8,128)S(1)} %get-tuple-element.12), channel_id=1, source_target_pairs={{0,24},{8,16},{16,8},{24,0},{1,25},{9,17},{17,9},{25,1},{2,26},{10... | collective-permute-start | bytes 307208 | tf_op jit(solution)/shard_map/ppermute | solution.py:355
  26.6 0.6 collective-permute-start.1
  27.2 0.8 dynamic-slice_bitcast_fusion.4
  28.0 5.8 %collective-permute-done.3.refs_3_ = f32[200,128]{1,0:T(8,128)S(1)} collective-permute-done((f32[200,128]{1,0:T(8,128)S(1)}, f32[200,128]{1,0:T(8,128)S(1)}, u32[]{:S(2)}, u32[]{:S(2)}) %collective-permute-start.3) | collective-permute-done | bytes 102432 | tf_op jit(solution)/shard_map/ppermute | solution.py:355
  33.8 9.8 %collective-permute-done.2.refs_2_ = f32[200,128]{1,0:T(8,128)S(1)} collective-permute-done((f32[200,128]{1,0:T(8,128)S(1)}, f32[200,128]{1,0:T(8,128)S(1)}, u32[]{:S(2)}, u32[]{:S(2)}) %collective-permute-start.2) | collective-permute-done | bytes 102432 | tf_op jit(solution)/shard_map/ppermute | solution.py:355
  43.6 24.4 %translate_and_interpolate.1 = f32[4,4,136,128]{3,2,1,0:T(8,128)} custom-call(s32[1]{0:T(128)} %bitcast.zed, s32[288,128]{1,0:T(8,128)S(1)} %maximum_convert_fusion.meta, f32[4,512,128]{2,1,0:T(8,128)S(1)} %all-to-all-done.main, f32[200,128]{1,0:T(8,128)S(1)} %get-tuple-element.11.refs_0_, f32[200,128]{1,0:T(8,128)S(1)} %collective-permute-done.1.refs_1_, ...), custom_call_target="tpu_custom_call" | custom-call | tf_op jit(solution)/shard_map/translate_and_interpolate/pallas_call | solution.py:411
  68.0 32.3 %all_to_all.10.parts = f32[16,136,128]{2,1,0:T(8,128)S(1)} all-to-all(f32[16,136,128]{2,1,0:T(8,128)} %bitcast.52), channel_id=1, replica_groups=mesh['zed'=4,'ring'=2,'dir'=4] {'zed','dir'}, dimensions={0} | all-to-all | bytes 2228224 | tf_op jit(solution)/shard_map/all_to_all | solution.py:427
  100.4 1.5 %join_parts.1 = f32[64,2,4,512]{3,2,1,0:T(4,128)} custom-call(f32[16,136,128]{2,1,0:T(8,128)S(1)} %all_to_all.10.parts), custom_call_target="tpu_custom_call" | custom-call | tf_op jit(solution)/shard_map/join_parts/pallas_call | solution.py:436
  (41 shorter events, 1.0 us)
Async XLA Ops:
  0.0 13.0 %copy-start = (s32[2048,4]{0,1:T(4,128)S(1)}, s32[2048,4]{0,1:T(4,128)}, u32[]{:S(2)}) copy-start(s32[2048,4]{0,1:T(4,128)} %param.18) | copy-start | bytes 98308
  2.6 9.7 %copy-start.3 = (s32[64]{0:T(128)S(1)}, s32[64]{0:T(128)}, u32[]{:S(2)}) copy-start(s32[64]{0:T(128)} %param.14) | copy-start | bytes 772
  2.6 10.0 %copy-start.5 = (s32[64]{0:T(128)S(1)}, s32[64]{0:T(128)}, u32[]{:S(2)}) copy-start(s32[64]{0:T(128)} %param.15) | copy-start | bytes 772
  2.6 11.2 %copy-start.1 = (s32[64,30]{0,1:T(8,128)S(1)}, s32[64,30]{0,1:T(8,128)}, u32[]{:S(2)}) copy-start(s32[64,30]{0,1:T(8,128)} %param.12) | copy-start | bytes 23044
  2.6 11.3 %copy-start.2 = (s32[64,30]{0,1:T(8,128)S(1)}, s32[64,30]{0,1:T(8,128)}, u32[]{:S(2)}) copy-start(s32[64,30]{0,1:T(8,128)} %param.13) | copy-start | bytes 23044
  2.6 11.5 %copy-start.4 = (s32[256]{0:T(256)S(1)}, s32[256]{0:T(256)}, u32[]{:S(2)}) copy-start(s32[256]{0:T(256)} %param.16) | copy-start | bytes 3076
  2.6 41.0 %all-to-all-start = ((f32[4,512,128]{2,1,0:T(8,128)}), f32[4,512,128]{2,1,0:T(8,128)S(1)}, u32[]{:S(2)}, u32[]{:S(2)}) async-start(f32[4,512,128]{2,1,0:T(8,128)} %pack_sources.2), calls=%async_computation | async-start | bytes 2097152 | tf_op jit(solution)/shard_map/all_to_all | solution.py:293
  10.7 9.1 %collective-permute-start = (f32[16,2,4,512]{3,2,1,0:T(4,128)}, f32[16,2,4,512]{3,2,1,0:T(4,128)}, u32[]{:S(2)}, u32[]{:S(2)}) collective-permute-start(f32[16,2,4,512]{3,2,1,0:T(4,128)} %bitcast.2), channel_id=1, source_target_pairs={{0,4},{4,0},{1,5},{5,1},{2,6},{6,2},{3,7},{7,3},{8,12},{12,8},{9,1... | collective-permute-start | bytes 786440 | tf_op jit(solution)/shard_map/ppermute | solution.py:291
  22.7 11.1 %collective-permute-start.3 = (f32[200,128]{1,0:T(8,128)S(1)}, f32[200,128]{1,0:T(8,128)S(1)}, u32[]{:S(2)}, u32[]{:S(2)}) collective-permute-start(f32[200,128]{1,0:T(8,128)S(1)} %get-tuple-element.12), channel_id=1, source_target_pairs={{0,24},{8,16},{16,8},{24,0},{1,25},{9,17},{17,9},{25,1},{2,26},{10... | collective-permute-start | bytes 307208 | tf_op jit(solution)/shard_map/ppermute | solution.py:355
  26.6 17.0 %collective-permute-start.2 = (f32[200,128]{1,0:T(8,128)S(1)}, f32[200,128]{1,0:T(8,128)S(1)}, u32[]{:S(2)}, u32[]{:S(2)}) collective-permute-start(f32[200,128]{1,0:T(8,128)S(1)} %get-tuple-element.13), channel_id=1, source_target_pairs={{0,16},{8,24},{16,0},{24,8},{1,17},{9,25},{17,1},{25,9},{2,18},{10... | collective-permute-start | bytes 307208 | tf_op jit(solution)/shard_map/ppermute | solution.py:355
  26.6 17.0 %collective-permute-start.1 = (f32[200,128]{1,0:T(8,128)S(1)}, f32[200,128]{1,0:T(8,128)S(1)}, u32[]{:S(2)}, u32[]{:S(2)}) collective-permute-start(f32[200,128]{1,0:T(8,128)S(1)} %get-tuple-element.14), channel_id=1, source_target_pairs={{0,8},{8,0},{16,24},{24,16},{1,9},{9,1},{17,25},{25,17},{2,10},{10... | collective-permute-start | bytes 307208 | tf_op jit(solution)/shard_map/ppermute | solution.py:355

commit v2 on v1

--- a/solution.py
+++ b/solution.py
@@ -105,12 +105,19 @@
     return pl.ds(pl.multiple_of(start, 2 * half), 2 * half)
 
 
-def fine_kernel(plan, size, edge_size, zed, meta, main, *refs):
+def fine_kernel(plan, size, edge_size, zed, lists, main, *refs):
     edges = refs[: planes if edge_size else 0]
     refs = refs[len(edges) :]
-    table, phases, high, low, out, field, moved, shifted, ready, sems = refs
+    table, phases, high, low, out, rims, meta, field, moved, shifted, ready, sems = refs
     rows, fine_rows = plan.rows, plan.fine_rows
     own = zed[0]
+
+    def bring(step):
+        return pltpu.make_async_copy(lists.at[step], meta.at[step % 2], sems.at[planes + step % 2])
+
+    bring(0).start()
+    lane = lax.broadcasted_iota(jnp.int32, rims.shape, 1)
+    rims[...] = ((lane < rim) | (lane >= lanes - rim)).astype(jnp.float32)
 
     def both(start):
         return pl.ds(pl.multiple_of(start, 4 * half), 4 * half)
@@ -141,21 +148,27 @@
     dest_count = out.shape[1]
     dest_rows = fine_rows // dest_count
 
-    def plane_step(plane, unused):
-        base = (own ^ plane) * plan.stride
+    def plane_step(turn, unused):
+        plane = own ^ turn
+        slot = turn % 2
+        bring(turn).wait()
+
+        @pl.when(turn + 1 < planes)
+        def _():
+            bring(turn + 1).start()
+
 
         def boxes_step(step, unused):
             ranks = [step * plan.together + each for each in range(plan.together)]
-            boxes = [meta[base + plan.order, rank] for rank in ranks]
-            turns = meta[base + plan.order, plan.turns + step]
+            boxes = [meta[slot, plan.order, rank] for rank in ranks]
+            turns = meta[slot, plan.order, plan.turns + step]
 
             def work(slot_count):
-                places = [base + box for box in boxes]
                 sums = [[blank, blank] for box in boxes]
-                for slot in range(slot_count):
+                for pair in range(slot_count):
                     for each in range(plan.together):
-                        value = field[both(meta[places[each], slot]), :]
-                        factor = table[tile(meta[places[each], plan.kinds + slot]), :]
+                        value = field[both(meta[slot, boxes[each], pair]), :]
+                        factor = table[tile(meta[slot, boxes[each], plan.kinds + pair]), :]
                         sums[each][0] += factor * value[: 2 * half]
                         sums[each][1] += factor * value[2 * half :]
                 for each in range(plan.together):
@@ -167,16 +180,16 @@
                     )
                     moved[both(boxes[each] * 4 * half), :] = with_turned(total)
 
-            for turn in range((plan.slots - plan.fixed) // plan.group + 1):
-                pl.when(turns == turn)(functools.partial(work, plan.fixed + turn * plan.group))
+            for more in range((plan.slots - plan.fixed) // plan.group + 1):
+                pl.when(turns == more)(functools.partial(work, plan.fixed + more * plan.group))
             return unused
 
         lax.fori_loop(0, rows // plan.together, boxes_step, 0)
 
         def fine_step(block, unused):
             for each in range(lanes):
-                value = moved[both(meta[base + plan.parent + block, each]), :]
-                phase = phases[both(meta[base + plan.octant + block, each]), :]
+                value = moved[both(meta[slot, plan.parent + block, each]), :]
+                phase = phases[both(meta[slot, plan.octant + block, each]), :]
                 value = value * phase
                 shifted[tile((block * lanes + each) * 2 * half), :] = value[: 2 * half] + value[2 * half :]
             return unused
@@ -221,13 +234,14 @@
         pltpu.make_async_copy(ready.at[plane], out.at[plane], sems.at[plane]).wait()
 
 
-def join_kernel(source_count, parts, out, whole):
+def join_kernel(source_count, parts, rims, out, whole):
     dest_rows = out.shape[0]
     dirs = parts.shape[0] // source_count
     over = jnp.concatenate(
         [parts[index, 2 * dest_rows :, :lanes] for index in range(parts.shape[0])], axis=0
     ).T[:dest_rows]
-    lane = lax.broadcasted_iota(jnp.int32, (dest_rows, lanes), 1)
+    low = lax.broadcasted_iota(jnp.int32, (dest_rows, lanes), 1) < rim
+    at_rim = jnp.broadcast_to(rims[...], (dest_rows, lanes)) < 0.5
     for source in range(source_count):
         for part in range(2):
             turned = []
@@ -235,9 +249,7 @@
                 first = (source * dirs + index) * 2 * half + part * half
                 turned.append(pltpu.roll(over, (lanes - rim - first) % lanes, 1))
             for index in range(dirs):
-                fix = jnp.where(lane < rim, turned[index - 1], 0.0) + jnp.where(
-                    lane >= lanes - rim, turned[(index + 1) % dirs], 0.0
-                )
+                fix = jnp.where(at_rim, jnp.where(low, turned[index - 1], turned[(index + 1) % dirs]), 0.0)
                 whole[
                     index, pl.ds(part * source_count + source, dest_rows, stride=2 * source_count), :
                 ] = parts[source * dirs + index, part * dest_rows : (part + 1) * dest_rows, :] + fix
@@ -328,20 +340,23 @@
     def across(one, width=lanes):
         return jnp.pad(one, ((0, 0), (0, width - one.shape[1])))
 
-    kinds_at = up(slots, lanes // 2)
+    kinds_at = slots
+    width = up(2 * slots, lanes // 2)
     turns_at = lanes // 2
-    assert 2 * kinds_at <= lanes and rows <= turns_at and fine_rows % lanes == 0
+    packed_rows = rows * width // lanes
+    assert width <= lanes and rows <= turns_at and fine_rows % lanes == 0
+    pair_list = across(jnp.concatenate([place * 4 * half, partner_types * 2 * half], axis=1), width)
     lists = [
-        jnp.concatenate(
-            [across(place * 4 * half, kinds_at), across(partner_types * 2 * half, lanes - kinds_at)], axis=1
-        ),
+        pair_list.reshape(packed_rows, lanes),
         (parent * 4 * half).reshape(-1, lanes),
         (child_octant * 4 * half).reshape(-1, lanes),
         across(jnp.concatenate([across(order[None], turns_at), turns[None]], axis=1)),
     ]
     offsets = [sum(one.shape[0] for one in lists[:count]) for count in range(len(lists) + 1)]
     stride = up(offsets[-1], 8)
-    plan = Plan(rows, slots, fine_rows, stride, kinds_at, *offsets[1:-1], turns_at, together, fixed, group)
+    shift = rows - packed_rows
+    places = [offset + shift for offset in offsets[1:-1]]
+    plan = Plan(rows, slots, fine_rows, stride + shift, kinds_at, *places, turns_at, together, fixed, group)
     meta = jnp.pad(jnp.concatenate(lists), ((0, stride - offsets[-1]), (0, 0))).astype(jnp.float32)
 
     if ring_count == 2:
@@ -355,7 +370,10 @@
             note = lax.ppermute(note, "zed", [(plane, plane ^ step) for plane in range(planes)])
         received.append(note)
     edge_part = edge_rows * 2 * half
-    meta = jnp.concatenate([note[edge_part:] for note in received]).astype(jnp.int32)
+    meta = jnp.stack([note[edge_part:] for note in received]).astype(jnp.int32)
+    pair_list = meta[:, :packed_rows].reshape(planes, rows, width)
+    pair_list = jnp.pad(pair_list, ((0, 0), (0, 0), (0, lanes - width)))
+    meta = jnp.concatenate([pair_list, meta[:, packed_rows:]], axis=1)
     if ring_count == 2:
         pieces = [arrived] + received
     else:
@@ -408,17 +426,22 @@
 
     whole = pl.BlockSpec(memory_space=pltpu.VMEM)
     message = (2 * dest_rows + 2 * half, kf_pad)
-    local_fine = pl.pallas_call(
+    local_fine, rims = pl.pallas_call(
         functools.partial(fine_kernel, plan, size, edge_rows),
-        out_shape=pltpu.HBM((planes, dir_count) + message, jnp.float32),
-        in_specs=[pl.BlockSpec(memory_space=pltpu.SMEM)] * 2 + [whole] * (len(pieces) + 4),
-        out_specs=pl.BlockSpec(memory_space=pltpu.HBM),
+        out_shape=[
+            pltpu.HBM((planes, dir_count) + message, jnp.float32),
+            jax.ShapeDtypeStruct((2 * half, lanes), jnp.float32),
+        ],
+        in_specs=[pl.BlockSpec(memory_space=pltpu.SMEM), pl.BlockSpec(memory_space=pl.ANY)]
+        + [whole] * (len(pieces) + 4),
+        out_specs=[pl.BlockSpec(memory_space=pltpu.HBM), whole],
         scratch_shapes=[
+            pltpu.SMEM((2, plan.stride, lanes), jnp.int32),
             pltpu.VMEM(((field_rows + 1) * 4 * half, lanes), jnp.float32),
             pltpu.VMEM((rows * 4 * half, lanes), jnp.float32),
             pltpu.VMEM((fine_rows * 2 * half, lanes), jnp.float32),
             pltpu.VMEM((planes, dir_count) + message, jnp.float32),
-            pltpu.SemaphoreType.DMA((planes,)),
+            pltpu.SemaphoreType.DMA((planes + 2,)),
         ],
         compiler_params=pltpu.CompilerParams(vmem_limit_bytes=48 * 2**20),
         name="translate_and_interpolate",
@@ -436,12 +459,12 @@
         return pl.pallas_call(
             functools.partial(join_kernel, source_count),
             out_shape=jax.ShapeDtypeStruct(result, jnp.float32),
-            in_specs=[whole],
+            in_specs=[whole] * 2,
             out_specs=whole,
             scratch_shapes=[pltpu.VMEM((dir_count, dest_rows * 2 * source_count, lanes), jnp.float32)],
             compiler_params=pltpu.CompilerParams(vmem_limit_bytes=24 * 2**20),
             name="join_parts",
-        )(parts)
+        )(parts, 1.0 - rims[:1])
     parts = parts.reshape((planes, dir_count) + message)
     main = parts[:, :, : 2 * dest_rows, :kf_dev].reshape(planes, dir_count, 2, dest_rows, kf_dev)
     over = parts[:, :, 2 * dest_rows :, :dest_rows].reshape(planes, dir_count, 2, 2 * rim, dest_rows)

time: 102 us -> 98.2 us (0.963)
  the two profiles are of different devices: /device:TPU:0 before, /device:TPU:11 now
where the time goes in v2:
time: 98.2 us; the launch traced here: 97.2 us
  waiting for transfers between devices  38.4 us (39%)
  Pallas kernels  28.3 us (29%)
  starting transfers between devices  17.8 us (18%)
  local copies, waits for them, and re-layouts  7.44 us (8%)
  other arithmetic  4.96 us (5%)
    all_to_all x1, waiting for transfers between devices, per_device(): lax.all_to_all(local_fine.reshape((planes * dir_count,) + message), ('zed...  26.3 us
    pallas_call x1, Pallas kernels, per_device(): pl.pallas_call(functools.partial(fine_kernel, plan, size, edge_rows), out...  22.4 us
    ppermute x3, waiting for transfers between devices, per_device(): lax.ppermute(note, 'zed', [(plane, plane ^ step) for plane in range(plane...  12 us
    all_to_all x1, starting transfers between devices, per_device(): lax.all_to_all(local_fine.reshape((planes * dir_count,) + message), ('zed...  8.33 us
    all_to_all x1, starting transfers between devices, per_device(): lax.all_to_all(packed, 'zed', split_axis=0, concat_axis=0, tiled=True)  4.9 us
    pallas_call x2, Pallas kernels, pack(): pl.pallas_call(functools.partial(pack_kernel, source_count), out_shape=pl...  4.36 us
    ppermute x3, starting transfers between devices, per_device(): lax.ppermute(note, 'zed', [(plane, plane ^ step) for plane in range(plane...  3.33 us
    reshape x1, local copies, waits for them, and re-layouts, per_device(): jnp.pad(trans_table, ((0, 0), (0, 0), (0, pad_dirs))).reshape(-1, lanes)  2.31 us
  transfers between devices with their start and end apart: 6, of which 2 were waited for; matrix products, arithmetic and copies ran while one was open for 13% of the time, Pallas kernels for 2%

profile of v2, /device:TPU:11, one launch (start us, length us, event | category | flops | bytes accessed | tf_op | source)
XLA Modules:
  0.0 97.2 jit_solution(114635031445465898)
XLA Ops:
  0.0 2.6 %pack_sources.2 = f32[4,512,128]{2,1,0:T(8,128)} custom-call(f32[64,2,4,512]{3,2,1,0:T(4,128)} %field.1), custom_call_target="tpu_custom_call" | custom-call | tf_op jit(solution)/shard_map/pack_sources/pallas_call | solution.py:94
  2.6 4.9 %all-to-all-start = ((f32[4,512,128]{2,1,0:T(8,128)}), f32[4,512,128]{2,1,0:T(8,128)S(1)}, u32[]{:S(2)}, u32[]{:S(2)}) async-start(f32[4,512,128]{2,1,0:T(8,128)} %pack_sources.2), calls=%async_computation | async-start | bytes 2097152 | tf_op jit(solution)/shard_map/all_to_all | solution.py:305
  7.5 1.7 %constant_dynamic-slice_fusion.2 = f32[2,1,2,1,2,2,2,4,512]{8,7,6,5,4,3,2,1,0:T(4,128)} fusion(f32[2,2,2,2,2,2,2,4,512]{8,7,6,5,4,3,2,1,0:T(4,128)} %bitcast.56, s32[]{:T(128)S(6)} %select_n.172), kind=kLoop, calls=%fused_computation.100 | loop fusion | bytes 524292 | tf_op jit(solution)/shard_map/jit(dynamic_index_in_dim)/dynamic_slice | solution.py:38
  9.2 1.2 %collective-permute-start = (f32[16,2,4,512]{3,2,1,0:T(4,128)}, f32[16,2,4,512]{3,2,1,0:T(4,128)}, u32[]{:S(2)}, u32[]{:S(2)}) collective-permute-start(f32[16,2,4,512]{3,2,1,0:T(4,128)} %bitcast.2), channel_id=1, source_target_pairs={{0,4},{4,0},{1,5},{5,1},{2,6},{6,2},{3,7},{7,3},{8,12},{12,8},{9,1... | collective-permute-start | bytes 786440 | tf_op jit(solution)/shard_map/ppermute | solution.py:303
  11.3 0.7 dynamic-slice_bitcast_fusion.4
  12.4 0.6 select_add_fusion
  13.0 0.6 select_add_fusion.1
  13.7 0.9 cosine_multiply_fusion
  14.6 0.2 fusion.29
  14.8 0.6 pad_convert_fusion.refs_0_
  15.4 2.3 %reshape.238.refs_4_ = f32[2528,128]{1,0:T(8,128)S(1)} reshape(f32[316,2,512]{2,1,0:T(2,128)} %param.11) | data formatting | bytes 2588672 | tf_op jit(solution)/shard_map/reshape | solution.py:388
  17.9 1.8 %pack_sources.3 = f32[4,168,128]{2,1,0:T(8,128)} custom-call(f32[16,2,4,512]{3,2,1,0:T(4,128)} %collective-permute-done.field, f32[40,128]{1,0:T(8,128)} %pad_convert_fusion.refs_0_), custom_call_target="tpu_custom_call" | custom-call | tf_op jit(solution)/shard_map/pack_sources/pallas_call | solution.py:94
  19.7 1.0 %dynamic-slice_bitcast_fusion.3 = (f32[168,128]{1,0:T(8,128)S(1)}, f32[168,128]{1,0:T(8,128)S(1)}, f32[168,128]{1,0:T(8,128)S(1)}, f32[168,128]{1,0:T(8,128)S(1)}) fusion(f32[4,168,128]{2,1,0:T(8,128)} %pack_sources.3, s32[]{:T(128)S(6)} %select_n.190, s32[]{:T(128)S(6)} %select_n.193, s32[]{:T(128)S(6)} %select_n.192, s32[]{:T(128)S(6)} %select_n.191), kind=kLoop, calls=%fused_computation.12 | loop fusion | bytes 688144 | tf_op jit(solution)/shard_map/jit(dynamic_index_in_dim)/squeeze | solution.py:368
  20.7 1.2 %collective-permute-start.3 = (f32[168,128]{1,0:T(8,128)S(1)}, f32[168,128]{1,0:T(8,128)S(1)}, u32[]{:S(2)}, u32[]{:S(2)}) collective-permute-start(f32[168,128]{1,0:T(8,128)S(1)} %get-tuple-element.16), channel_id=1, source_target_pairs={{0,24},{8,16},{16,8},{24,0},{1,25},{9,17},{17,9},{25,1},{2,26},{10... | collective-permute-start | bytes 258056 | tf_op jit(solution)/shard_map/ppermute | solution.py:370
  22.0 1.0 %collective-permute-start.2 = (f32[168,128]{1,0:T(8,128)S(1)}, f32[168,128]{1,0:T(8,128)S(1)}, u32[]{:S(2)}, u32[]{:S(2)}) collective-permute-start(f32[168,128]{1,0:T(8,128)S(1)} %get-tuple-element.17), channel_id=1, source_target_pairs={{0,16},{8,24},{16,0},{24,8},{1,17},{9,25},{17,1},{25,9},{2,18},{10... | collective-permute-start | bytes 258056 | tf_op jit(solution)/shard_map/ppermute | solution.py:370
  22.9 1.1 %collective-permute-start.1 = (f32[168,128]{1,0:T(8,128)S(1)}, f32[168,128]{1,0:T(8,128)S(1)}, u32[]{:S(2)}, u32[]{:S(2)}) collective-permute-start(f32[168,128]{1,0:T(8,128)S(1)} %get-tuple-element.18), channel_id=1, source_target_pairs={{0,8},{8,0},{16,24},{24,16},{1,9},{9,1},{17,25},{25,17},{2,10},{10... | collective-permute-start | bytes 258056 | tf_op jit(solution)/shard_map/ppermute | solution.py:370
  24.0 0.7 constant_dynamic-slice_fusion.1
  24.8 12.0 %collective-permute-done.3.refs_3_ = f32[168,128]{1,0:T(8,128)S(1)} collective-permute-done((f32[168,128]{1,0:T(8,128)S(1)}, f32[168,128]{1,0:T(8,128)S(1)}, u32[]{:S(2)}, u32[]{:S(2)}) %collective-permute-start.3) | collective-permute-done | bytes 86048 | tf_op jit(solution)/shard_map/ppermute | solution.py:370
  36.9 0.7 reshape.237
  37.6 0.9 pad_add_fusion.lists
  38.5 22.4 %translate_and_interpolate.1 = (f32[4,4,136,128]{3,2,1,0:T(8,128)}, f32[8,128]{1,0:T(8,128)S(1)}) custom-call(s32[1]{0:T(128)} %bitcast.zed, s32[4,72,128]{2,1,0:T(8,128)S(1)} %pad_add_fusion.lists, f32[4,512,128]{2,1,0:T(8,128)S(1)} %all-to-all-done.main, f32[168,128]{1,0:T(8,128)S(1)} %get-tuple-element.15.refs_0_, ...), custom_call_target="tpu_custom_call" | custom-call | tf_op jit(solution)/shard_map/translate_and_interpolate/pallas_call | solution.py:429
  60.9 8.3 %all-to-all-start.1 = ((f32[16,136,128]{2,1,0:T(8,128)}), f32[16,136,128]{2,1,0:T(8,128)S(1)}, u32[]{:S(2)}, u32[]{:S(2)}) async-start(f32[16,136,128]{2,1,0:T(8,128)} %bitcast.57), calls=%async_computation.1 | async-start | bytes 2228224 | tf_op jit(solution)/shard_map/all_to_all | solution.py:450
  69.3 26.3 %all-to-all-done.1.parts = f32[16,136,128]{2,1,0:T(8,128)S(1)} async-done(((f32[16,136,128]{2,1,0:T(8,128)}), f32[16,136,128]{2,1,0:T(8,128)S(1)}, u32[]{:S(2)}, u32[]{:S(2)}) %all-to-all-start.1) | async-done | bytes 1114144 | tf_op jit(solution)/shard_map/all_to_all | solution.py:450
  95.6 1.5 %join_parts.1 = f32[64,2,4,512]{3,2,1,0:T(4,128)} custom-call(f32[16,136,128]{2,1,0:T(8,128)S(1)} %all-to-all-done.1.parts, f32[1,128]{1,0:T(1,128)S(1)} %slice_subtract_fusion.rims), custom_call_target="tpu_custom_call" | custom-call | tf_op jit(solution)/shard_map/join_parts/pallas_call | solution.py:459
  (49 shorter events, 1.3 us)
Async XLA Ops:
  0.0 11.2 %copy-start = (s32[2048,4]{0,1:T(4,128)S(1)}, s32[2048,4]{0,1:T(4,128)}, u32[]{:S(2)}) copy-start(s32[2048,4]{0,1:T(4,128)} %param.18) | copy-start | bytes 98308
  2.6 7.9 %copy-start.3 = (s32[64]{0:T(128)S(1)}, s32[64]{0:T(128)}, u32[]{:S(2)}) copy-start(s32[64]{0:T(128)} %param.14) | copy-start | bytes 772
  2.6 8.2 %copy-start.5 = (s32[64]{0:T(128)S(1)}, s32[64]{0:T(128)}, u32[]{:S(2)}) copy-start(s32[64]{0:T(128)} %param.15) | copy-start | bytes 772
  2.6 9.4 %copy-start.1 = (s32[64,30]{0,1:T(8,128)S(1)}, s32[64,30]{0,1:T(8,128)}, u32[]{:S(2)}) copy-start(s32[64,30]{0,1:T(8,128)} %param.12) | copy-start | bytes 23044
  2.6 9.4 %copy-start.2 = (s32[64,30]{0,1:T(8,128)S(1)}, s32[64,30]{0,1:T(8,128)}, u32[]{:S(2)}) copy-start(s32[64,30]{0,1:T(8,128)} %param.13) | copy-start | bytes 23044
  2.6 35.9 %all-to-all-start = ((f32[4,512,128]{2,1,0:T(8,128)}), f32[4,512,128]{2,1,0:T(8,128)S(1)}, u32[]{:S(2)}, u32[]{:S(2)}) async-start(f32[4,512,128]{2,1,0:T(8,128)} %pack_sources.2), calls=%async_computation | async-start | bytes 2097152 | tf_op jit(solution)/shard_map/all_to_all | solution.py:305
  7.5 6.2 %copy-start.4 = (s32[256]{0:T(256)S(1)}, s32[256]{0:T(256)}, u32[]{:S(2)}) copy-start(s32[256]{0:T(256)} %param.16) | copy-start | bytes 3076
  9.2 8.7 %collective-permute-start = (f32[16,2,4,512]{3,2,1,0:T(4,128)}, f32[16,2,4,512]{3,2,1,0:T(4,128)}, u32[]{:S(2)}, u32[]{:S(2)}) collective-permute-start(f32[16,2,4,512]{3,2,1,0:T(4,128)} %bitcast.2), channel_id=1, source_target_pairs={{0,4},{4,0},{1,5},{5,1},{2,6},{6,2},{3,7},{7,3},{8,12},{12,8},{9,1... | collective-permute-start | bytes 786440 | tf_op jit(solution)/shard_map/ppermute | solution.py:303
  20.7 16.1 %collective-permute-start.3 = (f32[168,128]{1,0:T(8,128)S(1)}, f32[168,128]{1,0:T(8,128)S(1)}, u32[]{:S(2)}, u32[]{:S(2)}) collective-permute-start(f32[168,128]{1,0:T(8,128)S(1)} %get-tuple-element.16), channel_id=1, source_target_pairs={{0,24},{8,16},{16,8},{24,0},{1,25},{9,17},{17,9},{25,1},{2,26},{10... | collective-permute-start | bytes 258056 | tf_op jit(solution)/shard_map/ppermute | solution.py:370
  22.0 14.8 %collective-permute-start.2 = (f32[168,128]{1,0:T(8,128)S(1)}, f32[168,128]{1,0:T(8,128)S(1)}, u32[]{:S(2)}, u32[]{:S(2)}) collective-permute-start(f32[168,128]{1,0:T(8,128)S(1)} %get-tuple-element.17), channel_id=1, source_target_pairs={{0,16},{8,24},{16,0},{24,8},{1,17},{9,25},{17,1},{25,9},{2,18},{10... | collective-permute-start | bytes 258056 | tf_op jit(solution)/shard_map/ppermute | solution.py:370
  22.9 13.9 %collective-permute-start.1 = (f32[168,128]{1,0:T(8,128)S(1)}, f32[168,128]{1,0:T(8,128)S(1)}, u32[]{:S(2)}, u32[]{:S(2)}) collective-permute-start(f32[168,128]{1,0:T(8,128)S(1)} %get-tuple-element.18), channel_id=1, source_target_pairs={{0,8},{8,0},{16,24},{24,16},{1,9},{9,1},{17,25},{25,17},{2,10},{10... | collective-permute-start | bytes 258056 | tf_op jit(solution)/shard_map/ppermute | solution.py:370
  60.9 34.7 %all-to-all-start.1 = ((f32[16,136,128]{2,1,0:T(8,128)}), f32[16,136,128]{2,1,0:T(8,128)S(1)}, u32[]{:S(2)}, u32[]{:S(2)}) async-start(f32[16,136,128]{2,1,0:T(8,128)} %bitcast.57), calls=%async_computation.1 | async-start | bytes 2228224 | tf_op jit(solution)/shard_map/all_to_all | solution.py:450

commit v3 on v2

--- a/solution.py
+++ b/solution.py
@@ -105,19 +105,27 @@
     return pl.ds(pl.multiple_of(start, 2 * half), 2 * half)
 
 
-def fine_kernel(plan, size, edge_size, zed, lists, main, *refs):
-    edges = refs[: planes if edge_size else 0]
-    refs = refs[len(edges) :]
-    table, phases, high, low, out, rims, meta, field, moved, shifted, ready, sems = refs
+def fine_kernel(plan, size, edge_size, steps, filled, here, lists, *refs):
+    if filled:
+        field, refs = refs[0], refs[1:]
+        inputs = 0
+    else:
+        inputs = 1 + (planes if edge_size else 0)
+        main, edges, refs = refs[0], refs[1:inputs], refs[inputs:]
+    table, phases, high, low, refs = refs[0], refs[1], refs[2], refs[3], refs[4:]
+    if not filled:
+        field, refs = refs[0], refs[1:]
+    outs, (meta, moved, shifted, ready, spilled, sems) = refs[:-6], refs[-6:]
     rows, fine_rows = plan.rows, plan.fine_rows
-    own = zed[0]
-
-    def bring(step):
-        return pltpu.make_async_copy(lists.at[step], meta.at[step % 2], sems.at[planes + step % 2])
-
-    bring(0).start()
-    lane = lax.broadcasted_iota(jnp.int32, rims.shape, 1)
-    rims[...] = ((lane < rim) | (lane >= lanes - rim)).astype(jnp.float32)
+    own, own_dir = here[0], here[1]
+    dest_count = len(outs) // len(steps)
+    dest_rows = fine_rows // dest_count
+
+    def bring(turn):
+        return pltpu.make_async_copy(lists.at[steps[turn]], meta.at[turn], sems.at[turn])
+
+    for turn in range(len(steps)):
+        bring(turn).start()
 
     def both(start):
         return pl.ds(pl.multiple_of(start, 4 * half), 4 * half)
@@ -125,38 +133,30 @@
     def with_turned(value):
         return jnp.concatenate([value, pltpu.roll(value, half, 0)], axis=0)
 
-    for plane in range(planes):
-
-        def main_step(row, unused, plane=plane):
-            value = main[plane, tile(row * 2 * half), :]
-            field[both((plane * size + row) * 4 * half), :] = with_turned(value)
-            return unused
-
-        lax.fori_loop(0, size, main_step, 0, unroll=8)
-    for step, edge in enumerate(edges):
-        first = planes * size + (own ^ step) * edge_size
-
-        def edge_step(row, unused, first=first, edge=edge):
-            field[both((first + row) * 4 * half), :] = with_turned(edge[tile(row * 2 * half), :])
-            return unused
-
-        lax.fori_loop(0, edge_size, edge_step, 0, unroll=8)
-    field[both(planes * (size + edge_size) * 4 * half), :] = jnp.zeros((4 * half, lanes), jnp.float32)
+    if not filled:
+        for plane in range(planes):
+
+            def main_step(row, unused, plane=plane):
+                value = main[plane, tile(row * 2 * half), :]
+                field[both((plane * size + row) * 4 * half), :] = with_turned(value)
+                return unused
+
+            lax.fori_loop(0, size, main_step, 0, unroll=8)
+        for step, edge in enumerate(edges):
+            first = planes * size + (own ^ step) * edge_size
+
+            def edge_step(row, unused, first=first, edge=edge):
+                field[both((first + row) * 4 * half), :] = with_turned(edge[tile(row * 2 * half), :])
+                return unused
+
+            lax.fori_loop(0, edge_size, edge_step, 0, unroll=8)
+        field[both(planes * (size + edge_size) * 4 * half), :] = jnp.zeros((4 * half, lanes), jnp.float32)
 
     blank = jnp.zeros((2 * half, lanes), jnp.float32)
     sub = lax.broadcasted_iota(jnp.int32, (2 * half, lanes), 0)
-    dest_count = out.shape[1]
-    dest_rows = fine_rows // dest_count
-
-    def plane_step(turn, unused):
-        plane = own ^ turn
-        slot = turn % 2
-        bring(turn).wait()
-
-        @pl.when(turn + 1 < planes)
-        def _():
-            bring(turn + 1).start()
-
+
+    for slot in range(len(steps)):
+        bring(slot).wait()
 
         def boxes_step(step, unused):
             ranks = [step * plan.together + each for each in range(plan.together)]
@@ -195,7 +195,6 @@
             return unused
 
         lax.fori_loop(0, fine_rows // lanes, fine_step, 0)
-        width = ready.shape[3]
         left = jnp.concatenate(
             [
                 jnp.concatenate(
@@ -210,49 +209,45 @@
             axis=0,
         )
         result = three_pass(split(left), (high[...], low[...]), ((1,), (0,)))
+        width = ready.shape[1]
+        ready[...] = result[:, :width]
+        spilled[...] = result[:fine_rows, width:] + pltpu.roll(result[fine_rows:, width:], half, 1)
+        for dest in range(dest_count):
+            out = outs[slot * dest_count + dest]
+            start = (own_dir ^ dest) * dest_rows
+            for part in range(2):
+                chosen = pl.ds(pl.multiple_of(part * fine_rows + start, dest_rows), dest_rows)
+                out[part * dest_rows : (part + 1) * dest_rows, :] = ready[chosen, :]
+            spill = spilled[pl.ds(pl.multiple_of(start, dest_rows), dest_rows), :].T[: 2 * half]
+            blank_part = jnp.zeros((2 * half, width - dest_rows), jnp.float32)
+            out[2 * dest_rows :, :] = jnp.concatenate([spill, blank_part], axis=1)
+
+
+def join_kernel(source_count, here, *refs):
+    parts, (out, whole, over) = refs[:-3], refs[-3:]
+    dest_rows = out.shape[0]
+    dirs = len(parts) // source_count
+    low = lax.broadcasted_iota(jnp.int32, (dest_rows, lanes), 1) < rim
+    high = lax.broadcasted_iota(jnp.int32, (dest_rows, lanes), 1) >= lanes - rim
+    for index, part_ref in enumerate(parts):
+        source = here[0] ^ (index // dirs)
+        block = here[1] ^ (index % dirs)
+        over[tile((source * dirs + block) * 2 * half), :] = part_ref[2 * dest_rows :, :]
         for part in range(2):
-            for dest in range(dest_count):
-                start = part * fine_rows + dest * dest_rows
-                ready[plane, dest, part * dest_rows : (part + 1) * dest_rows, :] = result[
-                    start : start + dest_rows, :width
-                ]
-        spill = result[:fine_rows, width:] + pltpu.roll(result[fine_rows:, width:], half, 1)
-        spill = spill.T[: 2 * half]
-        for dest in range(dest_count):
-            ready[plane, dest, 2 * dest_rows :, :] = jnp.concatenate(
-                [
-                    spill[:, dest * dest_rows : (dest + 1) * dest_rows],
-                    jnp.zeros((2 * half, width - dest_rows), jnp.float32),
-                ],
-                axis=1,
-            )
-        pltpu.make_async_copy(ready.at[plane], out.at[plane], sems.at[plane]).start()
-        return unused
-
-    lax.fori_loop(0, planes, plane_step, 0)
-    for plane in range(planes):
-        pltpu.make_async_copy(ready.at[plane], out.at[plane], sems.at[plane]).wait()
-
-
-def join_kernel(source_count, parts, rims, out, whole):
-    dest_rows = out.shape[0]
-    dirs = parts.shape[0] // source_count
-    over = jnp.concatenate(
-        [parts[index, 2 * dest_rows :, :lanes] for index in range(parts.shape[0])], axis=0
-    ).T[:dest_rows]
-    low = lax.broadcasted_iota(jnp.int32, (dest_rows, lanes), 1) < rim
-    at_rim = jnp.broadcast_to(rims[...], (dest_rows, lanes)) < 0.5
+            whole[block, pl.ds(part * source_count + source, dest_rows, stride=2 * source_count), :] = part_ref[
+                part * dest_rows : (part + 1) * dest_rows, :
+            ]
+    spill = over[...].T[:dest_rows]
     for source in range(source_count):
         for part in range(2):
             turned = []
             for index in range(dirs):
                 first = (source * dirs + index) * 2 * half + part * half
-                turned.append(pltpu.roll(over, (lanes - rim - first) % lanes, 1))
+                turned.append(pltpu.roll(spill, (lanes - rim - first) % lanes, 1))
             for index in range(dirs):
-                fix = jnp.where(at_rim, jnp.where(low, turned[index - 1], turned[(index + 1) % dirs]), 0.0)
-                whole[
-                    index, pl.ds(part * source_count + source, dest_rows, stride=2 * source_count), :
-                ] = parts[source * dirs + index, part * dest_rows : (part + 1) * dest_rows, :] + fix
+                place = pl.ds(part * source_count + source, dest_rows, stride=2 * source_count)
+                fix = jnp.where(low, turned[index - 1], jnp.where(high, turned[(index + 1) % dirs], 0.0))
+                whole[index, place, :] = whole[index, place, :] + fix
 
     def row_step(row, unused):
         start = pl.multiple_of(row * 2 * source_count, 2 * source_count)
@@ -359,21 +354,22 @@
     plan = Plan(rows, slots, fine_rows, stride + shift, kinds_at, *places, turns_at, together, fixed, group)
     meta = jnp.pad(jnp.concatenate(lists), ((0, stride - offsets[-1]), (0, 0))).astype(jnp.float32)
 
-    if ring_count == 2:
-        notes = pack(edges, [meta])
-    else:
-        notes = jnp.broadcast_to(meta[None], (planes,) + meta.shape)
-    received = []
-    for step in range(planes):
-        note = lax.dynamic_index_in_dim(notes, zed ^ step, axis=0, keepdims=False)
-        if step:
-            note = lax.ppermute(note, "zed", [(plane, plane ^ step) for plane in range(planes)])
-        received.append(note)
-    edge_part = edge_rows * 2 * half
-    meta = jnp.stack([note[edge_part:] for note in received]).astype(jnp.int32)
+    def to_planes(note, step):
+        if step == 0:
+            return note
+        return lax.ppermute(note, "zed", [(plane, plane ^ step) for plane in range(planes)])
+
+    meta = jnp.stack([to_planes(meta, step) for step in range(planes)]).astype(jnp.int32)
     pair_list = meta[:, :packed_rows].reshape(planes, rows, width)
     pair_list = jnp.pad(pair_list, ((0, 0), (0, 0), (0, lanes - width)))
     meta = jnp.concatenate([pair_list, meta[:, packed_rows:]], axis=1)
+    received = []
+    if ring_count == 2:
+        notes = pack(edges, [])
+        received = [
+            to_planes(lax.dynamic_index_in_dim(notes, zed ^ step, axis=0, keepdims=False), step)
+            for step in range(planes)
+        ]
     if ring_count == 2:
         pieces = [arrived] + received
     else:
@@ -426,45 +422,68 @@
 
     whole = pl.BlockSpec(memory_space=pltpu.VMEM)
     message = (2 * dest_rows + 2 * half, kf_pad)
-    local_fine, rims = pl.pallas_call(
-        functools.partial(fine_kernel, plan, size, edge_rows),
-        out_shape=[
-            pltpu.HBM((planes, dir_count) + message, jnp.float32),
-            jax.ShapeDtypeStruct((2 * half, lanes), jnp.float32),
-        ],
-        in_specs=[pl.BlockSpec(memory_space=pltpu.SMEM), pl.BlockSpec(memory_space=pl.ANY)]
-        + [whole] * (len(pieces) + 4),
-        out_specs=[pl.BlockSpec(memory_space=pltpu.HBM), whole],
-        scratch_shapes=[
-            pltpu.SMEM((2, plan.stride, lanes), jnp.int32),
-            pltpu.VMEM(((field_rows + 1) * 4 * half, lanes), jnp.float32),
-            pltpu.VMEM((rows * 4 * half, lanes), jnp.float32),
-            pltpu.VMEM((fine_rows * 2 * half, lanes), jnp.float32),
-            pltpu.VMEM((planes, dir_count) + message, jnp.float32),
-            pltpu.SemaphoreType.DMA((planes + 2,)),
-        ],
-        compiler_params=pltpu.CompilerParams(vmem_limit_bytes=48 * 2**20),
-        name="translate_and_interpolate",
-    )(zed.reshape(1), meta, *pieces, table, phases, high, low)
-
-    parts = lax.all_to_all(
-        local_fine.reshape((planes * dir_count,) + message),
-        ("zed", "dir"),
-        split_axis=0,
-        concat_axis=0,
-        tiled=True,
-    )
+    scalars = pl.BlockSpec(memory_space=pltpu.SMEM)
+    here = jnp.stack([zed, dir_index])
+    field_shape = ((field_rows + 1) * 4 * half, lanes)
+    tables = [table, phases, high, low]
+
+    def fine(steps, inputs, filled):
+        count = len(steps) * dir_count
+        shapes = [] if filled else [jax.ShapeDtypeStruct(field_shape, jnp.float32)]
+        shapes += [jax.ShapeDtypeStruct(message, jnp.float32)] * count
+        return pl.pallas_call(
+            functools.partial(fine_kernel, plan, size, edge_rows, steps, filled),
+            out_shape=shapes,
+            in_specs=[scalars, pl.BlockSpec(memory_space=pl.ANY)] + [whole] * (len(inputs) + len(tables)),
+            out_specs=[whole] * len(shapes),
+            scratch_shapes=[
+                pltpu.SMEM((len(steps), plan.stride, lanes), jnp.int32),
+                pltpu.VMEM((rows * 4 * half, lanes), jnp.float32),
+                pltpu.VMEM((fine_rows * 2 * half, lanes), jnp.float32),
+                pltpu.VMEM((2 * fine_rows, kf_pad), jnp.float32),
+                pltpu.VMEM((fine_rows, lanes), jnp.float32),
+                pltpu.SemaphoreType.DMA((len(steps),)),
+            ],
+            compiler_params=pltpu.CompilerParams(vmem_limit_bytes=32 * 2**20),
+            name="translate_and_interpolate",
+        )(here, meta, *inputs, *tables)
+
+    field, *far = fine((3, 2), pieces, False)
+    near = fine((1, 0), [field], True)
+    order = [(step, turn) for step in (3, 2, 1, 0) for turn in range(dir_count)]
+    messages = dict(zip(order, [*far, *near]))
     result = (dest_rows, 2, source_count, fine_count)
     if kf_dev == lanes and planes * dir_count * 2 * half == lanes and dest_rows <= lanes:
+
+        def direct(step, turn):
+            if step == 0 and turn == 0:
+                return messages[step, turn]
+            pairs = [
+                (z * dir_count + d, (z ^ step) * dir_count + (d ^ turn))
+                for z in range(planes)
+                for d in range(dir_count)
+            ]
+            return lax.ppermute(messages[step, turn], ("zed", "dir"), pairs)
+
+        parts = {key: direct(*key) for key in order}
         return pl.pallas_call(
             functools.partial(join_kernel, source_count),
             out_shape=jax.ShapeDtypeStruct(result, jnp.float32),
-            in_specs=[whole] * 2,
+            in_specs=[scalars] + [whole] * len(order),
             out_specs=whole,
-            scratch_shapes=[pltpu.VMEM((dir_count, dest_rows * 2 * source_count, lanes), jnp.float32)],
+            scratch_shapes=[
+                pltpu.VMEM((dir_count, dest_rows * 2 * source_count, lanes), jnp.float32),
+                pltpu.VMEM((planes * dir_count * 2 * half, lanes), jnp.float32),
+            ],
             compiler_params=pltpu.CompilerParams(vmem_limit_bytes=24 * 2**20),
             name="join_parts",
-        )(parts, 1.0 - rims[:1])
+        )(here, *[parts[key] for key in sorted(order)])
+    parts = jnp.stack([messages[key] for key in sorted(order)]).reshape((planes, dir_count) + message)
+    parts = jnp.take(parts, zed ^ jnp.arange(planes, dtype=jnp.int32), axis=0)
+    parts = jnp.take(parts, dir_index ^ jnp.arange(dir_count, dtype=jnp.int32), axis=1)
+    parts = lax.all_to_all(
+        parts.reshape((planes * dir_count,) + message), ("zed", "dir"), split_axis=0, concat_axis=0, tiled=True
+    )
     parts = parts.reshape((planes, dir_count) + message)
     main = parts[:, :, : 2 * dest_rows, :kf_dev].reshape(planes, dir_count, 2, dest_rows, kf_dev)
     over = parts[:, :, 2 * dest_rows :, :dest_rows].reshape(planes, dir_count, 2, 2 * rim, dest_rows)

time: 98.2 us -> 109 us (1.11)
  starting transfers between devices: 17.8 us -> 38.1 us
  waiting for transfers between devices: 38.4 us -> 25.1 us
  Pallas kernels: 28.3 us -> 32.1 us
  local copies, waits for them, and re-layouts: 7.44 us -> 5.22 us
  other arithmetic: 4.96 us -> 7.03 us
    ppermute x3 -> x21, starting transfers between devices: 3.33 us -> 31.1 us  [the longest x15 25.1 us: direct(): return lax.ppermute(messages[step, turn], ('zed', 'dir'), pairs)]
    all_to_all x1 -> x0, waiting for transfers between devices: 26.3 us -> none  [per_device(): lax.all_to_all(local_fine.reshape((planes * dir_count,) + message), ('zed...]
    ppermute x3 -> x21, waiting for transfers between devices: 12 us -> 25.1 us  [the longest x6 13.7 us: to_planes(): lax.ppermute(note, 'zed', [(plane, plane ^ step) for plane in range(plane...]
    all_to_all x1 -> x0, starting transfers between devices: 8.33 us -> none  [per_device(): lax.all_to_all(local_fine.reshape((planes * dir_count,) + message), ('zed...]
    pallas_call x1 -> x2, Pallas kernels: 22.4 us -> 25.5 us  [fine(): pl.pallas_call(functools.partial(fine_kernel, plan, size, edge_rows, step...]
  transfers between devices with their start and end apart: 6 -> 23, of which waited for: 2 -> 6; matrix products, arithmetic and copies ran while one was open for 13% -> 7% of each run, Pallas kernels for 2% -> 4%
where the time goes in v3:
time: 109 us; the launch traced here: 108 us
  starting transfers between devices  38.1 us (35%)
  Pallas kernels  32.1 us (29%)
  waiting for transfers between devices  25.1 us (23%)
  other arithmetic  7.03 us (6%)
  local copies, waits for them, and re-layouts  5.22 us (5%)
    pallas_call x2, Pallas kernels, fine(): pl.pallas_call(functools.partial(fine_kernel, plan, size, edge_rows, step...  25.5 us
    ppermute x15, starting transfers between devices, direct(): return lax.ppermute(messages[step, turn], ('zed', 'dir'), pairs)  25.1 us
    ppermute x6, waiting for transfers between devices, to_planes(): lax.ppermute(note, 'zed', [(plane, plane ^ step) for plane in range(plane...  13.7 us
    ppermute x15, waiting for transfers between devices, direct(): return lax.ppermute(messages[step, turn], ('zed', 'dir'), pairs)  11.4 us
    ppermute x6, starting transfers between devices, to_planes(): lax.ppermute(note, 'zed', [(plane, plane ^ step) for plane in range(plane...  6.07 us
    all_to_all x1, starting transfers between devices, per_device(): lax.all_to_all(packed, 'zed', split_axis=0, concat_axis=0, tiled=True)  5.63 us
    pallas_call x2, Pallas kernels, pack(): pl.pallas_call(functools.partial(pack_kernel, source_count), out_shape=pl...  4.32 us
    reshape x1, local copies, waits for them, and re-layouts, per_device(): jnp.pad(trans_table, ((0, 0), (0, 0), (0, pad_dirs))).reshape(-1, lanes)  2.31 us
  transfers between devices with their start and end apart: 23, of which 6 were waited for; matrix products, arithmetic and copies ran while one was open for 7% of the time, Pallas kernels for 4%

profile of v3, /device:TPU:11, one launch (start us, length us, event | category | flops | bytes accessed | tf_op | source)
XLA Modules:
  0.0 107.7 jit_solution(136020739996060284)
XLA Ops:
  4.6 2.4 %collective-permute-start.1 = (f32[40,128]{1,0:T(8,128)S(1)}, f32[40,128]{1,0:T(8,128)S(1)}, u32[]{:S(2)}, u32[]{:S(2)}) collective-permute-start(f32[40,128]{1,0:T(8,128)S(1)} %get-tuple-element.50), channel_id=1, source_target_pairs={{0,16},{8,24},{16,0},{24,8},{1,17},{9,25},{17,1},{25,9},{2,18},{10... | collective-permute-start | bytes 61448 | tf_op jit(solution)/shard_map/ppermute | solution.py:360
  7.3 2.6 %pack_sources.2 = f32[4,512,128]{2,1,0:T(8,128)} custom-call(f32[64,2,4,512]{3,2,1,0:T(4,128)} %field.1), custom_call_target="tpu_custom_call" | custom-call | tf_op jit(solution)/shard_map/pack_sources/pallas_call | solution.py:94
  9.9 5.6 %all-to-all-start = ((f32[4,512,128]{2,1,0:T(8,128)}), f32[4,512,128]{2,1,0:T(8,128)S(1)}, u32[]{:S(2)}, u32[]{:S(2)}) async-start(f32[4,512,128]{2,1,0:T(8,128)} %pack_sources.2), calls=%async_computation | async-start | bytes 2097152 | tf_op jit(solution)/shard_map/all_to_all | solution.py:300
  16.5 1.3 %collective-permute-start.3 = (f32[16,2,4,512]{3,2,1,0:T(4,128)S(1)}, f32[16,2,4,512]{3,2,1,0:T(4,128)}, u32[]{:S(2)}, u32[]{:S(2)}) collective-permute-start(f32[16,2,4,512]{3,2,1,0:T(4,128)S(1)} %bitcast.57), channel_id=1, source_target_pairs={{0,4},{4,0},{1,5},{5,1},{2,6},{6,2},{3,7},{7,3},{8,12},{12,8},{9,1... | collective-permute-start | bytes 786440 | tf_op jit(solution)/shard_map/ppermute | solution.py:298
  21.3 2.3 %reshape.229.refs_5_.refs_1_ = f32[2528,128]{1,0:T(8,128)S(1)} reshape(f32[316,2,512]{2,1,0:T(2,128)} %param.11) | data formatting | bytes 2588672 | tf_op jit(solution)/shard_map/reshape | solution.py:384
  23.8 1.7 %pack_sources.3 = f32[4,128,128]{2,1,0:T(8,128)} custom-call(f32[16,2,4,512]{3,2,1,0:T(4,128)} %collective-permute-done.3.field), custom_call_target="tpu_custom_call" | custom-call | tf_op jit(solution)/shard_map/pack_sources/pallas_call | solution.py:94
  26.5 1.2 %collective-permute-start.6 = (f32[128,128]{1,0:T(8,128)S(1)}, f32[128,128]{1,0:T(8,128)S(1)}, u32[]{:S(2)}, u32[]{:S(2)}) collective-permute-start(f32[128,128]{1,0:T(8,128)S(1)} %get-tuple-element.45), channel_id=1, source_target_pairs={{0,24},{8,16},{16,8},{24,0},{1,25},{9,17},{17,9},{25,1},{2,26},{10... | collective-permute-start | bytes 196616 | tf_op jit(solution)/shard_map/ppermute | solution.py:360
  29.8 13.7 %collective-permute-done.6.refs_4_ = f32[128,128]{1,0:T(8,128)S(1)} collective-permute-done((f32[128,128]{1,0:T(8,128)S(1)}, f32[128,128]{1,0:T(8,128)S(1)}, u32[]{:S(2)}, u32[]{:S(2)}) %collective-permute-start.6) | collective-permute-done | bytes 65568 | tf_op jit(solution)/shard_map/ppermute | solution.py:360
  43.5 12.7 %translate_and_interpolate.2 = (f32[5136,128]{1,0:T(8,128)S(1)}, f32[136,128]{1,0:T(8,128)S(1)}, f32[136,128]{1,0:T(8,128)S(1)}, f32[136,128]{1,0:T(8,128)S(1)},...) custom-call(s32[2]{0:T(128)S(1)} %pad_add_fusion.3.here, ...), custom_call_target="tpu_custom_call" | custom-call | tf_op jit(solution)/shard_map/translate_and_interpolate/pallas_call | solution.py:434
  56.2 12.8 %translate_and_interpolate.3 = (f32[136,128]{1,0:T(8,128)S(1)}, f32[136,128]{1,0:T(8,128)S(1)}, f32[136,128]{1,0:T(8,128)S(1)}, f32[136,128]{1,0:T(8,128)S(1)}, ...) custom-call(s32[2]{0:T(128)S(1)} %pad_add_fusion.3.here, ...), custom_call_target="tpu_custom_call" | custom-call | tf_op jit(solution)/shard_map/translate_and_interpolate/pallas_call | solution.py:434
  69.0 2.5 %collective-permute-start.7 = (f32[136,128]{1,0:T(8,128)S(1)}, f32[136,128]{1,0:T(8,128)S(1)}, u32[]{:S(2)}, u32[]{:S(2)}) collective-permute-start(f32[136,128]{1,0:T(8,128)S(1)} %get-tuple-element.28), channel_id=1, source_target_pairs={{0,1},{1,0},{2,3},{3,2},{8,9},{9,8},{10,11},{11,10},{16,17},{17,16... | collective-permute-start | bytes 208904 | tf_op jit(solution)/shard_map/ppermute | solution.py:466
  71.8 1.4 %collective-permute-start.9 = (f32[136,128]{1,0:T(8,128)S(1)}, f32[136,128]{1,0:T(8,128)S(1)}, u32[]{:S(2)}, u32[]{:S(2)}) collective-permute-start(f32[136,128]{1,0:T(8,128)S(1)} %get-tuple-element.30), channel_id=1, source_target_pairs={{0,3},{1,2},{2,1},{3,0},{8,11},{9,10},{10,9},{11,8},{16,19},{17,18... | collective-permute-start | bytes 208904 | tf_op jit(solution)/shard_map/ppermute | solution.py:466
  73.3 1.9 %collective-permute-start.10 = (f32[136,128]{1,0:T(8,128)S(1)}, f32[136,128]{1,0:T(8,128)S(1)}, u32[]{:S(2)}, u32[]{:S(2)}) collective-permute-start(f32[136,128]{1,0:T(8,128)S(1)} %get-tuple-element.31), channel_id=1, source_target_pairs={{0,8},{1,9},{2,10},{3,11},{8,0},{9,1},{10,2},{11,3},{16,24},{17,25... | collective-permute-start | bytes 208904 | tf_op jit(solution)/shard_map/ppermute | solution.py:466
  75.2 1.7 %collective-permute-start.12 = (f32[136,128]{1,0:T(8,128)S(1)}, f32[136,128]{1,0:T(8,128)S(1)}, u32[]{:S(2)}, u32[]{:S(2)}) collective-permute-start(f32[136,128]{1,0:T(8,128)S(1)} %get-tuple-element.33), channel_id=1, source_target_pairs={{0,10},{1,11},{2,8},{3,9},{8,2},{9,3},{10,0},{11,1},{16,26},{17,27... | collective-permute-start | bytes 208904 | tf_op jit(solution)/shard_map/ppermute | solution.py:466
  76.9 1.2 %collective-permute-start.13 = (f32[136,128]{1,0:T(8,128)S(1)}, f32[136,128]{1,0:T(8,128)S(1)}, u32[]{:S(2)}, u32[]{:S(2)}) collective-permute-start(f32[136,128]{1,0:T(8,128)S(1)} %get-tuple-element.34), channel_id=1, source_target_pairs={{0,11},{1,10},{2,9},{3,8},{8,3},{9,2},{10,1},{11,0},{16,27},{17,26... | collective-permute-start | bytes 208904 | tf_op jit(solution)/shard_map/ppermute | solution.py:466
  78.1 1.4 %collective-permute-start.14 = (f32[136,128]{1,0:T(8,128)S(1)}, f32[136,128]{1,0:T(8,128)S(1)}, u32[]{:S(2)}, u32[]{:S(2)}) collective-permute-start(f32[136,128]{1,0:T(8,128)S(1)} %get-tuple-element.35), channel_id=1, source_target_pairs={{0,16},{1,17},{2,18},{3,19},{8,24},{9,25},{10,26},{11,27},{16,0},{... | collective-permute-start | bytes 208904 | tf_op jit(solution)/shard_map/ppermute | solution.py:466
  80.5 1.7 %collective-permute-start.16 = (f32[136,128]{1,0:T(8,128)S(1)}, f32[136,128]{1,0:T(8,128)S(1)}, u32[]{:S(2)}, u32[]{:S(2)}) collective-permute-start(f32[136,128]{1,0:T(8,128)S(1)} %get-tuple-element.37), channel_id=1, source_target_pairs={{0,18},{1,19},{2,16},{3,17},{8,26},{9,27},{10,24},{11,25},{16,2},{... | collective-permute-start | bytes 208904 | tf_op jit(solution)/shard_map/ppermute | solution.py:466
  82.2 2.1 %collective-permute-start.17 = (f32[136,128]{1,0:T(8,128)S(1)}, f32[136,128]{1,0:T(8,128)S(1)}, u32[]{:S(2)}, u32[]{:S(2)}) collective-permute-start(f32[136,128]{1,0:T(8,128)S(1)} %get-tuple-element.38), channel_id=1, source_target_pairs={{0,19},{1,18},{2,17},{3,16},{8,27},{9,26},{10,25},{11,24},{16,3},{... | collective-permute-start | bytes 208904 | tf_op jit(solution)/shard_map/ppermute | solution.py:466
  85.3 5.7 %collective-permute-start.19 = (f32[136,128]{1,0:T(8,128)S(1)}, f32[136,128]{1,0:T(8,128)S(1)}, u32[]{:S(2)}, u32[]{:S(2)}) collective-permute-start(f32[136,128]{1,0:T(8,128)S(1)} %get-tuple-element.40), channel_id=1, source_target_pairs={{0,25},{1,24},{2,27},{3,26},{8,17},{9,16},{10,19},{11,18},{16,9},{... | collective-permute-start | bytes 208904 | tf_op jit(solution)/shard_map/ppermute | solution.py:466
  91.5 3.1 %collective-permute-start.21 = (f32[136,128]{1,0:T(8,128)S(1)}, f32[136,128]{1,0:T(8,128)S(1)}, u32[]{:S(2)}, u32[]{:S(2)}) collective-permute-start(f32[136,128]{1,0:T(8,128)S(1)} %get-tuple-element.42), channel_id=1, source_target_pairs={{0,27},{1,26},{2,25},{3,24},{8,19},{9,18},{10,17},{11,16},{16,11},... | collective-permute-start | bytes 208904 | tf_op jit(solution)/shard_map/ppermute | solution.py:466
  94.6 4.8 %collective-permute-done.18.refs_12_ = f32[136,128]{1,0:T(8,128)S(1)} collective-permute-done((f32[136,128]{1,0:T(8,128)S(1)}, f32[136,128]{1,0:T(8,128)S(1)}, u32[]{:S(2)}, u32[]{:S(2)}) %collective-permute-start.18) | collective-permute-done | bytes 69664 | tf_op jit(solution)/shard_map/ppermute | solution.py:466
  99.4 3.7 %collective-permute-done.19.refs_13_ = f32[136,128]{1,0:T(8,128)S(1)} collective-permute-done((f32[136,128]{1,0:T(8,128)S(1)}, f32[136,128]{1,0:T(8,128)S(1)}, u32[]{:S(2)}, u32[]{:S(2)}) %collective-permute-start.19) | collective-permute-done | bytes 69664 | tf_op jit(solution)/shard_map/ppermute | solution.py:466
  103.7 1.8 %collective-permute-done.21.refs_15_ = f32[136,128]{1,0:T(8,128)S(1)} collective-permute-done((f32[136,128]{1,0:T(8,128)S(1)}, f32[136,128]{1,0:T(8,128)S(1)}, u32[]{:S(2)}, u32[]{:S(2)}) %collective-permute-start.21) | collective-permute-done | bytes 69664 | tf_op jit(solution)/shard_map/ppermute | solution.py:466
  105.5 2.2 %join_parts.1 = f32[64,2,4,512]{3,2,1,0:T(4,128)} custom-call(s32[2]{0:T(128)S(1)} %pad_add_fusion.3.here, f32[136,128]{1,0:T(8,128)S(1)} %get-tuple-element.27.refs_0_, f32[136,128]{1,0:T(8,128)S(1)} %collective-permute-done.7.refs_1_, f32[136,128]{1,0:T(8,128)S(1)} %collective-permute-done.8.refs_2_, f32[136,128]{1,0:T(8,128)S(1)} %collective-permute-done.9.refs_3_, ...), custom_call_target="tpu_custom_call" | custom-call | tf_op jit(solution)/shard_map/join_parts/pallas_call | solution.py:469
  (70 shorter events, 15.9 us)
Async XLA Ops:
  0.0 17.9 %copy-start = (s32[2048,4]{0,1:T(4,128)S(1)}, s32[2048,4]{0,1:T(4,128)}, u32[]{:S(2)}) copy-start(s32[2048,4]{0,1:T(4,128)} %param.18) | copy-start | bytes 98308
  4.6 19.0 %collective-permute-start.1 = (f32[40,128]{1,0:T(8,128)S(1)}, f32[40,128]{1,0:T(8,128)S(1)}, u32[]{:S(2)}, u32[]{:S(2)}) collective-permute-start(f32[40,128]{1,0:T(8,128)S(1)} %get-tuple-element.50), channel_id=1, source_target_pairs={{0,16},{8,24},{16,0},{24,8},{1,17},{9,25},{17,1},{25,9},{2,18},{10... | collective-permute-start | bytes 61448 | tf_op jit(solution)/shard_map/ppermute | solution.py:360
  7.0 16.6 %collective-permute-start = (f32[40,128]{1,0:T(8,128)S(1)}, f32[40,128]{1,0:T(8,128)S(1)}, u32[]{:S(2)}, u32[]{:S(2)}) collective-permute-start(f32[40,128]{1,0:T(8,128)S(1)} %get-tuple-element.50), channel_id=1, source_target_pairs={{0,8},{8,0},{16,24},{24,16},{1,9},{9,1},{17,25},{25,17},{2,10},{10... | collective-permute-start | bytes 61448 | tf_op jit(solution)/shard_map/ppermute | solution.py:360
  7.1 16.5 %collective-permute-start.2 = (f32[40,128]{1,0:T(8,128)S(1)}, f32[40,128]{1,0:T(8,128)S(1)}, u32[]{:S(2)}, u32[]{:S(2)}) collective-permute-start(f32[40,128]{1,0:T(8,128)S(1)} %get-tuple-element.50), channel_id=1, source_target_pairs={{0,24},{8,16},{16,8},{24,0},{1,25},{9,17},{17,9},{25,1},{2,26},{10... | collective-permute-start | bytes 61448 | tf_op jit(solution)/shard_map/ppermute | solution.py:360
  9.9 33.6 %all-to-all-start = ((f32[4,512,128]{2,1,0:T(8,128)}), f32[4,512,128]{2,1,0:T(8,128)S(1)}, u32[]{:S(2)}, u32[]{:S(2)}) async-start(f32[4,512,128]{2,1,0:T(8,128)} %pack_sources.2), calls=%async_computation | async-start | bytes 2097152 | tf_op jit(solution)/shard_map/all_to_all | solution.py:300
  16.5 7.2 %collective-permute-start.3 = (f32[16,2,4,512]{3,2,1,0:T(4,128)S(1)}, f32[16,2,4,512]{3,2,1,0:T(4,128)}, u32[]{:S(2)}, u32[]{:S(2)}) collective-permute-start(f32[16,2,4,512]{3,2,1,0:T(4,128)S(1)} %bitcast.57), channel_id=1, source_target_pairs={{0,4},{4,0},{1,5},{5,1},{2,6},{6,2},{3,7},{7,3},{8,12},{12,8},{9,1... | collective-permute-start | bytes 786440 | tf_op jit(solution)/shard_map/ppermute | solution.py:298
  26.5 17.0 %collective-permute-start.6 = (f32[128,128]{1,0:T(8,128)S(1)}, f32[128,128]{1,0:T(8,128)S(1)}, u32[]{:S(2)}, u32[]{:S(2)}) collective-permute-start(f32[128,128]{1,0:T(8,128)S(1)} %get-tuple-element.45), channel_id=1, source_target_pairs={{0,24},{8,16},{16,8},{24,0},{1,25},{9,17},{17,9},{25,1},{2,26},{10... | collective-permute-start | bytes 196616 | tf_op jit(solution)/shard_map/ppermute | solution.py:360
  27.7 15.8 %collective-permute-start.5 = (f32[128,128]{1,0:T(8,128)S(1)}, f32[128,128]{1,0:T(8,128)S(1)}, u32[]{:S(2)}, u32[]{:S(2)}) collective-permute-start(f32[128,128]{1,0:T(8,128)S(1)} %get-tuple-element.46), channel_id=1, source_target_pairs={{0,16},{8,24},{16,0},{24,8},{1,17},{9,25},{17,1},{25,9},{2,18},{10... | collective-permute-start | bytes 196616 | tf_op jit(solution)/shard_map/ppermute | solution.py:360
  28.7 14.8 %collective-permute-start.4 = (f32[128,128]{1,0:T(8,128)S(1)}, f32[128,128]{1,0:T(8,128)S(1)}, u32[]{:S(2)}, u32[]{:S(2)}) collective-permute-start(f32[128,128]{1,0:T(8,128)S(1)} %get-tuple-element.47), channel_id=1, source_target_pairs={{0,8},{8,0},{16,24},{24,16},{1,9},{9,1},{17,25},{25,17},{2,10},{10... | collective-permute-start | bytes 196616 | tf_op jit(solution)/shard_map/ppermute | solution.py:360
  69.0 6.2 %collective-permute-start.7 = (f32[136,128]{1,0:T(8,128)S(1)}, f32[136,128]{1,0:T(8,128)S(1)}, u32[]{:S(2)}, u32[]{:S(2)}) collective-permute-start(f32[136,128]{1,0:T(8,128)S(1)} %get-tuple-element.28), channel_id=1, source_target_pairs={{0,1},{1,0},{2,3},{3,2},{8,9},{9,8},{10,11},{11,10},{16,17},{17,16... | collective-permute-start | bytes 208904 | tf_op jit(solution)/shard_map/ppermute | solution.py:466
  71.6 5.4 %collective-permute-start.8 = (f32[136,128]{1,0:T(8,128)S(1)}, f32[136,128]{1,0:T(8,128)S(1)}, u32[]{:S(2)}, u32[]{:S(2)}) collective-permute-start(f32[136,128]{1,0:T(8,128)S(1)} %get-tuple-element.29), channel_id=1, source_target_pairs={{0,2},{1,3},{2,0},{3,1},{8,10},{9,11},{10,8},{11,9},{16,18},{17,19... | collective-permute-start | bytes 208904 | tf_op jit(solution)/shard_map/ppermute | solution.py:466
  71.8 6.3 %collective-permute-start.9 = (f32[136,128]{1,0:T(8,128)S(1)}, f32[136,128]{1,0:T(8,128)S(1)}, u32[]{:S(2)}, u32[]{:S(2)}) collective-permute-start(f32[136,128]{1,0:T(8,128)S(1)} %get-tuple-element.30), channel_id=1, source_target_pairs={{0,3},{1,2},{2,1},{3,0},{8,11},{9,10},{10,9},{11,8},{16,19},{17,18... | collective-permute-start | bytes 208904 | tf_op jit(solution)/shard_map/ppermute | solution.py:466
  73.3 6.3 %collective-permute-start.10 = (f32[136,128]{1,0:T(8,128)S(1)}, f32[136,128]{1,0:T(8,128)S(1)}, u32[]{:S(2)}, u32[]{:S(2)}) collective-permute-start(f32[136,128]{1,0:T(8,128)S(1)} %get-tuple-element.31), channel_id=1, source_target_pairs={{0,8},{1,9},{2,10},{3,11},{8,0},{9,1},{10,2},{11,3},{16,24},{17,25... | collective-permute-start | bytes 208904 | tf_op jit(solution)/shard_map/ppermute | solution.py:466
  75.1 5.4 %collective-permute-start.11 = (f32[136,128]{1,0:T(8,128)S(1)}, f32[136,128]{1,0:T(8,128)S(1)}, u32[]{:S(2)}, u32[]{:S(2)}) collective-permute-start(f32[136,128]{1,0:T(8,128)S(1)} %get-tuple-element.32), channel_id=1, source_target_pairs={{0,9},{1,8},{2,11},{3,10},{8,1},{9,0},{10,3},{11,2},{16,25},{17,24... | collective-permute-start | bytes 208904 | tf_op jit(solution)/shard_map/ppermute | solution.py:466
  75.2 7.0 %collective-permute-start.12 = (f32[136,128]{1,0:T(8,128)S(1)}, f32[136,128]{1,0:T(8,128)S(1)}, u32[]{:S(2)}, u32[]{:S(2)}) collective-permute-start(f32[136,128]{1,0:T(8,128)S(1)} %get-tuple-element.33), channel_id=1, source_target_pairs={{0,10},{1,11},{2,8},{3,9},{8,2},{9,3},{10,0},{11,1},{16,26},{17,27... | collective-permute-start | bytes 208904 | tf_op jit(solution)/shard_map/ppermute | solution.py:466
  76.9 7.4 %collective-permute-start.13 = (f32[136,128]{1,0:T(8,128)S(1)}, f32[136,128]{1,0:T(8,128)S(1)}, u32[]{:S(2)}, u32[]{:S(2)}) collective-permute-start(f32[136,128]{1,0:T(8,128)S(1)} %get-tuple-element.34), channel_id=1, source_target_pairs={{0,11},{1,10},{2,9},{3,8},{8,3},{9,2},{10,1},{11,0},{16,27},{17,26... | collective-permute-start | bytes 208904 | tf_op jit(solution)/shard_map/ppermute | solution.py:466
  78.1 7.1 %collective-permute-start.14 = (f32[136,128]{1,0:T(8,128)S(1)}, f32[136,128]{1,0:T(8,128)S(1)}, u32[]{:S(2)}, u32[]{:S(2)}) collective-permute-start(f32[136,128]{1,0:T(8,128)S(1)} %get-tuple-element.35), channel_id=1, source_target_pairs={{0,16},{1,17},{2,18},{3,19},{8,24},{9,25},{10,26},{11,27},{16,0},{... | collective-permute-start | bytes 208904 | tf_op jit(solution)/shard_map/ppermute | solution.py:466
  79.5 11.4 %collective-permute-start.15 = (f32[136,128]{1,0:T(8,128)S(1)}, f32[136,128]{1,0:T(8,128)S(1)}, u32[]{:S(2)}, u32[]{:S(2)}) collective-permute-start(f32[136,128]{1,0:T(8,128)S(1)} %get-tuple-element.36), channel_id=1, source_target_pairs={{0,17},{1,16},{2,19},{3,18},{8,25},{9,24},{10,27},{11,26},{16,1},{... | collective-permute-start | bytes 208904 | tf_op jit(solution)/shard_map/ppermute | solution.py:466
  80.5 10.9 %collective-permute-start.16 = (f32[136,128]{1,0:T(8,128)S(1)}, f32[136,128]{1,0:T(8,128)S(1)}, u32[]{:S(2)}, u32[]{:S(2)}) collective-permute-start(f32[136,128]{1,0:T(8,128)S(1)} %get-tuple-element.37), channel_id=1, source_target_pairs={{0,18},{1,19},{2,16},{3,17},{8,26},{9,27},{10,24},{11,25},{16,2},{... | collective-permute-start | bytes 208904 | tf_op jit(solution)/shard_map/ppermute | solution.py:466
  82.2 12.4 %collective-permute-start.17 = (f32[136,128]{1,0:T(8,128)S(1)}, f32[136,128]{1,0:T(8,128)S(1)}, u32[]{:S(2)}, u32[]{:S(2)}) collective-permute-start(f32[136,128]{1,0:T(8,128)S(1)} %get-tuple-element.38), channel_id=1, source_target_pairs={{0,19},{1,18},{2,17},{3,16},{8,27},{9,26},{10,25},{11,24},{16,3},{... | collective-permute-start | bytes 208904 | tf_op jit(solution)/shard_map/ppermute | solution.py:466
  84.3 15.0 %collective-permute-start.18 = (f32[136,128]{1,0:T(8,128)S(1)}, f32[136,128]{1,0:T(8,128)S(1)}, u32[]{:S(2)}, u32[]{:S(2)}) collective-permute-start(f32[136,128]{1,0:T(8,128)S(1)} %get-tuple-element.39), channel_id=1, source_target_pairs={{0,24},{1,25},{2,26},{3,27},{8,16},{9,17},{10,18},{11,19},{16,8},{... | collective-permute-start | bytes 208904 | tf_op jit(solution)/shard_map/ppermute | solution.py:466
  85.3 17.8 %collective-permute-start.19 = (f32[136,128]{1,0:T(8,128)S(1)}, f32[136,128]{1,0:T(8,128)S(1)}, u32[]{:S(2)}, u32[]{:S(2)}) collective-permute-start(f32[136,128]{1,0:T(8,128)S(1)} %get-tuple-element.40), channel_id=1, source_target_pairs={{0,25},{1,24},{2,27},{3,26},{8,17},{9,16},{10,19},{11,18},{16,9},{... | collective-permute-start | bytes 208904 | tf_op jit(solution)/shard_map/ppermute | solution.py:466
  91.0 12.8 %collective-permute-start.20 = (f32[136,128]{1,0:T(8,128)S(1)}, f32[136,128]{1,0:T(8,128)S(1)}, u32[]{:S(2)}, u32[]{:S(2)}) collective-permute-start(f32[136,128]{1,0:T(8,128)S(1)} %get-tuple-element.41), channel_id=1, source_target_pairs={{0,26},{1,27},{2,24},{3,25},{8,18},{9,19},{10,16},{11,17},{16,10},... | collective-permute-start | bytes 208904 | tf_op jit(solution)/shard_map/ppermute | solution.py:466
  91.5 14.0 %collective-permute-start.21 = (f32[136,128]{1,0:T(8,128)S(1)}, f32[136,128]{1,0:T(8,128)S(1)}, u32[]{:S(2)}, u32[]{:S(2)}) collective-permute-start(f32[136,128]{1,0:T(8,128)S(1)} %get-tuple-element.42), channel_id=1, source_target_pairs={{0,27},{1,26},{2,25},{3,24},{8,19},{9,18},{10,17},{11,16},{16,11},... | collective-permute-start | bytes 208904 | tf_op jit(solution)/shard_map/ppermute | solution.py:466

commit v4 on v2

--- a/solution.py
+++ b/solution.py
@@ -125,23 +125,14 @@
     def with_turned(value):
         return jnp.concatenate([value, pltpu.roll(value, half, 0)], axis=0)
 
+    part = size * 2 * half
+    edge_part = edge_size * 2 * half
     for plane in range(planes):
-
-        def main_step(row, unused, plane=plane):
-            value = main[plane, tile(row * 2 * half), :]
-            field[both((plane * size + row) * 4 * half), :] = with_turned(value)
-            return unused
-
-        lax.fori_loop(0, size, main_step, 0, unroll=8)
+        field[plane * part : (plane + 1) * part, :] = main[plane, :part, :]
     for step, edge in enumerate(edges):
-        first = planes * size + (own ^ step) * edge_size
-
-        def edge_step(row, unused, first=first, edge=edge):
-            field[both((first + row) * 4 * half), :] = with_turned(edge[tile(row * 2 * half), :])
-            return unused
-
-        lax.fori_loop(0, edge_size, edge_step, 0, unroll=8)
-    field[both(planes * (size + edge_size) * 4 * half), :] = jnp.zeros((4 * half, lanes), jnp.float32)
+        first = planes * part + (own ^ step) * edge_part
+        field[pl.ds(pl.multiple_of(first, edge_part), edge_part), :] = edge[:edge_part, :]
+    field[tile(planes * (part + edge_part)), :] = jnp.zeros((2 * half, lanes), jnp.float32)
 
     blank = jnp.zeros((2 * half, lanes), jnp.float32)
     sub = lax.broadcasted_iota(jnp.int32, (2 * half, lanes), 0)
@@ -167,10 +158,10 @@
                 sums = [[blank, blank] for box in boxes]
                 for pair in range(slot_count):
                     for each in range(plan.together):
-                        value = field[both(meta[slot, boxes[each], pair]), :]
+                        value = field[tile(meta[slot, boxes[each], pair]), :]
                         factor = table[tile(meta[slot, boxes[each], plan.kinds + pair]), :]
-                        sums[each][0] += factor * value[: 2 * half]
-                        sums[each][1] += factor * value[2 * half :]
+                        sums[each][0] += factor * value
+                        sums[each][1] += factor * pltpu.roll(value, half, 0)
                 for each in range(plan.together):
                     straight, crossed = sums[each]
                     total = jnp.where(
@@ -298,8 +289,11 @@
     field = jnp.pad(coarse_field, ((0, 0), (0, 0), (0, 0), (0, pad_dirs)))
     packed = pack(field, [])
     edge_rows = 0
+    after_pack = lax.optimization_barrier(
+        (packed, field, partner_ids, partner_types, partner_count, child_count, child_octant)
+    )
+    packed, field, partner_ids, partner_types, partner_count, child_count, child_octant = after_pack
     if ring_count == 2:
-        packed, field = lax.optimization_barrier((packed, field))
         edges = lax.ppermute(near_edge(field, ring), "ring", [(0, 1), (1, 0)])
         edge_rows = edges.shape[0]
     arrived = lax.all_to_all(packed, "zed", split_axis=0, concat_axis=0, tiled=True)
@@ -322,7 +316,7 @@
     place = jnp.where(live, place, field_rows)
     together = 4
     fixed = slots // 2
-    group = 5 if (slots - fixed) % 5 == 0 else 1
+    group = 3 if (slots - fixed) % 3 == 0 else 1
     index = jnp.arange(rows, dtype=jnp.int32)
     before = (partner_count[None, :] > partner_count[:, None]) | (
         (partner_count[None, :] == partner_count[:, None]) & (index[None, :] < index[:, None])
@@ -345,7 +339,7 @@
     turns_at = lanes // 2
     packed_rows = rows * width // lanes
     assert width <= lanes and rows <= turns_at and fine_rows % lanes == 0
-    pair_list = across(jnp.concatenate([place * 4 * half, partner_types * 2 * half], axis=1), width)
+    pair_list = across(jnp.concatenate([place * 2 * half, partner_types * 2 * half], axis=1), width)
     lists = [
         pair_list.reshape(packed_rows, lanes),
         (parent * 4 * half).reshape(-1, lanes),
@@ -359,21 +353,22 @@
     plan = Plan(rows, slots, fine_rows, stride + shift, kinds_at, *places, turns_at, together, fixed, group)
     meta = jnp.pad(jnp.concatenate(lists), ((0, stride - offsets[-1]), (0, 0))).astype(jnp.float32)
 
-    if ring_count == 2:
-        notes = pack(edges, [meta])
-    else:
-        notes = jnp.broadcast_to(meta[None], (planes,) + meta.shape)
-    received = []
-    for step in range(planes):
-        note = lax.dynamic_index_in_dim(notes, zed ^ step, axis=0, keepdims=False)
-        if step:
-            note = lax.ppermute(note, "zed", [(plane, plane ^ step) for plane in range(planes)])
-        received.append(note)
-    edge_part = edge_rows * 2 * half
-    meta = jnp.stack([note[edge_part:] for note in received]).astype(jnp.int32)
+    def to_planes(note, step):
+        if step == 0:
+            return note
+        return lax.ppermute(note, "zed", [(plane, plane ^ step) for plane in range(planes)])
+
+    meta = jnp.stack([to_planes(meta, step) for step in range(planes)]).astype(jnp.int32)
     pair_list = meta[:, :packed_rows].reshape(planes, rows, width)
     pair_list = jnp.pad(pair_list, ((0, 0), (0, 0), (0, lanes - width)))
     meta = jnp.concatenate([pair_list, meta[:, packed_rows:]], axis=1)
+    received = []
+    if ring_count == 2:
+        notes = pack(edges, [])
+        received = [
+            to_planes(lax.dynamic_index_in_dim(notes, zed ^ step, axis=0, keepdims=False), step)
+            for step in range(planes)
+        ]
     if ring_count == 2:
         pieces = [arrived] + received
     else:
@@ -437,7 +432,7 @@
         out_specs=[pl.BlockSpec(memory_space=pltpu.HBM), whole],
         scratch_shapes=[
             pltpu.SMEM((2, plan.stride, lanes), jnp.int32),
-            pltpu.VMEM(((field_rows + 1) * 4 * half, lanes), jnp.float32),
+            pltpu.VMEM(((field_rows + 1) * 2 * half, lanes), jnp.float32),
             pltpu.VMEM((rows * 4 * half, lanes), jnp.float32),
             pltpu.VMEM((fine_rows * 2 * half, lanes), jnp.float32),
             pltpu.VMEM((planes, dir_count) + message, jnp.float32),

time: 98.2 us -> 99.5 us (1.013)
  starting transfers between devices: 17.8 us -> 20.9 us
  local copies, waits for them, and re-layouts: 7.44 us -> 5.25 us
  waiting for transfers between devices: 38.4 us -> 40.1 us
  other arithmetic: 4.96 us -> 3.36 us
    ppermute x3 -> x6, starting transfers between devices: 3.33 us -> 6.07 us  [to_planes(): lax.ppermute(note, 'zed', [(plane, plane ^ step) for plane in range(plane...]
    ppermute x3 -> x6, waiting for transfers between devices: 12 us -> 13.8 us  [to_planes(): lax.ppermute(note, 'zed', [(plane, plane ^ step) for plane in range(plane...]
  transfers between devices with their start and end apart: 6 -> 9, of which waited for: 2 -> 2; matrix products, arithmetic and copies ran while one was open for 13% -> 8% of each run, Pallas kernels for 2% -> 2%
where the time goes in v4:
time: 99.5 us; the launch traced here: 99.1 us
  waiting for transfers between devices  40.1 us (40%)
  Pallas kernels  29.2 us (29%)
  starting transfers between devices  20.9 us (21%)
  local copies, waits for them, and re-layouts  5.25 us (5%)
  other arithmetic  3.36 us (3%)
    all_to_all x1, waiting for transfers between devices, per_device(): lax.all_to_all(local_fine.reshape((planes * dir_count,) + message), ('zed...  26.3 us
    pallas_call x1, Pallas kernels, per_device(): pl.pallas_call(functools.partial(fine_kernel, plan, size, edge_rows), out...  23.3 us
    ppermute x6, waiting for transfers between devices, to_planes(): lax.ppermute(note, 'zed', [(plane, plane ^ step) for plane in range(plane...  13.8 us
    all_to_all x1, starting transfers between devices, per_device(): lax.all_to_all(local_fine.reshape((planes * dir_count,) + message), ('zed...  7.91 us
    ppermute x6, starting transfers between devices, to_planes(): lax.ppermute(note, 'zed', [(plane, plane ^ step) for plane in range(plane...  6.07 us
    all_to_all x1, starting transfers between devices, per_device(): lax.all_to_all(packed, 'zed', split_axis=0, concat_axis=0, tiled=True)  5.63 us
    pallas_call x2, Pallas kernels, pack(): pl.pallas_call(functools.partial(pack_kernel, source_count), out_shape=pl...  4.35 us
    reshape x1, local copies, waits for them, and re-layouts, per_device(): jnp.pad(trans_table, ((0, 0), (0, 0), (0, pad_dirs))).reshape(-1, lanes)  2.32 us
  transfers between devices with their start and end apart: 9, of which 2 were waited for; matrix products, arithmetic and copies ran while one was open for 8% of the time, Pallas kernels for 2%

profile of v4, /device:TPU:11, one launch (start us, length us, event | category | flops | bytes accessed | tf_op | source)
XLA Modules:
  0.0 99.1 jit_solution(884376608612742476)
XLA Ops:
  0.1 2.6 %pack_sources.2 = f32[4,512,128]{2,1,0:T(8,128)} custom-call(f32[64,2,4,512]{3,2,1,0:T(4,128)} %field.1), custom_call_target="tpu_custom_call" | custom-call | tf_op jit(solution)/shard_map/pack_sources/pallas_call | solution.py:94
  2.7 0.2 convert_reduce_fusion.1
  3.0 0.2 select_reduce_fusion.2
  3.7 2.4 %collective-permute-start.1 = (f32[40,128]{1,0:T(8,128)S(1)}, f32[40,128]{1,0:T(8,128)S(1)}, u32[]{:S(2)}, u32[]{:S(2)}) collective-permute-start(f32[40,128]{1,0:T(8,128)S(1)} %get-tuple-element.30), channel_id=1, source_target_pairs={{0,16},{8,24},{16,0},{24,8},{1,17},{9,25},{17,1},{25,9},{2,18},{10... | collective-permute-start | bytes 61448 | tf_op jit(solution)/shard_map/ppermute | solution.py:359
  6.2 0.2 collective-permute-start.2
  6.4 5.6 %all-to-all-start = ((f32[4,512,128]{2,1,0:T(8,128)}), f32[4,512,128]{2,1,0:T(8,128)S(1)}, u32[]{:S(2)}, u32[]{:S(2)}) async-start(f32[4,512,128]{2,1,0:T(8,128)} %pack_sources.2), calls=%async_computation | async-start | bytes 2097152 | tf_op jit(solution)/shard_map/all_to_all | solution.py:299
  12.1 1.0 constant_dynamic-slice_fusion
  13.0 1.3 %collective-permute-start.3 = (f32[16,2,4,512]{3,2,1,0:T(4,128)S(1)}, f32[16,2,4,512]{3,2,1,0:T(4,128)}, u32[]{:S(2)}, u32[]{:S(2)}) collective-permute-start(f32[16,2,4,512]{3,2,1,0:T(4,128)S(1)} %bitcast.57), channel_id=1, source_target_pairs={{0,4},{4,0},{1,5},{5,1},{2,6},{6,2},{3,7},{7,3},{8,12},{12,8},{9,1... | collective-permute-start | bytes 786440 | tf_op jit(solution)/shard_map/ppermute | solution.py:297
  14.4 0.7 dynamic-slice_bitcast_fusion.4
  15.2 0.9 cosine_multiply_fusion
  16.1 0.6 select_add_fusion
  16.7 0.6 select_add_fusion.1
  17.4 0.2 fusion.29
  17.7 2.3 %reshape.236.refs_4_ = f32[2528,128]{1,0:T(8,128)S(1)} reshape(f32[316,2,512]{2,1,0:T(2,128)} %param.11) | data formatting | bytes 2588672 | tf_op jit(solution)/shard_map/reshape | solution.py:383
  20.2 1.8 %pack_sources.3 = f32[4,128,128]{2,1,0:T(8,128)} custom-call(f32[16,2,4,512]{3,2,1,0:T(4,128)} %collective-permute-done.3.field), custom_call_target="tpu_custom_call" | custom-call | tf_op jit(solution)/shard_map/pack_sources/pallas_call | solution.py:94
  22.0 1.0 dynamic-slice_bitcast_fusion
  22.9 1.2 %collective-permute-start.6 = (f32[128,128]{1,0:T(8,128)S(1)}, f32[128,128]{1,0:T(8,128)S(1)}, u32[]{:S(2)}, u32[]{:S(2)}) collective-permute-start(f32[128,128]{1,0:T(8,128)S(1)} %get-tuple-element.25), channel_id=1, source_target_pairs={{0,24},{8,16},{16,8},{24,0},{1,25},{9,17},{17,9},{25,1},{2,26},{10... | collective-permute-start | bytes 196616 | tf_op jit(solution)/shard_map/ppermute | solution.py:359
  24.2 1.0 collective-permute-start.5
  25.2 1.1 %collective-permute-start.4 = (f32[128,128]{1,0:T(8,128)S(1)}, f32[128,128]{1,0:T(8,128)S(1)}, u32[]{:S(2)}, u32[]{:S(2)}) collective-permute-start(f32[128,128]{1,0:T(8,128)S(1)} %get-tuple-element.27), channel_id=1, source_target_pairs={{0,8},{8,0},{16,24},{24,16},{1,9},{9,1},{17,25},{25,17},{2,10},{10... | collective-permute-start | bytes 196616 | tf_op jit(solution)/shard_map/ppermute | solution.py:359
  26.3 13.7 %collective-permute-done.6.refs_3_ = f32[128,128]{1,0:T(8,128)S(1)} collective-permute-done((f32[128,128]{1,0:T(8,128)S(1)}, f32[128,128]{1,0:T(8,128)S(1)}, u32[]{:S(2)}, u32[]{:S(2)}) %collective-permute-start.6) | collective-permute-done | bytes 65568 | tf_op jit(solution)/shard_map/ppermute | solution.py:359
  40.0 23.3 %translate_and_interpolate.1 = (f32[4,4,136,128]{3,2,1,0:T(8,128)}, f32[8,128]{1,0:T(8,128)S(1)}) custom-call(s32[1]{0:T(128)} %bitcast.zed, s32[4,72,128]{2,1,0:T(8,128)S(1)} %pad_add_fusion.lists, f32[4,512,128]{2,1,0:T(8,128)S(1)} %all-to-all-done.main, f32[128,128]{1,0:T(8,128)S(1)} %get-tuple-element.28.refs_0_, ...), custom_call_target="tpu_custom_call" | custom-call | tf_op jit(solution)/shard_map/translate_and_interpolate/pallas_call | solution.py:424
  63.3 7.9 %all-to-all-start.1 = ((f32[16,136,128]{2,1,0:T(8,128)}), f32[16,136,128]{2,1,0:T(8,128)S(1)}, u32[]{:S(2)}, u32[]{:S(2)}) async-start(f32[16,136,128]{2,1,0:T(8,128)} %bitcast.56), calls=%async_computation.1 | async-start | bytes 2228224 | tf_op jit(solution)/shard_map/all_to_all | solution.py:445
  71.2 26.3 %all-to-all-done.1.parts = f32[16,136,128]{2,1,0:T(8,128)S(1)} async-done(((f32[16,136,128]{2,1,0:T(8,128)}), f32[16,136,128]{2,1,0:T(8,128)S(1)}, u32[]{:S(2)}, u32[]{:S(2)}) %all-to-all-start.1) | async-done | bytes 1114144 | tf_op jit(solution)/shard_map/all_to_all | solution.py:445
  97.6 1.5 %join_parts.1 = f32[64,2,4,512]{3,2,1,0:T(4,128)} custom-call(f32[16,136,128]{2,1,0:T(8,128)S(1)} %all-to-all-done.1.parts, f32[1,128]{1,0:T(1,128)S(1)} %slice_subtract_fusion.rims), custom_call_target="tpu_custom_call" | custom-call | tf_op jit(solution)/shard_map/join_parts/pallas_call | solution.py:454
  (51 shorter events, 1.2 us)
Async XLA Ops:
  0.0 14.4 %copy-start = (s32[2048,4]{0,1:T(4,128)S(1)}, s32[2048,4]{0,1:T(4,128)}, u32[]{:S(2)}) copy-start(s32[2048,4]{0,1:T(4,128)} %param.18) | copy-start | bytes 98308
  0.0 2.7 %copy-start.4 = (s32[256]{0:T(256)S(1)}, s32[256]{0:T(256)}, u32[]{:S(2)}) copy-start(s32[256]{0:T(256)} %param.16) | copy-start | bytes 3076
  0.0 2.7 %copy-start.5 = (s32[64]{0:T(128)S(1)}, s32[64]{0:T(128)}, u32[]{:S(2)}) copy-start(s32[64]{0:T(128)} %param.15) | copy-start | bytes 772
  0.0 2.7 %copy-start.3 = (s32[64]{0:T(128)S(1)}, s32[64]{0:T(128)}, u32[]{:S(2)}) copy-start(s32[64]{0:T(128)} %param.14) | copy-start | bytes 772
  0.0 3.3 %copy-start.2 = (s32[64,30]{0,1:T(8,128)S(1)}, s32[64,30]{0,1:T(8,128)}, u32[]{:S(2)}) copy-start(s32[64,30]{0,1:T(8,128)} %param.13) | copy-start | bytes 23044
  0.0 3.3 %copy-start.1 = (s32[64,30]{0,1:T(8,128)S(1)}, s32[64,30]{0,1:T(8,128)}, u32[]{:S(2)}) copy-start(s32[64,30]{0,1:T(8,128)} %param.12) | copy-start | bytes 23044
  3.7 16.4 %collective-permute-start.1 = (f32[40,128]{1,0:T(8,128)S(1)}, f32[40,128]{1,0:T(8,128)S(1)}, u32[]{:S(2)}, u32[]{:S(2)}) collective-permute-start(f32[40,128]{1,0:T(8,128)S(1)} %get-tuple-element.30), channel_id=1, source_target_pairs={{0,16},{8,24},{16,0},{24,8},{1,17},{9,25},{17,1},{25,9},{2,18},{10... | collective-permute-start | bytes 61448 | tf_op jit(solution)/shard_map/ppermute | solution.py:359
  6.1 14.0 %collective-permute-start = (f32[40,128]{1,0:T(8,128)S(1)}, f32[40,128]{1,0:T(8,128)S(1)}, u32[]{:S(2)}, u32[]{:S(2)}) collective-permute-start(f32[40,128]{1,0:T(8,128)S(1)} %get-tuple-element.30), channel_id=1, source_target_pairs={{0,8},{8,0},{16,24},{24,16},{1,9},{9,1},{17,25},{25,17},{2,10},{10... | collective-permute-start | bytes 61448 | tf_op jit(solution)/shard_map/ppermute | solution.py:359
  6.2 13.8 %collective-permute-start.2 = (f32[40,128]{1,0:T(8,128)S(1)}, f32[40,128]{1,0:T(8,128)S(1)}, u32[]{:S(2)}, u32[]{:S(2)}) collective-permute-start(f32[40,128]{1,0:T(8,128)S(1)} %get-tuple-element.30), channel_id=1, source_target_pairs={{0,24},{8,16},{16,8},{24,0},{1,25},{9,17},{17,9},{25,1},{2,26},{10... | collective-permute-start | bytes 61448 | tf_op jit(solution)/shard_map/ppermute | solution.py:359
  6.4 33.6 %all-to-all-start = ((f32[4,512,128]{2,1,0:T(8,128)}), f32[4,512,128]{2,1,0:T(8,128)S(1)}, u32[]{:S(2)}, u32[]{:S(2)}) async-start(f32[4,512,128]{2,1,0:T(8,128)} %pack_sources.2), calls=%async_computation | async-start | bytes 2097152 | tf_op jit(solution)/shard_map/all_to_all | solution.py:299
  13.0 7.2 %collective-permute-start.3 = (f32[16,2,4,512]{3,2,1,0:T(4,128)S(1)}, f32[16,2,4,512]{3,2,1,0:T(4,128)}, u32[]{:S(2)}, u32[]{:S(2)}) collective-permute-start(f32[16,2,4,512]{3,2,1,0:T(4,128)S(1)} %bitcast.57), channel_id=1, source_target_pairs={{0,4},{4,0},{1,5},{5,1},{2,6},{6,2},{3,7},{7,3},{8,12},{12,8},{9,1... | collective-permute-start | bytes 786440 | tf_op jit(solution)/shard_map/ppermute | solution.py:297
  22.9 17.1 %collective-permute-start.6 = (f32[128,128]{1,0:T(8,128)S(1)}, f32[128,128]{1,0:T(8,128)S(1)}, u32[]{:S(2)}, u32[]{:S(2)}) collective-permute-start(f32[128,128]{1,0:T(8,128)S(1)} %get-tuple-element.25), channel_id=1, source_target_pairs={{0,24},{8,16},{16,8},{24,0},{1,25},{9,17},{17,9},{25,1},{2,26},{10... | collective-permute-start | bytes 196616 | tf_op jit(solution)/shard_map/ppermute | solution.py:359
  24.2 15.8 %collective-permute-start.5 = (f32[128,128]{1,0:T(8,128)S(1)}, f32[128,128]{1,0:T(8,128)S(1)}, u32[]{:S(2)}, u32[]{:S(2)}) collective-permute-start(f32[128,128]{1,0:T(8,128)S(1)} %get-tuple-element.26), channel_id=1, source_target_pairs={{0,16},{8,24},{16,0},{24,8},{1,17},{9,25},{17,1},{25,9},{2,18},{10... | collective-permute-start | bytes 196616 | tf_op jit(solution)/shard_map/ppermute | solution.py:359
  25.2 14.9 %collective-permute-start.4 = (f32[128,128]{1,0:T(8,128)S(1)}, f32[128,128]{1,0:T(8,128)S(1)}, u32[]{:S(2)}, u32[]{:S(2)}) collective-permute-start(f32[128,128]{1,0:T(8,128)S(1)} %get-tuple-element.27), channel_id=1, source_target_pairs={{0,8},{8,0},{16,24},{24,16},{1,9},{9,1},{17,25},{25,17},{2,10},{10... | collective-permute-start | bytes 196616 | tf_op jit(solution)/shard_map/ppermute | solution.py:359
  63.3 34.3 %all-to-all-start.1 = ((f32[16,136,128]{2,1,0:T(8,128)}), f32[16,136,128]{2,1,0:T(8,128)S(1)}, u32[]{:S(2)}, u32[]{:S(2)}) async-start(f32[16,136,128]{2,1,0:T(8,128)} %bitcast.56), calls=%async_computation.1 | async-start | bytes 2228224 | tf_op jit(solution)/shard_map/all_to_all | solution.py:445

commit v5 on v2

--- a/solution.py
+++ b/solution.py
@@ -14,9 +14,10 @@
 lanes = 128
 half = 4
 rim = 2
-
-
-plan_fields = ["rows", "slots", "fine_rows", "stride", "kinds", "parent", "octant", "order", "turns"]
+word_bits = 13
+
+
+plan_fields = ["rows", "slots", "fine_rows", "stride", "width", "parent", "order", "turns"]
 Plan = collections.namedtuple("Plan", plan_fields + ["together", "fixed", "group"])
 
 
@@ -54,13 +55,6 @@
     high = value.astype(jnp.bfloat16)
     low = (value - high.astype(jnp.float32)).astype(jnp.bfloat16)
     return high, low
-
-
-def three_pass(left, right, dims):
-    dot = functools.partial(
-        lax.dot_general, dimension_numbers=(dims, ((), ())), preferred_element_type=jnp.float32
-    )
-    return dot(left[0], right[0]) + (dot(left[0], right[1]) + dot(left[1], right[0]))
 
 
 def pack_kernel(source_count, field, *refs):
@@ -101,6 +95,10 @@
     )(field, *notes)
 
 
+def parts_of(word):
+    return lax.shift_right_logical(word, word_bits), word & (2**word_bits - 1)
+
+
 def tile(start):
     return pl.ds(pl.multiple_of(start, 2 * half), 2 * half)
 
@@ -108,7 +106,7 @@
 def fine_kernel(plan, size, edge_size, zed, lists, main, *refs):
     edges = refs[: planes if edge_size else 0]
     refs = refs[len(edges) :]
-    table, phases, high, low, out, rims, meta, field, moved, shifted, ready, sems = refs
+    table, phases, weights, out, rims, meta, field, moved, shifted, ready, sems = refs
     rows, fine_rows = plan.rows, plan.fine_rows
     own = zed[0]
 
@@ -167,8 +165,9 @@
                 sums = [[blank, blank] for box in boxes]
                 for pair in range(slot_count):
                     for each in range(plan.together):
-                        value = field[both(meta[slot, boxes[each], pair]), :]
-                        factor = table[tile(meta[slot, boxes[each], plan.kinds + pair]), :]
+                        place, kind = parts_of(meta[slot, step, each * plan.width + pair])
+                        value = field[both(place), :]
+                        factor = table[tile(kind), :]
                         sums[each][0] += factor * value[: 2 * half]
                         sums[each][1] += factor * value[2 * half :]
                 for each in range(plan.together):
@@ -188,9 +187,8 @@
 
         def fine_step(block, unused):
             for each in range(lanes):
-                value = moved[both(meta[slot, plan.parent + block, each]), :]
-                phase = phases[both(meta[slot, plan.octant + block, each]), :]
-                value = value * phase
+                parent, octant = parts_of(meta[slot, plan.parent + block, each])
+                value = moved[both(parent), :] * phases[both(octant), :]
                 shifted[tile((block * lanes + each) * 2 * half), :] = value[: 2 * half] + value[2 * half :]
             return unused
 
@@ -209,7 +207,10 @@
             ],
             axis=0,
         )
-        result = three_pass(split(left), (high[...], low[...]), ((1,), (0,)))
+        first, second = split(left)
+        result = jnp.dot(
+            jnp.concatenate([first, first, second], axis=1), weights[...], preferred_element_type=jnp.float32
+        )
         for part in range(2):
             for dest in range(dest_count):
                 start = part * fine_rows + dest * dest_rows
@@ -322,7 +323,7 @@
     place = jnp.where(live, place, field_rows)
     together = 4
     fixed = slots // 2
-    group = 5 if (slots - fixed) % 5 == 0 else 1
+    group = 3 if (slots - fixed) % 3 == 0 else 1
     index = jnp.arange(rows, dtype=jnp.int32)
     before = (partner_count[None, :] > partner_count[:, None]) | (
         (partner_count[None, :] == partner_count[:, None]) & (index[None, :] < index[:, None])
@@ -340,24 +341,33 @@
     def across(one, width=lanes):
         return jnp.pad(one, ((0, 0), (0, width - one.shape[1])))
 
-    kinds_at = slots
-    width = up(2 * slots, lanes // 2)
+    width = lanes // together
     turns_at = lanes // 2
-    packed_rows = rows * width // lanes
-    assert width <= lanes and rows <= turns_at and fine_rows % lanes == 0
-    pair_list = across(jnp.concatenate([place * 4 * half, partner_types * 2 * half], axis=1), width)
-    lists = [
-        pair_list.reshape(packed_rows, lanes),
-        (parent * 4 * half).reshape(-1, lanes),
-        (child_octant * 4 * half).reshape(-1, lanes),
-        across(jnp.concatenate([across(order[None], turns_at), turns[None]], axis=1)),
-    ]
-    offsets = [sum(one.shape[0] for one in lists[:count]) for count in range(len(lists) + 1)]
-    stride = up(offsets[-1], 8)
-    shift = rows - packed_rows
-    places = [offset + shift for offset in offsets[1:-1]]
-    plan = Plan(rows, slots, fine_rows, stride + shift, kinds_at, *places, turns_at, together, fixed, group)
-    meta = jnp.pad(jnp.concatenate(lists), ((0, stride - offsets[-1]), (0, 0))).astype(jnp.float32)
+    assert slots <= width and rows <= turns_at and fine_rows % lanes == 0
+    assert (field_rows + 1) * 4 * half < 2 ** (31 - word_bits) and type_count * 2 * half < 2**word_bits
+
+    def in_order(one):
+        one = jnp.sum(jnp.where(at_rank[:, :, None], across(one, width)[None], 0), axis=1)
+        return one.reshape(rows // together, lanes)
+
+    list_rows = rows // together
+    fine_lists = fine_rows // lanes
+    last = across(jnp.concatenate([across(order[None], turns_at), turns[None]], axis=1))
+    stride = up(list_rows + fine_lists + 1, 8)
+
+    def stacked(*parts):
+        meta = jnp.concatenate(parts)
+        return jnp.pad(meta, ((0, stride - meta.shape[0]), (0, 0))).astype(jnp.float32)
+
+    meta = jnp.concatenate(
+        [
+            stacked(in_order(place * 4 * half), (parent * 4 * half).reshape(-1, lanes)),
+            stacked(in_order(partner_types * 2 * half), (child_octant * 4 * half).reshape(-1, lanes), last),
+        ]
+    )
+    plan = Plan(
+        rows, slots, fine_rows, stride, width, list_rows, list_rows + fine_lists, turns_at, together, fixed, group
+    )
 
     if ring_count == 2:
         notes = pack(edges, [meta])
@@ -370,10 +380,8 @@
             note = lax.ppermute(note, "zed", [(plane, plane ^ step) for plane in range(planes)])
         received.append(note)
     edge_part = edge_rows * 2 * half
-    meta = jnp.stack([note[edge_part:] for note in received]).astype(jnp.int32)
-    pair_list = meta[:, :packed_rows].reshape(planes, rows, width)
-    pair_list = jnp.pad(pair_list, ((0, 0), (0, 0), (0, lanes - width)))
-    meta = jnp.concatenate([pair_list, meta[:, packed_rows:]], axis=1)
+    numbers = jnp.stack([note[edge_part:] for note in received]).astype(jnp.int32)
+    meta = numbers[:, :stride] * 2**word_bits + numbers[:, stride:]
     if ring_count == 2:
         pieces = [arrived] + received
     else:
@@ -423,6 +431,7 @@
     rounded = lax.reduce_precision(matrices, 8, 7)
     high = rounded.astype(jnp.bfloat16)
     low = (matrices - rounded).astype(jnp.bfloat16)
+    passes = jnp.concatenate([high, low, high], axis=0)
 
     whole = pl.BlockSpec(memory_space=pltpu.VMEM)
     message = (2 * dest_rows + 2 * half, kf_pad)
@@ -433,7 +442,7 @@
             jax.ShapeDtypeStruct((2 * half, lanes), jnp.float32),
         ],
         in_specs=[pl.BlockSpec(memory_space=pltpu.SMEM), pl.BlockSpec(memory_space=pl.ANY)]
-        + [whole] * (len(pieces) + 4),
+        + [whole] * (len(pieces) + 3),
         out_specs=[pl.BlockSpec(memory_space=pltpu.HBM), whole],
         scratch_shapes=[
             pltpu.SMEM((2, plan.stride, lanes), jnp.int32),
@@ -445,7 +454,7 @@
         ],
         compiler_params=pltpu.CompilerParams(vmem_limit_bytes=48 * 2**20),
         name="translate_and_interpolate",
-    )(zed.reshape(1), meta, *pieces, table, phases, high, low)
+    )(zed.reshape(1), meta, *pieces, table, phases, passes)
 
     parts = lax.all_to_all(
         local_fine.reshape((planes * dir_count,) + message),

time: 98.2 us -> 98.3 us (level)
  waiting for transfers between devices: 38.4 us -> 34.5 us
  other arithmetic: 4.96 us -> 8.09 us
    ppermute x3, waiting for transfers between devices: 12 us -> 8.19 us  [per_device(): lax.ppermute(note, 'zed', [(plane, plane ^ step) for plane in range(plane...]
    reduce_sum x0 -> x1, other arithmetic: none -> 2.24 us  [in_order(): jnp.sum(jnp.where(at_rank[:, :, None], across(one, width)[None], 0), axis=1)]
    unnamed x13 -> x16, local copies, waits for them, and re-layouts: 0.11 us -> 1.5 us
  transfers between devices with their start and end apart: 6 -> 6, of which waited for: 2 -> 2; matrix products, arithmetic and copies ran while one was open for 13% -> 15% of each run, Pallas kernels for 2% -> 2%
where the time goes in v5:
time: 98.3 us; the launch traced here: 97.4 us
  waiting for transfers between devices  34.5 us (35%)
  Pallas kernels  28.4 us (29%)
  starting transfers between devices  17.9 us (18%)
  local copies, waits for them, and re-layouts  8.17 us (8%)
  other arithmetic  8.09 us (8%)
    all_to_all x1, waiting for transfers between devices, per_device(): lax.all_to_all(local_fine.reshape((planes * dir_count,) + message), ('zed...  26.3 us
    pallas_call x1, Pallas kernels, per_device(): pl.pallas_call(functools.partial(fine_kernel, plan, size, edge_rows), out...  22.5 us
    all_to_all x1, starting transfers between devices, per_device(): lax.all_to_all(local_fine.reshape((planes * dir_count,) + message), ('zed...  8.42 us
    ppermute x3, waiting for transfers between devices, per_device(): lax.ppermute(note, 'zed', [(plane, plane ^ step) for plane in range(plane...  8.19 us
    all_to_all x1, starting transfers between devices, per_device(): lax.all_to_all(packed, 'zed', split_axis=0, concat_axis=0, tiled=True)  4.9 us
    pallas_call x2, Pallas kernels, pack(): pl.pallas_call(functools.partial(pack_kernel, source_count), out_shape=pl...  4.37 us
    ppermute x3, starting transfers between devices, per_device(): lax.ppermute(note, 'zed', [(plane, plane ^ step) for plane in range(plane...  3.33 us
    reshape x1, local copies, waits for them, and re-layouts, per_device(): jnp.pad(trans_table, ((0, 0), (0, 0), (0, pad_dirs))).reshape(-1, lanes)  2.31 us
  transfers between devices with their start and end apart: 6, of which 2 were waited for; matrix products, arithmetic and copies ran while one was open for 15% of the time, Pallas kernels for 2%

profile of v5, /device:TPU:11, one launch (start us, length us, event | category | flops | bytes accessed | tf_op | source)
XLA Modules:
  0.0 97.4 jit_solution(8809912613531130427)
XLA Ops:
  0.0 2.6 %pack_sources.2 = f32[4,512,128]{2,1,0:T(8,128)} custom-call(f32[64,2,4,512]{3,2,1,0:T(4,128)} %field.1), custom_call_target="tpu_custom_call" | custom-call | tf_op jit(solution)/shard_map/pack_sources/pallas_call | solution.py:88
  2.6 4.9 %all-to-all-start = ((f32[4,512,128]{2,1,0:T(8,128)}), f32[4,512,128]{2,1,0:T(8,128)S(1)}, u32[]{:S(2)}, u32[]{:S(2)}) async-start(f32[4,512,128]{2,1,0:T(8,128)} %pack_sources.2), calls=%async_computation | async-start | bytes 2097152 | tf_op jit(solution)/shard_map/all_to_all | solution.py:306
  7.5 1.7 %constant_dynamic-slice_fusion.2 = f32[2,1,2,1,2,2,2,4,512]{8,7,6,5,4,3,2,1,0:T(4,128)} fusion(f32[2,2,2,2,2,2,2,4,512]{8,7,6,5,4,3,2,1,0:T(4,128)} %bitcast.56, s32[]{:T(128)S(6)} %select_n.179), kind=kLoop, calls=%fused_computation.105 | loop fusion | bytes 524292 | tf_op jit(solution)/shard_map/jit(dynamic_index_in_dim)/dynamic_slice | solution.py:39
  9.2 1.2 %collective-permute-start = (f32[16,2,4,512]{3,2,1,0:T(4,128)}, f32[16,2,4,512]{3,2,1,0:T(4,128)}, u32[]{:S(2)}, u32[]{:S(2)}) collective-permute-start(f32[16,2,4,512]{3,2,1,0:T(4,128)} %bitcast.2), channel_id=1, source_target_pairs={{0,4},{4,0},{1,5},{5,1},{2,6},{6,2},{3,7},{7,3},{8,12},{12,8},{9,1... | collective-permute-start | bytes 786440 | tf_op jit(solution)/shard_map/ppermute | solution.py:304
  11.3 0.7 dynamic-slice_bitcast_fusion.4
  12.2 2.2 %select_reduce_fusion.1 = (s32[64,32]{1,0:T(8,128)S(1)}, s32[64,32]{1,0:T(8,128)S(1)}) fusion(s32[64,32]{0,1:T(8,128)S(1)} %pad.23, pred[64,64]{1,0:T(8,128)(4,1)S(1)} %iota_compare_fusion.3, s32[64,32]{0,1:T(8,128)S(1)} %pad.25), kind=kLoop, calls=%fused_computation.1 | loop fusion | flops 520192 | bytes 36864 | tf_op jit(solution)/shard_map/reduce_sum | solution.py:350
  14.6 0.6 select_add_fusion
  15.9 0.9 cosine_multiply_fusion
  16.9 0.8 fusion
  17.9 0.6 pad_maximum_fusion.2.refs_0_
  18.5 2.3 %reshape.257.refs_4_ = f32[2528,128]{1,0:T(8,128)S(1)} reshape(f32[316,2,512]{2,1,0:T(2,128)} %param.11) | data formatting | bytes 2588672 | tf_op jit(solution)/shard_map/reshape | solution.py:396
  20.9 1.1 %pad_maximum_fusion.refs_6_ = bf16[1536,256]{1,0:T(8,128)(2,1)S(1)} fusion(bf16[512,256]{1,0:T(8,128)(2,1)} %get-tuple-element.16, bf16[512,256]{1,0:T(8,128)(2,1)S(1)} %get-tuple-element.15), kind=kLoop, calls=%fused_computation.2 | loop fusion | flops 2359296 | bytes 1310720 | tf_op jit(solution)/shard_map/concatenate | solution.py:434
  22.0 1.8 %pack_sources.3 = f32[4,176,128]{2,1,0:T(8,128)} custom-call(f32[16,2,4,512]{3,2,1,0:T(4,128)} %collective-permute-done.field, f32[48,128]{1,0:T(8,128)} %pad_maximum_fusion.2.refs_0_), custom_call_target="tpu_custom_call" | custom-call | tf_op jit(solution)/shard_map/pack_sources/pallas_call | solution.py:88
  23.8 1.0 %dynamic-slice_bitcast_fusion.3 = (f32[176,128]{1,0:T(8,128)S(1)}, f32[176,128]{1,0:T(8,128)S(1)}, f32[176,128]{1,0:T(8,128)S(1)}, f32[176,128]{1,0:T(8,128)S(1)}) fusion(f32[4,176,128]{2,1,0:T(8,128)} %pack_sources.3, s32[]{:T(128)S(6)} %select_n.199, s32[]{:T(128)S(6)} %select_n.202, s32[]{:T(128)S(6)} %select_n.201, s32[]{:T(128)S(6)} %select_n.200), kind=kLoop, calls=%fused_computation.15 | loop fusion | bytes 720912 | tf_op jit(solution)/shard_map/jit(dynamic_index_in_dim)/squeeze | solution.py:378
  24.8 1.2 %collective-permute-start.3 = (f32[176,128]{1,0:T(8,128)S(1)}, f32[176,128]{1,0:T(8,128)S(1)}, u32[]{:S(2)}, u32[]{:S(2)}) collective-permute-start(f32[176,128]{1,0:T(8,128)S(1)} %get-tuple-element.18), channel_id=1, source_target_pairs={{0,24},{8,16},{16,8},{24,0},{1,25},{9,17},{17,9},{25,1},{2,26},{10... | collective-permute-start | bytes 270344 | tf_op jit(solution)/shard_map/ppermute | solution.py:380
  26.0 1.0 %collective-permute-start.2 = (f32[176,128]{1,0:T(8,128)S(1)}, f32[176,128]{1,0:T(8,128)S(1)}, u32[]{:S(2)}, u32[]{:S(2)}) collective-permute-start(f32[176,128]{1,0:T(8,128)S(1)} %get-tuple-element.19), channel_id=1, source_target_pairs={{0,16},{8,24},{16,0},{24,8},{1,17},{9,25},{17,1},{25,9},{2,18},{10... | collective-permute-start | bytes 270344 | tf_op jit(solution)/shard_map/ppermute | solution.py:380
  27.0 1.1 %collective-permute-start.1 = (f32[176,128]{1,0:T(8,128)S(1)}, f32[176,128]{1,0:T(8,128)S(1)}, u32[]{:S(2)}, u32[]{:S(2)}) collective-permute-start(f32[176,128]{1,0:T(8,128)S(1)} %get-tuple-element.20), channel_id=1, source_target_pairs={{0,8},{8,0},{16,24},{24,16},{1,9},{9,1},{17,25},{25,17},{2,10},{10... | collective-permute-start | bytes 270344 | tf_op jit(solution)/shard_map/ppermute | solution.py:380
  28.1 0.7 constant_dynamic-slice_fusion.1
  28.9 8.2 %collective-permute-done.3.refs_3_ = f32[176,128]{1,0:T(8,128)S(1)} collective-permute-done((f32[176,128]{1,0:T(8,128)S(1)}, f32[176,128]{1,0:T(8,128)S(1)}, u32[]{:S(2)}, u32[]{:S(2)}) %collective-permute-start.3) | collective-permute-done | bytes 90144 | tf_op jit(solution)/shard_map/ppermute | solution.py:380
  37.7 0.9 copy-done.2
  38.6 22.5 %translate_and_interpolate.1 = (f32[4,4,136,128]{3,2,1,0:T(8,128)}, f32[8,128]{1,0:T(8,128)S(1)}) custom-call(s32[1]{0:T(128)} %bitcast.zed, s32[4,24,128]{2,1,0:T(8,128)S(1)} %slice_add_fusion.lists, f32[4,512,128]{2,1,0:T(8,128)S(1)} %all-to-all-done.main, f32[176,128]{1,0:T(8,128)S(1)} %get-tuple-element.17.refs_0_, f32[176,128]{1,0:T(8,128)S(1)} %copy-done.2, ...), custom_call_target="tpu_custom_call" | custom-call | tf_op jit(solution)/shard_map/translate_and_interpolate/pallas_call | solution.py:438
  61.1 8.4 %all-to-all-start.1 = ((f32[16,136,128]{2,1,0:T(8,128)}), f32[16,136,128]{2,1,0:T(8,128)S(1)}, u32[]{:S(2)}, u32[]{:S(2)}) async-start(f32[16,136,128]{2,1,0:T(8,128)} %bitcast.57), calls=%async_computation.1 | async-start | bytes 2228224 | tf_op jit(solution)/shard_map/all_to_all | solution.py:459
  69.5 26.3 %all-to-all-done.1.parts = f32[16,136,128]{2,1,0:T(8,128)S(1)} async-done(((f32[16,136,128]{2,1,0:T(8,128)}), f32[16,136,128]{2,1,0:T(8,128)S(1)}, u32[]{:S(2)}, u32[]{:S(2)}) %all-to-all-start.1) | async-done | bytes 1114144 | tf_op jit(solution)/shard_map/all_to_all | solution.py:459
  95.9 1.5 %join_parts.1 = f32[64,2,4,512]{3,2,1,0:T(4,128)} custom-call(f32[16,136,128]{2,1,0:T(8,128)S(1)} %all-to-all-done.1.parts, f32[1,128]{1,0:T(1,128)S(1)} %slice_subtract_fusion.rims), custom_call_target="tpu_custom_call" | custom-call | tf_op jit(solution)/shard_map/join_parts/pallas_call | solution.py:468
  (57 shorter events, 2.7 us)
Async XLA Ops:
  0.0 11.3 %copy-start = (s32[2048,4]{0,1:T(4,128)S(1)}, s32[2048,4]{0,1:T(4,128)}, u32[]{:S(2)}) copy-start(s32[2048,4]{0,1:T(4,128)} %param.18) | copy-start | bytes 98308
  2.6 7.9 %copy-start.5 = (s32[64]{0:T(128)S(1)}, s32[64]{0:T(128)}, u32[]{:S(2)}) copy-start(s32[64]{0:T(128)} %param.14) | copy-start | bytes 772
  2.6 8.2 %copy-start.7 = (s32[64]{0:T(128)S(1)}, s32[64]{0:T(128)}, u32[]{:S(2)}) copy-start(s32[64]{0:T(128)} %param.15) | copy-start | bytes 772
  2.6 8.6 %copy-start.6 = (s32[256]{0:T(256)S(1)}, s32[256]{0:T(256)}, u32[]{:S(2)}) copy-start(s32[256]{0:T(256)} %param.16) | copy-start | bytes 3076
  2.6 9.4 %copy-start.3 = (s32[64,30]{0,1:T(8,128)S(1)}, s32[64,30]{0,1:T(8,128)}, u32[]{:S(2)}) copy-start(s32[64,30]{0,1:T(8,128)} %param.12) | copy-start | bytes 23044
  2.6 9.5 %copy-start.4 = (s32[64,30]{0,1:T(8,128)S(1)}, s32[64,30]{0,1:T(8,128)}, u32[]{:S(2)}) copy-start(s32[64,30]{0,1:T(8,128)} %param.13) | copy-start | bytes 23044
  2.6 35.1 %all-to-all-start = ((f32[4,512,128]{2,1,0:T(8,128)}), f32[4,512,128]{2,1,0:T(8,128)S(1)}, u32[]{:S(2)}, u32[]{:S(2)}) async-start(f32[4,512,128]{2,1,0:T(8,128)} %pack_sources.2), calls=%async_computation | async-start | bytes 2097152 | tf_op jit(solution)/shard_map/all_to_all | solution.py:306
  9.2 12.8 %collective-permute-start = (f32[16,2,4,512]{3,2,1,0:T(4,128)}, f32[16,2,4,512]{3,2,1,0:T(4,128)}, u32[]{:S(2)}, u32[]{:S(2)}) collective-permute-start(f32[16,2,4,512]{3,2,1,0:T(4,128)} %bitcast.2), channel_id=1, source_target_pairs={{0,4},{4,0},{1,5},{5,1},{2,6},{6,2},{3,7},{7,3},{8,12},{12,8},{9,1... | collective-permute-start | bytes 786440 | tf_op jit(solution)/shard_map/ppermute | solution.py:304
  24.8 12.3 %collective-permute-start.3 = (f32[176,128]{1,0:T(8,128)S(1)}, f32[176,128]{1,0:T(8,128)S(1)}, u32[]{:S(2)}, u32[]{:S(2)}) collective-permute-start(f32[176,128]{1,0:T(8,128)S(1)} %get-tuple-element.18), channel_id=1, source_target_pairs={{0,24},{8,16},{16,8},{24,0},{1,25},{9,17},{17,9},{25,1},{2,26},{10... | collective-permute-start | bytes 270344 | tf_op jit(solution)/shard_map/ppermute | solution.py:380
  26.0 11.0 %collective-permute-start.2 = (f32[176,128]{1,0:T(8,128)S(1)}, f32[176,128]{1,0:T(8,128)S(1)}, u32[]{:S(2)}, u32[]{:S(2)}) collective-permute-start(f32[176,128]{1,0:T(8,128)S(1)} %get-tuple-element.19), channel_id=1, source_target_pairs={{0,16},{8,24},{16,0},{24,8},{1,17},{9,25},{17,1},{25,9},{2,18},{10... | collective-permute-start | bytes 270344 | tf_op jit(solution)/shard_map/ppermute | solution.py:380
  27.0 10.1 %collective-permute-start.1 = (f32[176,128]{1,0:T(8,128)S(1)}, f32[176,128]{1,0:T(8,128)S(1)}, u32[]{:S(2)}, u32[]{:S(2)}) collective-permute-start(f32[176,128]{1,0:T(8,128)S(1)} %get-tuple-element.20), channel_id=1, source_target_pairs={{0,8},{8,0},{16,24},{24,16},{1,9},{9,1},{17,25},{25,17},{2,10},{10... | collective-permute-start | bytes 270344 | tf_op jit(solution)/shard_map/ppermute | solution.py:380
  37.1 0.6 copy-start.1
  37.7 0.9 copy-start.2
  61.1 34.8 %all-to-all-start.1 = ((f32[16,136,128]{2,1,0:T(8,128)}), f32[16,136,128]{2,1,0:T(8,128)S(1)}, u32[]{:S(2)}, u32[]{:S(2)}) async-start(f32[16,136,128]{2,1,0:T(8,128)} %bitcast.57), calls=%async_computation.1 | async-start | bytes 2228224 | tf_op jit(solution)/shard_map/all_to_all | solution.py:459

commit v6 on v5

--- a/solution.py
+++ b/solution.py
@@ -106,7 +106,7 @@
 def fine_kernel(plan, size, edge_size, zed, lists, main, *refs):
     edges = refs[: planes if edge_size else 0]
     refs = refs[len(edges) :]
-    table, phases, weights, out, rims, meta, field, moved, shifted, ready, sems = refs
+    table, phases, weights, out, rims, meta, field, moved, shifted, ready, landed, sems = refs
     rows, fine_rows = plan.rows, plan.fine_rows
     own = zed[0]
 
@@ -114,6 +114,11 @@
         return pltpu.make_async_copy(lists.at[step], meta.at[step % 2], sems.at[planes + step % 2])
 
     bring(0).start()
+    incoming = []
+    for step, edge in enumerate(edges):
+        chosen = edge.at[pl.ds(0, edge_size * 2 * half)]
+        incoming.append(pltpu.make_async_copy(chosen, landed.at[step], sems.at[planes + 2 + step]))
+        incoming[-1].start()
     lane = lax.broadcasted_iota(jnp.int32, rims.shape, 1)
     rims[...] = ((lane < rim) | (lane >= lanes - rim)).astype(jnp.float32)
 
@@ -133,9 +138,10 @@
         lax.fori_loop(0, size, main_step, 0, unroll=8)
     for step, edge in enumerate(edges):
         first = planes * size + (own ^ step) * edge_size
-
-        def edge_step(row, unused, first=first, edge=edge):
-            field[both((first + row) * 4 * half), :] = with_turned(edge[tile(row * 2 * half), :])
+        incoming[step].wait()
+
+        def edge_step(row, unused, first=first, step=step):
+            field[both((first + row) * 4 * half), :] = with_turned(landed[step, tile(row * 2 * half), :])
             return unused
 
         lax.fori_loop(0, edge_size, edge_step, 0, unroll=8)
@@ -155,35 +161,32 @@
         def _():
             bring(turn + 1).start()
 
-
-        def boxes_step(step, unused):
+        def boxes_step(slot_count, step, unused):
             ranks = [step * plan.together + each for each in range(plan.together)]
             boxes = [meta[slot, plan.order, rank] for rank in ranks]
-            turns = meta[slot, plan.order, plan.turns + step]
-
-            def work(slot_count):
-                sums = [[blank, blank] for box in boxes]
-                for pair in range(slot_count):
-                    for each in range(plan.together):
-                        place, kind = parts_of(meta[slot, step, each * plan.width + pair])
-                        value = field[both(place), :]
-                        factor = table[tile(kind), :]
-                        sums[each][0] += factor * value[: 2 * half]
-                        sums[each][1] += factor * value[2 * half :]
+            sums = [[blank, blank] for box in boxes]
+            for pair in range(slot_count):
                 for each in range(plan.together):
-                    straight, crossed = sums[each]
-                    total = jnp.where(
-                        sub < half,
-                        straight + pltpu.roll(straight, half, 0),
-                        pltpu.roll(crossed, half, 0) - crossed,
-                    )
-                    moved[both(boxes[each] * 4 * half), :] = with_turned(total)
-
-            for more in range((plan.slots - plan.fixed) // plan.group + 1):
-                pl.when(turns == more)(functools.partial(work, plan.fixed + more * plan.group))
+                    place, kind = parts_of(meta[slot, step, each * plan.width + pair])
+                    value = field[both(place), :]
+                    factor = table[tile(kind), :]
+                    sums[each][0] += factor * value[: 2 * half]
+                    sums[each][1] += factor * value[2 * half :]
+            for each in range(plan.together):
+                straight, crossed = sums[each]
+                total = jnp.where(
+                    sub < half,
+                    straight + pltpu.roll(straight, half, 0),
+                    pltpu.roll(crossed, half, 0) - crossed,
+                )
+                moved[both(boxes[each] * 4 * half), :] = with_turned(total)
             return unused
 
-        lax.fori_loop(0, rows // plan.together, boxes_step, 0)
+        start = 0
+        for more in reversed(range((plan.slots - plan.fixed) // plan.group + 1)):
+            end = meta[slot, plan.order, plan.turns + more]
+            lax.fori_loop(start, end, functools.partial(boxes_step, plan.fixed + more * plan.group), 0)
+            start = end
 
         def fine_step(block, unused):
             for each in range(lanes):
@@ -334,6 +337,8 @@
     first = rank[None, :] == index[: rows // together, None] * together
     longest = jnp.sum(jnp.where(first, partner_count[None, :], 0), axis=1)
     turns = jnp.maximum((longest - fixed + group - 1) // group, 0)
+    more = jnp.arange((slots - fixed) // group + 1, dtype=jnp.int32)
+    ends = jnp.sum((turns[None, :] >= more[:, None]).astype(jnp.int32), axis=1)
     bounds = jnp.sum(jnp.where(index[None, :] <= index[:, None], child_count[None, :], 0), axis=1)
     parent = jnp.sum(
         (bounds[None, :] <= jnp.arange(fine_rows, dtype=jnp.int32)[:, None]).astype(jnp.int32), axis=1
@@ -352,7 +357,7 @@
 
     list_rows = rows // together
     fine_lists = fine_rows // lanes
-    last = across(jnp.concatenate([across(order[None], turns_at), turns[None]], axis=1))
+    last = across(jnp.concatenate([across(order[None], turns_at), ends[None]], axis=1))
     stride = up(list_rows + fine_lists + 1, 8)
 
     def stacked(*parts):
@@ -371,6 +376,8 @@
 
     if ring_count == 2:
         notes = pack(edges, [meta])
+        after_notes = lax.optimization_barrier((notes, trans_table, dir_angles, stencil_ids, stencil_weights))
+        notes, trans_table, dir_angles, stencil_ids, stencil_weights = after_notes
     else:
         notes = jnp.broadcast_to(meta[None], (planes,) + meta.shape)
     received = []
@@ -442,7 +449,9 @@
             jax.ShapeDtypeStruct((2 * half, lanes), jnp.float32),
         ],
         in_specs=[pl.BlockSpec(memory_space=pltpu.SMEM), pl.BlockSpec(memory_space=pl.ANY)]
-        + [whole] * (len(pieces) + 3),
+        + [whole]
+        + [pl.BlockSpec(memory_space=pl.ANY)] * (len(pieces) - 1)
+        + [whole] * 3,
         out_specs=[pl.BlockSpec(memory_space=pltpu.HBM), whole],
         scratch_shapes=[
             pltpu.SMEM((2, plan.stride, lanes), jnp.int32),
@@ -450,7 +459,8 @@
             pltpu.VMEM((rows * 4 * half, lanes), jnp.float32),
             pltpu.VMEM((fine_rows * 2 * half, lanes), jnp.float32),
             pltpu.VMEM((planes, dir_count) + message, jnp.float32),
-            pltpu.SemaphoreType.DMA((planes + 2,)),
+            pltpu.VMEM((planes, max(edge_rows, 1) * 2 * half, lanes), jnp.float32),
+            pltpu.SemaphoreType.DMA((2 * planes + 2,)),
         ],
         compiler_params=pltpu.CompilerParams(vmem_limit_bytes=48 * 2**20),
         name="translate_and_interpolate",

time: 98.3 us -> 94.5 us (0.961)
  Pallas kernels: 28.4 us -> 25.5 us
  other arithmetic: 8.09 us -> 6.48 us
  waiting for transfers between devices: 34.5 us -> 35.5 us
    pallas_call x1, Pallas kernels: 22.5 us -> 19.6 us  [per_device(): pl.pallas_call(functools.partial(fine_kernel, plan, size, edge_rows), out...]
    ppermute x1, waiting for transfers between devices: 0.01 us -> 1.05 us  [per_device(): edges = lax.ppermute(near_edge(field, ring), 'ring', [(0, 1), (1, 0)])]
    concatenate x1, other arithmetic: 1.08 us -> 0.05 us  [per_device(): passes = jnp.concatenate([high, low, high], axis=0)]
  transfers between devices with their start and end apart: 6 -> 6, of which waited for: 2 -> 3; matrix products, arithmetic and copies ran while one was open for 15% -> 15% of each run, Pallas kernels for 2% -> 2%
where the time goes in v6:
time: 94.5 us; the launch traced here: 93.8 us
  waiting for transfers between devices  35.5 us (38%)
  Pallas kernels  25.5 us (27%)
  starting transfers between devices  17.9 us (19%)
  local copies, waits for them, and re-layouts  8.15 us (9%)
  other arithmetic  6.48 us (7%)
    all_to_all x1, waiting for transfers between devices, per_device(): lax.all_to_all(local_fine.reshape((planes * dir_count,) + message), ('zed...  26.3 us
    pallas_call x1, Pallas kernels, per_device(): pl.pallas_call(functools.partial(fine_kernel, plan, size, edge_rows), out...  19.6 us
    all_to_all x1, starting transfers between devices, per_device(): lax.all_to_all(local_fine.reshape((planes * dir_count,) + message), ('zed...  8.41 us
    ppermute x3, waiting for transfers between devices, per_device(): lax.ppermute(note, 'zed', [(plane, plane ^ step) for plane in range(plane...  8.11 us
    all_to_all x1, starting transfers between devices, per_device(): lax.all_to_all(packed, 'zed', split_axis=0, concat_axis=0, tiled=True)  4.9 us
    pallas_call x2, Pallas kernels, pack(): pl.pallas_call(functools.partial(pack_kernel, source_count), out_shape=pl...  4.35 us
    ppermute x3, starting transfers between devices, per_device(): lax.ppermute(note, 'zed', [(plane, plane ^ step) for plane in range(plane...  3.27 us
    reshape x1, local copies, waits for them, and re-layouts, per_device(): jnp.pad(trans_table, ((0, 0), (0, 0), (0, pad_dirs))).reshape(-1, lanes)  2.32 us
  transfers between devices with their start and end apart: 6, of which 3 were waited for; matrix products, arithmetic and copies ran while one was open for 15% of the time, Pallas kernels for 2%

profile of v6, /device:TPU:11, one launch (start us, length us, event | category | flops | bytes accessed | tf_op | source)
XLA Modules:
  0.0 93.8 jit_solution(2646334156690444681)
XLA Ops:
  0.0 2.6 %pack_sources.2 = f32[4,512,128]{2,1,0:T(8,128)} custom-call(f32[64,2,4,512]{3,2,1,0:T(4,128)} %field.1), custom_call_target="tpu_custom_call" | custom-call | tf_op jit(solution)/shard_map/pack_sources/pallas_call | solution.py:88
  2.6 4.9 %all-to-all-start = ((f32[4,512,128]{2,1,0:T(8,128)}), f32[4,512,128]{2,1,0:T(8,128)S(1)}, u32[]{:S(2)}, u32[]{:S(2)}) async-start(f32[4,512,128]{2,1,0:T(8,128)} %pack_sources.2), calls=%async_computation | async-start | bytes 2097152 | tf_op jit(solution)/shard_map/all_to_all | solution.py:309
  7.5 1.0 %constant_dynamic-slice_fusion.2 = f32[2,1,2,1,2,2,2,4,512]{8,7,6,5,4,3,2,1,0:T(4,128)S(1)} fusion(f32[2,2,2,2,2,2,2,4,512]{8,7,6,5,4,3,2,1,0:T(4,128)} %bitcast.49, s32[]{:T(128)S(6)} %select_n.176), kind=kLoop, calls=%fused_computation.107 | loop fusion | bytes 524292 | tf_op jit(solution)/shard_map/jit(dynamic_index_in_dim)/dynamic_slice | solution.py:39
  8.5 1.3 %collective-permute-start = (f32[16,2,4,512]{3,2,1,0:T(4,128)S(1)}, f32[16,2,4,512]{3,2,1,0:T(4,128)S(1)}, u32[]{:S(2)}, u32[]{:S(2)}) collective-permute-start(f32[16,2,4,512]{3,2,1,0:T(4,128)S(1)} %bitcast.51), channel_id=1, source_target_pairs={{0,4},{4,0},{1,5},{5,1},{2,6},{6,2},{3,7},{7,3},{8,12},{12,8},{9,1... | collective-permute-start | bytes 786440 | tf_op jit(solution)/shard_map/ppermute | solution.py:307
  10.9 2.2 %select_reduce_fusion.1 = (s32[64,32]{1,0:T(8,128)S(1)}, s32[64,32]{1,0:T(8,128)S(1)}) fusion(s32[64,32]{0,1:T(8,128)S(1)} %pad.23, pred[64,64]{1,0:T(8,128)(4,1)S(1)} %iota_compare_fusion.3, s32[64,32]{0,1:T(8,128)S(1)} %pad.25), kind=kLoop, calls=%fused_computation.1 | loop fusion | flops 520192 | bytes 36864 | tf_op jit(solution)/shard_map/reduce_sum | solution.py:355
  14.1 1.0 %collective-permute-done.field = f32[16,2,4,512]{3,2,1,0:T(4,128)S(1)} collective-permute-done((f32[16,2,4,512]{3,2,1,0:T(4,128)S(1)}, f32[16,2,4,512]{3,2,1,0:T(4,128)S(1)}, u32[]{:S(2)}, u32[]{:S(2)}) %collective-permute-start) | collective-permute-done | bytes 262176 | tf_op jit(solution)/shard_map/ppermute | solution.py:307
  15.1 0.7 copy-done.1
  15.8 1.8 %pack_sources.3 = f32[4,176,128]{2,1,0:T(8,128)} custom-call(f32[16,2,4,512]{3,2,1,0:T(4,128)} %copy-done.1, f32[48,128]{1,0:T(8,128)} %pad_maximum_fusion.2.refs_0_), custom_call_target="tpu_custom_call" | custom-call | tf_op jit(solution)/shard_map/pack_sources/pallas_call | solution.py:88
  17.6 0.7 dynamic-slice_bitcast_fusion.4
  18.3 1.7 %dynamic-slice_bitcast_fusion.3 = (f32[176,128]{1,0:T(8,128)S(1)}, f32[176,128]{1,0:T(8,128)}, f32[176,128]{1,0:T(8,128)}, f32[176,128]{1,0:T(8,128)}) fusion(f32[4,176,128]{2,1,0:T(8,128)} %pack_sources.3, s32[]{:T(128)S(6)} %select_n.196, s32[]{:T(128)S(6)} %select_n.199, s32[]{:T(128)S(6)} %select_n.198, s32[]{:T(128)S(6)} %select_n.197), kind=kLoop, calls=%fused_computation.15 | loop fusion | bytes 720912 | tf_op jit(solution)/shard_map/jit(dynamic_index_in_dim)/squeeze | solution.py:385
  20.1 1.2 %collective-permute-start.3 = (f32[176,128]{1,0:T(8,128)}, f32[176,128]{1,0:T(8,128)S(1)}, u32[]{:S(2)}, u32[]{:S(2)}) collective-permute-start(f32[176,128]{1,0:T(8,128)} %get-tuple-element.28), channel_id=1, source_target_pairs={{0,24},{8,16},{16,8},{24,0},{1,25},{9,17},{17,9},{25,1},{2,26},{10... | collective-permute-start | bytes 270344 | tf_op jit(solution)/shard_map/ppermute | solution.py:387
  21.3 1.2 %collective-permute-start.2 = (f32[176,128]{1,0:T(8,128)}, f32[176,128]{1,0:T(8,128)S(1)}, u32[]{:S(2)}, u32[]{:S(2)}) collective-permute-start(f32[176,128]{1,0:T(8,128)} %get-tuple-element.29), channel_id=1, source_target_pairs={{0,16},{8,24},{16,0},{24,8},{1,17},{9,25},{17,1},{25,9},{2,18},{10... | collective-permute-start | bytes 270344 | tf_op jit(solution)/shard_map/ppermute | solution.py:387
  22.5 0.9 collective-permute-start.1
  23.3 0.6 select_add_fusion
  24.0 0.6 select_add_fusion.1
  24.6 2.3 %reshape.223.refs_4_ = f32[2528,128]{1,0:T(8,128)S(1)} reshape(f32[316,2,512]{2,1,0:T(2,128)} %param.11) | data formatting | bytes 2588672 | tf_op jit(solution)/shard_map/reshape | solution.py:403
  26.9 0.9 cosine_multiply_fusion
  28.2 0.7 constant_dynamic-slice_fusion.1
  29.0 8.1 %collective-permute-done.3.refs_3_ = f32[176,128]{1,0:T(8,128)S(1)} collective-permute-done((f32[176,128]{1,0:T(8,128)}, f32[176,128]{1,0:T(8,128)S(1)}, u32[]{:S(2)}, u32[]{:S(2)}) %collective-permute-start.3) | collective-permute-done | bytes 90144 | tf_op jit(solution)/shard_map/ppermute | solution.py:387
  37.1 0.7 slice_bitcast_fusion.2
  37.9 19.6 %translate_and_interpolate.1 = (f32[4,4,136,128]{3,2,1,0:T(8,128)}, f32[8,128]{1,0:T(8,128)S(1)}) custom-call(s32[1]{0:T(128)} %bitcast.zed, s32[4,24,128]{2,1,0:T(8,128)S(1)} %slice_add_fusion.lists, f32[4,512,128]{2,1,0:T(8,128)S(1)} %all-to-all-done.main, f32[176,128]{1,0:T(8,128)S(1)} %get-tuple-element.27.refs_0_, ...), custom_call_target="tpu_custom_call" | custom-call | tf_op jit(solution)/shard_map/translate_and_interpolate/pallas_call | solution.py:445
  57.5 8.4 %all-to-all-start.1 = ((f32[16,136,128]{2,1,0:T(8,128)}), f32[16,136,128]{2,1,0:T(8,128)S(1)}, u32[]{:S(2)}, u32[]{:S(2)}) async-start(f32[16,136,128]{2,1,0:T(8,128)} %bitcast.50), calls=%async_computation.1 | async-start | bytes 2228224 | tf_op jit(solution)/shard_map/all_to_all | solution.py:469
  65.9 26.3 %all-to-all-done.1.parts = f32[16,136,128]{2,1,0:T(8,128)S(1)} async-done(((f32[16,136,128]{2,1,0:T(8,128)}), f32[16,136,128]{2,1,0:T(8,128)S(1)}, u32[]{:S(2)}, u32[]{:S(2)}) %all-to-all-start.1) | async-done | bytes 1114144 | tf_op jit(solution)/shard_map/all_to_all | solution.py:469
  92.3 1.5 %join_parts.1 = f32[64,2,4,512]{3,2,1,0:T(4,128)} custom-call(f32[16,136,128]{2,1,0:T(8,128)S(1)} %all-to-all-done.1.parts, f32[1,128]{1,0:T(1,128)S(1)} %slice_subtract_fusion.rims), custom_call_target="tpu_custom_call" | custom-call | tf_op jit(solution)/shard_map/join_parts/pallas_call | solution.py:478
  (56 shorter events, 2.3 us)
Async XLA Ops:
  0.0 17.6 %copy-start = (s32[2048,4]{0,1:T(4,128)S(1)}, s32[2048,4]{0,1:T(4,128)}, u32[]{:S(2)}) copy-start(s32[2048,4]{0,1:T(4,128)} %param.18) | copy-start | bytes 98308
  2.6 7.2 %copy-start.4 = (s32[64]{0:T(128)S(1)}, s32[64]{0:T(128)}, u32[]{:S(2)}) copy-start(s32[64]{0:T(128)} %param.14) | copy-start | bytes 772
  2.6 7.5 %copy-start.6 = (s32[64]{0:T(128)S(1)}, s32[64]{0:T(128)}, u32[]{:S(2)}) copy-start(s32[64]{0:T(128)} %param.15) | copy-start | bytes 772
  2.6 8.1 %copy-start.5 = (s32[256]{0:T(256)S(1)}, s32[256]{0:T(256)}, u32[]{:S(2)}) copy-start(s32[256]{0:T(256)} %param.16) | copy-start | bytes 3076
  2.6 8.1 %copy-start.2 = (s32[64,30]{0,1:T(8,128)S(1)}, s32[64,30]{0,1:T(8,128)}, u32[]{:S(2)}) copy-start(s32[64,30]{0,1:T(8,128)} %param.12) | copy-start | bytes 23044
  2.6 8.3 %copy-start.3 = (s32[64,30]{0,1:T(8,128)S(1)}, s32[64,30]{0,1:T(8,128)}, u32[]{:S(2)}) copy-start(s32[64,30]{0,1:T(8,128)} %param.13) | copy-start | bytes 23044
  2.6 35.2 %all-to-all-start = ((f32[4,512,128]{2,1,0:T(8,128)}), f32[4,512,128]{2,1,0:T(8,128)S(1)}, u32[]{:S(2)}, u32[]{:S(2)}) async-start(f32[4,512,128]{2,1,0:T(8,128)} %pack_sources.2), calls=%async_computation | async-start | bytes 2097152 | tf_op jit(solution)/shard_map/all_to_all | solution.py:309
  8.5 6.6 %collective-permute-start = (f32[16,2,4,512]{3,2,1,0:T(4,128)S(1)}, f32[16,2,4,512]{3,2,1,0:T(4,128)S(1)}, u32[]{:S(2)}, u32[]{:S(2)}) collective-permute-start(f32[16,2,4,512]{3,2,1,0:T(4,128)S(1)} %bitcast.51), channel_id=1, source_target_pairs={{0,4},{4,0},{1,5},{5,1},{2,6},{6,2},{3,7},{7,3},{8,12},{12,8},{9,1... | collective-permute-start | bytes 786440 | tf_op jit(solution)/shard_map/ppermute | solution.py:307
  15.1 0.7 copy-start.1
  20.1 17.0 %collective-permute-start.3 = (f32[176,128]{1,0:T(8,128)}, f32[176,128]{1,0:T(8,128)S(1)}, u32[]{:S(2)}, u32[]{:S(2)}) collective-permute-start(f32[176,128]{1,0:T(8,128)} %get-tuple-element.28), channel_id=1, source_target_pairs={{0,24},{8,16},{16,8},{24,0},{1,25},{9,17},{17,9},{25,1},{2,26},{10... | collective-permute-start | bytes 270344 | tf_op jit(solution)/shard_map/ppermute | solution.py:387
  21.3 15.8 %collective-permute-start.2 = (f32[176,128]{1,0:T(8,128)}, f32[176,128]{1,0:T(8,128)S(1)}, u32[]{:S(2)}, u32[]{:S(2)}) collective-permute-start(f32[176,128]{1,0:T(8,128)} %get-tuple-element.29), channel_id=1, source_target_pairs={{0,16},{8,24},{16,0},{24,8},{1,17},{9,25},{17,1},{25,9},{2,18},{10... | collective-permute-start | bytes 270344 | tf_op jit(solution)/shard_map/ppermute | solution.py:387
  22.5 14.6 %collective-permute-start.1 = (f32[176,128]{1,0:T(8,128)}, f32[176,128]{1,0:T(8,128)}, u32[]{:S(2)}, u32[]{:S(2)}) collective-permute-start(f32[176,128]{1,0:T(8,128)} %get-tuple-element.30), channel_id=1, source_target_pairs={{0,8},{8,0},{16,24},{24,16},{1,9},{9,1},{17,25},{25,17},{2,10},{10... | collective-permute-start | bytes 270344 | tf_op jit(solution)/shard_map/ppermute | solution.py:387
  57.5 34.8 %all-to-all-start.1 = ((f32[16,136,128]{2,1,0:T(8,128)}), f32[16,136,128]{2,1,0:T(8,128)S(1)}, u32[]{:S(2)}, u32[]{:S(2)}) async-start(f32[16,136,128]{2,1,0:T(8,128)} %bitcast.50), calls=%async_computation.1 | async-start | bytes 2228224 | tf_op jit(solution)/shard_map/all_to_all | solution.py:469

commit v7 on v6

--- a/solution.py
+++ b/solution.py
@@ -57,8 +57,8 @@
     return high, low
 
 
-def pack_kernel(source_count, field, *refs):
-    notes, (out, whole) = refs[:-2], refs[-2:]
+def pack_kernel(source_count, note_count, zed, field, *refs):
+    notes, outs, whole = refs[:note_count], refs[note_count:-1], refs[-1]
     rows = field.shape[0]
     stride = 2 * source_count
 
@@ -71,28 +71,29 @@
         return unused
 
     lax.fori_loop(0, rows, row_step, 0, unroll=8)
-    for source in range(source_count):
+    for step, out in enumerate(outs):
+        source = zed[0] ^ step
         for part in range(2):
             for block in range(half):
-                out[source, pl.ds(part * half + block, rows, stride=2 * half), :] = whole[
+                out[pl.ds(part * half + block, rows, stride=2 * half), :] = whole[
                     block, pl.ds(part * source_count + source, rows, stride=stride), :
                 ]
         for note in notes:
-            out[source, rows * 2 * half :, :] = note[...]
-
-
-def pack(field, notes):
+            out[rows * 2 * half :, :] = note[...]
+
+
+def pack(zed, field, notes):
     rows, _, source_count, width = field.shape
     length = rows * 2 * half + sum(note.shape[0] for note in notes)
     whole = pl.BlockSpec(memory_space=pltpu.VMEM)
     return pl.pallas_call(
-        functools.partial(pack_kernel, source_count),
-        out_shape=pltpu.HBM((source_count, length, lanes), jnp.float32),
-        in_specs=[whole] * (1 + len(notes)),
-        out_specs=whole,
+        functools.partial(pack_kernel, source_count, len(notes)),
+        out_shape=[jax.ShapeDtypeStruct((length, lanes), jnp.float32)] * planes,
+        in_specs=[pl.BlockSpec(memory_space=pltpu.SMEM)] + [whole] * (1 + len(notes)),
+        out_specs=[whole] * planes,
         scratch_shapes=[pltpu.VMEM((half, rows * 2 * source_count, lanes), jnp.float32)],
         name="pack_sources",
-    )(field, *notes)
+    )(zed, field, *notes)
 
 
 def parts_of(word):
@@ -103,7 +104,8 @@
     return pl.ds(pl.multiple_of(start, 2 * half), 2 * half)
 
 
-def fine_kernel(plan, size, edge_size, zed, lists, main, *refs):
+def fine_kernel(plan, size, edge_size, zed, lists, *refs):
+    mains, refs = refs[:planes], refs[planes:]
     edges = refs[: planes if edge_size else 0]
     refs = refs[len(edges) :]
     table, phases, weights, out, rims, meta, field, moved, shifted, ready, landed, sems = refs
@@ -128,11 +130,11 @@
     def with_turned(value):
         return jnp.concatenate([value, pltpu.roll(value, half, 0)], axis=0)
 
-    for plane in range(planes):
-
-        def main_step(row, unused, plane=plane):
-            value = main[plane, tile(row * 2 * half), :]
-            field[both((plane * size + row) * 4 * half), :] = with_turned(value)
+    for step, main in enumerate(mains):
+        first = (own ^ step) * size
+
+        def main_step(row, unused, first=first, main=main):
+            field[both((first + row) * 4 * half), :] = with_turned(main[tile(row * 2 * half), :])
             return unused
 
         lax.fori_loop(0, size, main_step, 0, unroll=8)
@@ -160,6 +162,8 @@
         @pl.when(turn + 1 < planes)
         def _():
             bring(turn + 1).start()
+
+        across = lanes // plan.width
 
         def boxes_step(slot_count, step, unused):
             ranks = [step * plan.together + each for each in range(plan.together)]
@@ -167,7 +171,8 @@
             sums = [[blank, blank] for box in boxes]
             for pair in range(slot_count):
                 for each in range(plan.together):
-                    place, kind = parts_of(meta[slot, step, each * plan.width + pair])
+                    row = step * (plan.together // across) + each // across
+                    place, kind = parts_of(meta[slot, row, each % across * plan.width + pair])
                     value = field[both(place), :]
                     factor = table[tile(kind), :]
                     sums[each][0] += factor * value[: 2 * half]
@@ -300,13 +305,20 @@
     dest_rows = fine_rows // dir_count
 
     field = jnp.pad(coarse_field, ((0, 0), (0, 0), (0, 0), (0, pad_dirs)))
-    packed = pack(field, [])
+    here = zed.reshape(1)
+    packed = pack(here, field, [])
     edge_rows = 0
     if ring_count == 2:
         packed, field = lax.optimization_barrier((packed, field))
         edges = lax.ppermute(near_edge(field, ring), "ring", [(0, 1), (1, 0)])
         edge_rows = edges.shape[0]
-    arrived = lax.all_to_all(packed, "zed", split_axis=0, concat_axis=0, tiled=True)
+
+    def to_planes(note, step):
+        if step == 0:
+            return note
+        return lax.ppermute(note, "zed", [(plane, plane ^ step) for plane in range(planes)])
+
+    arrived = [to_planes(packed[step], step) for step in (3, 2, 1, 0)][::-1]
 
     plane_of = partner_ids // (ring_count * rows)
     ring_of = partner_ids // rows % ring_count
@@ -324,7 +336,7 @@
         place = partner_ids
     field_rows = planes * (size + edge_rows)
     place = jnp.where(live, place, field_rows)
-    together = 4
+    together = 8
     fixed = slots // 2
     group = 3 if (slots - fixed) % 3 == 0 else 1
     index = jnp.arange(rows, dtype=jnp.int32)
@@ -346,16 +358,16 @@
     def across(one, width=lanes):
         return jnp.pad(one, ((0, 0), (0, width - one.shape[1])))
 
-    width = lanes // together
+    width = lanes // half
     turns_at = lanes // 2
     assert slots <= width and rows <= turns_at and fine_rows % lanes == 0
     assert (field_rows + 1) * 4 * half < 2 ** (31 - word_bits) and type_count * 2 * half < 2**word_bits
 
     def in_order(one):
         one = jnp.sum(jnp.where(at_rank[:, :, None], across(one, width)[None], 0), axis=1)
-        return one.reshape(rows // together, lanes)
-
-    list_rows = rows // together
+        return one.reshape(rows * width // lanes, lanes)
+
+    list_rows = rows * width // lanes
     fine_lists = fine_rows // lanes
     last = across(jnp.concatenate([across(order[None], turns_at), ends[None]], axis=1))
     stride = up(list_rows + fine_lists + 1, 8)
@@ -374,25 +386,16 @@
         rows, slots, fine_rows, stride, width, list_rows, list_rows + fine_lists, turns_at, together, fixed, group
     )
 
-    if ring_count == 2:
-        notes = pack(edges, [meta])
-        after_notes = lax.optimization_barrier((notes, trans_table, dir_angles, stencil_ids, stencil_weights))
-        notes, trans_table, dir_angles, stencil_ids, stencil_weights = after_notes
-    else:
-        notes = jnp.broadcast_to(meta[None], (planes,) + meta.shape)
-    received = []
-    for step in range(planes):
-        note = lax.dynamic_index_in_dim(notes, zed ^ step, axis=0, keepdims=False)
-        if step:
-            note = lax.ppermute(note, "zed", [(plane, plane ^ step) for plane in range(planes)])
-        received.append(note)
+    notes = pack(here, edges, [meta]) if ring_count == 2 else [meta] * planes
+    after_notes = lax.optimization_barrier((notes, trans_table, dir_angles, stencil_ids, stencil_weights))
+    notes, trans_table, dir_angles, stencil_ids, stencil_weights = after_notes
+    received = [to_planes(notes[step], step) for step in (3, 2, 1, 0)][::-1]
     edge_part = edge_rows * 2 * half
     numbers = jnp.stack([note[edge_part:] for note in received]).astype(jnp.int32)
     meta = numbers[:, :stride] * 2**word_bits + numbers[:, stride:]
-    if ring_count == 2:
-        pieces = [arrived] + received
-    else:
-        pieces = [lax.all_gather(arrived, "ring", axis=1, tiled=True)]
+    if ring_count != 2:
+        arrived = [lax.all_gather(one, "ring", axis=0, tiled=True) for one in arrived]
+        received = []
 
     def blocks(table):
         return jnp.pad(table, ((0, 0), (0, pad_dirs))).reshape(-1, half, lanes)
@@ -449,8 +452,8 @@
             jax.ShapeDtypeStruct((2 * half, lanes), jnp.float32),
         ],
         in_specs=[pl.BlockSpec(memory_space=pltpu.SMEM), pl.BlockSpec(memory_space=pl.ANY)]
-        + [whole]
-        + [pl.BlockSpec(memory_space=pl.ANY)] * (len(pieces) - 1)
+        + [whole] * planes
+        + [pl.BlockSpec(memory_space=pl.ANY)] * len(received)
         + [whole] * 3,
         out_specs=[pl.BlockSpec(memory_space=pltpu.HBM), whole],
         scratch_shapes=[
@@ -464,7 +467,7 @@
         ],
         compiler_params=pltpu.CompilerParams(vmem_limit_bytes=48 * 2**20),
         name="translate_and_interpolate",
-    )(zed.reshape(1), meta, *pieces, table, phases, passes)
+    )(here, meta, *arrived, *received, table, phases, passes)
 
     parts = lax.all_to_all(
         local_fine.reshape((planes * dir_count,) + message),

time: 94.5 us -> 93.8 us (level)
  waiting for transfers between devices: 35.5 us -> 38.4 us
  local copies, waits for them, and re-layouts: 8.15 us -> 5.66 us
  starting transfers between devices: 17.9 us -> 15.8 us
  Pallas kernels: 25.5 us -> 26.6 us
    all_to_all x1 -> x0, starting transfers between devices: 4.9 us -> none  [per_device(): lax.all_to_all(packed, 'zed', split_axis=0, concat_axis=0, tiled=True)]
    ppermute x3 -> x6, waiting for transfers between devices: 8.11 us -> 12.1 us  [to_planes(): lax.ppermute(note, 'zed', [(plane, plane ^ step) for plane in range(plane...]
    ppermute x3 -> x6, starting transfers between devices: 3.27 us -> 7.16 us  [to_planes(): lax.ppermute(note, 'zed', [(plane, plane ^ step) for plane in range(plane...]
    squeeze x1 -> x0, local copies, waits for them, and re-layouts: 1.75 us -> none  [per_device(): note = lax.dynamic_index_in_dim(notes, zed ^ step, axis=0, keepdims=False)]
    all_to_all x1, starting transfers between devices: 8.41 us -> 7.29 us  [per_device(): lax.all_to_all(local_fine.reshape((planes * dir_count,) + message), ('zed...]
    ppermute x1, waiting for transfers between devices: 1.05 us -> 0.01 us  [per_device(): edges = lax.ppermute(near_edge(field, ring), 'ring', [(0, 1), (1, 0)])]
    pallas_call x1, Pallas kernels: 19.6 us -> 20.6 us  [per_device(): pl.pallas_call(functools.partial(fine_kernel, plan, size, edge_rows), out...]
  transfers between devices with their start and end apart: 6 -> 8, of which waited for: 3 -> 4; matrix products, arithmetic and copies ran while one was open for 15% -> 11% of each run, Pallas kernels for 2% -> 2%
where the time goes in v7:
time: 93.8 us; the launch traced here: 93.2 us
  waiting for transfers between devices  38.4 us (41%)
  Pallas kernels  26.6 us (28%)
  starting transfers between devices  15.8 us (17%)
  other arithmetic  6.48 us (7%)
  local copies, waits for them, and re-layouts  5.66 us (6%)
    all_to_all x1, waiting for transfers between devices, per_device(): lax.all_to_all(local_fine.reshape((planes * dir_count,) + message), ('zed...  26.3 us
    pallas_call x1, Pallas kernels, per_device(): pl.pallas_call(functools.partial(fine_kernel, plan, size, edge_rows), out...  20.6 us
    ppermute x6, waiting for transfers between devices, to_planes(): lax.ppermute(note, 'zed', [(plane, plane ^ step) for plane in range(plane...  12.1 us
    all_to_all x1, starting transfers between devices, per_device(): lax.all_to_all(local_fine.reshape((planes * dir_count,) + message), ('zed...  7.29 us
    ppermute x6, starting transfers between devices, to_planes(): lax.ppermute(note, 'zed', [(plane, plane ^ step) for plane in range(plane...  7.16 us
    pallas_call x2, Pallas kernels, pack(): pl.pallas_call(functools.partial(pack_kernel, source_count, len(notes)),...  4.44 us
    reshape x1, local copies, waits for them, and re-layouts, per_device(): jnp.pad(trans_table, ((0, 0), (0, 0), (0, pad_dirs))).reshape(-1, lanes)  2.32 us
    reduce_sum x1, other arithmetic, in_order(): jnp.sum(jnp.where(at_rank[:, :, None], across(one, width)[None], 0), axis=1)  2.24 us
  transfers between devices with their start and end apart: 8, of which 4 were waited for; matrix products, arithmetic and copies ran while one was open for 11% of the time, Pallas kernels for 2%

profile of v7, /device:TPU:11, one launch (start us, length us, event | category | flops | bytes accessed | tf_op | source)
XLA Modules:
  0.0 93.2 jit_solution(7809455116813012176)
XLA Ops:
  0.1 2.6 %pack_sources.2 = (f32[512,128]{1,0:T(8,128)}, f32[512,128]{1,0:T(8,128)}, f32[512,128]{1,0:T(8,128)}, f32[512,128]{1,0:T(8,128)}) custom-call(s32[1]{0:T(128)} %bitcast.zed, f32[64,2,4,512]{3,2,1,0:T(4,128)} %field.1), custom_call_target="tpu_custom_call" | custom-call | tf_op jit(solution)/shard_map/pack_sources/pallas_call | solution.py:89
  2.7 1.0 %constant_dynamic-slice_fusion.1 = f32[2,1,2,1,2,2,2,4,512]{8,7,6,5,4,3,2,1,0:T(4,128)S(1)} fusion(f32[2,2,2,2,2,2,2,4,512]{8,7,6,5,4,3,2,1,0:T(4,128)} %bitcast.43, s32[]{:T(128)S(6)} %select_n.161), kind=kLoop, calls=%fused_computation.117 | loop fusion | bytes 524292 | tf_op jit(solution)/shard_map/jit(dynamic_index_in_dim)/dynamic_slice | solution.py:39
  3.7 1.3 %collective-permute-start = (f32[16,2,4,512]{3,2,1,0:T(4,128)S(1)}, f32[16,2,4,512]{3,2,1,0:T(4,128)S(1)}, u32[]{:S(2)}, u32[]{:S(2)}) collective-permute-start(f32[16,2,4,512]{3,2,1,0:T(4,128)S(1)} %bitcast.45), channel_id=1, source_target_pairs={{0,4},{4,0},{1,5},{5,1},{2,6},{6,2},{3,7},{7,3},{8,12},{12,8},{9,1... | collective-permute-start | bytes 786440 | tf_op jit(solution)/shard_map/ppermute | solution.py:313
  5.1 2.3 %collective-permute-start.5 = (f32[512,128]{1,0:T(8,128)}, f32[512,128]{1,0:T(8,128)S(1)}, u32[]{:S(2)}, u32[]{:S(2)}) collective-permute-start(f32[512,128]{1,0:T(8,128)} %get-tuple-element.43), channel_id=1, source_target_pairs={{0,16},{8,24},{16,0},{24,8},{1,17},{9,25},{17,1},{25,9},{2,18},{10... | collective-permute-start | bytes 786440 | tf_op jit(solution)/shard_map/ppermute | solution.py:319
  8.7 2.2 %select_reduce_fusion.1 = (s32[64,32]{1,0:T(8,128)S(1)}, s32[64,32]{1,0:T(8,128)S(1)}) fusion(s32[64,32]{0,1:T(8,128)S(1)} %pad.23, pred[64,64]{1,0:T(8,128)(4,1)S(1)} %iota_compare_fusion.3, s32[64,32]{0,1:T(8,128)S(1)} %pad.25), kind=kLoop, calls=%fused_computation.1 | loop fusion | flops 520192 | bytes 36864 | tf_op jit(solution)/shard_map/reduce_sum | solution.py:367
  11.3 0.6 pad_maximum_fusion.2.refs_0_
  11.9 0.7 copy-done.3
  12.6 1.8 %pack_sources.3 = (f32[176,128]{1,0:T(8,128)}, f32[176,128]{1,0:T(8,128)}, f32[176,128]{1,0:T(8,128)}, f32[176,128]{1,0:T(8,128)}) custom-call(s32[1]{0:T(128)} %bitcast.zed, f32[16,2,4,512]{3,2,1,0:T(4,128)} %copy-done.3, f32[48,128]{1,0:T(8,128)} %pad_maximum_fusion.2.refs_0_), custom_call_target="tpu_custom_call" | custom-call | tf_op jit(solution)/shard_map/pack_sources/pallas_call | solution.py:89
  14.4 0.7 dynamic-slice_bitcast_fusion
  15.1 0.7 slice_bitcast_fusion.3
  15.9 1.1 %collective-permute-start.1 = (f32[176,128]{1,0:T(8,128)}, f32[176,128]{1,0:T(8,128)S(1)}, u32[]{:S(2)}, u32[]{:S(2)}) collective-permute-start(f32[176,128]{1,0:T(8,128)} %get-tuple-element.38), channel_id=1, source_target_pairs={{0,8},{8,0},{16,24},{24,16},{1,9},{9,1},{17,25},{25,17},{2,10},{10... | collective-permute-start | bytes 270344 | tf_op jit(solution)/shard_map/ppermute | solution.py:319
  17.0 2.1 %collective-permute-start.2 = (f32[176,128]{1,0:T(8,128)}, f32[176,128]{1,0:T(8,128)S(1)}, u32[]{:S(2)}, u32[]{:S(2)}) collective-permute-start(f32[176,128]{1,0:T(8,128)} %get-tuple-element.39), channel_id=1, source_target_pairs={{0,16},{8,24},{16,0},{24,8},{1,17},{9,25},{17,1},{25,9},{2,18},{10... | collective-permute-start | bytes 270344 | tf_op jit(solution)/shard_map/ppermute | solution.py:319
  19.1 0.6 select_add_fusion
  19.7 0.6 select_add_fusion.1
  20.3 2.3 %reshape.221.refs_8_ = f32[2528,128]{1,0:T(8,128)S(1)} reshape(f32[316,2,512]{2,1,0:T(2,128)} %param.11) | data formatting | bytes 2588672 | tf_op jit(solution)/shard_map/reshape | solution.py:406
  22.6 0.9 cosine_multiply_fusion
  24.0 1.0 %collective-permute-done.1.refs_5_ = f32[176,128]{1,0:T(8,128)S(1)} collective-permute-done((f32[176,128]{1,0:T(8,128)}, f32[176,128]{1,0:T(8,128)S(1)}, u32[]{:S(2)}, u32[]{:S(2)}) %collective-permute-start.1) | collective-permute-done | bytes 90144 | tf_op jit(solution)/shard_map/ppermute | solution.py:319
  25.0 1.3 %collective-permute-start.3 = (f32[176,128]{1,0:T(8,128)S(1)}, f32[176,128]{1,0:T(8,128)S(1)}, u32[]{:S(2)}, u32[]{:S(2)}) collective-permute-start(f32[176,128]{1,0:T(8,128)S(1)} %copy-done.8), channel_id=1, source_target_pairs={{0,24},{8,16},{16,8},{24,0},{1,25},{9,17},{17,9},{25,1},{2,26},{10... | collective-permute-start | bytes 270344 | tf_op jit(solution)/shard_map/ppermute | solution.py:319
  26.3 8.6 %collective-permute-done.2.refs_6_ = f32[176,128]{1,0:T(8,128)S(1)} collective-permute-done((f32[176,128]{1,0:T(8,128)}, f32[176,128]{1,0:T(8,128)S(1)}, u32[]{:S(2)}, u32[]{:S(2)}) %collective-permute-start.2) | collective-permute-done | bytes 90144 | tf_op jit(solution)/shard_map/ppermute | solution.py:319
  34.9 2.4 %collective-permute-done.3.refs_7_ = f32[176,128]{1,0:T(8,128)S(1)} collective-permute-done((f32[176,128]{1,0:T(8,128)S(1)}, f32[176,128]{1,0:T(8,128)S(1)}, u32[]{:S(2)}, u32[]{:S(2)}) %collective-permute-start.3) | collective-permute-done | bytes 90144 | tf_op jit(solution)/shard_map/ppermute | solution.py:319
  37.4 20.6 %translate_and_interpolate.1 = (f32[4,4,136,128]{3,2,1,0:T(8,128)}, f32[8,128]{1,0:T(8,128)S(1)}) custom-call(s32[1]{0:T(128)} %bitcast.zed, s32[4,24,128]{2,1,0:T(8,128)S(1)} %slice_add_fusion.lists, f32[512,128]{1,0:T(8,128)S(1)} %copy-done.1, f32[512,128]{1,0:T(8,128)S(1)} %collective-permute-done.4.refs_1_, ...), custom_call_target="tpu_custom_call" | custom-call | tf_op jit(solution)/shard_map/translate_and_interpolate/pallas_call | solution.py:448
  58.1 7.3 %all-to-all-start = ((f32[16,136,128]{2,1,0:T(8,128)}), f32[16,136,128]{2,1,0:T(8,128)S(1)}, u32[]{:S(2)}, u32[]{:S(2)}) async-start(f32[16,136,128]{2,1,0:T(8,128)} %bitcast.44), calls=%async_computation | async-start | bytes 2228224 | tf_op jit(solution)/shard_map/all_to_all | solution.py:472
  65.4 26.3 %all-to-all-done.parts = f32[16,136,128]{2,1,0:T(8,128)S(1)} async-done(((f32[16,136,128]{2,1,0:T(8,128)}), f32[16,136,128]{2,1,0:T(8,128)S(1)}, u32[]{:S(2)}, u32[]{:S(2)}) %all-to-all-start) | async-done | bytes 1114144 | tf_op jit(solution)/shard_map/all_to_all | solution.py:472
  91.7 1.5 %join_parts.1 = f32[64,2,4,512]{3,2,1,0:T(4,128)} custom-call(f32[16,136,128]{2,1,0:T(8,128)S(1)} %all-to-all-done.parts, f32[1,128]{1,0:T(1,128)S(1)} %slice_subtract_fusion.rims), custom_call_target="tpu_custom_call" | custom-call | tf_op jit(solution)/shard_map/join_parts/pallas_call | solution.py:481
  (65 shorter events, 2.1 us)
Async XLA Ops:
  0.0 14.4 %copy-start = (s32[2048,4]{0,1:T(4,128)S(1)}, s32[2048,4]{0,1:T(4,128)}, u32[]{:S(2)}) copy-start(s32[2048,4]{0,1:T(4,128)} %param.18) | copy-start | bytes 98308
  0.0 7.6 %copy-start.6 = (s32[64]{0:T(128)S(1)}, s32[64]{0:T(128)}, u32[]{:S(2)}) copy-start(s32[64]{0:T(128)} %param.14) | copy-start | bytes 772
  0.0 8.0 %copy-start.9 = (s32[64]{0:T(128)S(1)}, s32[64]{0:T(128)}, u32[]{:S(2)}) copy-start(s32[64]{0:T(128)} %param.15) | copy-start | bytes 772
  0.0 8.5 %copy-start.7 = (s32[256]{0:T(256)S(1)}, s32[256]{0:T(256)}, u32[]{:S(2)}) copy-start(s32[256]{0:T(256)} %param.16) | copy-start | bytes 3076
  0.0 8.5 %copy-start.4 = (s32[64,30]{0,1:T(8,128)S(1)}, s32[64,30]{0,1:T(8,128)}, u32[]{:S(2)}) copy-start(s32[64,30]{0,1:T(8,128)} %param.12) | copy-start | bytes 23044
  0.0 8.6 %copy-start.5 = (s32[64,30]{0,1:T(8,128)S(1)}, s32[64,30]{0,1:T(8,128)}, u32[]{:S(2)}) copy-start(s32[64,30]{0,1:T(8,128)} %param.13) | copy-start | bytes 23044
  3.7 8.2 %collective-permute-start = (f32[16,2,4,512]{3,2,1,0:T(4,128)S(1)}, f32[16,2,4,512]{3,2,1,0:T(4,128)S(1)}, u32[]{:S(2)}, u32[]{:S(2)}) collective-permute-start(f32[16,2,4,512]{3,2,1,0:T(4,128)S(1)} %bitcast.45), channel_id=1, source_target_pairs={{0,4},{4,0},{1,5},{5,1},{2,6},{6,2},{3,7},{7,3},{8,12},{12,8},{9,1... | collective-permute-start | bytes 786440 | tf_op jit(solution)/shard_map/ppermute | solution.py:313
  5.0 32.4 %collective-permute-start.4 = (f32[512,128]{1,0:T(8,128)}, f32[512,128]{1,0:T(8,128)S(1)}, u32[]{:S(2)}, u32[]{:S(2)}) collective-permute-start(f32[512,128]{1,0:T(8,128)} %get-tuple-element.42), channel_id=1, source_target_pairs={{0,8},{8,0},{16,24},{24,16},{1,9},{9,1},{17,25},{25,17},{2,10},{10... | collective-permute-start | bytes 786440 | tf_op jit(solution)/shard_map/ppermute | solution.py:319
  5.1 32.3 %collective-permute-start.5 = (f32[512,128]{1,0:T(8,128)}, f32[512,128]{1,0:T(8,128)S(1)}, u32[]{:S(2)}, u32[]{:S(2)}) collective-permute-start(f32[512,128]{1,0:T(8,128)} %get-tuple-element.43), channel_id=1, source_target_pairs={{0,16},{8,24},{16,0},{24,8},{1,17},{9,25},{17,1},{25,9},{2,18},{10... | collective-permute-start | bytes 786440 | tf_op jit(solution)/shard_map/ppermute | solution.py:319
  7.4 30.0 %collective-permute-start.6 = (f32[512,128]{1,0:T(8,128)}, f32[512,128]{1,0:T(8,128)S(1)}, u32[]{:S(2)}, u32[]{:S(2)}) collective-permute-start(f32[512,128]{1,0:T(8,128)} %get-tuple-element.44), channel_id=1, source_target_pairs={{0,24},{8,16},{16,8},{24,0},{1,25},{9,17},{17,9},{25,1},{2,26},{10... | collective-permute-start | bytes 786440 | tf_op jit(solution)/shard_map/ppermute | solution.py:319
  11.9 0.7 copy-start.3
  15.9 9.1 %collective-permute-start.1 = (f32[176,128]{1,0:T(8,128)}, f32[176,128]{1,0:T(8,128)S(1)}, u32[]{:S(2)}, u32[]{:S(2)}) collective-permute-start(f32[176,128]{1,0:T(8,128)} %get-tuple-element.38), channel_id=1, source_target_pairs={{0,8},{8,0},{16,24},{24,16},{1,9},{9,1},{17,25},{25,17},{2,10},{10... | collective-permute-start | bytes 270344 | tf_op jit(solution)/shard_map/ppermute | solution.py:319
  17.0 17.9 %collective-permute-start.2 = (f32[176,128]{1,0:T(8,128)}, f32[176,128]{1,0:T(8,128)S(1)}, u32[]{:S(2)}, u32[]{:S(2)}) collective-permute-start(f32[176,128]{1,0:T(8,128)} %get-tuple-element.39), channel_id=1, source_target_pairs={{0,16},{8,24},{16,0},{24,8},{1,17},{9,25},{17,1},{25,9},{2,18},{10... | collective-permute-start | bytes 270344 | tf_op jit(solution)/shard_map/ppermute | solution.py:319
  22.6 2.4 %copy-start.8 = (f32[176,128]{1,0:T(8,128)S(1)}, f32[176,128]{1,0:T(8,128)}, u32[]{:S(2)}) copy-start(f32[176,128]{1,0:T(8,128)} %get-tuple-element.40) | copy-start | bytes 270340
  23.6 13.8 %copy-start.1 = (f32[512,128]{1,0:T(8,128)S(1)}, f32[512,128]{1,0:T(8,128)}, u32[]{:S(2)}) copy-start(f32[512,128]{1,0:T(8,128)} %get-tuple-element.41.refs_0_) | copy-start | bytes 786436
  23.6 13.8 %copy-start.2 = (f32[176,128]{1,0:T(8,128)S(1)}, f32[176,128]{1,0:T(8,128)}, u32[]{:S(2)}) copy-start(f32[176,128]{1,0:T(8,128)} %get-tuple-element.37.refs_4_) | copy-start | bytes 270340
  25.0 12.3 %collective-permute-start.3 = (f32[176,128]{1,0:T(8,128)S(1)}, f32[176,128]{1,0:T(8,128)S(1)}, u32[]{:S(2)}, u32[]{:S(2)}) collective-permute-start(f32[176,128]{1,0:T(8,128)S(1)} %copy-done.8), channel_id=1, source_target_pairs={{0,24},{8,16},{16,8},{24,0},{1,25},{9,17},{17,9},{25,1},{2,26},{10... | collective-permute-start | bytes 270344 | tf_op jit(solution)/shard_map/ppermute | solution.py:319
  58.1 33.6 %all-to-all-start = ((f32[16,136,128]{2,1,0:T(8,128)}), f32[16,136,128]{2,1,0:T(8,128)S(1)}, u32[]{:S(2)}, u32[]{:S(2)}) async-start(f32[16,136,128]{2,1,0:T(8,128)} %bitcast.44), calls=%async_computation | async-start | bytes 2228224 | tf_op jit(solution)/shard_map/all_to_all | solution.py:472

commit v8 on v7

--- a/solution.py
+++ b/solution.py
@@ -15,6 +15,7 @@
 half = 4
 rim = 2
 word_bits = 13
+grain = 32
 
 
 plan_fields = ["rows", "slots", "fine_rows", "stride", "width", "parent", "order", "turns"]
@@ -28,16 +29,6 @@
 def edge_bits(rows):
     bits = rows.bit_length() - 1
     return bits, [place for place in range(2, bits) if place % 2 == bits % 2]
-
-
-def near_edge(block, ring):
-    rows = block.shape[0]
-    bits, fixed = edge_bits(rows)
-    tail = block.shape[1:]
-    picked = block.reshape((2,) * bits + tail)
-    for place in fixed:
-        picked = lax.dynamic_index_in_dim(picked, 1 - ring, axis=bits - 1 - place, keepdims=True)
-    return picked.reshape((rows >> len(fixed),) + tail)
 
 
 def edge_rank(local, rows):
@@ -57,10 +48,17 @@
     return high, low
 
 
-def pack_kernel(source_count, note_count, zed, field, *refs):
+def pack_kernel(source_count, note_count, here, field, *refs):
     notes, outs, whole = refs[:note_count], refs[note_count:-1], refs[-1]
     rows = field.shape[0]
     stride = 2 * source_count
+    if len(outs) > planes:
+        bits, fixed = edge_bits(rows)
+        free = [place for place in range(bits) if place not in fixed]
+        side = (1 - here[1]) * sum(2**place for place in fixed)
+        for index in range(outs[planes].shape[0]):
+            base = sum((index // 2**order % 2) * 2**place for order, place in enumerate(free))
+            outs[planes][index] = field[base + side]
 
     def row_step(row, unused):
         both = jnp.concatenate([field[row, 0], field[row, 1]], axis=0)
@@ -71,8 +69,8 @@
         return unused
 
     lax.fori_loop(0, rows, row_step, 0, unroll=8)
-    for step, out in enumerate(outs):
-        source = zed[0] ^ step
+    for step, out in enumerate(outs[:planes]):
+        source = here[0] ^ step
         for part in range(2):
             for block in range(half):
                 out[pl.ds(part * half + block, rows, stride=2 * half), :] = whole[
@@ -82,18 +80,19 @@
             out[rows * 2 * half :, :] = note[...]
 
 
-def pack(zed, field, notes):
+def pack(here, field, notes, edge_rows):
     rows, _, source_count, width = field.shape
     length = rows * 2 * half + sum(note.shape[0] for note in notes)
     whole = pl.BlockSpec(memory_space=pltpu.VMEM)
+    edges = [jax.ShapeDtypeStruct((edge_rows,) + field.shape[1:], jnp.float32)] if edge_rows else []
     return pl.pallas_call(
         functools.partial(pack_kernel, source_count, len(notes)),
-        out_shape=[jax.ShapeDtypeStruct((length, lanes), jnp.float32)] * planes,
+        out_shape=[jax.ShapeDtypeStruct((length, lanes), jnp.float32)] * planes + edges,
         in_specs=[pl.BlockSpec(memory_space=pltpu.SMEM)] + [whole] * (1 + len(notes)),
-        out_specs=[whole] * planes,
+        out_specs=[whole] * (planes + len(edges)),
         scratch_shapes=[pltpu.VMEM((half, rows * 2 * source_count, lanes), jnp.float32)],
         name="pack_sources",
-    )(zed, field, *notes)
+    )(here, field, *notes)
 
 
 def parts_of(word):
@@ -108,7 +107,7 @@
     mains, refs = refs[:planes], refs[planes:]
     edges = refs[: planes if edge_size else 0]
     refs = refs[len(edges) :]
-    table, phases, weights, out, rims, meta, field, moved, shifted, ready, landed, sems = refs
+    table, phases, weights, out, rims, meta, field, moved, shifted, left, ready, landed, sems = refs
     rows, fine_rows = plan.rows, plan.fine_rows
     own = zed[0]
 
@@ -202,22 +201,22 @@
 
         lax.fori_loop(0, fine_rows // lanes, fine_step, 0)
         width = ready.shape[3]
-        left = jnp.concatenate(
-            [
-                jnp.concatenate(
-                    [
-                        shifted[pl.ds(part * half + block, fine_rows, stride=2 * half), :]
-                        for block in range(half)
-                    ],
-                    axis=1,
-                )
-                for part in range(2)
-            ],
-            axis=0,
-        )
-        first, second = split(left)
+        depth = half * lanes
+
+        def split_step(chunk, unused):
+            for part in range(2):
+                rows_of = pl.ds(pl.multiple_of(part * fine_rows + chunk * grain, grain), grain)
+                for block in range(half):
+                    begin = chunk * grain * 2 * half + part * half + block
+                    value = shifted[pl.ds(begin, grain, stride=2 * half), :]
+                    high, low = split(value)
+                    left[rows_of, block * lanes : (block + 1) * lanes] = high
+                    left[rows_of, depth + block * lanes : depth + (block + 1) * lanes] = low
+            return unused
+
+        lax.fori_loop(0, fine_rows // grain, split_step, 0, unroll=2)
         result = jnp.dot(
-            jnp.concatenate([first, first, second], axis=1), weights[...], preferred_element_type=jnp.float32
+            jnp.concatenate([left[:, :depth], left[...]], axis=1), weights[...], preferred_element_type=jnp.float32
         )
         for part in range(2):
             for dest in range(dest_count):
@@ -305,13 +304,15 @@
     dest_rows = fine_rows // dir_count
 
     field = jnp.pad(coarse_field, ((0, 0), (0, 0), (0, 0), (0, pad_dirs)))
-    here = zed.reshape(1)
-    packed = pack(here, field, [])
-    edge_rows = 0
-    if ring_count == 2:
-        packed, field = lax.optimization_barrier((packed, field))
-        edges = lax.ppermute(near_edge(field, ring), "ring", [(0, 1), (1, 0)])
-        edge_rows = edges.shape[0]
+    here = jnp.stack([zed, ring])
+    edge_rows = rows >> len(edge_bits(rows)[1]) if ring_count == 2 else 0
+    packed = pack(here, field, [], edge_rows)
+    after_pack = lax.optimization_barrier(
+        (packed, partner_ids, partner_types, partner_count, child_count, child_octant)
+    )
+    packed, partner_ids, partner_types, partner_count, child_count, child_octant = after_pack
+    if edge_rows:
+        edges = lax.ppermute(packed[planes], "ring", [(0, 1), (1, 0)])
 
     def to_planes(note, step):
         if step == 0:
@@ -336,7 +337,7 @@
         place = partner_ids
     field_rows = planes * (size + edge_rows)
     place = jnp.where(live, place, field_rows)
-    together = 8
+    together = 4
     fixed = slots // 2
     group = 3 if (slots - fixed) % 3 == 0 else 1
     index = jnp.arange(rows, dtype=jnp.int32)
@@ -386,7 +387,7 @@
         rows, slots, fine_rows, stride, width, list_rows, list_rows + fine_lists, turns_at, together, fixed, group
     )
 
-    notes = pack(here, edges, [meta]) if ring_count == 2 else [meta] * planes
+    notes = pack(here, edges, [meta], 0) if edge_rows else [meta] * planes
     after_notes = lax.optimization_barrier((notes, trans_table, dir_angles, stencil_ids, stencil_weights))
     notes, trans_table, dir_angles, stencil_ids, stencil_weights = after_notes
     received = [to_planes(notes[step], step) for step in (3, 2, 1, 0)][::-1]
@@ -441,7 +442,7 @@
     rounded = lax.reduce_precision(matrices, 8, 7)
     high = rounded.astype(jnp.bfloat16)
     low = (matrices - rounded).astype(jnp.bfloat16)
-    passes = jnp.concatenate([high, low, high], axis=0)
+    passes = jnp.concatenate([low, high, high], axis=0)
 
     whole = pl.BlockSpec(memory_space=pltpu.VMEM)
     message = (2 * dest_rows + 2 * half, kf_pad)
@@ -461,6 +462,7 @@
             pltpu.VMEM(((field_rows + 1) * 4 * half, lanes), jnp.float32),
             pltpu.VMEM((rows * 4 * half, lanes), jnp.float32),
             pltpu.VMEM((fine_rows * 2 * half, lanes), jnp.float32),
+            pltpu.VMEM((2 * fine_rows, 2 * kc_pad), jnp.bfloat16),
             pltpu.VMEM((planes, dir_count) + message, jnp.float32),
             pltpu.VMEM((planes, max(edge_rows, 1) * 2 * half, lanes), jnp.float32),
             pltpu.SemaphoreType.DMA((2 * planes + 2,)),

time: 93.8 us -> 93.3 us (level)
  other arithmetic: 6.48 us -> 9.79 us
  waiting for transfers between devices: 38.4 us -> 36.8 us
  starting transfers between devices: 15.8 us -> 14.5 us
  local copies, waits for them, and re-layouts: 5.66 us -> 4.68 us
    ppermute x6, waiting for transfers between devices: 12.1 us -> 10.5 us  [to_planes(): lax.ppermute(note, 'zed', [(plane, plane ^ step) for plane in range(plane...]
    ppermute x6, starting transfers between devices: 7.16 us -> 6.01 us  [to_planes(): lax.ppermute(note, 'zed', [(plane, plane ^ step) for plane in range(plane...]
    dynamic_slice x1 -> x0, local copies, waits for them, and re-layouts: 0.97 us -> none  [near_edge(): lax.dynamic_index_in_dim(picked, 1 - ring, axis=bits - 1 - place, keepdim...]
  transfers between devices with their start and end apart: 8 -> 8, of which waited for: 4 -> 4; matrix products, arithmetic and copies ran while one was open for 11% -> 14% of each run, Pallas kernels for 2% -> 2%
where the time goes in v8:
time: 93.3 us; the launch traced here: 92.9 us
  waiting for transfers between devices  36.8 us (39%)
  Pallas kernels  26.8 us (29%)
  starting transfers between devices  14.5 us (16%)
  other arithmetic  9.79 us (10%)
  local copies, waits for them, and re-layouts  4.68 us (5%)
    all_to_all x1, waiting for transfers between devices, per_device(): lax.all_to_all(local_fine.reshape((planes * dir_count,) + message), ('zed...  26.3 us
    pallas_call x1, Pallas kernels, per_device(): pl.pallas_call(functools.partial(fine_kernel, plan, size, edge_rows), out...  20.7 us
    ppermute x6, waiting for transfers between devices, to_planes(): lax.ppermute(note, 'zed', [(plane, plane ^ step) for plane in range(plane...  10.5 us
    all_to_all x1, starting transfers between devices, per_device(): lax.all_to_all(local_fine.reshape((planes * dir_count,) + message), ('zed...  7.24 us
    ppermute x6, starting transfers between devices, to_planes(): lax.ppermute(note, 'zed', [(plane, plane ^ step) for plane in range(plane...  6.01 us
    pallas_call x2, Pallas kernels, pack(): pl.pallas_call(functools.partial(pack_kernel, source_count, len(notes)),...  4.54 us
    reshape x1, local copies, waits for them, and re-layouts, per_device(): jnp.pad(trans_table, ((0, 0), (0, 0), (0, pad_dirs))).reshape(-1, lanes)  2.32 us
    reduce_sum x1, other arithmetic, in_order(): jnp.sum(jnp.where(at_rank[:, :, None], across(one, width)[None], 0), axis=1)  2.24 us
  transfers between devices with their start and end apart: 8, of which 4 were waited for; matrix products, arithmetic and copies ran while one was open for 14% of the time, Pallas kernels for 2%

profile of v8, /device:TPU:11, one launch (start us, length us, event | category | flops | bytes accessed | tf_op | source)
XLA Modules:
  0.0 92.9 jit_solution(1369099799149157325)
XLA Ops:
  0.6 2.7 %pack_sources.2 = (f32[512,128]{1,0:T(8,128)}, f32[512,128]{1,0:T(8,128)}, f32[512,128]{1,0:T(8,128)}, f32[512,128]{1,0:T(8,128)}, f32[16,2,4,512]{3,2,1,0:T(4,128)}) custom-call(s32[2]{0:T(128)} %pad_add_fusion.2.here.zed, f32[64,2,4,512]{3,2,1,0:T(4,128)} %field.1), custom_call_target="tpu_custom_call" | custom-call | tf_op jit(solution)/shard_map/pack_sources/pallas_call | solution.py:88
  3.3 1.2 %collective-permute-start = (f32[16,2,4,512]{3,2,1,0:T(4,128)}, f32[16,2,4,512]{3,2,1,0:T(4,128)S(1)}, u32[]{:S(2)}, u32[]{:S(2)}) collective-permute-start(f32[16,2,4,512]{3,2,1,0:T(4,128)} %get-tuple-element.39), channel_id=1, source_target_pairs={{0,4},{4,0},{1,5},{5,1},{2,6},{6,2},{3,7},{7,3},{8,12},{12,8},{9,1... | collective-permute-start | bytes 786440 | tf_op jit(solution)/shard_map/ppermute | solution.py:315
  4.7 2.3 %collective-permute-start.5 = (f32[512,128]{1,0:T(8,128)}, f32[512,128]{1,0:T(8,128)S(1)}, u32[]{:S(2)}, u32[]{:S(2)}) collective-permute-start(f32[512,128]{1,0:T(8,128)} %get-tuple-element.55), channel_id=1, source_target_pairs={{0,16},{8,24},{16,0},{24,8},{1,17},{9,25},{17,1},{25,9},{2,18},{10... | collective-permute-start | bytes 786440 | tf_op jit(solution)/shard_map/ppermute | solution.py:320
  7.2 0.9 select_reduce_fusion.3
  8.3 0.7 multiply_bitcast_fusion
  9.0 0.8 select_reduce_fusion.4
  10.0 0.8 fusion.13
  10.9 2.2 %select_reduce_fusion.1 = (s32[64,32]{1,0:T(8,128)S(1)}, s32[64,32]{1,0:T(8,128)S(1)}) fusion(s32[64,32]{0,1:T(8,128)S(1)} %pad.23, pred[64,64]{1,0:T(8,128)(4,1)S(1)} %iota_compare_fusion.3, s32[64,32]{0,1:T(8,128)S(1)} %pad.25), kind=kLoop, calls=%fused_computation.1 | loop fusion | flops 520192 | bytes 36864 | tf_op jit(solution)/shard_map/reduce_sum | solution.py:368
  13.5 0.6 pad_maximum_fusion.2.refs_0_
  14.1 0.7 copy-done.4
  14.8 1.9 %pack_sources.3 = (f32[176,128]{1,0:T(8,128)}, f32[176,128]{1,0:T(8,128)}, f32[176,128]{1,0:T(8,128)}, f32[176,128]{1,0:T(8,128)}) custom-call(s32[2]{0:T(128)} %pad_add_fusion.2.here.zed, f32[16,2,4,512]{3,2,1,0:T(4,128)} %copy-done.4, f32[48,128]{1,0:T(8,128)} %pad_maximum_fusion.2.refs_0_), custom_call_target="tpu_custom_call" | custom-call | tf_op jit(solution)/shard_map/pack_sources/pallas_call | solution.py:88
  16.7 0.7 dynamic-slice_bitcast_fusion
  17.4 0.7 slice_bitcast_fusion.3
  18.1 1.1 %collective-permute-start.1 = (f32[176,128]{1,0:T(8,128)}, f32[176,128]{1,0:T(8,128)S(1)}, u32[]{:S(2)}, u32[]{:S(2)}) collective-permute-start(f32[176,128]{1,0:T(8,128)} %get-tuple-element.50), channel_id=1, source_target_pairs={{0,8},{8,0},{16,24},{24,16},{1,9},{9,1},{17,25},{25,17},{2,10},{10... | collective-permute-start | bytes 270344 | tf_op jit(solution)/shard_map/ppermute | solution.py:320
  19.3 2.1 %collective-permute-start.2 = (f32[176,128]{1,0:T(8,128)}, f32[176,128]{1,0:T(8,128)S(1)}, u32[]{:S(2)}, u32[]{:S(2)}) collective-permute-start(f32[176,128]{1,0:T(8,128)} %get-tuple-element.51), channel_id=1, source_target_pairs={{0,16},{8,24},{16,0},{24,8},{1,17},{9,25},{17,1},{25,9},{2,18},{10... | collective-permute-start | bytes 270344 | tf_op jit(solution)/shard_map/ppermute | solution.py:320
  22.0 0.6 select_add_fusion.1
  22.6 2.3 %reshape.209.refs_8_ = f32[2528,128]{1,0:T(8,128)S(1)} reshape(f32[316,2,512]{2,1,0:T(2,128)} %param.11) | data formatting | bytes 2588672 | tf_op jit(solution)/shard_map/reshape | solution.py:407
  24.9 0.9 cosine_multiply_fusion
  26.6 7.8 %collective-permute-done.2.refs_6_ = f32[176,128]{1,0:T(8,128)S(1)} collective-permute-done((f32[176,128]{1,0:T(8,128)}, f32[176,128]{1,0:T(8,128)S(1)}, u32[]{:S(2)}, u32[]{:S(2)}) %collective-permute-start.2) | collective-permute-done | bytes 90144 | tf_op jit(solution)/shard_map/ppermute | solution.py:320
  34.4 2.5 %collective-permute-done.3.refs_7_ = f32[176,128]{1,0:T(8,128)S(1)} collective-permute-done((f32[176,128]{1,0:T(8,128)S(1)}, f32[176,128]{1,0:T(8,128)S(1)}, u32[]{:S(2)}, u32[]{:S(2)}) %collective-permute-start.3) | collective-permute-done | bytes 90144 | tf_op jit(solution)/shard_map/ppermute | solution.py:320
  37.0 20.7 %translate_and_interpolate.1 = (f32[4,4,136,128]{3,2,1,0:T(8,128)}, f32[8,128]{1,0:T(8,128)S(1)}) custom-call(s32[2]{0:T(128)S(1)} %copy-done.3, s32[4,24,128]{2,1,0:T(8,128)S(1)} %slice_add_fusion.lists, f32[512,128]{1,0:T(8,128)S(1)} %copy-done.1, f32[512,128]{1,0:T(8,128)S(1)} %collective-permute-done.4.refs_1_, ...), custom_call_target="tpu_custom_call" | custom-call | tf_op jit(solution)/shard_map/translate_and_interpolate/pallas_call | solution.py:449
  57.7 7.2 %all-to-all-start = ((f32[16,136,128]{2,1,0:T(8,128)}), f32[16,136,128]{2,1,0:T(8,128)S(1)}, u32[]{:S(2)}, u32[]{:S(2)}) async-start(f32[16,136,128]{2,1,0:T(8,128)} %bitcast.40), calls=%async_computation | async-start | bytes 2228224 | tf_op jit(solution)/shard_map/all_to_all | solution.py:474
  65.0 26.3 %all-to-all-done.parts = f32[16,136,128]{2,1,0:T(8,128)S(1)} async-done(((f32[16,136,128]{2,1,0:T(8,128)}), f32[16,136,128]{2,1,0:T(8,128)S(1)}, u32[]{:S(2)}, u32[]{:S(2)}) %all-to-all-start) | async-done | bytes 1114144 | tf_op jit(solution)/shard_map/all_to_all | solution.py:474
  91.3 1.5 %join_parts.1 = f32[64,2,4,512]{3,2,1,0:T(4,128)} custom-call(f32[16,136,128]{2,1,0:T(8,128)S(1)} %all-to-all-done.parts, f32[1,128]{1,0:T(1,128)S(1)} %slice_subtract_fusion.rims), custom_call_target="tpu_custom_call" | custom-call | tf_op jit(solution)/shard_map/join_parts/pallas_call | solution.py:483
  (56 shorter events, 3.1 us)
Async XLA Ops:
  0.0 16.7 %copy-start = (s32[2048,4]{0,1:T(4,128)S(1)}, s32[2048,4]{0,1:T(4,128)}, u32[]{:S(2)}) copy-start(s32[2048,4]{0,1:T(4,128)} %param.18) | copy-start | bytes 98308
  3.3 10.8 %collective-permute-start = (f32[16,2,4,512]{3,2,1,0:T(4,128)}, f32[16,2,4,512]{3,2,1,0:T(4,128)S(1)}, u32[]{:S(2)}, u32[]{:S(2)}) collective-permute-start(f32[16,2,4,512]{3,2,1,0:T(4,128)} %get-tuple-element.39), channel_id=1, source_target_pairs={{0,4},{4,0},{1,5},{5,1},{2,6},{6,2},{3,7},{7,3},{8,12},{12,8},{9,1... | collective-permute-start | bytes 786440 | tf_op jit(solution)/shard_map/ppermute | solution.py:315
  4.5 32.4 %collective-permute-start.4 = (f32[512,128]{1,0:T(8,128)}, f32[512,128]{1,0:T(8,128)S(1)}, u32[]{:S(2)}, u32[]{:S(2)}) collective-permute-start(f32[512,128]{1,0:T(8,128)} %get-tuple-element.54), channel_id=1, source_target_pairs={{0,8},{8,0},{16,24},{24,16},{1,9},{9,1},{17,25},{25,17},{2,10},{10... | collective-permute-start | bytes 786440 | tf_op jit(solution)/shard_map/ppermute | solution.py:320
  4.7 32.3 %collective-permute-start.5 = (f32[512,128]{1,0:T(8,128)}, f32[512,128]{1,0:T(8,128)S(1)}, u32[]{:S(2)}, u32[]{:S(2)}) collective-permute-start(f32[512,128]{1,0:T(8,128)} %get-tuple-element.55), channel_id=1, source_target_pairs={{0,16},{8,24},{16,0},{24,8},{1,17},{9,25},{17,1},{25,9},{2,18},{10... | collective-permute-start | bytes 786440 | tf_op jit(solution)/shard_map/ppermute | solution.py:320
  7.0 30.0 %collective-permute-start.6 = (f32[512,128]{1,0:T(8,128)}, f32[512,128]{1,0:T(8,128)S(1)}, u32[]{:S(2)}, u32[]{:S(2)}) collective-permute-start(f32[512,128]{1,0:T(8,128)} %get-tuple-element.56), channel_id=1, source_target_pairs={{0,24},{8,16},{16,8},{24,0},{1,25},{9,17},{17,9},{25,1},{2,26},{10... | collective-permute-start | bytes 786440 | tf_op jit(solution)/shard_map/ppermute | solution.py:320
  14.1 0.7 copy-start.4
  18.1 8.3 %collective-permute-start.1 = (f32[176,128]{1,0:T(8,128)}, f32[176,128]{1,0:T(8,128)S(1)}, u32[]{:S(2)}, u32[]{:S(2)}) collective-permute-start(f32[176,128]{1,0:T(8,128)} %get-tuple-element.50), channel_id=1, source_target_pairs={{0,8},{8,0},{16,24},{24,16},{1,9},{9,1},{17,25},{25,17},{2,10},{10... | collective-permute-start | bytes 270344 | tf_op jit(solution)/shard_map/ppermute | solution.py:320
  19.3 15.1 %collective-permute-start.2 = (f32[176,128]{1,0:T(8,128)}, f32[176,128]{1,0:T(8,128)S(1)}, u32[]{:S(2)}, u32[]{:S(2)}) collective-permute-start(f32[176,128]{1,0:T(8,128)} %get-tuple-element.51), channel_id=1, source_target_pairs={{0,16},{8,24},{16,0},{24,8},{1,17},{9,25},{17,1},{25,9},{2,18},{10... | collective-permute-start | bytes 270344 | tf_op jit(solution)/shard_map/ppermute | solution.py:320
  24.9 1.6 %copy-start.5 = (f32[176,128]{1,0:T(8,128)S(1)}, f32[176,128]{1,0:T(8,128)}, u32[]{:S(2)}) copy-start(f32[176,128]{1,0:T(8,128)} %get-tuple-element.52) | copy-start | bytes 270340
  25.8 11.1 %copy-start.1 = (f32[512,128]{1,0:T(8,128)S(1)}, f32[512,128]{1,0:T(8,128)}, u32[]{:S(2)}) copy-start(f32[512,128]{1,0:T(8,128)} %get-tuple-element.53.refs_0_) | copy-start | bytes 786436
  25.8 11.1 %copy-start.2 = (f32[176,128]{1,0:T(8,128)S(1)}, f32[176,128]{1,0:T(8,128)}, u32[]{:S(2)}) copy-start(f32[176,128]{1,0:T(8,128)} %get-tuple-element.49.refs_4_) | copy-start | bytes 270340
  25.9 11.1 %copy-start.3 = (s32[2]{0:T(128)S(1)}, s32[2]{0:T(128)}, u32[]{:S(2)}) copy-start(s32[2]{0:T(128)} %pad_add_fusion.2.here.zed) | copy-start | bytes 28
  26.5 10.4 %collective-permute-start.3 = (f32[176,128]{1,0:T(8,128)S(1)}, f32[176,128]{1,0:T(8,128)S(1)}, u32[]{:S(2)}, u32[]{:S(2)}) collective-permute-start(f32[176,128]{1,0:T(8,128)S(1)} %copy-done.5), channel_id=1, source_target_pairs={{0,24},{8,16},{16,8},{24,0},{1,25},{9,17},{17,9},{25,1},{2,26},{10... | collective-permute-start | bytes 270344 | tf_op jit(solution)/shard_map/ppermute | solution.py:320
  57.7 33.6 %all-to-all-start = ((f32[16,136,128]{2,1,0:T(8,128)}), f32[16,136,128]{2,1,0:T(8,128)S(1)}, u32[]{:S(2)}, u32[]{:S(2)}) async-start(f32[16,136,128]{2,1,0:T(8,128)} %bitcast.40), calls=%async_computation | async-start | bytes 2228224 | tf_op jit(solution)/shard_map/all_to_all | solution.py:474

commit v9 on v8

--- a/solution.py
+++ b/solution.py
@@ -48,14 +48,14 @@
     return high, low
 
 
-def pack_kernel(source_count, note_count, here, field, *refs):
+def pack_kernel(source_count, note_count, zed, ring, field, *refs):
     notes, outs, whole = refs[:note_count], refs[note_count:-1], refs[-1]
     rows = field.shape[0]
     stride = 2 * source_count
     if len(outs) > planes:
         bits, fixed = edge_bits(rows)
         free = [place for place in range(bits) if place not in fixed]
-        side = (1 - here[1]) * sum(2**place for place in fixed)
+        side = (1 - ring[0]) * sum(2**place for place in fixed)
         for index in range(outs[planes].shape[0]):
             base = sum((index // 2**order % 2) * 2**place for order, place in enumerate(free))
             outs[planes][index] = field[base + side]
@@ -70,7 +70,7 @@
 
     lax.fori_loop(0, rows, row_step, 0, unroll=8)
     for step, out in enumerate(outs[:planes]):
-        source = here[0] ^ step
+        source = zed[0] ^ step
         for part in range(2):
             for block in range(half):
                 out[pl.ds(part * half + block, rows, stride=2 * half), :] = whole[
@@ -88,11 +88,11 @@
     return pl.pallas_call(
         functools.partial(pack_kernel, source_count, len(notes)),
         out_shape=[jax.ShapeDtypeStruct((length, lanes), jnp.float32)] * planes + edges,
-        in_specs=[pl.BlockSpec(memory_space=pltpu.SMEM)] + [whole] * (1 + len(notes)),
+        in_specs=[pl.BlockSpec(memory_space=pltpu.SMEM)] * 2 + [whole] * (1 + len(notes)),
         out_specs=[whole] * (planes + len(edges)),
         scratch_shapes=[pltpu.VMEM((half, rows * 2 * source_count, lanes), jnp.float32)],
         name="pack_sources",
-    )(here, field, *notes)
+    )(*here, field, *notes)
 
 
 def parts_of(word):
@@ -304,13 +304,9 @@
     dest_rows = fine_rows // dir_count
 
     field = jnp.pad(coarse_field, ((0, 0), (0, 0), (0, 0), (0, pad_dirs)))
-    here = jnp.stack([zed, ring])
+    here = zed.reshape(1), ring.reshape(1)
     edge_rows = rows >> len(edge_bits(rows)[1]) if ring_count == 2 else 0
     packed = pack(here, field, [], edge_rows)
-    after_pack = lax.optimization_barrier(
-        (packed, partner_ids, partner_types, partner_count, child_count, child_octant)
-    )
-    packed, partner_ids, partner_types, partner_count, child_count, child_octant = after_pack
     if edge_rows:
         edges = lax.ppermute(packed[planes], "ring", [(0, 1), (1, 0)])
 
@@ -339,7 +335,7 @@
     place = jnp.where(live, place, field_rows)
     together = 4
     fixed = slots // 2
-    group = 3 if (slots - fixed) % 3 == 0 else 1
+    group = 5 if (slots - fixed) % 5 == 0 else 1
     index = jnp.arange(rows, dtype=jnp.int32)
     before = (partner_count[None, :] > partner_count[:, None]) | (
         (partner_count[None, :] == partner_count[:, None]) & (index[None, :] < index[:, None])
@@ -469,7 +465,7 @@
         ],
         compiler_params=pltpu.CompilerParams(vmem_limit_bytes=48 * 2**20),
         name="translate_and_interpolate",
-    )(here, meta, *arrived, *received, table, phases, passes)
+    )(here[0], meta, *arrived, *received, table, phases, passes)
 
     parts = lax.all_to_all(
         local_fine.reshape((planes * dir_count,) + message),

time: 93.3 us -> 92.6 us (level)
  waiting for transfers between devices: 36.8 us -> 35.2 us
    ppermute x6, waiting for transfers between devices: 10.5 us -> 8.89 us  [to_planes(): lax.ppermute(note, 'zed', [(plane, plane ^ step) for plane in range(plane...]
  transfers between devices with their start and end apart: 8 -> 8, of which waited for: 4 -> 3; matrix products, arithmetic and copies ran while one was open for 14% -> 16% of each run, Pallas kernels for 2% -> 2%
where the time goes in v9:
time: 92.6 us; the launch traced here: 91.9 us
  waiting for transfers between devices  35.2 us (38%)
  Pallas kernels  26.4 us (29%)
  starting transfers between devices  14.7 us (16%)
  other arithmetic  10.7 us (12%)
  local copies, waits for them, and re-layouts  4.67 us (5%)
    all_to_all x1, waiting for transfers between devices, per_device(): lax.all_to_all(local_fine.reshape((planes * dir_count,) + message), ('zed...  26.3 us
    pallas_call x1, Pallas kernels, per_device(): pl.pallas_call(functools.partial(fine_kernel, plan, size, edge_rows), out...  20.3 us
    ppermute x6, waiting for transfers between devices, to_planes(): lax.ppermute(note, 'zed', [(plane, plane ^ step) for plane in range(plane...  8.89 us
    all_to_all x1, starting transfers between devices, per_device(): lax.all_to_all(local_fine.reshape((planes * dir_count,) + message), ('zed...  7.24 us
    ppermute x6, starting transfers between devices, to_planes(): lax.ppermute(note, 'zed', [(plane, plane ^ step) for plane in range(plane...  6.21 us
    pallas_call x2, Pallas kernels, pack(): pl.pallas_call(functools.partial(pack_kernel, source_count, len(notes)),...  4.47 us
    reshape x1, local copies, waits for them, and re-layouts, per_device(): jnp.pad(trans_table, ((0, 0), (0, 0), (0, pad_dirs))).reshape(-1, lanes)  2.32 us
    reduce_sum x1, other arithmetic, in_order(): jnp.sum(jnp.where(at_rank[:, :, None], across(one, width)[None], 0), axis=1)  2.24 us
  transfers between devices with their start and end apart: 8, of which 3 were waited for; matrix products, arithmetic and copies ran while one was open for 16% of the time, Pallas kernels for 2%

profile of v9, /device:TPU:11, one launch (start us, length us, event | category | flops | bytes accessed | tf_op | source)
XLA Modules:
  0.0 91.9 jit_solution(7892609382137526103)
XLA Ops:
  0.0 2.7 %pack_sources.2 = (f32[512,128]{1,0:T(8,128)}, f32[512,128]{1,0:T(8,128)}, f32[512,128]{1,0:T(8,128)}, f32[512,128]{1,0:T(8,128)}, f32[16,2,4,512]{3,2,1,0:T(4,128)}) custom-call(s32[1]{0:T(128)} %bitcast.zed, s32[1]{0:T(128)} %bitcast.1.ring, f32[64,2,4,512]{3,2,1,0:T(4,128)} %field.1), custom_call_target="tpu_custom_call" | custom-call | tf_op jit(solution)/shard_map/pack_sources/pallas_call | solution.py:88
  2.7 1.2 %collective-permute-start = (f32[16,2,4,512]{3,2,1,0:T(4,128)}, f32[16,2,4,512]{3,2,1,0:T(4,128)S(1)}, u32[]{:S(2)}, u32[]{:S(2)}) collective-permute-start(f32[16,2,4,512]{3,2,1,0:T(4,128)} %get-tuple-element.24), channel_id=1, source_target_pairs={{0,4},{4,0},{1,5},{5,1},{2,6},{6,2},{3,7},{7,3},{8,12},{12,8},{9,1... | collective-permute-start | bytes 786440 | tf_op jit(solution)/shard_map/ppermute | solution.py:311
  4.1 2.3 %collective-permute-start.5 = (f32[512,128]{1,0:T(8,128)}, f32[512,128]{1,0:T(8,128)S(1)}, u32[]{:S(2)}, u32[]{:S(2)}) collective-permute-start(f32[512,128]{1,0:T(8,128)} %get-tuple-element.35), channel_id=1, source_target_pairs={{0,16},{8,24},{16,0},{24,8},{1,17},{9,25},{17,1},{25,9},{2,18},{10... | collective-permute-start | bytes 786440 | tf_op jit(solution)/shard_map/ppermute | solution.py:316
  6.6 0.9 convert_reduce_fusion.1
  7.6 0.8 select_reduce_fusion.3
  8.6 0.8 select_reduce_fusion.4
  9.5 0.7 multiply_bitcast_fusion
  10.2 0.8 fusion.13
  11.0 0.7 broadcast_multiply_fusion.1
  11.8 2.2 %select_reduce_fusion.1 = (s32[64,32]{1,0:T(8,128)S(1)}, s32[64,32]{1,0:T(8,128)S(1)}) fusion(s32[64,32]{0,1:T(8,128)S(1)} %pad.23, pred[64,64]{1,0:T(8,128)(4,1)S(1)} %iota_compare_fusion.3, s32[64,32]{0,1:T(8,128)S(1)} %pad.25), kind=kLoop, calls=%fused_computation.1 | loop fusion | flops 520192 | bytes 36864 | tf_op jit(solution)/shard_map/reduce_sum | solution.py:364
  15.0 0.7 copy-done.3
  15.7 1.8 %pack_sources.3 = (f32[176,128]{1,0:T(8,128)}, f32[176,128]{1,0:T(8,128)}, f32[176,128]{1,0:T(8,128)}, f32[176,128]{1,0:T(8,128)}) custom-call(s32[1]{0:T(128)} %bitcast.zed, s32[1]{0:T(128)} %bitcast.1.ring, f32[16,2,4,512]{3,2,1,0:T(4,128)} %copy-done.3, f32[48,128]{1,0:T(8,128)} %pad_maximum_fusion.2.refs_0_), custom_call_target="tpu_custom_call" | custom-call | tf_op jit(solution)/shard_map/pack_sources/pallas_call | solution.py:88
  17.5 0.7 dynamic-slice_bitcast_fusion
  18.2 0.7 slice_bitcast_fusion.3
  18.9 1.1 %collective-permute-start.1 = (f32[176,128]{1,0:T(8,128)}, f32[176,128]{1,0:T(8,128)S(1)}, u32[]{:S(2)}, u32[]{:S(2)}) collective-permute-start(f32[176,128]{1,0:T(8,128)} %get-tuple-element.30), channel_id=1, source_target_pairs={{0,8},{8,0},{16,24},{24,16},{1,9},{9,1},{17,25},{25,17},{2,10},{10... | collective-permute-start | bytes 270344 | tf_op jit(solution)/shard_map/ppermute | solution.py:316
  20.1 2.1 %collective-permute-start.2 = (f32[176,128]{1,0:T(8,128)}, f32[176,128]{1,0:T(8,128)S(1)}, u32[]{:S(2)}, u32[]{:S(2)}) collective-permute-start(f32[176,128]{1,0:T(8,128)} %get-tuple-element.31), channel_id=1, source_target_pairs={{0,16},{8,24},{16,0},{24,8},{1,17},{9,25},{17,1},{25,9},{2,18},{10... | collective-permute-start | bytes 270344 | tf_op jit(solution)/shard_map/ppermute | solution.py:316
  23.4 2.3 %reshape.217.refs_8_ = f32[2528,128]{1,0:T(8,128)S(1)} reshape(f32[316,2,512]{2,1,0:T(2,128)} %param.11) | data formatting | bytes 2588672 | tf_op jit(solution)/shard_map/reshape | solution.py:403
  25.7 0.9 %cosine_multiply_fusion = (f32[1,512]{1,0:T(1,128)S(1)}, f32[1,512]{1,0:T(1,128)S(1)}, f32[1,512]{1,0:T(1,128)S(1)}) fusion(f32[2,2048]{1,0:T(2,128)} %param.17, s32[]{:T(128)S(6)} %add.227, s32[]{:T(128)S(6)} %select_n.174), kind=kLoop, calls=%fused_computation.105 | loop fusion | flops 1024 | bytes 10248 | tf_op jit(solution)/shard_map/mul | solution.py:409
  27.4 6.4 %collective-permute-done.2.refs_6_ = f32[176,128]{1,0:T(8,128)S(1)} collective-permute-done((f32[176,128]{1,0:T(8,128)}, f32[176,128]{1,0:T(8,128)S(1)}, u32[]{:S(2)}, u32[]{:S(2)}) %collective-permute-start.2) | collective-permute-done | bytes 90144 | tf_op jit(solution)/shard_map/ppermute | solution.py:316
  33.8 2.5 %collective-permute-done.3.refs_7_ = f32[176,128]{1,0:T(8,128)S(1)} collective-permute-done((f32[176,128]{1,0:T(8,128)S(1)}, f32[176,128]{1,0:T(8,128)S(1)}, u32[]{:S(2)}, u32[]{:S(2)}) %collective-permute-start.3) | collective-permute-done | bytes 90144 | tf_op jit(solution)/shard_map/ppermute | solution.py:316
  36.4 20.3 %translate_and_interpolate.1 = (f32[4,4,136,128]{3,2,1,0:T(8,128)}, f32[8,128]{1,0:T(8,128)S(1)}) custom-call(s32[1]{0:T(128)} %bitcast.zed, s32[4,24,128]{2,1,0:T(8,128)S(1)} %slice_add_fusion.lists, f32[512,128]{1,0:T(8,128)S(1)} %copy-done.1, f32[512,128]{1,0:T(8,128)S(1)} %collective-permute-done.4.refs_1_, ...), custom_call_target="tpu_custom_call" | custom-call | tf_op jit(solution)/shard_map/translate_and_interpolate/pallas_call | solution.py:445
  56.7 7.2 %all-to-all-start = ((f32[16,136,128]{2,1,0:T(8,128)}), f32[16,136,128]{2,1,0:T(8,128)S(1)}, u32[]{:S(2)}, u32[]{:S(2)}) async-start(f32[16,136,128]{2,1,0:T(8,128)} %bitcast.40), calls=%async_computation | async-start | bytes 2228224 | tf_op jit(solution)/shard_map/all_to_all | solution.py:470
  64.0 26.3 %all-to-all-done.parts = f32[16,136,128]{2,1,0:T(8,128)S(1)} async-done(((f32[16,136,128]{2,1,0:T(8,128)}), f32[16,136,128]{2,1,0:T(8,128)S(1)}, u32[]{:S(2)}, u32[]{:S(2)}) %all-to-all-start) | async-done | bytes 1114144 | tf_op jit(solution)/shard_map/all_to_all | solution.py:470
  90.3 1.5 %join_parts.1 = f32[64,2,4,512]{3,2,1,0:T(4,128)} custom-call(f32[16,136,128]{2,1,0:T(8,128)S(1)} %all-to-all-done.parts, f32[1,128]{1,0:T(1,128)S(1)} %slice_subtract_fusion.rims), custom_call_target="tpu_custom_call" | custom-call | tf_op jit(solution)/shard_map/join_parts/pallas_call | solution.py:479
  (54 shorter events, 3.7 us)
Async XLA Ops:
  0.0 17.5 %copy-start = (s32[2048,4]{0,1:T(4,128)S(1)}, s32[2048,4]{0,1:T(4,128)}, u32[]{:S(2)}) copy-start(s32[2048,4]{0,1:T(4,128)} %param.18) | copy-start | bytes 98308
  2.7 12.3 %collective-permute-start = (f32[16,2,4,512]{3,2,1,0:T(4,128)}, f32[16,2,4,512]{3,2,1,0:T(4,128)S(1)}, u32[]{:S(2)}, u32[]{:S(2)}) collective-permute-start(f32[16,2,4,512]{3,2,1,0:T(4,128)} %get-tuple-element.24), channel_id=1, source_target_pairs={{0,4},{4,0},{1,5},{5,1},{2,6},{6,2},{3,7},{7,3},{8,12},{12,8},{9,1... | collective-permute-start | bytes 786440 | tf_op jit(solution)/shard_map/ppermute | solution.py:311
  3.9 32.4 %collective-permute-start.4 = (f32[512,128]{1,0:T(8,128)}, f32[512,128]{1,0:T(8,128)S(1)}, u32[]{:S(2)}, u32[]{:S(2)}) collective-permute-start(f32[512,128]{1,0:T(8,128)} %get-tuple-element.34), channel_id=1, source_target_pairs={{0,8},{8,0},{16,24},{24,16},{1,9},{9,1},{17,25},{25,17},{2,10},{10... | collective-permute-start | bytes 786440 | tf_op jit(solution)/shard_map/ppermute | solution.py:316
  4.1 32.3 %collective-permute-start.5 = (f32[512,128]{1,0:T(8,128)}, f32[512,128]{1,0:T(8,128)S(1)}, u32[]{:S(2)}, u32[]{:S(2)}) collective-permute-start(f32[512,128]{1,0:T(8,128)} %get-tuple-element.35), channel_id=1, source_target_pairs={{0,16},{8,24},{16,0},{24,8},{1,17},{9,25},{17,1},{25,9},{2,18},{10... | collective-permute-start | bytes 786440 | tf_op jit(solution)/shard_map/ppermute | solution.py:316
  6.4 30.0 %collective-permute-start.6 = (f32[512,128]{1,0:T(8,128)}, f32[512,128]{1,0:T(8,128)S(1)}, u32[]{:S(2)}, u32[]{:S(2)}) collective-permute-start(f32[512,128]{1,0:T(8,128)} %get-tuple-element.36), channel_id=1, source_target_pairs={{0,24},{8,16},{16,8},{24,0},{1,25},{9,17},{17,9},{25,1},{2,26},{10... | collective-permute-start | bytes 786440 | tf_op jit(solution)/shard_map/ppermute | solution.py:316
  15.0 0.7 copy-start.3
  18.9 8.1 %collective-permute-start.1 = (f32[176,128]{1,0:T(8,128)}, f32[176,128]{1,0:T(8,128)S(1)}, u32[]{:S(2)}, u32[]{:S(2)}) collective-permute-start(f32[176,128]{1,0:T(8,128)} %get-tuple-element.30), channel_id=1, source_target_pairs={{0,8},{8,0},{16,24},{24,16},{1,9},{9,1},{17,25},{25,17},{2,10},{10... | collective-permute-start | bytes 270344 | tf_op jit(solution)/shard_map/ppermute | solution.py:316
  20.1 13.7 %collective-permute-start.2 = (f32[176,128]{1,0:T(8,128)}, f32[176,128]{1,0:T(8,128)S(1)}, u32[]{:S(2)}, u32[]{:S(2)}) collective-permute-start(f32[176,128]{1,0:T(8,128)} %get-tuple-element.31), channel_id=1, source_target_pairs={{0,16},{8,24},{16,0},{24,8},{1,17},{9,25},{17,1},{25,9},{2,18},{10... | collective-permute-start | bytes 270344 | tf_op jit(solution)/shard_map/ppermute | solution.py:316
  25.7 1.4 %copy-start.4 = (f32[176,128]{1,0:T(8,128)S(1)}, f32[176,128]{1,0:T(8,128)}, u32[]{:S(2)}) copy-start(f32[176,128]{1,0:T(8,128)} %get-tuple-element.32) | copy-start | bytes 270340
  26.6 9.7 %copy-start.1 = (f32[512,128]{1,0:T(8,128)S(1)}, f32[512,128]{1,0:T(8,128)}, u32[]{:S(2)}) copy-start(f32[512,128]{1,0:T(8,128)} %get-tuple-element.33.refs_0_) | copy-start | bytes 786436
  26.6 9.7 %copy-start.2 = (f32[176,128]{1,0:T(8,128)S(1)}, f32[176,128]{1,0:T(8,128)}, u32[]{:S(2)}) copy-start(f32[176,128]{1,0:T(8,128)} %get-tuple-element.29.refs_4_) | copy-start | bytes 270340
  27.1 9.2 %collective-permute-start.3 = (f32[176,128]{1,0:T(8,128)S(1)}, f32[176,128]{1,0:T(8,128)S(1)}, u32[]{:S(2)}, u32[]{:S(2)}) collective-permute-start(f32[176,128]{1,0:T(8,128)S(1)} %copy-done.4), channel_id=1, source_target_pairs={{0,24},{8,16},{16,8},{24,0},{1,25},{9,17},{17,9},{25,1},{2,26},{10... | collective-permute-start | bytes 270344 | tf_op jit(solution)/shard_map/ppermute | solution.py:316
  56.7 33.6 %all-to-all-start = ((f32[16,136,128]{2,1,0:T(8,128)}), f32[16,136,128]{2,1,0:T(8,128)S(1)}, u32[]{:S(2)}, u32[]{:S(2)}) async-start(f32[16,136,128]{2,1,0:T(8,128)} %bitcast.40), calls=%async_computation | async-start | bytes 2228224 | tf_op jit(solution)/shard_map/all_to_all | solution.py:470

commit v10 on v9

--- a/solution.py
+++ b/solution.py
@@ -50,6 +50,8 @@
 
 def pack_kernel(source_count, note_count, zed, ring, field, *refs):
     notes, outs, whole = refs[:note_count], refs[note_count:-1], refs[-1]
+    if note_count:
+        near, notes = notes[-1], notes[:-1]
     rows = field.shape[0]
     stride = 2 * source_count
     if len(outs) > planes:
@@ -76,18 +78,23 @@
                 out[pl.ds(part * half + block, rows, stride=2 * half), :] = whole[
                     block, pl.ds(part * source_count + source, rows, stride=stride), :
                 ]
+        end = rows * 2 * half
         for note in notes:
-            out[rows * 2 * half :, :] = note[...]
+            out[end : end + note.shape[0], :] = note[...]
+            end += note.shape[0]
+        if note_count and step == 1:
+            out[end:, :] = near[...]
 
 
 def pack(here, field, notes, edge_rows):
     rows, _, source_count, width = field.shape
-    length = rows * 2 * half + sum(note.shape[0] for note in notes)
+    lengths = [rows * 2 * half + sum(note.shape[0] for note in notes[:-1])] * planes
+    lengths[1] += sum(note.shape[0] for note in notes[-1:])
     whole = pl.BlockSpec(memory_space=pltpu.VMEM)
     edges = [jax.ShapeDtypeStruct((edge_rows,) + field.shape[1:], jnp.float32)] if edge_rows else []
     return pl.pallas_call(
         functools.partial(pack_kernel, source_count, len(notes)),
-        out_shape=[jax.ShapeDtypeStruct((length, lanes), jnp.float32)] * planes + edges,
+        out_shape=[jax.ShapeDtypeStruct((length, lanes), jnp.float32) for length in lengths] + edges,
         in_specs=[pl.BlockSpec(memory_space=pltpu.SMEM)] * 2 + [whole] * (1 + len(notes)),
         out_specs=[whole] * (planes + len(edges)),
         scratch_shapes=[pltpu.VMEM((half, rows * 2 * source_count, lanes), jnp.float32)],
@@ -103,10 +110,12 @@
     return pl.ds(pl.multiple_of(start, 2 * half), 2 * half)
 
 
-def fine_kernel(plan, size, edge_size, zed, lists, *refs):
+def fine_kernel(plan, size, edge_size, near_at, zed, lists, *refs):
     mains, refs = refs[:planes], refs[planes:]
-    edges = refs[: planes if edge_size else 0]
+    edges = refs[: planes - 1 if edge_size else 0]
     refs = refs[len(edges) :]
+    if edge_size:
+        edges = [edges[0], edges[1], mains[2], edges[2]]
     table, phases, weights, out, rims, meta, field, moved, shifted, left, ready, landed, sems = refs
     rows, fine_rows = plan.rows, plan.fine_rows
     own = zed[0]
@@ -116,7 +125,8 @@
 
     bring(0).start()
     incoming = []
-    for step, edge in enumerate(edges):
+    for index, edge in enumerate(edges):
+        step = planes - 1 - index
         chosen = edge.at[pl.ds(0, edge_size * 2 * half)]
         incoming.append(pltpu.make_async_copy(chosen, landed.at[step], sems.at[planes + 2 + step]))
         incoming[-1].start()
@@ -129,17 +139,20 @@
     def with_turned(value):
         return jnp.concatenate([value, pltpu.roll(value, half, 0)], axis=0)
 
-    for step, main in enumerate(mains):
+    for index, main in enumerate(mains):
+        step = planes - 1 - index
         first = (own ^ step) * size
-
-        def main_step(row, unused, first=first, main=main):
-            field[both((first + row) * 4 * half), :] = with_turned(main[tile(row * 2 * half), :])
+        begin = near_at if step == 1 else 0
+
+        def main_step(row, unused, first=first, main=main, begin=begin):
+            field[both((first + row) * 4 * half), :] = with_turned(main[tile(begin + row * 2 * half), :])
             return unused
 
         lax.fori_loop(0, size, main_step, 0, unroll=8)
-    for step, edge in enumerate(edges):
+    for index in range(len(edges)):
+        step = planes - 1 - index
         first = planes * size + (own ^ step) * edge_size
-        incoming[step].wait()
+        incoming[index].wait()
 
         def edge_step(row, unused, first=first, step=step):
             field[both((first + row) * 4 * half), :] = with_turned(landed[step, tile(row * 2 * half), :])
@@ -154,7 +167,7 @@
     dest_rows = fine_rows // dest_count
 
     def plane_step(turn, unused):
-        plane = own ^ turn
+        plane = own ^ (planes - 1 - turn)
         slot = turn % 2
         bring(turn).wait()
 
@@ -315,7 +328,7 @@
             return note
         return lax.ppermute(note, "zed", [(plane, plane ^ step) for plane in range(planes)])
 
-    arrived = [to_planes(packed[step], step) for step in (3, 2, 1, 0)][::-1]
+    arrived = [to_planes(packed[step], step) for step in ((3, 2) if edge_rows else (3, 2, 1))]
 
     plane_of = partner_ids // (ring_count * rows)
     ring_of = partner_ids // rows % ring_count
@@ -383,15 +396,19 @@
         rows, slots, fine_rows, stride, width, list_rows, list_rows + fine_lists, turns_at, together, fixed, group
     )
 
-    notes = pack(here, edges, [meta], 0) if edge_rows else [meta] * planes
+    notes = pack(here, edges, [meta, packed[1]], 0) if edge_rows else [meta] * planes
     after_notes = lax.optimization_barrier((notes, trans_table, dir_angles, stencil_ids, stencil_weights))
     notes, trans_table, dir_angles, stencil_ids, stencil_weights = after_notes
-    received = [to_planes(notes[step], step) for step in (3, 2, 1, 0)][::-1]
+    received = [to_planes(notes[step], step) for step in (3, 2, 1, 0)]
     edge_part = edge_rows * 2 * half
-    numbers = jnp.stack([note[edge_part:] for note in received]).astype(jnp.int32)
+    numbers = jnp.stack([note[edge_part : edge_part + 2 * stride] for note in received]).astype(jnp.int32)
     meta = numbers[:, :stride] * 2**word_bits + numbers[:, stride:]
-    if ring_count != 2:
-        arrived = [lax.all_gather(one, "ring", axis=0, tiled=True) for one in arrived]
+    near_at = 0
+    if edge_rows:
+        near_at = edge_part + 2 * stride
+        arrived = arrived + [received.pop(2), packed[0]]
+    else:
+        arrived = [lax.all_gather(one, "ring", axis=0, tiled=True) for one in arrived + [packed[0]]]
         received = []
 
     def blocks(table):
@@ -443,7 +460,7 @@
     whole = pl.BlockSpec(memory_space=pltpu.VMEM)
     message = (2 * dest_rows + 2 * half, kf_pad)
     local_fine, rims = pl.pallas_call(
-        functools.partial(fine_kernel, plan, size, edge_rows),
+        functools.partial(fine_kernel, plan, size, edge_rows, near_at),
         out_shape=[
             pltpu.HBM((planes, dir_count) + message, jnp.float32),
             jax.ShapeDtypeStruct((2 * half, lanes), jnp.float32),

time: 92.6 us -> 95.9 us (1.036)
  waiting for transfers between devices: 35.2 us -> 37.7 us
    ppermute x6 -> x5, waiting for transfers between devices: 8.89 us -> 11.4 us  [to_planes(): lax.ppermute(note, 'zed', [(plane, plane ^ step) for plane in range(plane...]
    ppermute x6 -> x5, starting transfers between devices: 6.21 us -> 5.92 us  [to_planes(): lax.ppermute(note, 'zed', [(plane, plane ^ step) for plane in range(plane...]
  transfers between devices with their start and end apart: 8 -> 7, of which waited for: 3 -> 4; matrix products, arithmetic and copies ran while one was open for 16% -> 15% of each run, Pallas kernels for 2% -> 2%
where the time goes in v10:
time: 95.9 us; the launch traced here: 95.4 us
  waiting for transfers between devices  37.7 us (39%)
  Pallas kernels  27 us (28%)
  starting transfers between devices  15.2 us (16%)
  other arithmetic  10.6 us (11%)
  local copies, waits for them, and re-layouts  4.66 us (5%)
    all_to_all x1, waiting for transfers between devices, per_device(): lax.all_to_all(local_fine.reshape((planes * dir_count,) + message), ('zed...  26.3 us
    pallas_call x1, Pallas kernels, per_device(): pl.pallas_call(functools.partial(fine_kernel, plan, size, edge_rows, near...  20.8 us
    ppermute x5, waiting for transfers between devices, to_planes(): lax.ppermute(note, 'zed', [(plane, plane ^ step) for plane in range(plane...  11.4 us
    all_to_all x1, starting transfers between devices, per_device(): lax.all_to_all(local_fine.reshape((planes * dir_count,) + message), ('zed...  8.02 us
    ppermute x5, starting transfers between devices, to_planes(): lax.ppermute(note, 'zed', [(plane, plane ^ step) for plane in range(plane...  5.92 us
    pallas_call x2, Pallas kernels, pack(): pl.pallas_call(functools.partial(pack_kernel, source_count, len(notes)),...  4.64 us
    reshape x1, local copies, waits for them, and re-layouts, per_device(): jnp.pad(trans_table, ((0, 0), (0, 0), (0, pad_dirs))).reshape(-1, lanes)  2.31 us
    reduce_sum x1, other arithmetic, in_order(): jnp.sum(jnp.where(at_rank[:, :, None], across(one, width)[None], 0), axis=1)  2.24 us
  transfers between devices with their start and end apart: 7, of which 4 were waited for; matrix products, arithmetic and copies ran while one was open for 15% of the time, Pallas kernels for 2%

profile of v10, /device:TPU:11, one launch (start us, length us, event | category | flops | bytes accessed | tf_op | source)
XLA Modules:
  0.0 95.4 jit_solution(2961944752861460080)
XLA Ops:
  0.0 2.7 %pack_sources.2 = (f32[512,128]{1,0:T(8,128)}, f32[512,128]{1,0:T(8,128)}, f32[512,128]{1,0:T(8,128)}, f32[512,128]{1,0:T(8,128)}, f32[16,2,4,512]{3,2,1,0:T(4,128)}) custom-call(s32[1]{0:T(128)} %bitcast.zed, s32[1]{0:T(128)} %bitcast.1.ring, f32[64,2,4,512]{3,2,1,0:T(4,128)} %field.1), custom_call_target="tpu_custom_call" | custom-call | tf_op jit(solution)/shard_map/pack_sources/pallas_call | solution.py:95
  2.7 1.2 %collective-permute-start = (f32[16,2,4,512]{3,2,1,0:T(4,128)}, f32[16,2,4,512]{3,2,1,0:T(4,128)S(1)}, u32[]{:S(2)}, u32[]{:S(2)}) collective-permute-start(f32[16,2,4,512]{3,2,1,0:T(4,128)} %get-tuple-element.24), channel_id=1, source_target_pairs={{0,4},{4,0},{1,5},{5,1},{2,6},{6,2},{3,7},{7,3},{8,12},{12,8},{9,1... | collective-permute-start | bytes 786440 | tf_op jit(solution)/shard_map/ppermute | solution.py:324
  3.9 1.3 %collective-permute-start.4 = (f32[512,128]{1,0:T(8,128)}, f32[512,128]{1,0:T(8,128)S(1)}, u32[]{:S(2)}, u32[]{:S(2)}) collective-permute-start(f32[512,128]{1,0:T(8,128)} %get-tuple-element.34), channel_id=1, source_target_pairs={{0,24},{8,16},{16,8},{24,0},{1,25},{9,17},{17,9},{25,1},{2,26},{10... | collective-permute-start | bytes 786440 | tf_op jit(solution)/shard_map/ppermute | solution.py:329
  5.2 1.0 %collective-permute-start.5 = (f32[512,128]{1,0:T(8,128)}, f32[512,128]{1,0:T(8,128)S(1)}, u32[]{:S(2)}, u32[]{:S(2)}) collective-permute-start(f32[512,128]{1,0:T(8,128)} %get-tuple-element.35), channel_id=1, source_target_pairs={{0,16},{8,24},{16,0},{24,8},{1,17},{9,25},{17,1},{25,9},{2,18},{10... | collective-permute-start | bytes 786440 | tf_op jit(solution)/shard_map/ppermute | solution.py:329
  6.3 0.9 convert_reduce_fusion.1
  7.3 0.8 select_reduce_fusion.3
  8.2 0.8 select_reduce_fusion.4
  9.9 0.8 fusion.13
  10.7 0.7 broadcast_multiply_fusion.1
  11.4 2.2 %select_reduce_fusion.1 = (s32[64,32]{1,0:T(8,128)S(1)}, s32[64,32]{1,0:T(8,128)S(1)}) fusion(s32[64,32]{0,1:T(8,128)S(1)} %pad.23, pred[64,64]{1,0:T(8,128)(4,1)S(1)} %iota_compare_fusion.3, s32[64,32]{0,1:T(8,128)S(1)} %pad.25), kind=kLoop, calls=%fused_computation.1 | loop fusion | flops 520192 | bytes 36864 | tf_op jit(solution)/shard_map/reduce_sum | solution.py:377
  14.6 0.7 copy-done.3
  15.3 2.0 %pack_sources.3 = (f32[176,128]{1,0:T(8,128)}, f32[688,128]{1,0:T(8,128)}, f32[176,128]{1,0:T(8,128)}, f32[176,128]{1,0:T(8,128)}) custom-call(s32[1]{0:T(128)} %bitcast.zed, s32[1]{0:T(128)} %bitcast.1.ring, f32[16,2,4,512]{3,2,1,0:T(4,128)} %copy-done.3, f32[48,128]{1,0:T(8,128)} %pad_maximum_fusion.2.refs_0_, f32[512,128]{1,0:T(8,128)} %get-tuple-element.25.refs_1_), custom_call_target="tpu_custom_call" | custom-call | tf_op jit(solution)/shard_map/pack_sources/pallas_call | solution.py:95
  18.0 0.7 slice_bitcast_fusion.3
  18.8 2.4 %collective-permute-start.1 = (f32[176,128]{1,0:T(8,128)}, f32[176,128]{1,0:T(8,128)S(1)}, u32[]{:S(2)}, u32[]{:S(2)}) collective-permute-start(f32[176,128]{1,0:T(8,128)} %get-tuple-element.30), channel_id=1, source_target_pairs={{0,24},{8,16},{16,8},{24,0},{1,25},{9,17},{17,9},{25,1},{2,26},{10... | collective-permute-start | bytes 270344 | tf_op jit(solution)/shard_map/ppermute | solution.py:329
  21.1 0.9 collective-permute-start.2
  23.6 2.3 %reshape.217.refs_7_ = f32[2528,128]{1,0:T(8,128)S(1)} reshape(f32[316,2,512]{2,1,0:T(2,128)} %param.11) | data formatting | bytes 2588672 | tf_op jit(solution)/shard_map/reshape | solution.py:420
  25.9 0.9 cosine_multiply_fusion
  27.2 6.9 %collective-permute-done.1.refs_4_ = f32[176,128]{1,0:T(8,128)S(1)} collective-permute-done((f32[176,128]{1,0:T(8,128)}, f32[176,128]{1,0:T(8,128)S(1)}, u32[]{:S(2)}, u32[]{:S(2)}) %collective-permute-start.1) | collective-permute-done | bytes 90144 | tf_op jit(solution)/shard_map/ppermute | solution.py:329
  34.1 0.7 collective-permute-done.2.refs_5_
  34.8 3.8 %collective-permute-done.3.refs_2_ = f32[688,128]{1,0:T(8,128)S(1)} collective-permute-done((f32[688,128]{1,0:T(8,128)}, f32[688,128]{1,0:T(8,128)S(1)}, u32[]{:S(2)}, u32[]{:S(2)}) %collective-permute-start.3) | collective-permute-done | bytes 352288 | tf_op jit(solution)/shard_map/ppermute | solution.py:329
  38.7 20.8 %translate_and_interpolate.1 = (f32[4,4,136,128]{3,2,1,0:T(8,128)}, f32[8,128]{1,0:T(8,128)S(1)}) custom-call(s32[1]{0:T(128)} %bitcast.zed, s32[4,24,128]{2,1,0:T(8,128)S(1)} %slice_add_fusion.lists, f32[512,128]{1,0:T(8,128)S(1)} %collective-permute-done.4.refs_0_, f32[512,128]{1,0:T(8,128)S(1)} %collective-permute-done.5.refs_1_, ...), custom_call_target="tpu_custom_call" | custom-call | tf_op jit(solution)/shard_map/translate_and_interpolate/pallas_call | solution.py:462
  59.5 8.0 %all-to-all-start = ((f32[16,136,128]{2,1,0:T(8,128)}), f32[16,136,128]{2,1,0:T(8,128)S(1)}, u32[]{:S(2)}, u32[]{:S(2)}) async-start(f32[16,136,128]{2,1,0:T(8,128)} %bitcast.40), calls=%async_computation | async-start | bytes 2228224 | tf_op jit(solution)/shard_map/all_to_all | solution.py:487
  67.5 26.3 %all-to-all-done.parts = f32[16,136,128]{2,1,0:T(8,128)S(1)} async-done(((f32[16,136,128]{2,1,0:T(8,128)}), f32[16,136,128]{2,1,0:T(8,128)S(1)}, u32[]{:S(2)}, u32[]{:S(2)}) %all-to-all-start) | async-done | bytes 1114144 | tf_op jit(solution)/shard_map/all_to_all | solution.py:487
  93.9 1.5 %join_parts.1 = f32[64,2,4,512]{3,2,1,0:T(4,128)} custom-call(f32[16,136,128]{2,1,0:T(8,128)S(1)} %all-to-all-done.parts, f32[1,128]{1,0:T(1,128)S(1)} %slice_subtract_fusion.rims), custom_call_target="tpu_custom_call" | custom-call | tf_op jit(solution)/shard_map/join_parts/pallas_call | solution.py:496
  (50 shorter events, 4.7 us)
Async XLA Ops:
  0.0 17.3 %copy-start = (s32[2048,4]{0,1:T(4,128)S(1)}, s32[2048,4]{0,1:T(4,128)}, u32[]{:S(2)}) copy-start(s32[2048,4]{0,1:T(4,128)} %param.18) | copy-start | bytes 98308
  2.7 11.9 %collective-permute-start = (f32[16,2,4,512]{3,2,1,0:T(4,128)}, f32[16,2,4,512]{3,2,1,0:T(4,128)S(1)}, u32[]{:S(2)}, u32[]{:S(2)}) collective-permute-start(f32[16,2,4,512]{3,2,1,0:T(4,128)} %get-tuple-element.24), channel_id=1, source_target_pairs={{0,4},{4,0},{1,5},{5,1},{2,6},{6,2},{3,7},{7,3},{8,12},{12,8},{9,1... | collective-permute-start | bytes 786440 | tf_op jit(solution)/shard_map/ppermute | solution.py:324
  3.9 34.7 %collective-permute-start.4 = (f32[512,128]{1,0:T(8,128)}, f32[512,128]{1,0:T(8,128)S(1)}, u32[]{:S(2)}, u32[]{:S(2)}) collective-permute-start(f32[512,128]{1,0:T(8,128)} %get-tuple-element.34), channel_id=1, source_target_pairs={{0,24},{8,16},{16,8},{24,0},{1,25},{9,17},{17,9},{25,1},{2,26},{10... | collective-permute-start | bytes 786440 | tf_op jit(solution)/shard_map/ppermute | solution.py:329
  5.2 33.4 %collective-permute-start.5 = (f32[512,128]{1,0:T(8,128)}, f32[512,128]{1,0:T(8,128)S(1)}, u32[]{:S(2)}, u32[]{:S(2)}) collective-permute-start(f32[512,128]{1,0:T(8,128)} %get-tuple-element.35), channel_id=1, source_target_pairs={{0,16},{8,24},{16,0},{24,8},{1,17},{9,25},{17,1},{25,9},{2,18},{10... | collective-permute-start | bytes 786440 | tf_op jit(solution)/shard_map/ppermute | solution.py:329
  14.6 0.7 copy-start.3
  18.8 15.3 %collective-permute-start.1 = (f32[176,128]{1,0:T(8,128)}, f32[176,128]{1,0:T(8,128)S(1)}, u32[]{:S(2)}, u32[]{:S(2)}) collective-permute-start(f32[176,128]{1,0:T(8,128)} %get-tuple-element.30), channel_id=1, source_target_pairs={{0,24},{8,16},{16,8},{24,0},{1,25},{9,17},{17,9},{25,1},{2,26},{10... | collective-permute-start | bytes 270344 | tf_op jit(solution)/shard_map/ppermute | solution.py:329
  21.1 13.7 %collective-permute-start.2 = (f32[176,128]{1,0:T(8,128)}, f32[176,128]{1,0:T(8,128)S(1)}, u32[]{:S(2)}, u32[]{:S(2)}) collective-permute-start(f32[176,128]{1,0:T(8,128)} %get-tuple-element.31), channel_id=1, source_target_pairs={{0,16},{8,24},{16,0},{24,8},{1,17},{9,25},{17,1},{25,9},{2,18},{10... | collective-permute-start | bytes 270344 | tf_op jit(solution)/shard_map/ppermute | solution.py:329
  23.2 15.4 %collective-permute-start.3 = (f32[688,128]{1,0:T(8,128)}, f32[688,128]{1,0:T(8,128)S(1)}, u32[]{:S(2)}, u32[]{:S(2)}) collective-permute-start(f32[688,128]{1,0:T(8,128)} %get-tuple-element.32), channel_id=1, source_target_pairs={{0,8},{8,0},{16,24},{24,16},{1,9},{9,1},{17,25},{25,17},{2,10},{10... | collective-permute-start | bytes 1056776 | tf_op jit(solution)/shard_map/ppermute | solution.py:329
  26.8 11.8 %copy-start.1 = (f32[512,128]{1,0:T(8,128)S(1)}, f32[512,128]{1,0:T(8,128)}, u32[]{:S(2)}) copy-start(f32[512,128]{1,0:T(8,128)} %get-tuple-element.36.refs_3_) | copy-start | bytes 786436
  26.8 11.8 %copy-start.2 = (f32[176,128]{1,0:T(8,128)S(1)}, f32[176,128]{1,0:T(8,128)}, u32[]{:S(2)}) copy-start(f32[176,128]{1,0:T(8,128)} %get-tuple-element.33.refs_6_) | copy-start | bytes 270340
  59.5 34.4 %all-to-all-start = ((f32[16,136,128]{2,1,0:T(8,128)}), f32[16,136,128]{2,1,0:T(8,128)S(1)}, u32[]{:S(2)}, u32[]{:S(2)}) async-start(f32[16,136,128]{2,1,0:T(8,128)} %bitcast.40), calls=%async_computation | async-start | bytes 2228224 | tf_op jit(solution)/shard_map/all_to_all | solution.py:487

commit v11 on v9

--- a/solution.py
+++ b/solution.py
@@ -103,10 +103,10 @@
     return pl.ds(pl.multiple_of(start, 2 * half), 2 * half)
 
 
-def fine_kernel(plan, size, edge_size, zed, lists, *refs):
+def fine_kernel(plan, size, edge_size, zed, *refs):
     mains, refs = refs[:planes], refs[planes:]
     edges = refs[: planes if edge_size else 0]
-    refs = refs[len(edges) :]
+    lists, refs = refs[len(edges)], refs[len(edges) + 1 :]
     table, phases, weights, out, rims, meta, field, moved, shifted, left, ready, landed, sems = refs
     rows, fine_rows = plan.rows, plan.fine_rows
     own = zed[0]
@@ -116,9 +116,9 @@
 
     bring(0).start()
     incoming = []
-    for step, edge in enumerate(edges):
+    for index, edge in enumerate(edges):
         chosen = edge.at[pl.ds(0, edge_size * 2 * half)]
-        incoming.append(pltpu.make_async_copy(chosen, landed.at[step], sems.at[planes + 2 + step]))
+        incoming.append(pltpu.make_async_copy(chosen, landed.at[index], sems.at[planes + 2 + index]))
         incoming[-1].start()
     lane = lax.broadcasted_iota(jnp.int32, rims.shape, 1)
     rims[...] = ((lane < rim) | (lane >= lanes - rim)).astype(jnp.float32)
@@ -137,12 +137,12 @@
             return unused
 
         lax.fori_loop(0, size, main_step, 0, unroll=8)
-    for step, edge in enumerate(edges):
-        first = planes * size + (own ^ step) * edge_size
-        incoming[step].wait()
-
-        def edge_step(row, unused, first=first, step=step):
-            field[both((first + row) * 4 * half), :] = with_turned(landed[step, tile(row * 2 * half), :])
+    for index in range(len(edges)):
+        first = planes * size + (own ^ (planes - 1 - index)) * edge_size
+        incoming[index].wait()
+
+        def edge_step(row, unused, first=first, index=index):
+            field[both((first + row) * 4 * half), :] = with_turned(landed[index, tile(row * 2 * half), :])
             return unused
 
         lax.fori_loop(0, edge_size, edge_step, 0, unroll=8)
@@ -154,7 +154,7 @@
     dest_rows = fine_rows // dest_count
 
     def plane_step(turn, unused):
-        plane = own ^ turn
+        plane = own ^ (planes - 1 - turn)
         slot = turn % 2
         bring(turn).wait()
 
@@ -386,7 +386,7 @@
     notes = pack(here, edges, [meta], 0) if edge_rows else [meta] * planes
     after_notes = lax.optimization_barrier((notes, trans_table, dir_angles, stencil_ids, stencil_weights))
     notes, trans_table, dir_angles, stencil_ids, stencil_weights = after_notes
-    received = [to_planes(notes[step], step) for step in (3, 2, 1, 0)][::-1]
+    received = [to_planes(notes[step], step) for step in (3, 2, 1, 0)]
     edge_part = edge_rows * 2 * half
     numbers = jnp.stack([note[edge_part:] for note in received]).astype(jnp.int32)
     meta = numbers[:, :stride] * 2**word_bits + numbers[:, stride:]
@@ -448,9 +448,9 @@
             pltpu.HBM((planes, dir_count) + message, jnp.float32),
             jax.ShapeDtypeStruct((2 * half, lanes), jnp.float32),
         ],
-        in_specs=[pl.BlockSpec(memory_space=pltpu.SMEM), pl.BlockSpec(memory_space=pl.ANY)]
+        in_specs=[pl.BlockSpec(memory_space=pltpu.SMEM)]
         + [whole] * planes
-        + [pl.BlockSpec(memory_space=pl.ANY)] * len(received)
+        + [pl.BlockSpec(memory_space=pl.ANY)] * (len(received) + 1)
         + [whole] * 3,
         out_specs=[pl.BlockSpec(memory_space=pltpu.HBM), whole],
         scratch_shapes=[
@@ -465,7 +465,7 @@
         ],
         compiler_params=pltpu.CompilerParams(vmem_limit_bytes=48 * 2**20),
         name="translate_and_interpolate",
-    )(here[0], meta, *arrived, *received, table, phases, passes)
+    )(here[0], *arrived, *received, meta, table, phases, passes)
 
     parts = lax.all_to_all(
         local_fine.reshape((planes * dir_count,) + message),

time: 92.6 us -> 95 us (1.026)
  starting transfers between devices: 14.7 us -> 15.9 us
  waiting for transfers between devices: 35.2 us -> 36.4 us
    all_to_all x1, starting transfers between devices: 7.24 us -> 8.82 us  [per_device(): lax.all_to_all(local_fine.reshape((planes * dir_count,) + message), ('zed...]
    ppermute x6, waiting for transfers between devices: 8.89 us -> 10 us  [to_planes(): lax.ppermute(note, 'zed', [(plane, plane ^ step) for plane in range(plane...]
  transfers between devices with their start and end apart: 8 -> 8, of which waited for: 3 -> 4; matrix products, arithmetic and copies ran while one was open for 16% -> 15% of each run, Pallas kernels for 2% -> 2%
where the time goes in v11:
time: 95 us; the launch traced here: 94.3 us
  waiting for transfers between devices  36.4 us (38%)
  Pallas kernels  26.5 us (28%)
  starting transfers between devices  15.9 us (17%)
  other arithmetic  10.7 us (11%)
  local copies, waits for them, and re-layouts  4.67 us (5%)
    all_to_all x1, waiting for transfers between devices, per_device(): lax.all_to_all(local_fine.reshape((planes * dir_count,) + message), ('zed...  26.3 us
    pallas_call x1, Pallas kernels, per_device(): pl.pallas_call(functools.partial(fine_kernel, plan, size, edge_rows), out...  20.5 us
    ppermute x6, waiting for transfers between devices, to_planes(): lax.ppermute(note, 'zed', [(plane, plane ^ step) for plane in range(plane...  10 us
    all_to_all x1, starting transfers between devices, per_device(): lax.all_to_all(local_fine.reshape((planes * dir_count,) + message), ('zed...  8.82 us
    ppermute x6, starting transfers between devices, to_planes(): lax.ppermute(note, 'zed', [(plane, plane ^ step) for plane in range(plane...  5.86 us
    pallas_call x2, Pallas kernels, pack(): pl.pallas_call(functools.partial(pack_kernel, source_count, len(notes)),...  4.47 us
    reshape x1, local copies, waits for them, and re-layouts, per_device(): jnp.pad(trans_table, ((0, 0), (0, 0), (0, pad_dirs))).reshape(-1, lanes)  2.32 us
    reduce_sum x1, other arithmetic, in_order(): jnp.sum(jnp.where(at_rank[:, :, None], across(one, width)[None], 0), axis=1)  2.24 us
  transfers between devices with their start and end apart: 8, of which 4 were waited for; matrix products, arithmetic and copies ran while one was open for 15% of the time, Pallas kernels for 2%

profile of v11, /device:TPU:11, one launch (start us, length us, event | category | flops | bytes accessed | tf_op | source)
XLA Modules:
  0.0 94.3 jit_solution(12786223278277111202)
XLA Ops:
  0.0 2.7 %pack_sources.2 = (f32[512,128]{1,0:T(8,128)}, f32[512,128]{1,0:T(8,128)}, f32[512,128]{1,0:T(8,128)}, f32[512,128]{1,0:T(8,128)}, f32[16,2,4,512]{3,2,1,0:T(4,128)}) custom-call(s32[1]{0:T(128)} %bitcast.zed, s32[1]{0:T(128)} %bitcast.1.ring, f32[64,2,4,512]{3,2,1,0:T(4,128)} %field.1), custom_call_target="tpu_custom_call" | custom-call | tf_op jit(solution)/shard_map/pack_sources/pallas_call | solution.py:88
  2.8 2.3 %collective-permute-start.1 = (f32[512,128]{1,0:T(8,128)}, f32[512,128]{1,0:T(8,128)S(1)}, u32[]{:S(2)}, u32[]{:S(2)}) collective-permute-start(f32[512,128]{1,0:T(8,128)} %get-tuple-element.26), channel_id=1, source_target_pairs={{0,16},{8,24},{16,0},{24,8},{1,17},{9,25},{17,1},{25,9},{2,18},{10... | collective-permute-start | bytes 786440 | tf_op jit(solution)/shard_map/ppermute | solution.py:316
  5.3 1.2 %collective-permute-start.3 = (f32[16,2,4,512]{3,2,1,0:T(4,128)}, f32[16,2,4,512]{3,2,1,0:T(4,128)S(1)}, u32[]{:S(2)}, u32[]{:S(2)}) collective-permute-start(f32[16,2,4,512]{3,2,1,0:T(4,128)} %get-tuple-element.28), channel_id=1, source_target_pairs={{0,4},{4,0},{1,5},{5,1},{2,6},{6,2},{3,7},{7,3},{8,12},{12,8},{9,1... | collective-permute-start | bytes 786440 | tf_op jit(solution)/shard_map/ppermute | solution.py:311
  6.6 0.9 convert_reduce_fusion.1
  7.6 0.8 select_reduce_fusion.3
  8.6 0.8 select_reduce_fusion.4
  10.2 0.8 fusion.13
  11.0 0.7 broadcast_multiply_fusion.1
  11.8 2.2 %select_reduce_fusion.1 = (s32[64,32]{1,0:T(8,128)S(1)}, s32[64,32]{1,0:T(8,128)S(1)}) fusion(s32[64,32]{0,1:T(8,128)S(1)} %pad.23, pred[64,64]{1,0:T(8,128)(4,1)S(1)} %iota_compare_fusion.3, s32[64,32]{0,1:T(8,128)S(1)} %pad.25), kind=kLoop, calls=%fused_computation.1 | loop fusion | flops 520192 | bytes 36864 | tf_op jit(solution)/shard_map/reduce_sum | solution.py:364
  15.0 0.7 copy-done.3
  15.7 1.8 %pack_sources.3 = (f32[176,128]{1,0:T(8,128)}, f32[176,128]{1,0:T(8,128)}, f32[176,128]{1,0:T(8,128)}, f32[176,128]{1,0:T(8,128)}) custom-call(s32[1]{0:T(128)} %bitcast.zed, s32[1]{0:T(128)} %bitcast.1.ring, f32[16,2,4,512]{3,2,1,0:T(4,128)} %copy-done.3, f32[48,128]{1,0:T(8,128)} %pad_maximum_fusion.2.refs_0_), custom_call_target="tpu_custom_call" | custom-call | tf_op jit(solution)/shard_map/pack_sources/pallas_call | solution.py:88
  17.5 0.7 dynamic-slice_bitcast_fusion
  18.2 0.7 slice_bitcast_fusion.3
  18.9 1.3 %collective-permute-start.4 = (f32[176,128]{1,0:T(8,128)}, f32[176,128]{1,0:T(8,128)S(1)}, u32[]{:S(2)}, u32[]{:S(2)}) collective-permute-start(f32[176,128]{1,0:T(8,128)} %get-tuple-element.33), channel_id=1, source_target_pairs={{0,24},{8,16},{16,8},{24,0},{1,25},{9,17},{17,9},{25,1},{2,26},{10... | collective-permute-start | bytes 270344 | tf_op jit(solution)/shard_map/ppermute | solution.py:316
  20.2 1.9 %collective-permute-start.5 = (f32[176,128]{1,0:T(8,128)}, f32[176,128]{1,0:T(8,128)S(1)}, u32[]{:S(2)}, u32[]{:S(2)}) collective-permute-start(f32[176,128]{1,0:T(8,128)} %get-tuple-element.34), channel_id=1, source_target_pairs={{0,16},{8,24},{16,0},{24,8},{1,17},{9,25},{17,1},{25,9},{2,18},{10... | collective-permute-start | bytes 270344 | tf_op jit(solution)/shard_map/ppermute | solution.py:316
  23.4 2.3 %reshape.217.refs_9_ = f32[2528,128]{1,0:T(8,128)S(1)} reshape(f32[316,2,512]{2,1,0:T(2,128)} %param.11) | data formatting | bytes 2588672 | tf_op jit(solution)/shard_map/reshape | solution.py:403
  25.7 0.9 cosine_multiply_fusion
  27.0 6.6 %collective-permute-done.4.refs_4_ = f32[176,128]{1,0:T(8,128)S(1)} collective-permute-done((f32[176,128]{1,0:T(8,128)}, f32[176,128]{1,0:T(8,128)S(1)}, u32[]{:S(2)}, u32[]{:S(2)}) %collective-permute-start.4) | collective-permute-done | bytes 90144 | tf_op jit(solution)/shard_map/ppermute | solution.py:316
  33.7 1.1 %collective-permute-done.5.refs_5_ = f32[176,128]{1,0:T(8,128)S(1)} collective-permute-done((f32[176,128]{1,0:T(8,128)}, f32[176,128]{1,0:T(8,128)S(1)}, u32[]{:S(2)}, u32[]{:S(2)}) %collective-permute-start.5) | collective-permute-done | bytes 90144 | tf_op jit(solution)/shard_map/ppermute | solution.py:316
  34.8 2.3 %collective-permute-done.6.refs_6_ = f32[176,128]{1,0:T(8,128)S(1)} collective-permute-done((f32[176,128]{1,0:T(8,128)S(1)}, f32[176,128]{1,0:T(8,128)S(1)}, u32[]{:S(2)}, u32[]{:S(2)}) %collective-permute-start.6) | collective-permute-done | bytes 90144 | tf_op jit(solution)/shard_map/ppermute | solution.py:316
  37.1 20.5 %translate_and_interpolate.1 = (f32[4,4,136,128]{3,2,1,0:T(8,128)}, f32[8,128]{1,0:T(8,128)S(1)}) custom-call(s32[1]{0:T(128)} %bitcast.zed, f32[512,128]{1,0:T(8,128)S(1)} %copy-done.1, f32[512,128]{1,0:T(8,128)S(1)} %collective-permute-done.refs_1_, f32[512,128]{1,0:T(8,128)S(1)} %collective-permute-done.1.refs_2_, ...), custom_call_target="tpu_custom_call" | custom-call | tf_op jit(solution)/shard_map/translate_and_interpolate/pallas_call | solution.py:445
  57.6 8.8 %all-to-all-start = ((f32[16,136,128]{2,1,0:T(8,128)}), f32[16,136,128]{2,1,0:T(8,128)S(1)}, u32[]{:S(2)}, u32[]{:S(2)}) async-start(f32[16,136,128]{2,1,0:T(8,128)} %bitcast.40), calls=%async_computation | async-start | bytes 2228224 | tf_op jit(solution)/shard_map/all_to_all | solution.py:470
  66.4 26.3 %all-to-all-done.parts = f32[16,136,128]{2,1,0:T(8,128)S(1)} async-done(((f32[16,136,128]{2,1,0:T(8,128)}), f32[16,136,128]{2,1,0:T(8,128)S(1)}, u32[]{:S(2)}, u32[]{:S(2)}) %all-to-all-start) | async-done | bytes 1114144 | tf_op jit(solution)/shard_map/all_to_all | solution.py:470
  92.8 1.5 %join_parts.1 = f32[64,2,4,512]{3,2,1,0:T(4,128)} custom-call(f32[16,136,128]{2,1,0:T(8,128)S(1)} %all-to-all-done.parts, f32[1,128]{1,0:T(1,128)S(1)} %slice_subtract_fusion.rims), custom_call_target="tpu_custom_call" | custom-call | tf_op jit(solution)/shard_map/join_parts/pallas_call | solution.py:479
  (54 shorter events, 4.0 us)
Async XLA Ops:
  0.0 17.5 %copy-start = (s32[2048,4]{0,1:T(4,128)S(1)}, s32[2048,4]{0,1:T(4,128)}, u32[]{:S(2)}) copy-start(s32[2048,4]{0,1:T(4,128)} %param.18) | copy-start | bytes 98308
  2.7 34.4 %collective-permute-start = (f32[512,128]{1,0:T(8,128)}, f32[512,128]{1,0:T(8,128)S(1)}, u32[]{:S(2)}, u32[]{:S(2)}) collective-permute-start(f32[512,128]{1,0:T(8,128)} %get-tuple-element.25), channel_id=1, source_target_pairs={{0,8},{8,0},{16,24},{24,16},{1,9},{9,1},{17,25},{25,17},{2,10},{10... | collective-permute-start | bytes 786440 | tf_op jit(solution)/shard_map/ppermute | solution.py:316
  2.8 34.2 %collective-permute-start.1 = (f32[512,128]{1,0:T(8,128)}, f32[512,128]{1,0:T(8,128)S(1)}, u32[]{:S(2)}, u32[]{:S(2)}) collective-permute-start(f32[512,128]{1,0:T(8,128)} %get-tuple-element.26), channel_id=1, source_target_pairs={{0,16},{8,24},{16,0},{24,8},{1,17},{9,25},{17,1},{25,9},{2,18},{10... | collective-permute-start | bytes 786440 | tf_op jit(solution)/shard_map/ppermute | solution.py:316
  5.2 31.9 %collective-permute-start.2 = (f32[512,128]{1,0:T(8,128)}, f32[512,128]{1,0:T(8,128)S(1)}, u32[]{:S(2)}, u32[]{:S(2)}) collective-permute-start(f32[512,128]{1,0:T(8,128)} %get-tuple-element.27), channel_id=1, source_target_pairs={{0,24},{8,16},{16,8},{24,0},{1,25},{9,17},{17,9},{25,1},{2,26},{10... | collective-permute-start | bytes 786440 | tf_op jit(solution)/shard_map/ppermute | solution.py:316
  5.3 9.6 %collective-permute-start.3 = (f32[16,2,4,512]{3,2,1,0:T(4,128)}, f32[16,2,4,512]{3,2,1,0:T(4,128)S(1)}, u32[]{:S(2)}, u32[]{:S(2)}) collective-permute-start(f32[16,2,4,512]{3,2,1,0:T(4,128)} %get-tuple-element.28), channel_id=1, source_target_pairs={{0,4},{4,0},{1,5},{5,1},{2,6},{6,2},{3,7},{7,3},{8,12},{12,8},{9,1... | collective-permute-start | bytes 786440 | tf_op jit(solution)/shard_map/ppermute | solution.py:311
  15.0 0.7 copy-start.3
  18.9 14.7 %collective-permute-start.4 = (f32[176,128]{1,0:T(8,128)}, f32[176,128]{1,0:T(8,128)S(1)}, u32[]{:S(2)}, u32[]{:S(2)}) collective-permute-start(f32[176,128]{1,0:T(8,128)} %get-tuple-element.33), channel_id=1, source_target_pairs={{0,24},{8,16},{16,8},{24,0},{1,25},{9,17},{17,9},{25,1},{2,26},{10... | collective-permute-start | bytes 270344 | tf_op jit(solution)/shard_map/ppermute | solution.py:316
  20.2 14.6 %collective-permute-start.5 = (f32[176,128]{1,0:T(8,128)}, f32[176,128]{1,0:T(8,128)S(1)}, u32[]{:S(2)}, u32[]{:S(2)}) collective-permute-start(f32[176,128]{1,0:T(8,128)} %get-tuple-element.34), channel_id=1, source_target_pairs={{0,16},{8,24},{16,0},{24,8},{1,17},{9,25},{17,1},{25,9},{2,18},{10... | collective-permute-start | bytes 270344 | tf_op jit(solution)/shard_map/ppermute | solution.py:316
  25.7 8.0 %copy-start.4 = (f32[176,128]{1,0:T(8,128)S(1)}, f32[176,128]{1,0:T(8,128)}, u32[]{:S(2)}) copy-start(f32[176,128]{1,0:T(8,128)} %get-tuple-element.35) | copy-start | bytes 270340
  26.6 10.5 %copy-start.1 = (f32[512,128]{1,0:T(8,128)S(1)}, f32[512,128]{1,0:T(8,128)}, u32[]{:S(2)}) copy-start(f32[512,128]{1,0:T(8,128)} %get-tuple-element.24.refs_0_) | copy-start | bytes 786436
  26.6 10.5 %copy-start.2 = (f32[176,128]{1,0:T(8,128)S(1)}, f32[176,128]{1,0:T(8,128)}, u32[]{:S(2)}) copy-start(f32[176,128]{1,0:T(8,128)} %get-tuple-element.36.refs_7_) | copy-start | bytes 270340
  33.7 3.4 %collective-permute-start.6 = (f32[176,128]{1,0:T(8,128)S(1)}, f32[176,128]{1,0:T(8,128)S(1)}, u32[]{:S(2)}, u32[]{:S(2)}) collective-permute-start(f32[176,128]{1,0:T(8,128)S(1)} %copy-done.4), channel_id=1, source_target_pairs={{0,8},{8,0},{16,24},{24,16},{1,9},{9,1},{17,25},{25,17},{2,10},{10... | collective-permute-start | bytes 270344 | tf_op jit(solution)/shard_map/ppermute | solution.py:316
  57.6 35.2 %all-to-all-start = ((f32[16,136,128]{2,1,0:T(8,128)}), f32[16,136,128]{2,1,0:T(8,128)S(1)}, u32[]{:S(2)}, u32[]{:S(2)}) async-start(f32[16,136,128]{2,1,0:T(8,128)} %bitcast.40), calls=%async_computation | async-start | bytes 2228224 | tf_op jit(solution)/shard_map/all_to_all | solution.py:470

commit v12 on v11

--- a/solution.py
+++ b/solution.py
@@ -91,6 +91,7 @@
         in_specs=[pl.BlockSpec(memory_space=pltpu.SMEM)] * 2 + [whole] * (1 + len(notes)),
         out_specs=[whole] * (planes + len(edges)),
         scratch_shapes=[pltpu.VMEM((half, rows * 2 * source_count, lanes), jnp.float32)],
+        compiler_params=pltpu.CompilerParams(vmem_limit_bytes=24 * 2**20),
         name="pack_sources",
     )(*here, field, *notes)
 
@@ -138,7 +139,7 @@
 
         lax.fori_loop(0, size, main_step, 0, unroll=8)
     for index in range(len(edges)):
-        first = planes * size + (own ^ (planes - 1 - index)) * edge_size
+        first = planes * size + (own ^ index) * edge_size
         incoming[index].wait()
 
         def edge_step(row, unused, first=first, index=index):
@@ -154,7 +155,7 @@
     dest_rows = fine_rows // dest_count
 
     def plane_step(turn, unused):
-        plane = own ^ (planes - 1 - turn)
+        plane = own ^ turn
         slot = turn % 2
         bring(turn).wait()
 
@@ -360,9 +361,17 @@
     assert slots <= width and rows <= turns_at and fine_rows % lanes == 0
     assert (field_rows + 1) * 4 * half < 2 ** (31 - word_bits) and type_count * 2 * half < 2**word_bits
 
-    def in_order(one):
-        one = jnp.sum(jnp.where(at_rank[:, :, None], across(one, width)[None], 0), axis=1)
-        return one.reshape(rows * width // lanes, lanes)
+    in_order = jnp.dot(
+        at_rank.astype(jnp.float32),
+        jnp.concatenate([across(place * 4 * half, width), across(partner_types * 2 * half, width)], axis=1).astype(
+            jnp.float32
+        ),
+        precision=lax.Precision.HIGHEST,
+        preferred_element_type=jnp.float32,
+    )
+
+    def listed(side):
+        return in_order[:, side * width : (side + 1) * width].reshape(rows * width // lanes, lanes)
 
     list_rows = rows * width // lanes
     fine_lists = fine_rows // lanes
@@ -370,13 +379,13 @@
     stride = up(list_rows + fine_lists + 1, 8)
 
     def stacked(*parts):
-        meta = jnp.concatenate(parts)
-        return jnp.pad(meta, ((0, stride - meta.shape[0]), (0, 0))).astype(jnp.float32)
+        meta = jnp.concatenate([part.astype(jnp.float32) for part in parts])
+        return jnp.pad(meta, ((0, stride - meta.shape[0]), (0, 0)))
 
     meta = jnp.concatenate(
         [
-            stacked(in_order(place * 4 * half), (parent * 4 * half).reshape(-1, lanes)),
-            stacked(in_order(partner_types * 2 * half), (child_octant * 4 * half).reshape(-1, lanes), last),
+            stacked(listed(0), (parent * 4 * half).reshape(-1, lanes)),
+            stacked(listed(1), (child_octant * 4 * half).reshape(-1, lanes), last),
         ]
     )
     plan = Plan(
@@ -386,7 +395,7 @@
     notes = pack(here, edges, [meta], 0) if edge_rows else [meta] * planes
     after_notes = lax.optimization_barrier((notes, trans_table, dir_angles, stencil_ids, stencil_weights))
     notes, trans_table, dir_angles, stencil_ids, stencil_weights = after_notes
-    received = [to_planes(notes[step], step) for step in (3, 2, 1, 0)]
+    received = [to_planes(notes[step], step) for step in range(planes)]
     edge_part = edge_rows * 2 * half
     numbers = jnp.stack([note[edge_part:] for note in received]).astype(jnp.int32)
     meta = numbers[:, :stride] * 2**word_bits + numbers[:, stride:]

time: 95 us -> 90.3 us (0.951)
  Pallas kernels: 26.5 us -> 23.4 us
  starting transfers between devices: 15.9 us -> 14.8 us
    pallas_call x2, Pallas kernels: 4.47 us -> 1.18 us  [pack(): pl.pallas_call(functools.partial(pack_kernel, source_count, len(notes)),...]
    reduce_sum x1 -> x0, other arithmetic: 2.24 us -> none  [in_order(): jnp.sum(jnp.where(at_rank[:, :, None], across(one, width)[None], 0), axis=1)]
    all_to_all x1, starting transfers between devices: 8.82 us -> 7.01 us  [per_device(): lax.all_to_all(local_fine.reshape((planes * dir_count,) + message), ('zed...]
    add x2, other arithmetic: 1.21 us -> 2.69 us  [interp(): matrix + jnp.where(ids[point][None, :] == targets[:, None], weights[point...]
    convert_element_type x1, other arithmetic: 0.07 us -> 1.1 us  [per_device(): low = (matrices - rounded).astype(jnp.bfloat16)]
  transfers between devices with their start and end apart: 8 -> 8, of which waited for: 4 -> 3; matrix products, arithmetic and copies ran while one was open for 15% -> 15% of each run, Pallas kernels for 2% -> 1%
where the time goes in v12:
time: 90.3 us; the launch traced here: 89.8 us
  waiting for transfers between devices  36.5 us (40%)
  Pallas kernels  23.4 us (26%)
  starting transfers between devices  14.8 us (16%)
  other arithmetic  10.2 us (11%)
  local copies, waits for them, and re-layouts  4.6 us (5%)
    all_to_all x1, waiting for transfers between devices, per_device(): lax.all_to_all(local_fine.reshape((planes * dir_count,) + message), ('zed...  26.3 us
    pallas_call x1, Pallas kernels, per_device(): pl.pallas_call(functools.partial(fine_kernel, plan, size, edge_rows), out...  20.7 us
    ppermute x6, waiting for transfers between devices, to_planes(): lax.ppermute(note, 'zed', [(plane, plane ^ step) for plane in range(plane...  10.1 us
    all_to_all x1, starting transfers between devices, per_device(): lax.all_to_all(local_fine.reshape((planes * dir_count,) + message), ('zed...  7.01 us
    ppermute x6, starting transfers between devices, to_planes(): lax.ppermute(note, 'zed', [(plane, plane ^ step) for plane in range(plane...  6.53 us
    add x2, other arithmetic, interp(): matrix + jnp.where(ids[point][None, :] == targets[:, None], weights[point...  2.69 us
    reshape x1, local copies, waits for them, and re-layouts, per_device(): jnp.pad(trans_table, ((0, 0), (0, 0), (0, pad_dirs))).reshape(-1, lanes)  2.31 us
  transfers between devices with their start and end apart: 8, of which 3 were waited for; matrix products, arithmetic and copies ran while one was open for 15% of the time, Pallas kernels for 1%

profile of v12, /device:TPU:11, one launch (start us, length us, event | category | flops | bytes accessed | tf_op | source)
XLA Modules:
  0.0 89.8 jit_solution(5858705573077909375)
XLA Ops:
  0.0 1.2 %copy-done.1 = f32[64,2,4,512]{3,2,1,0:T(4,128)S(1)} copy-done((f32[64,2,4,512]{3,2,1,0:T(4,128)S(1)}, f32[64,2,4,512]{3,2,1,0:T(4,128)}, u32[]{:S(2)}) %copy-start.1) | copy-done | bytes 1048600
  1.9 2.3 %collective-permute-start.1 = (f32[512,128]{1,0:T(8,128)S(1)}, f32[512,128]{1,0:T(8,128)S(1)}, u32[]{:S(2)}, u32[]{:S(2)}) collective-permute-start(f32[512,128]{1,0:T(8,128)S(1)} %get-tuple-element.26), channel_id=1, source_target_pairs={{0,16},{8,24},{16,0},{24,8},{1,17},{9,25},{17,1},{25,9},{2,18},{10... | collective-permute-start | bytes 786440 | tf_op jit(solution)/shard_map/ppermute | solution.py:317
  4.4 1.2 %collective-permute-start.3 = (f32[16,2,4,512]{3,2,1,0:T(4,128)S(1)}, f32[16,2,4,512]{3,2,1,0:T(4,128)S(1)}, u32[]{:S(2)}, u32[]{:S(2)}) collective-permute-start(f32[16,2,4,512]{3,2,1,0:T(4,128)S(1)} %get-tuple-element.28), channel_id=1, source_target_pairs={{0,4},{4,0},{1,5},{5,1},{2,6},{6,2},{3,7},{7,3},{8,12},{12,8},{9,1... | collective-permute-start | bytes 786440 | tf_op jit(solution)/shard_map/ppermute | solution.py:312
  5.6 0.5 fusion.38
  6.2 0.9 %convert_reduce_fusion.1 = s32[64]{0:T(128)S(1)} fusion(s32[64]{0:T(128)} %param.14), kind=kLoop, calls=%fused_computation.23 | loop fusion | flops 28608 | bytes 512 | tf_op jit(solution)/shard_map/reduce_sum | solution.py:344
  7.2 0.8 select_reduce_fusion.1
  8.1 0.8 select_reduce_fusion.2
  9.2 0.7 convert_bitcast_fusion
  9.9 0.8 fusion.17
  11.3 0.8 pack_sources.3
  12.1 0.7 dynamic-slice_bitcast_fusion
  12.9 1.2 %collective-permute-start.4 = (f32[176,128]{1,0:T(8,128)}, f32[176,128]{1,0:T(8,128)S(1)}, u32[]{:S(2)}, u32[]{:S(2)}) collective-permute-start(f32[176,128]{1,0:T(8,128)} %get-tuple-element.34), channel_id=1, source_target_pairs={{0,8},{8,0},{16,24},{24,16},{1,9},{9,1},{17,25},{25,17},{2,10},{10... | collective-permute-start | bytes 270344 | tf_op jit(solution)/shard_map/ppermute | solution.py:317
  14.0 2.2 %collective-permute-start.5 = (f32[176,128]{1,0:T(8,128)}, f32[176,128]{1,0:T(8,128)S(1)}, u32[]{:S(2)}, u32[]{:S(2)}) collective-permute-start(f32[176,128]{1,0:T(8,128)} %get-tuple-element.35), channel_id=1, source_target_pairs={{0,16},{8,24},{16,0},{24,8},{1,17},{9,25},{17,1},{25,9},{2,18},{10... | collective-permute-start | bytes 270344 | tf_op jit(solution)/shard_map/ppermute | solution.py:317
  16.2 1.3 %select_add_fusion = f32[4,512]{0,1:T(8,128)} fusion(f32[512]{0:T(512)S(1)} %bitcast.51, f32[512]{0:T(512)S(1)} %bitcast.53, f32[512]{0:T(512)S(1)} %bitcast.55, f32[512]{0:T(512)S(1)} %bitcast.49, s32[4]{0:T(128)S(1)} %and_select_fusion, s32[512]{0:T(512)S(1)} %bitcast.43, s32[512]{0:T(512)S(1)} %bitcast.45, s32[512]{0:T(512)S(1)} %bitcast.47, ...), kind=kLoop, calls=%fused_computation.7 | loop fusion | flops 22528 | bytes 24592 | tf_op jit(solution)/shard_map/add | solution.py:434
  17.6 1.3 %select_add_fusion.1 = f32[128,512]{0,1:T(8,128)} fusion(f32[512]{0:T(512)S(1)} %bitcast.52, f32[512]{0:T(512)S(1)} %bitcast.54, f32[512]{0:T(512)S(1)} %bitcast.56, f32[512]{0:T(512)S(1)} %bitcast.50, s32[128]{0:T(128)S(1)} %iota_add_fusion.2, s32[512]{0:T(512)S(1)} %bitcast.44, s32[512]{0:T(512)S(1)} %bitcast.46, s32[512]{0:T(512)S(1)} %bitcast.48, ...), kind=kLoop, calls=%fused_computation.8 | loop fusion | flops 720896 | bytes 279040 | tf_op jit(solution)/shard_map/add | solution.py:434
  18.9 2.3 %reshape.197.refs_9_ = f32[2528,128]{1,0:T(8,128)S(1)} reshape(f32[316,2,512]{2,1,0:T(2,128)} %param.11) | data formatting | bytes 2588672 | tf_op jit(solution)/shard_map/reshape | solution.py:412
  21.2 0.9 %cosine_multiply_fusion = (f32[1,512]{1,0:T(1,128)S(1)}, f32[1,512]{1,0:T(1,128)S(1)}, f32[1,512]{1,0:T(1,128)S(1)}) fusion(f32[2,2048]{1,0:T(2,128)} %param.17, s32[]{:T(128)S(6)} %add.225, s32[]{:T(128)S(6)} %select_n.165), kind=kLoop, calls=%fused_computation.109 | loop fusion | flops 1024 | bytes 10248 | tf_op jit(solution)/shard_map/mul | solution.py:418
  22.1 1.1 %fusion = (bf16[512,256]{1,0:T(8,128)(2,1)S(1)}, bf16[512,256]{1,0:T(8,128)(2,1)S(1)}) fusion(f32[4,512]{0,1:T(8,128)} %select_add_fusion, f32[128,512]{0,1:T(8,128)} %select_add_fusion.1), kind=kLoop, calls=%fused_computation.3 | loop fusion | flops 917504 | bytes 794624 | tf_op jit(solution)/shard_map/convert_element_type | solution.py:449
  24.1 7.7 %collective-permute-done.5.refs_6_ = f32[176,128]{1,0:T(8,128)S(1)} collective-permute-done((f32[176,128]{1,0:T(8,128)}, f32[176,128]{1,0:T(8,128)S(1)}, u32[]{:S(2)}, u32[]{:S(2)}) %collective-permute-start.5) | collective-permute-done | bytes 90144 | tf_op jit(solution)/shard_map/ppermute | solution.py:317
  31.7 2.4 %collective-permute-done.6.refs_7_ = f32[176,128]{1,0:T(8,128)S(1)} collective-permute-done((f32[176,128]{1,0:T(8,128)S(1)}, f32[176,128]{1,0:T(8,128)S(1)}, u32[]{:S(2)}, u32[]{:S(2)}) %collective-permute-start.6) | collective-permute-done | bytes 90144 | tf_op jit(solution)/shard_map/ppermute | solution.py:317
  34.2 20.7 %translate_and_interpolate.1 = (f32[4,4,136,128]{3,2,1,0:T(8,128)}, f32[8,128]{1,0:T(8,128)S(1)}) custom-call(s32[1]{0:T(128)} %bitcast.zed, f32[512,128]{1,0:T(8,128)S(1)} %get-tuple-element.24.refs_0_, f32[512,128]{1,0:T(8,128)S(1)} %collective-permute-done.refs_1_, f32[512,128]{1,0:T(8,128)S(1)} %collective-permute-done.1.refs_2_, ...), custom_call_target="tpu_custom_call" | custom-call | tf_op jit(solution)/shard_map/translate_and_interpolate/pallas_call | solution.py:454
  54.9 7.0 %all-to-all-start = ((f32[16,136,128]{2,1,0:T(8,128)}), f32[16,136,128]{2,1,0:T(8,128)S(1)}, u32[]{:S(2)}, u32[]{:S(2)}) async-start(f32[16,136,128]{2,1,0:T(8,128)} %bitcast.40), calls=%async_computation | async-start | bytes 2228224 | tf_op jit(solution)/shard_map/all_to_all | solution.py:479
  61.9 26.3 %all-to-all-done.parts = f32[16,136,128]{2,1,0:T(8,128)S(1)} async-done(((f32[16,136,128]{2,1,0:T(8,128)}), f32[16,136,128]{2,1,0:T(8,128)S(1)}, u32[]{:S(2)}, u32[]{:S(2)}) %all-to-all-start) | async-done | bytes 1114144 | tf_op jit(solution)/shard_map/all_to_all | solution.py:479
  88.3 1.5 %join_parts.1 = f32[64,2,4,512]{3,2,1,0:T(4,128)} custom-call(f32[16,136,128]{2,1,0:T(8,128)S(1)} %all-to-all-done.parts, f32[1,128]{1,0:T(1,128)S(1)} %slice_subtract_fusion.rims), custom_call_target="tpu_custom_call" | custom-call | tf_op jit(solution)/shard_map/join_parts/pallas_call | solution.py:488
  (49 shorter events, 2.7 us)
Async XLA Ops:
  0.0 12.1 %copy-start = (s32[2048,4]{0,1:T(4,128)S(1)}, s32[2048,4]{0,1:T(4,128)}, u32[]{:S(2)}) copy-start(s32[2048,4]{0,1:T(4,128)} %param.18) | copy-start | bytes 98308
  0.0 1.2 %copy-start.1 = (f32[64,2,4,512]{3,2,1,0:T(4,128)S(1)}, f32[64,2,4,512]{3,2,1,0:T(4,128)}, u32[]{:S(2)}) copy-start(f32[64,2,4,512]{3,2,1,0:T(4,128)} %field.1) | copy-start | bytes 3145732
  1.6 32.6 %collective-permute-start = (f32[512,128]{1,0:T(8,128)S(1)}, f32[512,128]{1,0:T(8,128)S(1)}, u32[]{:S(2)}, u32[]{:S(2)}) collective-permute-start(f32[512,128]{1,0:T(8,128)S(1)} %get-tuple-element.25), channel_id=1, source_target_pairs={{0,8},{8,0},{16,24},{24,16},{1,9},{9,1},{17,25},{25,17},{2,10},{10... | collective-permute-start | bytes 786440 | tf_op jit(solution)/shard_map/ppermute | solution.py:317
  1.9 32.3 %collective-permute-start.1 = (f32[512,128]{1,0:T(8,128)S(1)}, f32[512,128]{1,0:T(8,128)S(1)}, u32[]{:S(2)}, u32[]{:S(2)}) collective-permute-start(f32[512,128]{1,0:T(8,128)S(1)} %get-tuple-element.26), channel_id=1, source_target_pairs={{0,16},{8,24},{16,0},{24,8},{1,17},{9,25},{17,1},{25,9},{2,18},{10... | collective-permute-start | bytes 786440 | tf_op jit(solution)/shard_map/ppermute | solution.py:317
  4.2 30.0 %collective-permute-start.2 = (f32[512,128]{1,0:T(8,128)S(1)}, f32[512,128]{1,0:T(8,128)S(1)}, u32[]{:S(2)}, u32[]{:S(2)}) collective-permute-start(f32[512,128]{1,0:T(8,128)S(1)} %get-tuple-element.27), channel_id=1, source_target_pairs={{0,24},{8,16},{16,8},{24,0},{1,25},{9,17},{17,9},{25,1},{2,26},{10... | collective-permute-start | bytes 786440 | tf_op jit(solution)/shard_map/ppermute | solution.py:317
  4.4 7.0 %collective-permute-start.3 = (f32[16,2,4,512]{3,2,1,0:T(4,128)S(1)}, f32[16,2,4,512]{3,2,1,0:T(4,128)S(1)}, u32[]{:S(2)}, u32[]{:S(2)}) collective-permute-start(f32[16,2,4,512]{3,2,1,0:T(4,128)S(1)} %get-tuple-element.28), channel_id=1, source_target_pairs={{0,4},{4,0},{1,5},{5,1},{2,6},{6,2},{3,7},{7,3},{8,12},{12,8},{9,1... | collective-permute-start | bytes 786440 | tf_op jit(solution)/shard_map/ppermute | solution.py:312
  12.9 10.7 %collective-permute-start.4 = (f32[176,128]{1,0:T(8,128)}, f32[176,128]{1,0:T(8,128)S(1)}, u32[]{:S(2)}, u32[]{:S(2)}) collective-permute-start(f32[176,128]{1,0:T(8,128)} %get-tuple-element.34), channel_id=1, source_target_pairs={{0,8},{8,0},{16,24},{24,16},{1,9},{9,1},{17,25},{25,17},{2,10},{10... | collective-permute-start | bytes 270344 | tf_op jit(solution)/shard_map/ppermute | solution.py:317
  14.0 17.7 %collective-permute-start.5 = (f32[176,128]{1,0:T(8,128)}, f32[176,128]{1,0:T(8,128)S(1)}, u32[]{:S(2)}, u32[]{:S(2)}) collective-permute-start(f32[176,128]{1,0:T(8,128)} %get-tuple-element.35), channel_id=1, source_target_pairs={{0,16},{8,24},{16,0},{24,8},{1,17},{9,25},{17,1},{25,9},{2,18},{10... | collective-permute-start | bytes 270344 | tf_op jit(solution)/shard_map/ppermute | solution.py:317
  21.2 2.1 %copy-start.2 = (f32[8]{0:T(128)S(1)}, f32[8]{0:T(128)}, u32[]{:S(2)}) copy-start(f32[8]{0:T(128)} %get-tuple-element.62) | copy-start | bytes 100
  23.6 10.6 %collective-permute-start.6 = (f32[176,128]{1,0:T(8,128)S(1)}, f32[176,128]{1,0:T(8,128)S(1)}, u32[]{:S(2)}, u32[]{:S(2)}) collective-permute-start(f32[176,128]{1,0:T(8,128)S(1)} %get-tuple-element.36), channel_id=1, source_target_pairs={{0,24},{8,16},{16,8},{24,0},{1,25},{9,17},{17,9},{25,1},{2,26},{10... | collective-permute-start | bytes 270344 | tf_op jit(solution)/shard_map/ppermute | solution.py:317
  54.9 33.4 %all-to-all-start = ((f32[16,136,128]{2,1,0:T(8,128)}), f32[16,136,128]{2,1,0:T(8,128)S(1)}, u32[]{:S(2)}, u32[]{:S(2)}) async-start(f32[16,136,128]{2,1,0:T(8,128)} %bitcast.40), calls=%async_computation | async-start | bytes 2228224 | tf_op jit(solution)/shard_map/all_to_all | solution.py:479

commit v13 on v12

--- a/solution.py
+++ b/solution.py
@@ -15,7 +15,6 @@
 half = 4
 rim = 2
 word_bits = 13
-grain = 32
 
 
 plan_fields = ["rows", "slots", "fine_rows", "stride", "width", "parent", "order", "turns"]
@@ -108,7 +107,7 @@
     mains, refs = refs[:planes], refs[planes:]
     edges = refs[: planes if edge_size else 0]
     lists, refs = refs[len(edges)], refs[len(edges) + 1 :]
-    table, phases, weights, out, rims, meta, field, moved, shifted, left, ready, landed, sems = refs
+    table, phases, weights, out, rims, meta, field, moved, shifted, ready, landed, sems = refs
     rows, fine_rows = plan.rows, plan.fine_rows
     own = zed[0]
 
@@ -130,8 +129,8 @@
     def with_turned(value):
         return jnp.concatenate([value, pltpu.roll(value, half, 0)], axis=0)
 
-    for step, main in enumerate(mains):
-        first = (own ^ step) * size
+    for index, main in enumerate(mains):
+        first = (own ^ (planes - 1 - index)) * size
 
         def main_step(row, unused, first=first, main=main):
             field[both((first + row) * 4 * half), :] = with_turned(main[tile(row * 2 * half), :])
@@ -202,22 +201,22 @@
 
         lax.fori_loop(0, fine_rows // lanes, fine_step, 0)
         width = ready.shape[3]
-        depth = half * lanes
-
-        def split_step(chunk, unused):
-            for part in range(2):
-                rows_of = pl.ds(pl.multiple_of(part * fine_rows + chunk * grain, grain), grain)
-                for block in range(half):
-                    begin = chunk * grain * 2 * half + part * half + block
-                    value = shifted[pl.ds(begin, grain, stride=2 * half), :]
-                    high, low = split(value)
-                    left[rows_of, block * lanes : (block + 1) * lanes] = high
-                    left[rows_of, depth + block * lanes : depth + (block + 1) * lanes] = low
-            return unused
-
-        lax.fori_loop(0, fine_rows // grain, split_step, 0, unroll=2)
+        left = jnp.concatenate(
+            [
+                jnp.concatenate(
+                    [
+                        shifted[pl.ds(part * half + block, fine_rows, stride=2 * half), :]
+                        for block in range(half)
+                    ],
+                    axis=1,
+                )
+                for part in range(2)
+            ],
+            axis=0,
+        )
+        first, second = split(left)
         result = jnp.dot(
-            jnp.concatenate([left[:, :depth], left[...]], axis=1), weights[...], preferred_element_type=jnp.float32
+            jnp.concatenate([first, first, second], axis=1), weights[...], preferred_element_type=jnp.float32
         )
         for part in range(2):
             for dest in range(dest_count):
@@ -316,7 +315,7 @@
             return note
         return lax.ppermute(note, "zed", [(plane, plane ^ step) for plane in range(planes)])
 
-    arrived = [to_planes(packed[step], step) for step in (3, 2, 1, 0)][::-1]
+    arrived = [to_planes(packed[step], step) for step in (3, 2, 1, 0)]
 
     plane_of = partner_ids // (ring_count * rows)
     ring_of = partner_ids // rows % ring_count
@@ -336,7 +335,7 @@
     place = jnp.where(live, place, field_rows)
     together = 4
     fixed = slots // 2
-    group = 5 if (slots - fixed) % 5 == 0 else 1
+    group = 3 if (slots - fixed) % 3 == 0 else 1
     index = jnp.arange(rows, dtype=jnp.int32)
     before = (partner_count[None, :] > partner_count[:, None]) | (
         (partner_count[None, :] == partner_count[:, None]) & (index[None, :] < index[:, None])
@@ -447,7 +446,7 @@
     rounded = lax.reduce_precision(matrices, 8, 7)
     high = rounded.astype(jnp.bfloat16)
     low = (matrices - rounded).astype(jnp.bfloat16)
-    passes = jnp.concatenate([low, high, high], axis=0)
+    passes = jnp.concatenate([high, low, high], axis=0)
 
     whole = pl.BlockSpec(memory_space=pltpu.VMEM)
     message = (2 * dest_rows + 2 * half, kf_pad)
@@ -467,12 +466,11 @@
             pltpu.VMEM(((field_rows + 1) * 4 * half, lanes), jnp.float32),
             pltpu.VMEM((rows * 4 * half, lanes), jnp.float32),
             pltpu.VMEM((fine_rows * 2 * half, lanes), jnp.float32),
-            pltpu.VMEM((2 * fine_rows, 2 * kc_pad), jnp.bfloat16),
             pltpu.VMEM((planes, dir_count) + message, jnp.float32),
             pltpu.VMEM((planes, max(edge_rows, 1) * 2 * half, lanes), jnp.float32),
             pltpu.SemaphoreType.DMA((2 * planes + 2,)),
         ],
-        compiler_params=pltpu.CompilerParams(vmem_limit_bytes=48 * 2**20),
+        compiler_params=pltpu.CompilerParams(vmem_limit_bytes=24 * 2**20),
         name="translate_and_interpolate",
     )(here[0], *arrived, *received, meta, table, phases, passes)
 

time: 90.3 us -> 87.8 us (0.972)
  Pallas kernels: 23.4 us -> 22.2 us
  starting transfers between devices: 14.8 us -> 13.8 us
    pallas_call x1, Pallas kernels: 20.7 us -> 19.4 us  [per_device(): pl.pallas_call(functools.partial(fine_kernel, plan, size, edge_rows), out...]
  transfers between devices with their start and end apart: 8 -> 8, of which waited for: 3 -> 4; matrix products, arithmetic and copies ran while one was open for 15% -> 16% of each run, Pallas kernels for 1% -> 1%
where the time goes in v13:
time: 87.8 us; the launch traced here: 87.3 us
  waiting for transfers between devices  36.1 us (41%)
  Pallas kernels  22.2 us (25%)
  starting transfers between devices  13.8 us (16%)
  other arithmetic  10.2 us (12%)
  local copies, waits for them, and re-layouts  4.6 us (5%)
    all_to_all x1, waiting for transfers between devices, per_device(): lax.all_to_all(local_fine.reshape((planes * dir_count,) + message), ('zed...  26.3 us
    pallas_call x1, Pallas kernels, per_device(): pl.pallas_call(functools.partial(fine_kernel, plan, size, edge_rows), out...  19.4 us
    ppermute x6, waiting for transfers between devices, to_planes(): lax.ppermute(note, 'zed', [(plane, plane ^ step) for plane in range(plane...  9.77 us
    all_to_all x1, starting transfers between devices, per_device(): lax.all_to_all(local_fine.reshape((planes * dir_count,) + message), ('zed...  6.54 us
    ppermute x6, starting transfers between devices, to_planes(): lax.ppermute(note, 'zed', [(plane, plane ^ step) for plane in range(plane...  6.07 us
    add x2, other arithmetic, interp(): matrix + jnp.where(ids[point][None, :] == targets[:, None], weights[point...  2.69 us
    reshape x1, local copies, waits for them, and re-layouts, per_device(): jnp.pad(trans_table, ((0, 0), (0, 0), (0, pad_dirs))).reshape(-1, lanes)  2.31 us
  transfers between devices with their start and end apart: 8, of which 4 were waited for; matrix products, arithmetic and copies ran while one was open for 16% of the time, Pallas kernels for 1%

profile of v13, /device:TPU:11, one launch (start us, length us, event | category | flops | bytes accessed | tf_op | source)
XLA Modules:
  0.0 87.3 jit_solution(6722228824423615148)
XLA Ops:
  0.0 1.2 %copy-done.1 = f32[64,2,4,512]{3,2,1,0:T(4,128)S(1)} copy-done((f32[64,2,4,512]{3,2,1,0:T(4,128)S(1)}, f32[64,2,4,512]{3,2,1,0:T(4,128)}, u32[]{:S(2)}) %copy-start.1) | copy-done | bytes 1048600
  1.6 1.4 %collective-permute-start = (f32[512,128]{1,0:T(8,128)S(1)}, f32[512,128]{1,0:T(8,128)S(1)}, u32[]{:S(2)}, u32[]{:S(2)}) collective-permute-start(f32[512,128]{1,0:T(8,128)S(1)} %get-tuple-element.24), channel_id=1, source_target_pairs={{0,24},{8,16},{16,8},{24,0},{1,25},{9,17},{17,9},{25,1},{2,26},{10... | collective-permute-start | bytes 786440 | tf_op jit(solution)/shard_map/ppermute | solution.py:316
  3.0 1.1 %collective-permute-start.1 = (f32[512,128]{1,0:T(8,128)S(1)}, f32[512,128]{1,0:T(8,128)S(1)}, u32[]{:S(2)}, u32[]{:S(2)}) collective-permute-start(f32[512,128]{1,0:T(8,128)S(1)} %get-tuple-element.25), channel_id=1, source_target_pairs={{0,16},{8,24},{16,0},{24,8},{1,17},{9,25},{17,1},{25,9},{2,18},{10... | collective-permute-start | bytes 786440 | tf_op jit(solution)/shard_map/ppermute | solution.py:316
  4.1 1.1 %collective-permute-start.2 = (f32[512,128]{1,0:T(8,128)S(1)}, f32[512,128]{1,0:T(8,128)S(1)}, u32[]{:S(2)}, u32[]{:S(2)}) collective-permute-start(f32[512,128]{1,0:T(8,128)S(1)} %get-tuple-element.26), channel_id=1, source_target_pairs={{0,8},{8,0},{16,24},{24,16},{1,9},{9,1},{17,25},{25,17},{2,10},{10... | collective-permute-start | bytes 786440 | tf_op jit(solution)/shard_map/ppermute | solution.py:316
  5.2 1.2 %collective-permute-start.3 = (f32[16,2,4,512]{3,2,1,0:T(4,128)S(1)}, f32[16,2,4,512]{3,2,1,0:T(4,128)S(1)}, u32[]{:S(2)}, u32[]{:S(2)}) collective-permute-start(f32[16,2,4,512]{3,2,1,0:T(4,128)S(1)} %get-tuple-element.28), channel_id=1, source_target_pairs={{0,4},{4,0},{1,5},{5,1},{2,6},{6,2},{3,7},{7,3},{8,12},{12,8},{9,1... | collective-permute-start | bytes 786440 | tf_op jit(solution)/shard_map/ppermute | solution.py:311
  7.0 0.9 %convert_reduce_fusion.1 = s32[64]{0:T(128)S(1)} fusion(s32[64]{0:T(128)} %param.14), kind=kLoop, calls=%fused_computation.23 | loop fusion | flops 28608 | bytes 512 | tf_op jit(solution)/shard_map/reduce_sum | solution.py:343
  8.0 0.8 select_reduce_fusion.1
  9.0 0.8 select_reduce_fusion.2
  10.0 0.7 convert_bitcast_fusion
  10.7 0.8 fusion.17
  12.2 0.8 pack_sources.3
  13.0 0.7 dynamic-slice_bitcast_fusion
  14.1 2.1 %collective-permute-start.5 = (f32[176,128]{1,0:T(8,128)}, f32[176,128]{1,0:T(8,128)S(1)}, u32[]{:S(2)}, u32[]{:S(2)}) collective-permute-start(f32[176,128]{1,0:T(8,128)} %get-tuple-element.35), channel_id=1, source_target_pairs={{0,16},{8,24},{16,0},{24,8},{1,17},{9,25},{17,1},{25,9},{2,18},{10... | collective-permute-start | bytes 270344 | tf_op jit(solution)/shard_map/ppermute | solution.py:316
  16.2 1.3 %select_add_fusion = f32[4,512]{0,1:T(8,128)} fusion(f32[512]{0:T(512)S(1)} %bitcast.51, f32[512]{0:T(512)S(1)} %bitcast.53, f32[512]{0:T(512)S(1)} %bitcast.55, f32[512]{0:T(512)S(1)} %bitcast.49, s32[4]{0:T(128)S(1)} %and_select_fusion, s32[512]{0:T(512)S(1)} %bitcast.43, s32[512]{0:T(512)S(1)} %bitcast.45, s32[512]{0:T(512)S(1)} %bitcast.47, ...), kind=kLoop, calls=%fused_computation.7 | loop fusion | flops 22528 | bytes 24592 | tf_op jit(solution)/shard_map/add | solution.py:433
  17.6 1.3 %select_add_fusion.1 = f32[128,512]{0,1:T(8,128)} fusion(f32[512]{0:T(512)S(1)} %bitcast.52, f32[512]{0:T(512)S(1)} %bitcast.54, f32[512]{0:T(512)S(1)} %bitcast.56, f32[512]{0:T(512)S(1)} %bitcast.50, s32[128]{0:T(128)S(1)} %iota_add_fusion.2, s32[512]{0:T(512)S(1)} %bitcast.44, s32[512]{0:T(512)S(1)} %bitcast.46, s32[512]{0:T(512)S(1)} %bitcast.48, ...), kind=kLoop, calls=%fused_computation.8 | loop fusion | flops 720896 | bytes 279040 | tf_op jit(solution)/shard_map/add | solution.py:433
  18.9 2.3 %reshape.197.refs_9_ = f32[2528,128]{1,0:T(8,128)S(1)} reshape(f32[316,2,512]{2,1,0:T(2,128)} %param.11) | data formatting | bytes 2588672 | tf_op jit(solution)/shard_map/reshape | solution.py:411
  21.2 0.9 %cosine_multiply_fusion = (f32[1,512]{1,0:T(1,128)S(1)}, f32[1,512]{1,0:T(1,128)S(1)}, f32[1,512]{1,0:T(1,128)S(1)}) fusion(f32[2,2048]{1,0:T(2,128)} %param.17, s32[]{:T(128)S(6)} %add.225, s32[]{:T(128)S(6)} %select_n.165), kind=kLoop, calls=%fused_computation.111 | loop fusion | flops 1024 | bytes 10248 | tf_op jit(solution)/shard_map/mul | solution.py:417
  22.1 1.1 %fusion = (bf16[512,256]{1,0:T(8,128)(2,1)S(1)}, bf16[512,256]{1,0:T(8,128)(2,1)S(1)}) fusion(f32[4,512]{0,1:T(8,128)} %select_add_fusion, f32[128,512]{0,1:T(8,128)} %select_add_fusion.1), kind=kLoop, calls=%fused_computation.3 | loop fusion | flops 917504 | bytes 794624 | tf_op jit(solution)/shard_map/convert_element_type | solution.py:448
  24.2 6.5 %collective-permute-done.5.refs_6_ = f32[176,128]{1,0:T(8,128)S(1)} collective-permute-done((f32[176,128]{1,0:T(8,128)}, f32[176,128]{1,0:T(8,128)S(1)}, u32[]{:S(2)}, u32[]{:S(2)}) %collective-permute-start.5) | collective-permute-done | bytes 90144 | tf_op jit(solution)/shard_map/ppermute | solution.py:316
  30.7 2.6 %collective-permute-done.6.refs_7_ = f32[176,128]{1,0:T(8,128)S(1)} collective-permute-done((f32[176,128]{1,0:T(8,128)S(1)}, f32[176,128]{1,0:T(8,128)S(1)}, u32[]{:S(2)}, u32[]{:S(2)}) %collective-permute-start.6) | collective-permute-done | bytes 90144 | tf_op jit(solution)/shard_map/ppermute | solution.py:316
  33.4 19.4 %translate_and_interpolate.1 = (f32[4,4,136,128]{3,2,1,0:T(8,128)}, f32[8,128]{1,0:T(8,128)S(1)}) custom-call(s32[1]{0:T(128)} %bitcast.zed, f32[512,128]{1,0:T(8,128)S(1)} %collective-permute-done.refs_0_, f32[512,128]{1,0:T(8,128)S(1)} %collective-permute-done.1.refs_1_, f32[512,128]{1,0:T(8,128)S(1)} %collective-permute-done.2.refs_2_, ...), custom_call_target="tpu_custom_call" | custom-call | tf_op jit(solution)/shard_map/translate_and_interpolate/pallas_call | solution.py:453
  52.9 6.5 %all-to-all-start = ((f32[16,136,128]{2,1,0:T(8,128)}), f32[16,136,128]{2,1,0:T(8,128)S(1)}, u32[]{:S(2)}, u32[]{:S(2)}) async-start(f32[16,136,128]{2,1,0:T(8,128)} %bitcast.40), calls=%async_computation | async-start | bytes 2228224 | tf_op jit(solution)/shard_map/all_to_all | solution.py:477
  59.4 26.3 %all-to-all-done.parts = f32[16,136,128]{2,1,0:T(8,128)S(1)} async-done(((f32[16,136,128]{2,1,0:T(8,128)}), f32[16,136,128]{2,1,0:T(8,128)S(1)}, u32[]{:S(2)}, u32[]{:S(2)}) %all-to-all-start) | async-done | bytes 1114144 | tf_op jit(solution)/shard_map/all_to_all | solution.py:477
  85.7 1.5 %join_parts.1 = f32[64,2,4,512]{3,2,1,0:T(4,128)} custom-call(f32[16,136,128]{2,1,0:T(8,128)S(1)} %all-to-all-done.parts, f32[1,128]{1,0:T(1,128)S(1)} %slice_subtract_fusion.rims), custom_call_target="tpu_custom_call" | custom-call | tf_op jit(solution)/shard_map/join_parts/pallas_call | solution.py:486
  (49 shorter events, 3.4 us)
Async XLA Ops:
  0.0 13.0 %copy-start = (s32[2048,4]{0,1:T(4,128)S(1)}, s32[2048,4]{0,1:T(4,128)}, u32[]{:S(2)}) copy-start(s32[2048,4]{0,1:T(4,128)} %param.18) | copy-start | bytes 98308
  0.0 1.2 %copy-start.1 = (f32[64,2,4,512]{3,2,1,0:T(4,128)S(1)}, f32[64,2,4,512]{3,2,1,0:T(4,128)}, u32[]{:S(2)}) copy-start(f32[64,2,4,512]{3,2,1,0:T(4,128)} %field.1) | copy-start | bytes 3145732
  1.6 31.7 %collective-permute-start = (f32[512,128]{1,0:T(8,128)S(1)}, f32[512,128]{1,0:T(8,128)S(1)}, u32[]{:S(2)}, u32[]{:S(2)}) collective-permute-start(f32[512,128]{1,0:T(8,128)S(1)} %get-tuple-element.24), channel_id=1, source_target_pairs={{0,24},{8,16},{16,8},{24,0},{1,25},{9,17},{17,9},{25,1},{2,26},{10... | collective-permute-start | bytes 786440 | tf_op jit(solution)/shard_map/ppermute | solution.py:316
  3.0 30.4 %collective-permute-start.1 = (f32[512,128]{1,0:T(8,128)S(1)}, f32[512,128]{1,0:T(8,128)S(1)}, u32[]{:S(2)}, u32[]{:S(2)}) collective-permute-start(f32[512,128]{1,0:T(8,128)S(1)} %get-tuple-element.25), channel_id=1, source_target_pairs={{0,16},{8,24},{16,0},{24,8},{1,17},{9,25},{17,1},{25,9},{2,18},{10... | collective-permute-start | bytes 786440 | tf_op jit(solution)/shard_map/ppermute | solution.py:316
  4.1 29.3 %collective-permute-start.2 = (f32[512,128]{1,0:T(8,128)S(1)}, f32[512,128]{1,0:T(8,128)S(1)}, u32[]{:S(2)}, u32[]{:S(2)}) collective-permute-start(f32[512,128]{1,0:T(8,128)S(1)} %get-tuple-element.26), channel_id=1, source_target_pairs={{0,8},{8,0},{16,24},{24,16},{1,9},{9,1},{17,25},{25,17},{2,10},{10... | collective-permute-start | bytes 786440 | tf_op jit(solution)/shard_map/ppermute | solution.py:316
  5.2 7.0 %collective-permute-start.3 = (f32[16,2,4,512]{3,2,1,0:T(4,128)S(1)}, f32[16,2,4,512]{3,2,1,0:T(4,128)S(1)}, u32[]{:S(2)}, u32[]{:S(2)}) collective-permute-start(f32[16,2,4,512]{3,2,1,0:T(4,128)S(1)} %get-tuple-element.28), channel_id=1, source_target_pairs={{0,4},{4,0},{1,5},{5,1},{2,6},{6,2},{3,7},{7,3},{8,12},{12,8},{9,1... | collective-permute-start | bytes 786440 | tf_op jit(solution)/shard_map/ppermute | solution.py:311
  13.7 10.5 %collective-permute-start.4 = (f32[176,128]{1,0:T(8,128)}, f32[176,128]{1,0:T(8,128)S(1)}, u32[]{:S(2)}, u32[]{:S(2)}) collective-permute-start(f32[176,128]{1,0:T(8,128)} %get-tuple-element.34), channel_id=1, source_target_pairs={{0,8},{8,0},{16,24},{24,16},{1,9},{9,1},{17,25},{25,17},{2,10},{10... | collective-permute-start | bytes 270344 | tf_op jit(solution)/shard_map/ppermute | solution.py:316
  14.1 16.6 %collective-permute-start.5 = (f32[176,128]{1,0:T(8,128)}, f32[176,128]{1,0:T(8,128)S(1)}, u32[]{:S(2)}, u32[]{:S(2)}) collective-permute-start(f32[176,128]{1,0:T(8,128)} %get-tuple-element.35), channel_id=1, source_target_pairs={{0,16},{8,24},{16,0},{24,8},{1,17},{9,25},{17,1},{25,9},{2,18},{10... | collective-permute-start | bytes 270344 | tf_op jit(solution)/shard_map/ppermute | solution.py:316
  21.2 2.1 %copy-start.2 = (f32[8]{0:T(128)S(1)}, f32[8]{0:T(128)}, u32[]{:S(2)}) copy-start(f32[8]{0:T(128)} %get-tuple-element.62) | copy-start | bytes 100
  24.2 9.1 %collective-permute-start.6 = (f32[176,128]{1,0:T(8,128)S(1)}, f32[176,128]{1,0:T(8,128)S(1)}, u32[]{:S(2)}, u32[]{:S(2)}) collective-permute-start(f32[176,128]{1,0:T(8,128)S(1)} %get-tuple-element.36), channel_id=1, source_target_pairs={{0,24},{8,16},{16,8},{24,0},{1,25},{9,17},{17,9},{25,1},{2,26},{10... | collective-permute-start | bytes 270344 | tf_op jit(solution)/shard_map/ppermute | solution.py:316
  52.9 32.9 %all-to-all-start = ((f32[16,136,128]{2,1,0:T(8,128)}), f32[16,136,128]{2,1,0:T(8,128)S(1)}, u32[]{:S(2)}, u32[]{:S(2)}) async-start(f32[16,136,128]{2,1,0:T(8,128)} %bitcast.40), calls=%async_computation | async-start | bytes 2228224 | tf_op jit(solution)/shard_map/all_to_all | solution.py:477

commit v14 on v13

--- a/solution.py
+++ b/solution.py
@@ -392,9 +392,11 @@
     )
 
     notes = pack(here, edges, [meta], 0) if edge_rows else [meta] * planes
-    after_notes = lax.optimization_barrier((notes, trans_table, dir_angles, stencil_ids, stencil_weights))
-    notes, trans_table, dir_angles, stencil_ids, stencil_weights = after_notes
     received = [to_planes(notes[step], step) for step in range(planes)]
+    near, trans_table, dir_angles, stencil_ids, stencil_weights = lax.optimization_barrier(
+        (received[1], trans_table, dir_angles, stencil_ids, stencil_weights)
+    )
+    received[1] = near
     edge_part = edge_rows * 2 * half
     numbers = jnp.stack([note[edge_part:] for note in received]).astype(jnp.int32)
     meta = numbers[:, :stride] * 2**word_bits + numbers[:, stride:]

time: 87.8 us -> 95.5 us (1.088)
  waiting for transfers between devices: 36.1 us -> 45 us
  other arithmetic: 10.2 us -> 9.03 us
    ppermute x6, waiting for transfers between devices: 9.77 us -> 18.5 us  [to_planes(): lax.ppermute(note, 'zed', [(plane, plane ^ step) for plane in range(plane...]
    add x2, other arithmetic: 2.69 us -> 1.21 us  [interp(): matrix + jnp.where(ids[point][None, :] == targets[:, None], weights[point...]
    concatenate x1, other arithmetic: 0.05 us -> 1.16 us  [per_device(): passes = jnp.concatenate([high, low, high], axis=0)]
  transfers between devices with their start and end apart: 8 -> 8, of which waited for: 4 -> 5; matrix products, arithmetic and copies ran while one was open for 16% -> 13% of each run, Pallas kernels for 1% -> 0%
where the time goes in v14:
time: 95.5 us; the launch traced here: 95.1 us
  waiting for transfers between devices  45 us (47%)
  Pallas kernels  22.4 us (23%)
  starting transfers between devices  13.7 us (14%)
  other arithmetic  9.03 us (9%)
  local copies, waits for them, and re-layouts  4.6 us (5%)
    all_to_all x1, waiting for transfers between devices, per_device(): lax.all_to_all(local_fine.reshape((planes * dir_count,) + message), ('zed...  26.3 us
    pallas_call x1, Pallas kernels, per_device(): pl.pallas_call(functools.partial(fine_kernel, plan, size, edge_rows), out...  19.6 us
    ppermute x6, waiting for transfers between devices, to_planes(): lax.ppermute(note, 'zed', [(plane, plane ^ step) for plane in range(plane...  18.5 us
    all_to_all x1, starting transfers between devices, per_device(): lax.all_to_all(local_fine.reshape((planes * dir_count,) + message), ('zed...  6.52 us
    ppermute x6, starting transfers between devices, to_planes(): lax.ppermute(note, 'zed', [(plane, plane ^ step) for plane in range(plane...  5.93 us
    reshape x1, local copies, waits for them, and re-layouts, per_device(): jnp.pad(trans_table, ((0, 0), (0, 0), (0, pad_dirs))).reshape(-1, lanes)  2.32 us
  transfers between devices with their start and end apart: 8, of which 5 were waited for; matrix products, arithmetic and copies ran while one was open for 13% of the time, Pallas kernels for 0%

profile of v14, /device:TPU:11, one launch (start us, length us, event | category | flops | bytes accessed | tf_op | source)
XLA Modules:
  0.0 95.1 jit_solution(6502235321806749287)
XLA Ops:
  0.0 1.2 %copy-done.1 = f32[64,2,4,512]{3,2,1,0:T(4,128)S(1)} copy-done((f32[64,2,4,512]{3,2,1,0:T(4,128)S(1)}, f32[64,2,4,512]{3,2,1,0:T(4,128)}, u32[]{:S(2)}) %copy-start.1) | copy-done | bytes 1048600
  1.2 1.1 %pack_sources.2 = (f32[512,128]{1,0:T(8,128)S(1)}, f32[512,128]{1,0:T(8,128)S(1)}, f32[512,128]{1,0:T(8,128)S(1)}, f32[512,128]{1,0:T(8,128)}, f32[16,2,4,512]{3,2,1,0:T(4,128)S(1)}) custom-call(s32[1]{0:T(128)} %bitcast.zed, s32[1]{0:T(128)} %bitcast.1.ring, f32[64,2,4,512]{3,2,1,0:T(4,128)S(1)} %copy-done.1), custom_call_target="tpu_custom_call" | custom-call | tf_op jit(solution)/shard_map/pack_sources/pallas_call | solution.py:87
  2.3 1.3 %collective-permute-start = (f32[512,128]{1,0:T(8,128)}, f32[512,128]{1,0:T(8,128)S(1)}, u32[]{:S(2)}, u32[]{:S(2)}) collective-permute-start(f32[512,128]{1,0:T(8,128)} %get-tuple-element.21), channel_id=1, source_target_pairs={{0,24},{8,16},{16,8},{24,0},{1,25},{9,17},{17,9},{25,1},{2,26},{10... | collective-permute-start | bytes 786440 | tf_op jit(solution)/shard_map/ppermute | solution.py:316
  3.6 1.0 %collective-permute-start.1 = (f32[512,128]{1,0:T(8,128)S(1)}, f32[512,128]{1,0:T(8,128)S(1)}, u32[]{:S(2)}, u32[]{:S(2)}) collective-permute-start(f32[512,128]{1,0:T(8,128)S(1)} %get-tuple-element.22), channel_id=1, source_target_pairs={{0,16},{8,24},{16,0},{24,8},{1,17},{9,25},{17,1},{25,9},{2,18},{10... | collective-permute-start | bytes 786440 | tf_op jit(solution)/shard_map/ppermute | solution.py:316
  4.7 1.2 %collective-permute-start.2 = (f32[512,128]{1,0:T(8,128)S(1)}, f32[512,128]{1,0:T(8,128)S(1)}, u32[]{:S(2)}, u32[]{:S(2)}) collective-permute-start(f32[512,128]{1,0:T(8,128)S(1)} %get-tuple-element.23), channel_id=1, source_target_pairs={{0,8},{8,0},{16,24},{24,16},{1,9},{9,1},{17,25},{25,17},{2,10},{10... | collective-permute-start | bytes 786440 | tf_op jit(solution)/shard_map/ppermute | solution.py:316
  5.8 1.2 %collective-permute-start.3 = (f32[16,2,4,512]{3,2,1,0:T(4,128)S(1)}, f32[16,2,4,512]{3,2,1,0:T(4,128)S(1)}, u32[]{:S(2)}, u32[]{:S(2)}) collective-permute-start(f32[16,2,4,512]{3,2,1,0:T(4,128)S(1)} %get-tuple-element.25), channel_id=1, source_target_pairs={{0,4},{4,0},{1,5},{5,1},{2,6},{6,2},{3,7},{7,3},{8,12},{12,8},{9,1... | collective-permute-start | bytes 786440 | tf_op jit(solution)/shard_map/ppermute | solution.py:311
  7.1 0.9 convert_reduce_fusion.1
  8.1 0.8 select_reduce_fusion.1
  9.0 0.8 select_reduce_fusion.2
  10.1 0.7 convert_bitcast_fusion
  10.8 0.8 fusion.17
  12.7 2.2 %collective-permute-start.5 = (f32[176,128]{1,0:T(8,128)S(1)}, f32[176,128]{1,0:T(8,128)S(1)}, u32[]{:S(2)}, u32[]{:S(2)}) collective-permute-start(f32[176,128]{1,0:T(8,128)S(1)} %get-tuple-element.29), channel_id=1, source_target_pairs={{0,16},{8,24},{16,0},{24,8},{1,17},{9,25},{17,1},{25,9},{2,18},{10... | collective-permute-start | bytes 270344 | tf_op jit(solution)/shard_map/ppermute | solution.py:316
  14.9 10.1 %collective-permute-done.4.refs_5_ = f32[176,128]{1,0:T(8,128)S(1)} collective-permute-done((f32[176,128]{1,0:T(8,128)S(1)}, f32[176,128]{1,0:T(8,128)S(1)}, u32[]{:S(2)}, u32[]{:S(2)}) %collective-permute-start.4) | collective-permute-done | bytes 90144 | tf_op jit(solution)/shard_map/ppermute | solution.py:316
  25.1 0.7 dynamic-slice_bitcast_fusion
  25.8 5.7 %collective-permute-done.5.refs_6_ = f32[176,128]{1,0:T(8,128)S(1)} collective-permute-done((f32[176,128]{1,0:T(8,128)S(1)}, f32[176,128]{1,0:T(8,128)S(1)}, u32[]{:S(2)}, u32[]{:S(2)}) %collective-permute-start.5) | collective-permute-done | bytes 90144 | tf_op jit(solution)/shard_map/ppermute | solution.py:316
  31.5 2.7 %collective-permute-done.6.refs_7_ = f32[176,128]{1,0:T(8,128)S(1)} collective-permute-done((f32[176,128]{1,0:T(8,128)S(1)}, f32[176,128]{1,0:T(8,128)S(1)}, u32[]{:S(2)}, u32[]{:S(2)}) %collective-permute-start.6) | collective-permute-done | bytes 90144 | tf_op jit(solution)/shard_map/ppermute | solution.py:316
  35.5 0.9 cosine_multiply_fusion
  36.4 0.9 fusion
  37.5 2.3 %reshape.197.refs_9_ = f32[2528,128]{1,0:T(8,128)S(1)} reshape(f32[316,2,512]{2,1,0:T(2,128)} %param.11) | data formatting | bytes 2588672 | tf_op jit(solution)/shard_map/reshape | solution.py:413
  39.8 1.2 %pad_maximum_fusion.refs_11_ = bf16[1536,256]{1,0:T(8,128)(2,1)S(1)} fusion(bf16[512,256]{1,0:T(8,128)(2,1)} %get-tuple-element.38, bf16[512,256]{1,0:T(8,128)(2,1)} %get-tuple-element.37), kind=kLoop, calls=%fused_computation | loop fusion | flops 2359296 | bytes 1310720 | tf_op jit(solution)/shard_map/concatenate | solution.py:451
  41.0 19.6 %translate_and_interpolate.1 = (f32[4,4,136,128]{3,2,1,0:T(8,128)}, f32[8,128]{1,0:T(8,128)S(1)}) custom-call(s32[1]{0:T(128)} %bitcast.zed, f32[512,128]{1,0:T(8,128)S(1)} %collective-permute-done.refs_0_, f32[512,128]{1,0:T(8,128)S(1)} %collective-permute-done.1.refs_1_, f32[512,128]{1,0:T(8,128)S(1)} %collective-permute-done.2.refs_2_, ...), custom_call_target="tpu_custom_call" | custom-call | tf_op jit(solution)/shard_map/translate_and_interpolate/pallas_call | solution.py:455
  60.6 6.5 %all-to-all-start = ((f32[16,136,128]{2,1,0:T(8,128)}), f32[16,136,128]{2,1,0:T(8,128)S(1)}, u32[]{:S(2)}, u32[]{:S(2)}) async-start(f32[16,136,128]{2,1,0:T(8,128)} %bitcast.40), calls=%async_computation | async-start | bytes 2228224 | tf_op jit(solution)/shard_map/all_to_all | solution.py:479
  67.2 26.3 %all-to-all-done.parts = f32[16,136,128]{2,1,0:T(8,128)S(1)} async-done(((f32[16,136,128]{2,1,0:T(8,128)}), f32[16,136,128]{2,1,0:T(8,128)S(1)}, u32[]{:S(2)}, u32[]{:S(2)}) %all-to-all-start) | async-done | bytes 1114144 | tf_op jit(solution)/shard_map/all_to_all | solution.py:479
  93.5 1.5 %join_parts.1 = f32[64,2,4,512]{3,2,1,0:T(4,128)} custom-call(f32[16,136,128]{2,1,0:T(8,128)S(1)} %all-to-all-done.parts, f32[1,128]{1,0:T(1,128)S(1)} %slice_subtract_fusion.rims), custom_call_target="tpu_custom_call" | custom-call | tf_op jit(solution)/shard_map/join_parts/pallas_call | solution.py:488
  (47 shorter events, 3.0 us)
Async XLA Ops:
  0.0 25.1 %copy-start = (s32[2048,4]{0,1:T(4,128)S(1)}, s32[2048,4]{0,1:T(4,128)}, u32[]{:S(2)}) copy-start(s32[2048,4]{0,1:T(4,128)} %param.18) | copy-start | bytes 98308
  0.0 1.2 %copy-start.1 = (f32[64,2,4,512]{3,2,1,0:T(4,128)S(1)}, f32[64,2,4,512]{3,2,1,0:T(4,128)}, u32[]{:S(2)}) copy-start(f32[64,2,4,512]{3,2,1,0:T(4,128)} %field.1) | copy-start | bytes 3145732
  2.3 38.7 %collective-permute-start = (f32[512,128]{1,0:T(8,128)}, f32[512,128]{1,0:T(8,128)S(1)}, u32[]{:S(2)}, u32[]{:S(2)}) collective-permute-start(f32[512,128]{1,0:T(8,128)} %get-tuple-element.21), channel_id=1, source_target_pairs={{0,24},{8,16},{16,8},{24,0},{1,25},{9,17},{17,9},{25,1},{2,26},{10... | collective-permute-start | bytes 786440 | tf_op jit(solution)/shard_map/ppermute | solution.py:316
  3.6 37.4 %collective-permute-start.1 = (f32[512,128]{1,0:T(8,128)S(1)}, f32[512,128]{1,0:T(8,128)S(1)}, u32[]{:S(2)}, u32[]{:S(2)}) collective-permute-start(f32[512,128]{1,0:T(8,128)S(1)} %get-tuple-element.22), channel_id=1, source_target_pairs={{0,16},{8,24},{16,0},{24,8},{1,17},{9,25},{17,1},{25,9},{2,18},{10... | collective-permute-start | bytes 786440 | tf_op jit(solution)/shard_map/ppermute | solution.py:316
  4.7 36.4 %collective-permute-start.2 = (f32[512,128]{1,0:T(8,128)S(1)}, f32[512,128]{1,0:T(8,128)S(1)}, u32[]{:S(2)}, u32[]{:S(2)}) collective-permute-start(f32[512,128]{1,0:T(8,128)S(1)} %get-tuple-element.23), channel_id=1, source_target_pairs={{0,8},{8,0},{16,24},{24,16},{1,9},{9,1},{17,25},{25,17},{2,10},{10... | collective-permute-start | bytes 786440 | tf_op jit(solution)/shard_map/ppermute | solution.py:316
  5.8 6.6 %collective-permute-start.3 = (f32[16,2,4,512]{3,2,1,0:T(4,128)S(1)}, f32[16,2,4,512]{3,2,1,0:T(4,128)S(1)}, u32[]{:S(2)}, u32[]{:S(2)}) collective-permute-start(f32[16,2,4,512]{3,2,1,0:T(4,128)S(1)} %get-tuple-element.25), channel_id=1, source_target_pairs={{0,4},{4,0},{1,5},{5,1},{2,6},{6,2},{3,7},{7,3},{8,12},{12,8},{9,1... | collective-permute-start | bytes 786440 | tf_op jit(solution)/shard_map/ppermute | solution.py:311
  12.5 12.6 %collective-permute-start.4 = (f32[176,128]{1,0:T(8,128)S(1)}, f32[176,128]{1,0:T(8,128)S(1)}, u32[]{:S(2)}, u32[]{:S(2)}) collective-permute-start(f32[176,128]{1,0:T(8,128)S(1)} %get-tuple-element.27), channel_id=1, source_target_pairs={{0,8},{8,0},{16,24},{24,16},{1,9},{9,1},{17,25},{25,17},{2,10},{10... | collective-permute-start | bytes 270344 | tf_op jit(solution)/shard_map/ppermute | solution.py:316
  12.7 18.7 %collective-permute-start.5 = (f32[176,128]{1,0:T(8,128)S(1)}, f32[176,128]{1,0:T(8,128)S(1)}, u32[]{:S(2)}, u32[]{:S(2)}) collective-permute-start(f32[176,128]{1,0:T(8,128)S(1)} %get-tuple-element.29), channel_id=1, source_target_pairs={{0,16},{8,24},{16,0},{24,8},{1,17},{9,25},{17,1},{25,9},{2,18},{10... | collective-permute-start | bytes 270344 | tf_op jit(solution)/shard_map/ppermute | solution.py:316
  25.1 9.1 %collective-permute-start.6 = (f32[176,128]{1,0:T(8,128)S(1)}, f32[176,128]{1,0:T(8,128)S(1)}, u32[]{:S(2)}, u32[]{:S(2)}) collective-permute-start(f32[176,128]{1,0:T(8,128)S(1)} %get-tuple-element.30), channel_id=1, source_target_pairs={{0,24},{8,16},{16,8},{24,0},{1,25},{9,17},{17,9},{25,1},{2,26},{10... | collective-permute-start | bytes 270344 | tf_op jit(solution)/shard_map/ppermute | solution.py:316
  60.6 32.9 %all-to-all-start = ((f32[16,136,128]{2,1,0:T(8,128)}), f32[16,136,128]{2,1,0:T(8,128)S(1)}, u32[]{:S(2)}, u32[]{:S(2)}) async-start(f32[16,136,128]{2,1,0:T(8,128)} %bitcast.40), calls=%async_computation | async-start | bytes 2228224 | tf_op jit(solution)/shard_map/all_to_all | solution.py:479

commit v15 on v13

--- a/solution.py
+++ b/solution.py
@@ -315,7 +315,7 @@
             return note
         return lax.ppermute(note, "zed", [(plane, plane ^ step) for plane in range(planes)])
 
-    arrived = [to_planes(packed[step], step) for step in (3, 2, 1, 0)]
+    arrived = [to_planes(packed[step], step) for step in (3, 2)]
 
     plane_of = partner_ids // (ring_count * rows)
     ring_of = partner_ids // rows % ring_count
@@ -392,9 +392,12 @@
     )
 
     notes = pack(here, edges, [meta], 0) if edge_rows else [meta] * planes
-    after_notes = lax.optimization_barrier((notes, trans_table, dir_angles, stencil_ids, stencil_weights))
-    notes, trans_table, dir_angles, stencil_ids, stencil_weights = after_notes
+    after_notes = lax.optimization_barrier(
+        (notes, packed[1], trans_table, dir_angles, stencil_ids, stencil_weights)
+    )
+    notes, near, trans_table, dir_angles, stencil_ids, stencil_weights = after_notes
     received = [to_planes(notes[step], step) for step in range(planes)]
+    arrived += [to_planes(near, 1), packed[0]]
     edge_part = edge_rows * 2 * half
     numbers = jnp.stack([note[edge_part:] for note in received]).astype(jnp.int32)
     meta = numbers[:, :stride] * 2**word_bits + numbers[:, stride:]

time: 87.8 us -> 91.9 us (1.047)
  waiting for transfers between devices: 36.1 us -> 38.7 us
  starting transfers between devices: 13.8 us -> 15.7 us
  Pallas kernels: 22.2 us -> 21.1 us
    ppermute x6, waiting for transfers between devices: 9.77 us -> 12.4 us  [to_planes(): lax.ppermute(note, 'zed', [(plane, plane ^ step) for plane in range(plane...]
    ppermute x6, starting transfers between devices: 6.07 us -> 7.23 us  [to_planes(): lax.ppermute(note, 'zed', [(plane, plane ^ step) for plane in range(plane...]
  transfers between devices with their start and end apart: 8 -> 8, of which waited for: 4 -> 4; matrix products, arithmetic and copies ran while one was open for 16% -> 16% of each run, Pallas kernels for 1% -> 0%
where the time goes in v15:
time: 91.9 us; the launch traced here: 91.4 us
  waiting for transfers between devices  38.7 us (42%)
  Pallas kernels  21.1 us (23%)
  starting transfers between devices  15.7 us (17%)
  other arithmetic  10.7 us (12%)
  local copies, waits for them, and re-layouts  4.62 us (5%)
    all_to_all x1, waiting for transfers between devices, per_device(): lax.all_to_all(local_fine.reshape((planes * dir_count,) + message), ('zed...  26.3 us
    pallas_call x1, Pallas kernels, per_device(): pl.pallas_call(functools.partial(fine_kernel, plan, size, edge_rows), out...  19 us
    ppermute x6, waiting for transfers between devices, to_planes(): lax.ppermute(note, 'zed', [(plane, plane ^ step) for plane in range(plane...  12.4 us
    all_to_all x1, starting transfers between devices, per_device(): lax.all_to_all(local_fine.reshape((planes * dir_count,) + message), ('zed...  7.26 us
    ppermute x6, starting transfers between devices, to_planes(): lax.ppermute(note, 'zed', [(plane, plane ^ step) for plane in range(plane...  7.23 us
    add x2, other arithmetic, interp(): matrix + jnp.where(ids[point][None, :] == targets[:, None], weights[point...  2.69 us
    reshape x1, local copies, waits for them, and re-layouts, per_device(): jnp.pad(trans_table, ((0, 0), (0, 0), (0, pad_dirs))).reshape(-1, lanes)  2.31 us
  transfers between devices with their start and end apart: 8, of which 4 were waited for; matrix products, arithmetic and copies ran while one was open for 16% of the time, Pallas kernels for 0%

profile of v15, /device:TPU:11, one launch (start us, length us, event | category | flops | bytes accessed | tf_op | source)
XLA Modules:
  0.0 91.4 jit_solution(14218938040676750076)
XLA Ops:
  0.0 1.2 %copy-done.1 = f32[64,2,4,512]{3,2,1,0:T(4,128)S(1)} copy-done((f32[64,2,4,512]{3,2,1,0:T(4,128)S(1)}, f32[64,2,4,512]{3,2,1,0:T(4,128)}, u32[]{:S(2)}) %copy-start.1) | copy-done | bytes 1048600
  1.6 1.4 %collective-permute-start = (f32[512,128]{1,0:T(8,128)S(1)}, f32[512,128]{1,0:T(8,128)S(1)}, u32[]{:S(2)}, u32[]{:S(2)}) collective-permute-start(f32[512,128]{1,0:T(8,128)S(1)} %get-tuple-element.25), channel_id=1, source_target_pairs={{0,24},{8,16},{16,8},{24,0},{1,25},{9,17},{17,9},{25,1},{2,26},{10... | collective-permute-start | bytes 786440 | tf_op jit(solution)/shard_map/ppermute | solution.py:316
  3.0 1.1 %collective-permute-start.1 = (f32[512,128]{1,0:T(8,128)S(1)}, f32[512,128]{1,0:T(8,128)S(1)}, u32[]{:S(2)}, u32[]{:S(2)}) collective-permute-start(f32[512,128]{1,0:T(8,128)S(1)} %get-tuple-element.26), channel_id=1, source_target_pairs={{0,16},{8,24},{16,0},{24,8},{1,17},{9,25},{17,1},{25,9},{2,18},{10... | collective-permute-start | bytes 786440 | tf_op jit(solution)/shard_map/ppermute | solution.py:316
  4.1 1.2 %collective-permute-start.2 = (f32[16,2,4,512]{3,2,1,0:T(4,128)S(1)}, f32[16,2,4,512]{3,2,1,0:T(4,128)S(1)}, u32[]{:S(2)}, u32[]{:S(2)}) collective-permute-start(f32[16,2,4,512]{3,2,1,0:T(4,128)S(1)} %get-tuple-element.27), channel_id=1, source_target_pairs={{0,4},{4,0},{1,5},{5,1},{2,6},{6,2},{3,7},{7,3},{8,12},{12,8},{9,1... | collective-permute-start | bytes 786440 | tf_op jit(solution)/shard_map/ppermute | solution.py:311
  6.5 0.9 convert_reduce_fusion.1
  7.5 0.8 select_reduce_fusion.1
  8.4 0.8 select_reduce_fusion.2
  10.2 0.8 fusion.17
  11.8 0.7 dynamic-slice_bitcast_fusion
  12.5 1.2 %collective-permute-start.4 = (f32[176,128]{1,0:T(8,128)S(1)}, f32[176,128]{1,0:T(8,128)S(1)}, u32[]{:S(2)}, u32[]{:S(2)}) collective-permute-start(f32[176,128]{1,0:T(8,128)S(1)} %get-tuple-element.36), channel_id=1, source_target_pairs={{0,8},{8,0},{16,24},{24,16},{1,9},{9,1},{17,25},{25,17},{2,10},{10... | collective-permute-start | bytes 270344 | tf_op jit(solution)/shard_map/ppermute | solution.py:316
  13.7 2.4 %collective-permute-start.5 = (f32[176,128]{1,0:T(8,128)S(1)}, f32[176,128]{1,0:T(8,128)S(1)}, u32[]{:S(2)}, u32[]{:S(2)}) collective-permute-start(f32[176,128]{1,0:T(8,128)S(1)} %get-tuple-element.37), channel_id=1, source_target_pairs={{0,16},{8,24},{16,0},{24,8},{1,17},{9,25},{17,1},{25,9},{2,18},{10... | collective-permute-start | bytes 270344 | tf_op jit(solution)/shard_map/ppermute | solution.py:316
  16.1 1.3 %select_add_fusion = f32[4,512]{0,1:T(8,128)} fusion(f32[512]{0:T(512)S(1)} %bitcast.51, f32[512]{0:T(512)S(1)} %bitcast.53, f32[512]{0:T(512)S(1)} %bitcast.55, f32[512]{0:T(512)S(1)} %bitcast.49, s32[4]{0:T(128)S(1)} %and_select_fusion, s32[512]{0:T(512)S(1)} %bitcast.43, s32[512]{0:T(512)S(1)} %bitcast.45, s32[512]{0:T(512)S(1)} %bitcast.47, ...), kind=kLoop, calls=%fused_computation.7 | loop fusion | flops 22528 | bytes 24592 | tf_op jit(solution)/shard_map/add | solution.py:436
  17.4 1.3 %select_add_fusion.1 = f32[128,512]{0,1:T(8,128)} fusion(f32[512]{0:T(512)S(1)} %bitcast.52, f32[512]{0:T(512)S(1)} %bitcast.54, f32[512]{0:T(512)S(1)} %bitcast.56, f32[512]{0:T(512)S(1)} %bitcast.50, s32[128]{0:T(128)S(1)} %iota_add_fusion.2, s32[512]{0:T(512)S(1)} %bitcast.44, s32[512]{0:T(512)S(1)} %bitcast.46, s32[512]{0:T(512)S(1)} %bitcast.48, ...), kind=kLoop, calls=%fused_computation.8 | loop fusion | flops 720896 | bytes 279040 | tf_op jit(solution)/shard_map/add | solution.py:436
  18.8 2.3 %reshape.197.refs_9_ = f32[2528,128]{1,0:T(8,128)S(1)} reshape(f32[316,2,512]{2,1,0:T(2,128)} %param.11) | data formatting | bytes 2588672 | tf_op jit(solution)/shard_map/reshape | solution.py:414
  21.1 0.9 %cosine_multiply_fusion = (f32[1,512]{1,0:T(1,128)S(1)}, f32[1,512]{1,0:T(1,128)S(1)}, f32[1,512]{1,0:T(1,128)S(1)}) fusion(f32[2,2048]{1,0:T(2,128)} %param.17, s32[]{:T(128)S(6)} %add.225, s32[]{:T(128)S(6)} %select_n.165), kind=kLoop, calls=%fused_computation.111 | loop fusion | flops 1024 | bytes 10248 | tf_op jit(solution)/shard_map/mul | solution.py:420
  22.0 1.1 %fusion = (bf16[512,256]{1,0:T(8,128)(2,1)S(1)}, bf16[512,256]{1,0:T(8,128)(2,1)S(1)}) fusion(f32[4,512]{0,1:T(8,128)} %select_add_fusion, f32[128,512]{0,1:T(8,128)} %select_add_fusion.1), kind=kLoop, calls=%fused_computation.3 | loop fusion | flops 917504 | bytes 794624 | tf_op jit(solution)/shard_map/convert_element_type | solution.py:451
  23.5 1.2 %collective-permute-start.3 = (f32[512,128]{1,0:T(8,128)S(1)}, f32[512,128]{1,0:T(8,128)S(1)}, u32[]{:S(2)}, u32[]{:S(2)}) collective-permute-start(f32[512,128]{1,0:T(8,128)S(1)} %get-tuple-element.33), channel_id=1, source_target_pairs={{0,8},{8,0},{16,24},{24,16},{1,9},{9,1},{17,25},{25,17},{2,10},{10... | collective-permute-start | bytes 786440 | tf_op jit(solution)/shard_map/ppermute | solution.py:316
  24.7 5.9 %collective-permute-done.5.refs_6_ = f32[176,128]{1,0:T(8,128)S(1)} collective-permute-done((f32[176,128]{1,0:T(8,128)S(1)}, f32[176,128]{1,0:T(8,128)S(1)}, u32[]{:S(2)}, u32[]{:S(2)}) %collective-permute-start.5) | collective-permute-done | bytes 90144 | tf_op jit(solution)/shard_map/ppermute | solution.py:316
  30.7 2.7 %collective-permute-done.6.refs_7_ = f32[176,128]{1,0:T(8,128)S(1)} collective-permute-done((f32[176,128]{1,0:T(8,128)S(1)}, f32[176,128]{1,0:T(8,128)S(1)}, u32[]{:S(2)}, u32[]{:S(2)}) %collective-permute-start.6) | collective-permute-done | bytes 90144 | tf_op jit(solution)/shard_map/ppermute | solution.py:316
  33.5 3.7 %collective-permute-done.3.refs_2_ = f32[512,128]{1,0:T(8,128)S(1)} collective-permute-done((f32[512,128]{1,0:T(8,128)S(1)}, f32[512,128]{1,0:T(8,128)S(1)}, u32[]{:S(2)}, u32[]{:S(2)}) %collective-permute-start.3) | collective-permute-done | bytes 262176 | tf_op jit(solution)/shard_map/ppermute | solution.py:316
  37.2 19.0 %translate_and_interpolate.1 = (f32[4,4,136,128]{3,2,1,0:T(8,128)}, f32[8,128]{1,0:T(8,128)S(1)}) custom-call(s32[1]{0:T(128)} %bitcast.zed, f32[512,128]{1,0:T(8,128)S(1)} %collective-permute-done.refs_0_, f32[512,128]{1,0:T(8,128)S(1)} %collective-permute-done.1.refs_1_, f32[512,128]{1,0:T(8,128)S(1)} %collective-permute-done.3.refs_2_, ...), custom_call_target="tpu_custom_call" | custom-call | tf_op jit(solution)/shard_map/translate_and_interpolate/pallas_call | solution.py:456
  56.2 7.3 %all-to-all-start = ((f32[16,136,128]{2,1,0:T(8,128)}), f32[16,136,128]{2,1,0:T(8,128)S(1)}, u32[]{:S(2)}, u32[]{:S(2)}) async-start(f32[16,136,128]{2,1,0:T(8,128)} %bitcast.40), calls=%async_computation | async-start | bytes 2228224 | tf_op jit(solution)/shard_map/all_to_all | solution.py:480
  63.5 26.3 %all-to-all-done.parts = f32[16,136,128]{2,1,0:T(8,128)S(1)} async-done(((f32[16,136,128]{2,1,0:T(8,128)}), f32[16,136,128]{2,1,0:T(8,128)S(1)}, u32[]{:S(2)}, u32[]{:S(2)}) %all-to-all-start) | async-done | bytes 1114144 | tf_op jit(solution)/shard_map/all_to_all | solution.py:480
  89.8 1.5 %join_parts.1 = f32[64,2,4,512]{3,2,1,0:T(4,128)} custom-call(f32[16,136,128]{2,1,0:T(8,128)S(1)} %all-to-all-done.parts, f32[1,128]{1,0:T(1,128)S(1)} %slice_subtract_fusion.rims), custom_call_target="tpu_custom_call" | custom-call | tf_op jit(solution)/shard_map/join_parts/pallas_call | solution.py:489
  (53 shorter events, 3.7 us)
Async XLA Ops:
  0.0 11.8 %copy-start = (s32[2048,4]{0,1:T(4,128)S(1)}, s32[2048,4]{0,1:T(4,128)}, u32[]{:S(2)}) copy-start(s32[2048,4]{0,1:T(4,128)} %param.18) | copy-start | bytes 98308
  0.0 1.2 %copy-start.1 = (f32[64,2,4,512]{3,2,1,0:T(4,128)S(1)}, f32[64,2,4,512]{3,2,1,0:T(4,128)}, u32[]{:S(2)}) copy-start(f32[64,2,4,512]{3,2,1,0:T(4,128)} %field.1) | copy-start | bytes 3145732
  1.6 31.8 %collective-permute-start = (f32[512,128]{1,0:T(8,128)S(1)}, f32[512,128]{1,0:T(8,128)S(1)}, u32[]{:S(2)}, u32[]{:S(2)}) collective-permute-start(f32[512,128]{1,0:T(8,128)S(1)} %get-tuple-element.25), channel_id=1, source_target_pairs={{0,24},{8,16},{16,8},{24,0},{1,25},{9,17},{17,9},{25,1},{2,26},{10... | collective-permute-start | bytes 786440 | tf_op jit(solution)/shard_map/ppermute | solution.py:316
  3.0 30.4 %collective-permute-start.1 = (f32[512,128]{1,0:T(8,128)S(1)}, f32[512,128]{1,0:T(8,128)S(1)}, u32[]{:S(2)}, u32[]{:S(2)}) collective-permute-start(f32[512,128]{1,0:T(8,128)S(1)} %get-tuple-element.26), channel_id=1, source_target_pairs={{0,16},{8,24},{16,0},{24,8},{1,17},{9,25},{17,1},{25,9},{2,18},{10... | collective-permute-start | bytes 786440 | tf_op jit(solution)/shard_map/ppermute | solution.py:316
  4.1 7.5 %collective-permute-start.2 = (f32[16,2,4,512]{3,2,1,0:T(4,128)S(1)}, f32[16,2,4,512]{3,2,1,0:T(4,128)S(1)}, u32[]{:S(2)}, u32[]{:S(2)}) collective-permute-start(f32[16,2,4,512]{3,2,1,0:T(4,128)S(1)} %get-tuple-element.27), channel_id=1, source_target_pairs={{0,4},{4,0},{1,5},{5,1},{2,6},{6,2},{3,7},{7,3},{8,12},{12,8},{9,1... | collective-permute-start | bytes 786440 | tf_op jit(solution)/shard_map/ppermute | solution.py:311
  12.5 11.0 %collective-permute-start.4 = (f32[176,128]{1,0:T(8,128)S(1)}, f32[176,128]{1,0:T(8,128)S(1)}, u32[]{:S(2)}, u32[]{:S(2)}) collective-permute-start(f32[176,128]{1,0:T(8,128)S(1)} %get-tuple-element.36), channel_id=1, source_target_pairs={{0,8},{8,0},{16,24},{24,16},{1,9},{9,1},{17,25},{25,17},{2,10},{10... | collective-permute-start | bytes 270344 | tf_op jit(solution)/shard_map/ppermute | solution.py:316
  13.7 17.0 %collective-permute-start.5 = (f32[176,128]{1,0:T(8,128)S(1)}, f32[176,128]{1,0:T(8,128)S(1)}, u32[]{:S(2)}, u32[]{:S(2)}) collective-permute-start(f32[176,128]{1,0:T(8,128)S(1)} %get-tuple-element.37), channel_id=1, source_target_pairs={{0,16},{8,24},{16,0},{24,8},{1,17},{9,25},{17,1},{25,9},{2,18},{10... | collective-permute-start | bytes 270344 | tf_op jit(solution)/shard_map/ppermute | solution.py:316
  16.1 17.3 %collective-permute-start.6 = (f32[176,128]{1,0:T(8,128)S(1)}, f32[176,128]{1,0:T(8,128)S(1)}, u32[]{:S(2)}, u32[]{:S(2)}) collective-permute-start(f32[176,128]{1,0:T(8,128)S(1)} %get-tuple-element.38), channel_id=1, source_target_pairs={{0,24},{8,16},{16,8},{24,0},{1,25},{9,17},{17,9},{25,1},{2,26},{10... | collective-permute-start | bytes 270344 | tf_op jit(solution)/shard_map/ppermute | solution.py:316
  21.1 2.1 %copy-start.2 = (f32[8]{0:T(128)S(1)}, f32[8]{0:T(128)}, u32[]{:S(2)}) copy-start(f32[8]{0:T(128)} %fusion.44) | copy-start | bytes 100
  21.1 2.1 %copy-start.3 = (f32[8]{0:T(128)S(1)}, f32[8]{0:T(128)}, u32[]{:S(2)}) copy-start(f32[8]{0:T(128)} %get-tuple-element.63) | copy-start | bytes 100
  21.1 2.1 %copy-start.4 = (f32[8]{0:T(128)S(1)}, f32[8]{0:T(128)}, u32[]{:S(2)}) copy-start(f32[8]{0:T(128)} %get-tuple-element.64) | copy-start | bytes 100
  23.5 13.7 %collective-permute-start.3 = (f32[512,128]{1,0:T(8,128)S(1)}, f32[512,128]{1,0:T(8,128)S(1)}, u32[]{:S(2)}, u32[]{:S(2)}) collective-permute-start(f32[512,128]{1,0:T(8,128)S(1)} %get-tuple-element.33), channel_id=1, source_target_pairs={{0,8},{8,0},{16,24},{24,16},{1,9},{9,1},{17,25},{25,17},{2,10},{10... | collective-permute-start | bytes 786440 | tf_op jit(solution)/shard_map/ppermute | solution.py:316
  56.2 33.6 %all-to-all-start = ((f32[16,136,128]{2,1,0:T(8,128)}), f32[16,136,128]{2,1,0:T(8,128)S(1)}, u32[]{:S(2)}, u32[]{:S(2)}) async-start(f32[16,136,128]{2,1,0:T(8,128)} %bitcast.40), calls=%async_computation | async-start | bytes 2228224 | tf_op jit(solution)/shard_map/all_to_all | solution.py:480

commit v16 on v13

--- a/solution.py
+++ b/solution.py
@@ -89,7 +89,7 @@
         out_shape=[jax.ShapeDtypeStruct((length, lanes), jnp.float32)] * planes + edges,
         in_specs=[pl.BlockSpec(memory_space=pltpu.SMEM)] * 2 + [whole] * (1 + len(notes)),
         out_specs=[whole] * (planes + len(edges)),
-        scratch_shapes=[pltpu.VMEM((half, rows * 2 * source_count, lanes), jnp.float32)],
+        scratch_shapes=[pltpu.VMEM((half, (rows + 1) * 2 * source_count, lanes), jnp.float32)],
         compiler_params=pltpu.CompilerParams(vmem_limit_bytes=24 * 2**20),
         name="pack_sources",
     )(*here, field, *notes)
@@ -465,7 +465,7 @@
             pltpu.SMEM((2, plan.stride, lanes), jnp.int32),
             pltpu.VMEM(((field_rows + 1) * 4 * half, lanes), jnp.float32),
             pltpu.VMEM((rows * 4 * half, lanes), jnp.float32),
-            pltpu.VMEM((fine_rows * 2 * half, lanes), jnp.float32),
+            pltpu.VMEM(((fine_rows + 1) * 2 * half, lanes), jnp.float32),
             pltpu.VMEM((planes, dir_count) + message, jnp.float32),
             pltpu.VMEM((planes, max(edge_rows, 1) * 2 * half, lanes), jnp.float32),
             pltpu.SemaphoreType.DMA((2 * planes + 2,)),
@@ -488,7 +488,7 @@
             out_shape=jax.ShapeDtypeStruct(result, jnp.float32),
             in_specs=[whole] * 2,
             out_specs=whole,
-            scratch_shapes=[pltpu.VMEM((dir_count, dest_rows * 2 * source_count, lanes), jnp.float32)],
+            scratch_shapes=[pltpu.VMEM((dir_count, (dest_rows + 1) * 2 * source_count, lanes), jnp.float32)],
             compiler_params=pltpu.CompilerParams(vmem_limit_bytes=24 * 2**20),
             name="join_parts",
         )(parts, 1.0 - rims[:1])

time: 87.8 us -> 87.5 us (level)
  no operation moved by 1% of the time
where the time goes in v16:
time: 87.5 us; the launch traced here: 87.2 us
  waiting for transfers between devices  36.1 us (41%)
  Pallas kernels  22 us (25%)
  starting transfers between devices  13.9 us (16%)
  other arithmetic  10.2 us (12%)
  local copies, waits for them, and re-layouts  4.6 us (5%)
    all_to_all x1, waiting for transfers between devices, per_device(): lax.all_to_all(local_fine.reshape((planes * dir_count,) + message), ('zed...  26.3 us
    pallas_call x1, Pallas kernels, per_device(): pl.pallas_call(functools.partial(fine_kernel, plan, size, edge_rows), out...  19.3 us
    ppermute x6, waiting for transfers between devices, to_planes(): lax.ppermute(note, 'zed', [(plane, plane ^ step) for plane in range(plane...  9.77 us
    all_to_all x1, starting transfers between devices, per_device(): lax.all_to_all(local_fine.reshape((planes * dir_count,) + message), ('zed...  6.55 us
    ppermute x6, starting transfers between devices, to_planes(): lax.ppermute(note, 'zed', [(plane, plane ^ step) for plane in range(plane...  6.07 us
    add x2, other arithmetic, interp(): matrix + jnp.where(ids[point][None, :] == targets[:, None], weights[point...  2.69 us
    reshape x1, local copies, waits for them, and re-layouts, per_device(): jnp.pad(trans_table, ((0, 0), (0, 0), (0, pad_dirs))).reshape(-1, lanes)  2.31 us
  transfers between devices with their start and end apart: 8, of which 4 were waited for; matrix products, arithmetic and copies ran while one was open for 16% of the time, Pallas kernels for 1%

profile of v16, /device:TPU:11, one launch (start us, length us, event | category | flops | bytes accessed | tf_op | source)
XLA Modules:
  0.0 87.2 jit_solution(5280577386767586915)
XLA Ops:
  0.0 1.2 %copy-done.1 = f32[64,2,4,512]{3,2,1,0:T(4,128)S(1)} copy-done((f32[64,2,4,512]{3,2,1,0:T(4,128)S(1)}, f32[64,2,4,512]{3,2,1,0:T(4,128)}, u32[]{:S(2)}) %copy-start.1) | copy-done | bytes 1048600
  1.6 1.4 %collective-permute-start = (f32[512,128]{1,0:T(8,128)S(1)}, f32[512,128]{1,0:T(8,128)S(1)}, u32[]{:S(2)}, u32[]{:S(2)}) collective-permute-start(f32[512,128]{1,0:T(8,128)S(1)} %get-tuple-element.24), channel_id=1, source_target_pairs={{0,24},{8,16},{16,8},{24,0},{1,25},{9,17},{17,9},{25,1},{2,26},{10... | collective-permute-start | bytes 786440 | tf_op jit(solution)/shard_map/ppermute | solution.py:316
  3.0 1.1 %collective-permute-start.1 = (f32[512,128]{1,0:T(8,128)S(1)}, f32[512,128]{1,0:T(8,128)S(1)}, u32[]{:S(2)}, u32[]{:S(2)}) collective-permute-start(f32[512,128]{1,0:T(8,128)S(1)} %get-tuple-element.25), channel_id=1, source_target_pairs={{0,16},{8,24},{16,0},{24,8},{1,17},{9,25},{17,1},{25,9},{2,18},{10... | collective-permute-start | bytes 786440 | tf_op jit(solution)/shard_map/ppermute | solution.py:316
  4.1 1.1 %collective-permute-start.2 = (f32[512,128]{1,0:T(8,128)S(1)}, f32[512,128]{1,0:T(8,128)S(1)}, u32[]{:S(2)}, u32[]{:S(2)}) collective-permute-start(f32[512,128]{1,0:T(8,128)S(1)} %get-tuple-element.26), channel_id=1, source_target_pairs={{0,8},{8,0},{16,24},{24,16},{1,9},{9,1},{17,25},{25,17},{2,10},{10... | collective-permute-start | bytes 786440 | tf_op jit(solution)/shard_map/ppermute | solution.py:316
  5.2 1.2 %collective-permute-start.3 = (f32[16,2,4,512]{3,2,1,0:T(4,128)S(1)}, f32[16,2,4,512]{3,2,1,0:T(4,128)S(1)}, u32[]{:S(2)}, u32[]{:S(2)}) collective-permute-start(f32[16,2,4,512]{3,2,1,0:T(4,128)S(1)} %get-tuple-element.28), channel_id=1, source_target_pairs={{0,4},{4,0},{1,5},{5,1},{2,6},{6,2},{3,7},{7,3},{8,12},{12,8},{9,1... | collective-permute-start | bytes 786440 | tf_op jit(solution)/shard_map/ppermute | solution.py:311
  7.0 0.9 %convert_reduce_fusion.1 = s32[64]{0:T(128)S(1)} fusion(s32[64]{0:T(128)} %param.14), kind=kLoop, calls=%fused_computation.23 | loop fusion | flops 28608 | bytes 512 | tf_op jit(solution)/shard_map/reduce_sum | solution.py:343
  8.0 0.8 select_reduce_fusion.1
  9.0 0.8 select_reduce_fusion.2
  10.0 0.7 convert_bitcast_fusion
  10.7 0.8 fusion.17
  12.2 0.8 pack_sources.3
  13.0 0.7 dynamic-slice_bitcast_fusion
  14.1 2.1 %collective-permute-start.5 = (f32[176,128]{1,0:T(8,128)}, f32[176,128]{1,0:T(8,128)S(1)}, u32[]{:S(2)}, u32[]{:S(2)}) collective-permute-start(f32[176,128]{1,0:T(8,128)} %get-tuple-element.35), channel_id=1, source_target_pairs={{0,16},{8,24},{16,0},{24,8},{1,17},{9,25},{17,1},{25,9},{2,18},{10... | collective-permute-start | bytes 270344 | tf_op jit(solution)/shard_map/ppermute | solution.py:316
  16.2 1.3 %select_add_fusion = f32[4,512]{0,1:T(8,128)} fusion(f32[512]{0:T(512)S(1)} %bitcast.51, f32[512]{0:T(512)S(1)} %bitcast.53, f32[512]{0:T(512)S(1)} %bitcast.55, f32[512]{0:T(512)S(1)} %bitcast.49, s32[4]{0:T(128)S(1)} %and_select_fusion, s32[512]{0:T(512)S(1)} %bitcast.43, s32[512]{0:T(512)S(1)} %bitcast.45, s32[512]{0:T(512)S(1)} %bitcast.47, ...), kind=kLoop, calls=%fused_computation.7 | loop fusion | flops 22528 | bytes 24592 | tf_op jit(solution)/shard_map/add | solution.py:433
  17.6 1.3 %select_add_fusion.1 = f32[128,512]{0,1:T(8,128)} fusion(f32[512]{0:T(512)S(1)} %bitcast.52, f32[512]{0:T(512)S(1)} %bitcast.54, f32[512]{0:T(512)S(1)} %bitcast.56, f32[512]{0:T(512)S(1)} %bitcast.50, s32[128]{0:T(128)S(1)} %iota_add_fusion.2, s32[512]{0:T(512)S(1)} %bitcast.44, s32[512]{0:T(512)S(1)} %bitcast.46, s32[512]{0:T(512)S(1)} %bitcast.48, ...), kind=kLoop, calls=%fused_computation.8 | loop fusion | flops 720896 | bytes 279040 | tf_op jit(solution)/shard_map/add | solution.py:433
  18.9 2.3 %reshape.197.refs_9_ = f32[2528,128]{1,0:T(8,128)S(1)} reshape(f32[316,2,512]{2,1,0:T(2,128)} %param.11) | data formatting | bytes 2588672 | tf_op jit(solution)/shard_map/reshape | solution.py:411
  21.2 0.9 %cosine_multiply_fusion = (f32[1,512]{1,0:T(1,128)S(1)}, f32[1,512]{1,0:T(1,128)S(1)}, f32[1,512]{1,0:T(1,128)S(1)}) fusion(f32[2,2048]{1,0:T(2,128)} %param.17, s32[]{:T(128)S(6)} %add.225, s32[]{:T(128)S(6)} %select_n.165), kind=kLoop, calls=%fused_computation.111 | loop fusion | flops 1024 | bytes 10248 | tf_op jit(solution)/shard_map/mul | solution.py:417
  22.1 1.1 %fusion = (bf16[512,256]{1,0:T(8,128)(2,1)S(1)}, bf16[512,256]{1,0:T(8,128)(2,1)S(1)}) fusion(f32[4,512]{0,1:T(8,128)} %select_add_fusion, f32[128,512]{0,1:T(8,128)} %select_add_fusion.1), kind=kLoop, calls=%fused_computation.3 | loop fusion | flops 917504 | bytes 794624 | tf_op jit(solution)/shard_map/convert_element_type | solution.py:448
  24.2 6.5 %collective-permute-done.5.refs_6_ = f32[176,128]{1,0:T(8,128)S(1)} collective-permute-done((f32[176,128]{1,0:T(8,128)}, f32[176,128]{1,0:T(8,128)S(1)}, u32[]{:S(2)}, u32[]{:S(2)}) %collective-permute-start.5) | collective-permute-done | bytes 90144 | tf_op jit(solution)/shard_map/ppermute | solution.py:316
  30.7 2.6 %collective-permute-done.6.refs_7_ = f32[176,128]{1,0:T(8,128)S(1)} collective-permute-done((f32[176,128]{1,0:T(8,128)S(1)}, f32[176,128]{1,0:T(8,128)S(1)}, u32[]{:S(2)}, u32[]{:S(2)}) %collective-permute-start.6) | collective-permute-done | bytes 90144 | tf_op jit(solution)/shard_map/ppermute | solution.py:316
  33.4 19.3 %translate_and_interpolate.1 = (f32[4,4,136,128]{3,2,1,0:T(8,128)}, f32[8,128]{1,0:T(8,128)S(1)}) custom-call(s32[1]{0:T(128)} %bitcast.zed, f32[512,128]{1,0:T(8,128)S(1)} %collective-permute-done.refs_0_, f32[512,128]{1,0:T(8,128)S(1)} %collective-permute-done.1.refs_1_, f32[512,128]{1,0:T(8,128)S(1)} %collective-permute-done.2.refs_2_, ...), custom_call_target="tpu_custom_call" | custom-call | tf_op jit(solution)/shard_map/translate_and_interpolate/pallas_call | solution.py:453
  52.7 6.5 %all-to-all-start = ((f32[16,136,128]{2,1,0:T(8,128)}), f32[16,136,128]{2,1,0:T(8,128)S(1)}, u32[]{:S(2)}, u32[]{:S(2)}) async-start(f32[16,136,128]{2,1,0:T(8,128)} %bitcast.40), calls=%async_computation | async-start | bytes 2228224 | tf_op jit(solution)/shard_map/all_to_all | solution.py:477
  59.3 26.3 %all-to-all-done.parts = f32[16,136,128]{2,1,0:T(8,128)S(1)} async-done(((f32[16,136,128]{2,1,0:T(8,128)}), f32[16,136,128]{2,1,0:T(8,128)S(1)}, u32[]{:S(2)}, u32[]{:S(2)}) %all-to-all-start) | async-done | bytes 1114144 | tf_op jit(solution)/shard_map/all_to_all | solution.py:477
  85.6 1.6 %join_parts.1 = f32[64,2,4,512]{3,2,1,0:T(4,128)} custom-call(f32[16,136,128]{2,1,0:T(8,128)S(1)} %all-to-all-done.parts, f32[1,128]{1,0:T(1,128)S(1)} %slice_subtract_fusion.rims), custom_call_target="tpu_custom_call" | custom-call | tf_op jit(solution)/shard_map/join_parts/pallas_call | solution.py:486
  (49 shorter events, 3.4 us)
Async XLA Ops:
  0.0 13.0 %copy-start = (s32[2048,4]{0,1:T(4,128)S(1)}, s32[2048,4]{0,1:T(4,128)}, u32[]{:S(2)}) copy-start(s32[2048,4]{0,1:T(4,128)} %param.18) | copy-start | bytes 98308
  0.0 1.2 %copy-start.1 = (f32[64,2,4,512]{3,2,1,0:T(4,128)S(1)}, f32[64,2,4,512]{3,2,1,0:T(4,128)}, u32[]{:S(2)}) copy-start(f32[64,2,4,512]{3,2,1,0:T(4,128)} %field.1) | copy-start | bytes 3145732
  1.6 31.7 %collective-permute-start = (f32[512,128]{1,0:T(8,128)S(1)}, f32[512,128]{1,0:T(8,128)S(1)}, u32[]{:S(2)}, u32[]{:S(2)}) collective-permute-start(f32[512,128]{1,0:T(8,128)S(1)} %get-tuple-element.24), channel_id=1, source_target_pairs={{0,24},{8,16},{16,8},{24,0},{1,25},{9,17},{17,9},{25,1},{2,26},{10... | collective-permute-start | bytes 786440 | tf_op jit(solution)/shard_map/ppermute | solution.py:316
  3.0 30.4 %collective-permute-start.1 = (f32[512,128]{1,0:T(8,128)S(1)}, f32[512,128]{1,0:T(8,128)S(1)}, u32[]{:S(2)}, u32[]{:S(2)}) collective-permute-start(f32[512,128]{1,0:T(8,128)S(1)} %get-tuple-element.25), channel_id=1, source_target_pairs={{0,16},{8,24},{16,0},{24,8},{1,17},{9,25},{17,1},{25,9},{2,18},{10... | collective-permute-start | bytes 786440 | tf_op jit(solution)/shard_map/ppermute | solution.py:316
  4.1 29.3 %collective-permute-start.2 = (f32[512,128]{1,0:T(8,128)S(1)}, f32[512,128]{1,0:T(8,128)S(1)}, u32[]{:S(2)}, u32[]{:S(2)}) collective-permute-start(f32[512,128]{1,0:T(8,128)S(1)} %get-tuple-element.26), channel_id=1, source_target_pairs={{0,8},{8,0},{16,24},{24,16},{1,9},{9,1},{17,25},{25,17},{2,10},{10... | collective-permute-start | bytes 786440 | tf_op jit(solution)/shard_map/ppermute | solution.py:316
  5.2 7.0 %collective-permute-start.3 = (f32[16,2,4,512]{3,2,1,0:T(4,128)S(1)}, f32[16,2,4,512]{3,2,1,0:T(4,128)S(1)}, u32[]{:S(2)}, u32[]{:S(2)}) collective-permute-start(f32[16,2,4,512]{3,2,1,0:T(4,128)S(1)} %get-tuple-element.28), channel_id=1, source_target_pairs={{0,4},{4,0},{1,5},{5,1},{2,6},{6,2},{3,7},{7,3},{8,12},{12,8},{9,1... | collective-permute-start | bytes 786440 | tf_op jit(solution)/shard_map/ppermute | solution.py:311
  13.7 10.5 %collective-permute-start.4 = (f32[176,128]{1,0:T(8,128)}, f32[176,128]{1,0:T(8,128)S(1)}, u32[]{:S(2)}, u32[]{:S(2)}) collective-permute-start(f32[176,128]{1,0:T(8,128)} %get-tuple-element.34), channel_id=1, source_target_pairs={{0,8},{8,0},{16,24},{24,16},{1,9},{9,1},{17,25},{25,17},{2,10},{10... | collective-permute-start | bytes 270344 | tf_op jit(solution)/shard_map/ppermute | solution.py:316
  14.1 16.6 %collective-permute-start.5 = (f32[176,128]{1,0:T(8,128)}, f32[176,128]{1,0:T(8,128)S(1)}, u32[]{:S(2)}, u32[]{:S(2)}) collective-permute-start(f32[176,128]{1,0:T(8,128)} %get-tuple-element.35), channel_id=1, source_target_pairs={{0,16},{8,24},{16,0},{24,8},{1,17},{9,25},{17,1},{25,9},{2,18},{10... | collective-permute-start | bytes 270344 | tf_op jit(solution)/shard_map/ppermute | solution.py:316
  21.2 2.1 %copy-start.2 = (f32[8]{0:T(128)S(1)}, f32[8]{0:T(128)}, u32[]{:S(2)}) copy-start(f32[8]{0:T(128)} %get-tuple-element.62) | copy-start | bytes 100
  24.2 9.1 %collective-permute-start.6 = (f32[176,128]{1,0:T(8,128)S(1)}, f32[176,128]{1,0:T(8,128)S(1)}, u32[]{:S(2)}, u32[]{:S(2)}) collective-permute-start(f32[176,128]{1,0:T(8,128)S(1)} %get-tuple-element.36), channel_id=1, source_target_pairs={{0,24},{8,16},{16,8},{24,0},{1,25},{9,17},{17,9},{25,1},{2,26},{10... | collective-permute-start | bytes 270344 | tf_op jit(solution)/shard_map/ppermute | solution.py:316
  52.7 32.9 %all-to-all-start = ((f32[16,136,128]{2,1,0:T(8,128)}), f32[16,136,128]{2,1,0:T(8,128)S(1)}, u32[]{:S(2)}, u32[]{:S(2)}) async-start(f32[16,136,128]{2,1,0:T(8,128)} %bitcast.40), calls=%async_computation | async-start | bytes 2228224 | tf_op jit(solution)/shard_map/all_to_all | solution.py:477

commit v17 on v16

--- a/solution.py
+++ b/solution.py
@@ -201,30 +201,25 @@
 
         lax.fori_loop(0, fine_rows // lanes, fine_step, 0)
         width = ready.shape[3]
-        left = jnp.concatenate(
-            [
-                jnp.concatenate(
-                    [
-                        shifted[pl.ds(part * half + block, fine_rows, stride=2 * half), :]
-                        for block in range(half)
-                    ],
-                    axis=1,
-                )
-                for part in range(2)
-            ],
-            axis=0,
-        )
-        first, second = split(left)
-        result = jnp.dot(
-            jnp.concatenate([first, first, second], axis=1), weights[...], preferred_element_type=jnp.float32
-        )
+        spill = jnp.zeros((fine_rows, lanes), jnp.float32)
         for part in range(2):
+            left = jnp.concatenate(
+                [
+                    shifted[pl.ds(part * half + block, fine_rows, stride=2 * half), :]
+                    for block in range(half)
+                ],
+                axis=1,
+            )
+            first, second = split(left)
+            result = jnp.dot(
+                jnp.concatenate([first, first, second], axis=1), weights[...], preferred_element_type=jnp.float32
+            )
             for dest in range(dest_count):
-                start = part * fine_rows + dest * dest_rows
                 ready[plane, dest, part * dest_rows : (part + 1) * dest_rows, :] = result[
-                    start : start + dest_rows, :width
+                    dest * dest_rows : (dest + 1) * dest_rows, :width
                 ]
-        spill = result[:fine_rows, width:] + pltpu.roll(result[fine_rows:, width:], half, 1)
+            over = result[:, width:]
+            spill = spill + (pltpu.roll(over, half, 1) if part else over)
         spill = spill.T[: 2 * half]
         for dest in range(dest_count):
             ready[plane, dest, 2 * dest_rows :, :] = jnp.concatenate(

time: 87.5 us -> 87.3 us (level)
  no operation moved by 1% of the time
where the time goes in v17:
time: 87.3 us; the launch traced here: 86.9 us
  waiting for transfers between devices  36.1 us (41%)
  Pallas kernels  21.7 us (25%)
  starting transfers between devices  13.9 us (16%)
  other arithmetic  10.2 us (12%)
  local copies, waits for them, and re-layouts  4.6 us (5%)
    all_to_all x1, waiting for transfers between devices, per_device(): lax.all_to_all(local_fine.reshape((planes * dir_count,) + message), ('zed...  26.3 us
    pallas_call x1, Pallas kernels, per_device(): pl.pallas_call(functools.partial(fine_kernel, plan, size, edge_rows), out...  19 us
    ppermute x6, waiting for transfers between devices, to_planes(): lax.ppermute(note, 'zed', [(plane, plane ^ step) for plane in range(plane...  9.77 us
    all_to_all x1, starting transfers between devices, per_device(): lax.all_to_all(local_fine.reshape((planes * dir_count,) + message), ('zed...  6.54 us
    ppermute x6, starting transfers between devices, to_planes(): lax.ppermute(note, 'zed', [(plane, plane ^ step) for plane in range(plane...  6.07 us
    add x2, other arithmetic, interp(): matrix + jnp.where(ids[point][None, :] == targets[:, None], weights[point...  2.69 us
    reshape x1, local copies, waits for them, and re-layouts, per_device(): jnp.pad(trans_table, ((0, 0), (0, 0), (0, pad_dirs))).reshape(-1, lanes)  2.31 us
  transfers between devices with their start and end apart: 8, of which 4 were waited for; matrix products, arithmetic and copies ran while one was open for 16% of the time, Pallas kernels for 1%

profile of v17, /device:TPU:11, one launch (start us, length us, event | category | flops | bytes accessed | tf_op | source)
XLA Modules:
  0.0 86.9 jit_solution(9405330500873450442)
XLA Ops:
  0.0 1.2 %copy-done.1 = f32[64,2,4,512]{3,2,1,0:T(4,128)S(1)} copy-done((f32[64,2,4,512]{3,2,1,0:T(4,128)S(1)}, f32[64,2,4,512]{3,2,1,0:T(4,128)}, u32[]{:S(2)}) %copy-start.1) | copy-done | bytes 1048600
  1.6 1.4 %collective-permute-start = (f32[512,128]{1,0:T(8,128)S(1)}, f32[512,128]{1,0:T(8,128)S(1)}, u32[]{:S(2)}, u32[]{:S(2)}) collective-permute-start(f32[512,128]{1,0:T(8,128)S(1)} %get-tuple-element.24), channel_id=1, source_target_pairs={{0,24},{8,16},{16,8},{24,0},{1,25},{9,17},{17,9},{25,1},{2,26},{10... | collective-permute-start | bytes 786440 | tf_op jit(solution)/shard_map/ppermute | solution.py:311
  3.0 1.1 %collective-permute-start.1 = (f32[512,128]{1,0:T(8,128)S(1)}, f32[512,128]{1,0:T(8,128)S(1)}, u32[]{:S(2)}, u32[]{:S(2)}) collective-permute-start(f32[512,128]{1,0:T(8,128)S(1)} %get-tuple-element.25), channel_id=1, source_target_pairs={{0,16},{8,24},{16,0},{24,8},{1,17},{9,25},{17,1},{25,9},{2,18},{10... | collective-permute-start | bytes 786440 | tf_op jit(solution)/shard_map/ppermute | solution.py:311
  4.1 1.1 %collective-permute-start.2 = (f32[512,128]{1,0:T(8,128)S(1)}, f32[512,128]{1,0:T(8,128)S(1)}, u32[]{:S(2)}, u32[]{:S(2)}) collective-permute-start(f32[512,128]{1,0:T(8,128)S(1)} %get-tuple-element.26), channel_id=1, source_target_pairs={{0,8},{8,0},{16,24},{24,16},{1,9},{9,1},{17,25},{25,17},{2,10},{10... | collective-permute-start | bytes 786440 | tf_op jit(solution)/shard_map/ppermute | solution.py:311
  5.2 1.2 %collective-permute-start.3 = (f32[16,2,4,512]{3,2,1,0:T(4,128)S(1)}, f32[16,2,4,512]{3,2,1,0:T(4,128)S(1)}, u32[]{:S(2)}, u32[]{:S(2)}) collective-permute-start(f32[16,2,4,512]{3,2,1,0:T(4,128)S(1)} %get-tuple-element.28), channel_id=1, source_target_pairs={{0,4},{4,0},{1,5},{5,1},{2,6},{6,2},{3,7},{7,3},{8,12},{12,8},{9,1... | collective-permute-start | bytes 786440 | tf_op jit(solution)/shard_map/ppermute | solution.py:306
  7.0 0.9 %convert_reduce_fusion.1 = s32[64]{0:T(128)S(1)} fusion(s32[64]{0:T(128)} %param.14), kind=kLoop, calls=%fused_computation.23 | loop fusion | flops 28608 | bytes 512 | tf_op jit(solution)/shard_map/reduce_sum | solution.py:338
  8.0 0.8 select_reduce_fusion.1
  9.0 0.8 select_reduce_fusion.2
  10.0 0.7 convert_bitcast_fusion
  10.7 0.8 fusion.17
  12.2 0.8 pack_sources.3
  13.0 0.7 dynamic-slice_bitcast_fusion
  14.1 2.1 %collective-permute-start.5 = (f32[176,128]{1,0:T(8,128)}, f32[176,128]{1,0:T(8,128)S(1)}, u32[]{:S(2)}, u32[]{:S(2)}) collective-permute-start(f32[176,128]{1,0:T(8,128)} %get-tuple-element.35), channel_id=1, source_target_pairs={{0,16},{8,24},{16,0},{24,8},{1,17},{9,25},{17,1},{25,9},{2,18},{10... | collective-permute-start | bytes 270344 | tf_op jit(solution)/shard_map/ppermute | solution.py:311
  16.2 1.3 %select_add_fusion = f32[4,512]{0,1:T(8,128)} fusion(f32[512]{0:T(512)S(1)} %bitcast.51, f32[512]{0:T(512)S(1)} %bitcast.53, f32[512]{0:T(512)S(1)} %bitcast.55, f32[512]{0:T(512)S(1)} %bitcast.49, s32[4]{0:T(128)S(1)} %and_select_fusion, s32[512]{0:T(512)S(1)} %bitcast.43, s32[512]{0:T(512)S(1)} %bitcast.45, s32[512]{0:T(512)S(1)} %bitcast.47, ...), kind=kLoop, calls=%fused_computation.7 | loop fusion | flops 22528 | bytes 24592 | tf_op jit(solution)/shard_map/add | solution.py:428
  17.6 1.3 %select_add_fusion.1 = f32[128,512]{0,1:T(8,128)} fusion(f32[512]{0:T(512)S(1)} %bitcast.52, f32[512]{0:T(512)S(1)} %bitcast.54, f32[512]{0:T(512)S(1)} %bitcast.56, f32[512]{0:T(512)S(1)} %bitcast.50, s32[128]{0:T(128)S(1)} %iota_add_fusion.2, s32[512]{0:T(512)S(1)} %bitcast.44, s32[512]{0:T(512)S(1)} %bitcast.46, s32[512]{0:T(512)S(1)} %bitcast.48, ...), kind=kLoop, calls=%fused_computation.8 | loop fusion | flops 720896 | bytes 279040 | tf_op jit(solution)/shard_map/add | solution.py:428
  18.9 2.3 %reshape.197.refs_9_ = f32[2528,128]{1,0:T(8,128)S(1)} reshape(f32[316,2,512]{2,1,0:T(2,128)} %param.11) | data formatting | bytes 2588672 | tf_op jit(solution)/shard_map/reshape | solution.py:406
  21.2 0.9 %cosine_multiply_fusion = (f32[1,512]{1,0:T(1,128)S(1)}, f32[1,512]{1,0:T(1,128)S(1)}, f32[1,512]{1,0:T(1,128)S(1)}) fusion(f32[2,2048]{1,0:T(2,128)} %param.17, s32[]{:T(128)S(6)} %add.225, s32[]{:T(128)S(6)} %select_n.165), kind=kLoop, calls=%fused_computation.111 | loop fusion | flops 1024 | bytes 10248 | tf_op jit(solution)/shard_map/mul | solution.py:412
  22.1 1.1 %fusion = (bf16[512,256]{1,0:T(8,128)(2,1)S(1)}, bf16[512,256]{1,0:T(8,128)(2,1)S(1)}) fusion(f32[4,512]{0,1:T(8,128)} %select_add_fusion, f32[128,512]{0,1:T(8,128)} %select_add_fusion.1), kind=kLoop, calls=%fused_computation.3 | loop fusion | flops 917504 | bytes 794624 | tf_op jit(solution)/shard_map/convert_element_type | solution.py:443
  24.2 6.5 %collective-permute-done.5.refs_6_ = f32[176,128]{1,0:T(8,128)S(1)} collective-permute-done((f32[176,128]{1,0:T(8,128)}, f32[176,128]{1,0:T(8,128)S(1)}, u32[]{:S(2)}, u32[]{:S(2)}) %collective-permute-start.5) | collective-permute-done | bytes 90144 | tf_op jit(solution)/shard_map/ppermute | solution.py:311
  30.7 2.6 %collective-permute-done.6.refs_7_ = f32[176,128]{1,0:T(8,128)S(1)} collective-permute-done((f32[176,128]{1,0:T(8,128)S(1)}, f32[176,128]{1,0:T(8,128)S(1)}, u32[]{:S(2)}, u32[]{:S(2)}) %collective-permute-start.6) | collective-permute-done | bytes 90144 | tf_op jit(solution)/shard_map/ppermute | solution.py:311
  33.4 19.0 %translate_and_interpolate.1 = (f32[4,4,136,128]{3,2,1,0:T(8,128)}, f32[8,128]{1,0:T(8,128)S(1)}) custom-call(s32[1]{0:T(128)} %bitcast.zed, f32[512,128]{1,0:T(8,128)S(1)} %collective-permute-done.refs_0_, f32[512,128]{1,0:T(8,128)S(1)} %collective-permute-done.1.refs_1_, f32[512,128]{1,0:T(8,128)S(1)} %collective-permute-done.2.refs_2_, ...), custom_call_target="tpu_custom_call" | custom-call | tf_op jit(solution)/shard_map/translate_and_interpolate/pallas_call | solution.py:448
  52.4 6.5 %all-to-all-start = ((f32[16,136,128]{2,1,0:T(8,128)}), f32[16,136,128]{2,1,0:T(8,128)S(1)}, u32[]{:S(2)}, u32[]{:S(2)}) async-start(f32[16,136,128]{2,1,0:T(8,128)} %bitcast.40), calls=%async_computation | async-start | bytes 2228224 | tf_op jit(solution)/shard_map/all_to_all | solution.py:472
  59.0 26.3 %all-to-all-done.parts = f32[16,136,128]{2,1,0:T(8,128)S(1)} async-done(((f32[16,136,128]{2,1,0:T(8,128)}), f32[16,136,128]{2,1,0:T(8,128)S(1)}, u32[]{:S(2)}, u32[]{:S(2)}) %all-to-all-start) | async-done | bytes 1114144 | tf_op jit(solution)/shard_map/all_to_all | solution.py:472
  85.3 1.6 %join_parts.1 = f32[64,2,4,512]{3,2,1,0:T(4,128)} custom-call(f32[16,136,128]{2,1,0:T(8,128)S(1)} %all-to-all-done.parts, f32[1,128]{1,0:T(1,128)S(1)} %slice_subtract_fusion.rims), custom_call_target="tpu_custom_call" | custom-call | tf_op jit(solution)/shard_map/join_parts/pallas_call | solution.py:481
  (49 shorter events, 3.4 us)
Async XLA Ops:
  0.0 13.0 %copy-start = (s32[2048,4]{0,1:T(4,128)S(1)}, s32[2048,4]{0,1:T(4,128)}, u32[]{:S(2)}) copy-start(s32[2048,4]{0,1:T(4,128)} %param.18) | copy-start | bytes 98308
  0.0 1.2 %copy-start.1 = (f32[64,2,4,512]{3,2,1,0:T(4,128)S(1)}, f32[64,2,4,512]{3,2,1,0:T(4,128)}, u32[]{:S(2)}) copy-start(f32[64,2,4,512]{3,2,1,0:T(4,128)} %field.1) | copy-start | bytes 3145732
  1.6 31.7 %collective-permute-start = (f32[512,128]{1,0:T(8,128)S(1)}, f32[512,128]{1,0:T(8,128)S(1)}, u32[]{:S(2)}, u32[]{:S(2)}) collective-permute-start(f32[512,128]{1,0:T(8,128)S(1)} %get-tuple-element.24), channel_id=1, source_target_pairs={{0,24},{8,16},{16,8},{24,0},{1,25},{9,17},{17,9},{25,1},{2,26},{10... | collective-permute-start | bytes 786440 | tf_op jit(solution)/shard_map/ppermute | solution.py:311
  3.0 30.4 %collective-permute-start.1 = (f32[512,128]{1,0:T(8,128)S(1)}, f32[512,128]{1,0:T(8,128)S(1)}, u32[]{:S(2)}, u32[]{:S(2)}) collective-permute-start(f32[512,128]{1,0:T(8,128)S(1)} %get-tuple-element.25), channel_id=1, source_target_pairs={{0,16},{8,24},{16,0},{24,8},{1,17},{9,25},{17,1},{25,9},{2,18},{10... | collective-permute-start | bytes 786440 | tf_op jit(solution)/shard_map/ppermute | solution.py:311
  4.1 29.3 %collective-permute-start.2 = (f32[512,128]{1,0:T(8,128)S(1)}, f32[512,128]{1,0:T(8,128)S(1)}, u32[]{:S(2)}, u32[]{:S(2)}) collective-permute-start(f32[512,128]{1,0:T(8,128)S(1)} %get-tuple-element.26), channel_id=1, source_target_pairs={{0,8},{8,0},{16,24},{24,16},{1,9},{9,1},{17,25},{25,17},{2,10},{10... | collective-permute-start | bytes 786440 | tf_op jit(solution)/shard_map/ppermute | solution.py:311
  5.2 7.0 %collective-permute-start.3 = (f32[16,2,4,512]{3,2,1,0:T(4,128)S(1)}, f32[16,2,4,512]{3,2,1,0:T(4,128)S(1)}, u32[]{:S(2)}, u32[]{:S(2)}) collective-permute-start(f32[16,2,4,512]{3,2,1,0:T(4,128)S(1)} %get-tuple-element.28), channel_id=1, source_target_pairs={{0,4},{4,0},{1,5},{5,1},{2,6},{6,2},{3,7},{7,3},{8,12},{12,8},{9,1... | collective-permute-start | bytes 786440 | tf_op jit(solution)/shard_map/ppermute | solution.py:306
  13.7 10.5 %collective-permute-start.4 = (f32[176,128]{1,0:T(8,128)}, f32[176,128]{1,0:T(8,128)S(1)}, u32[]{:S(2)}, u32[]{:S(2)}) collective-permute-start(f32[176,128]{1,0:T(8,128)} %get-tuple-element.34), channel_id=1, source_target_pairs={{0,8},{8,0},{16,24},{24,16},{1,9},{9,1},{17,25},{25,17},{2,10},{10... | collective-permute-start | bytes 270344 | tf_op jit(solution)/shard_map/ppermute | solution.py:311
  14.1 16.6 %collective-permute-start.5 = (f32[176,128]{1,0:T(8,128)}, f32[176,128]{1,0:T(8,128)S(1)}, u32[]{:S(2)}, u32[]{:S(2)}) collective-permute-start(f32[176,128]{1,0:T(8,128)} %get-tuple-element.35), channel_id=1, source_target_pairs={{0,16},{8,24},{16,0},{24,8},{1,17},{9,25},{17,1},{25,9},{2,18},{10... | collective-permute-start | bytes 270344 | tf_op jit(solution)/shard_map/ppermute | solution.py:311
  21.2 2.1 %copy-start.2 = (f32[8]{0:T(128)S(1)}, f32[8]{0:T(128)}, u32[]{:S(2)}) copy-start(f32[8]{0:T(128)} %get-tuple-element.62) | copy-start | bytes 100
  24.2 9.1 %collective-permute-start.6 = (f32[176,128]{1,0:T(8,128)S(1)}, f32[176,128]{1,0:T(8,128)S(1)}, u32[]{:S(2)}, u32[]{:S(2)}) collective-permute-start(f32[176,128]{1,0:T(8,128)S(1)} %get-tuple-element.36), channel_id=1, source_target_pairs={{0,24},{8,16},{16,8},{24,0},{1,25},{9,17},{17,9},{25,1},{2,26},{10... | collective-permute-start | bytes 270344 | tf_op jit(solution)/shard_map/ppermute | solution.py:311
  52.4 32.9 %all-to-all-start = ((f32[16,136,128]{2,1,0:T(8,128)}), f32[16,136,128]{2,1,0:T(8,128)S(1)}, u32[]{:S(2)}, u32[]{:S(2)}) async-start(f32[16,136,128]{2,1,0:T(8,128)} %bitcast.40), calls=%async_computation | async-start | bytes 2228224 | tf_op jit(solution)/shard_map/all_to_all | solution.py:472

commit v18 on v17

--- a/solution.py
+++ b/solution.py
@@ -201,25 +201,28 @@
 
         lax.fori_loop(0, fine_rows // lanes, fine_step, 0)
         width = ready.shape[3]
-        spill = jnp.zeros((fine_rows, lanes), jnp.float32)
-        for part in range(2):
-            left = jnp.concatenate(
-                [
-                    shifted[pl.ds(part * half + block, fine_rows, stride=2 * half), :]
-                    for block in range(half)
-                ],
-                axis=1,
-            )
-            first, second = split(left)
-            result = jnp.dot(
-                jnp.concatenate([first, first, second], axis=1), weights[...], preferred_element_type=jnp.float32
-            )
-            for dest in range(dest_count):
-                ready[plane, dest, part * dest_rows : (part + 1) * dest_rows, :] = result[
-                    dest * dest_rows : (dest + 1) * dest_rows, :width
-                ]
-            over = result[:, width:]
-            spill = spill + (pltpu.roll(over, half, 1) if part else over)
+        chunk_rows = fine_rows // 2
+        spills = [jnp.zeros((chunk_rows, lanes), jnp.float32)] * 2
+        for chunk in range(2):
+            for part in range(2):
+                begin = chunk * chunk_rows * 2 * half + part * half
+                left = jnp.concatenate(
+                    [shifted[pl.ds(begin + block, chunk_rows, stride=2 * half), :] for block in range(half)],
+                    axis=1,
+                )
+                first, second = split(left)
+                result = jnp.dot(
+                    jnp.concatenate([first, first, second], axis=1),
+                    weights[...],
+                    preferred_element_type=jnp.float32,
+                )
+                for dest in range(dest_count // 2):
+                    ready[
+                        plane, chunk * dest_count // 2 + dest, part * dest_rows : (part + 1) * dest_rows, :
+                    ] = result[dest * dest_rows : (dest + 1) * dest_rows, :width]
+                over = result[:, width:]
+                spills[chunk] = spills[chunk] + (pltpu.roll(over, half, 1) if part else over)
+        spill = jnp.concatenate(spills, axis=0)
         spill = spill.T[: 2 * half]
         for dest in range(dest_count):
             ready[plane, dest, 2 * dest_rows :, :] = jnp.concatenate(

time: 87.3 us -> 87.6 us (level)
  no operation moved by 1% of the time
where the time goes in v18:
time: 87.6 us; the launch traced here: 87.2 us
  waiting for transfers between devices  36.1 us (41%)
  Pallas kernels  22.1 us (25%)
  starting transfers between devices  13.9 us (16%)
  other arithmetic  10.2 us (12%)
  local copies, waits for them, and re-layouts  4.6 us (5%)
    all_to_all x1, waiting for transfers between devices, per_device(): lax.all_to_all(local_fine.reshape((planes * dir_count,) + message), ('zed...  26.3 us
    pallas_call x1, Pallas kernels, per_device(): pl.pallas_call(functools.partial(fine_kernel, plan, size, edge_rows), out...  19.4 us
    ppermute x6, waiting for transfers between devices, to_planes(): lax.ppermute(note, 'zed', [(plane, plane ^ step) for plane in range(plane...  9.77 us
    all_to_all x1, starting transfers between devices, per_device(): lax.all_to_all(local_fine.reshape((planes * dir_count,) + message), ('zed...  6.54 us
    ppermute x6, starting transfers between devices, to_planes(): lax.ppermute(note, 'zed', [(plane, plane ^ step) for plane in range(plane...  6.07 us
    add x2, other arithmetic, interp(): matrix + jnp.where(ids[point][None, :] == targets[:, None], weights[point...  2.69 us
    reshape x1, local copies, waits for them, and re-layouts, per_device(): jnp.pad(trans_table, ((0, 0), (0, 0), (0, pad_dirs))).reshape(-1, lanes)  2.31 us
  transfers between devices with their start and end apart: 8, of which 4 were waited for; matrix products, arithmetic and copies ran while one was open for 16% of the time, Pallas kernels for 1%

profile of v18, /device:TPU:11, one launch (start us, length us, event | category | flops | bytes accessed | tf_op | source)
XLA Modules:
  0.0 87.2 jit_solution(9027779724300388038)
XLA Ops:
  0.0 1.2 %copy-done.1 = f32[64,2,4,512]{3,2,1,0:T(4,128)S(1)} copy-done((f32[64,2,4,512]{3,2,1,0:T(4,128)S(1)}, f32[64,2,4,512]{3,2,1,0:T(4,128)}, u32[]{:S(2)}) %copy-start.1) | copy-done | bytes 1048600
  1.6 1.4 %collective-permute-start = (f32[512,128]{1,0:T(8,128)S(1)}, f32[512,128]{1,0:T(8,128)S(1)}, u32[]{:S(2)}, u32[]{:S(2)}) collective-permute-start(f32[512,128]{1,0:T(8,128)S(1)} %get-tuple-element.24), channel_id=1, source_target_pairs={{0,24},{8,16},{16,8},{24,0},{1,25},{9,17},{17,9},{25,1},{2,26},{10... | collective-permute-start | bytes 786440 | tf_op jit(solution)/shard_map/ppermute | solution.py:314
  3.0 1.1 %collective-permute-start.1 = (f32[512,128]{1,0:T(8,128)S(1)}, f32[512,128]{1,0:T(8,128)S(1)}, u32[]{:S(2)}, u32[]{:S(2)}) collective-permute-start(f32[512,128]{1,0:T(8,128)S(1)} %get-tuple-element.25), channel_id=1, source_target_pairs={{0,16},{8,24},{16,0},{24,8},{1,17},{9,25},{17,1},{25,9},{2,18},{10... | collective-permute-start | bytes 786440 | tf_op jit(solution)/shard_map/ppermute | solution.py:314
  4.1 1.1 %collective-permute-start.2 = (f32[512,128]{1,0:T(8,128)S(1)}, f32[512,128]{1,0:T(8,128)S(1)}, u32[]{:S(2)}, u32[]{:S(2)}) collective-permute-start(f32[512,128]{1,0:T(8,128)S(1)} %get-tuple-element.26), channel_id=1, source_target_pairs={{0,8},{8,0},{16,24},{24,16},{1,9},{9,1},{17,25},{25,17},{2,10},{10... | collective-permute-start | bytes 786440 | tf_op jit(solution)/shard_map/ppermute | solution.py:314
  5.2 1.2 %collective-permute-start.3 = (f32[16,2,4,512]{3,2,1,0:T(4,128)S(1)}, f32[16,2,4,512]{3,2,1,0:T(4,128)S(1)}, u32[]{:S(2)}, u32[]{:S(2)}) collective-permute-start(f32[16,2,4,512]{3,2,1,0:T(4,128)S(1)} %get-tuple-element.28), channel_id=1, source_target_pairs={{0,4},{4,0},{1,5},{5,1},{2,6},{6,2},{3,7},{7,3},{8,12},{12,8},{9,1... | collective-permute-start | bytes 786440 | tf_op jit(solution)/shard_map/ppermute | solution.py:309
  7.0 0.9 %convert_reduce_fusion.1 = s32[64]{0:T(128)S(1)} fusion(s32[64]{0:T(128)} %param.14), kind=kLoop, calls=%fused_computation.23 | loop fusion | flops 28608 | bytes 512 | tf_op jit(solution)/shard_map/reduce_sum | solution.py:341
  8.0 0.8 select_reduce_fusion.1
  9.0 0.8 select_reduce_fusion.2
  10.0 0.7 convert_bitcast_fusion
  10.7 0.8 fusion.17
  12.2 0.8 pack_sources.3
  13.0 0.7 dynamic-slice_bitcast_fusion
  14.1 2.1 %collective-permute-start.5 = (f32[176,128]{1,0:T(8,128)}, f32[176,128]{1,0:T(8,128)S(1)}, u32[]{:S(2)}, u32[]{:S(2)}) collective-permute-start(f32[176,128]{1,0:T(8,128)} %get-tuple-element.35), channel_id=1, source_target_pairs={{0,16},{8,24},{16,0},{24,8},{1,17},{9,25},{17,1},{25,9},{2,18},{10... | collective-permute-start | bytes 270344 | tf_op jit(solution)/shard_map/ppermute | solution.py:314
  16.2 1.3 %select_add_fusion = f32[4,512]{0,1:T(8,128)} fusion(f32[512]{0:T(512)S(1)} %bitcast.51, f32[512]{0:T(512)S(1)} %bitcast.53, f32[512]{0:T(512)S(1)} %bitcast.55, f32[512]{0:T(512)S(1)} %bitcast.49, s32[4]{0:T(128)S(1)} %and_select_fusion, s32[512]{0:T(512)S(1)} %bitcast.43, s32[512]{0:T(512)S(1)} %bitcast.45, s32[512]{0:T(512)S(1)} %bitcast.47, ...), kind=kLoop, calls=%fused_computation.7 | loop fusion | flops 22528 | bytes 24592 | tf_op jit(solution)/shard_map/add | solution.py:431
  17.6 1.3 %select_add_fusion.1 = f32[128,512]{0,1:T(8,128)} fusion(f32[512]{0:T(512)S(1)} %bitcast.52, f32[512]{0:T(512)S(1)} %bitcast.54, f32[512]{0:T(512)S(1)} %bitcast.56, f32[512]{0:T(512)S(1)} %bitcast.50, s32[128]{0:T(128)S(1)} %iota_add_fusion.2, s32[512]{0:T(512)S(1)} %bitcast.44, s32[512]{0:T(512)S(1)} %bitcast.46, s32[512]{0:T(512)S(1)} %bitcast.48, ...), kind=kLoop, calls=%fused_computation.8 | loop fusion | flops 720896 | bytes 279040 | tf_op jit(solution)/shard_map/add | solution.py:431
  18.9 2.3 %reshape.197.refs_9_ = f32[2528,128]{1,0:T(8,128)S(1)} reshape(f32[316,2,512]{2,1,0:T(2,128)} %param.11) | data formatting | bytes 2588672 | tf_op jit(solution)/shard_map/reshape | solution.py:409
  21.2 0.9 %cosine_multiply_fusion = (f32[1,512]{1,0:T(1,128)S(1)}, f32[1,512]{1,0:T(1,128)S(1)}, f32[1,512]{1,0:T(1,128)S(1)}) fusion(f32[2,2048]{1,0:T(2,128)} %param.17, s32[]{:T(128)S(6)} %add.225, s32[]{:T(128)S(6)} %select_n.165), kind=kLoop, calls=%fused_computation.111 | loop fusion | flops 1024 | bytes 10248 | tf_op jit(solution)/shard_map/mul | solution.py:415
  22.1 1.1 %fusion = (bf16[512,256]{1,0:T(8,128)(2,1)S(1)}, bf16[512,256]{1,0:T(8,128)(2,1)S(1)}) fusion(f32[4,512]{0,1:T(8,128)} %select_add_fusion, f32[128,512]{0,1:T(8,128)} %select_add_fusion.1), kind=kLoop, calls=%fused_computation.3 | loop fusion | flops 917504 | bytes 794624 | tf_op jit(solution)/shard_map/convert_element_type | solution.py:446
  24.2 6.5 %collective-permute-done.5.refs_6_ = f32[176,128]{1,0:T(8,128)S(1)} collective-permute-done((f32[176,128]{1,0:T(8,128)}, f32[176,128]{1,0:T(8,128)S(1)}, u32[]{:S(2)}, u32[]{:S(2)}) %collective-permute-start.5) | collective-permute-done | bytes 90144 | tf_op jit(solution)/shard_map/ppermute | solution.py:314
  30.7 2.6 %collective-permute-done.6.refs_7_ = f32[176,128]{1,0:T(8,128)S(1)} collective-permute-done((f32[176,128]{1,0:T(8,128)S(1)}, f32[176,128]{1,0:T(8,128)S(1)}, u32[]{:S(2)}, u32[]{:S(2)}) %collective-permute-start.6) | collective-permute-done | bytes 90144 | tf_op jit(solution)/shard_map/ppermute | solution.py:314
  33.4 19.4 %translate_and_interpolate.1 = (f32[4,4,136,128]{3,2,1,0:T(8,128)}, f32[8,128]{1,0:T(8,128)S(1)}) custom-call(s32[1]{0:T(128)} %bitcast.zed, f32[512,128]{1,0:T(8,128)S(1)} %collective-permute-done.refs_0_, f32[512,128]{1,0:T(8,128)S(1)} %collective-permute-done.1.refs_1_, f32[512,128]{1,0:T(8,128)S(1)} %collective-permute-done.2.refs_2_, ...), custom_call_target="tpu_custom_call" | custom-call | tf_op jit(solution)/shard_map/translate_and_interpolate/pallas_call | solution.py:451
  52.8 6.5 %all-to-all-start = ((f32[16,136,128]{2,1,0:T(8,128)}), f32[16,136,128]{2,1,0:T(8,128)S(1)}, u32[]{:S(2)}, u32[]{:S(2)}) async-start(f32[16,136,128]{2,1,0:T(8,128)} %bitcast.40), calls=%async_computation | async-start | bytes 2228224 | tf_op jit(solution)/shard_map/all_to_all | solution.py:475
  59.3 26.3 %all-to-all-done.parts = f32[16,136,128]{2,1,0:T(8,128)S(1)} async-done(((f32[16,136,128]{2,1,0:T(8,128)}), f32[16,136,128]{2,1,0:T(8,128)S(1)}, u32[]{:S(2)}, u32[]{:S(2)}) %all-to-all-start) | async-done | bytes 1114144 | tf_op jit(solution)/shard_map/all_to_all | solution.py:475
  85.7 1.6 %join_parts.1 = f32[64,2,4,512]{3,2,1,0:T(4,128)} custom-call(f32[16,136,128]{2,1,0:T(8,128)S(1)} %all-to-all-done.parts, f32[1,128]{1,0:T(1,128)S(1)} %slice_subtract_fusion.rims), custom_call_target="tpu_custom_call" | custom-call | tf_op jit(solution)/shard_map/join_parts/pallas_call | solution.py:484
  (49 shorter events, 3.4 us)
Async XLA Ops:
  0.0 13.0 %copy-start = (s32[2048,4]{0,1:T(4,128)S(1)}, s32[2048,4]{0,1:T(4,128)}, u32[]{:S(2)}) copy-start(s32[2048,4]{0,1:T(4,128)} %param.18) | copy-start | bytes 98308
  0.0 1.2 %copy-start.1 = (f32[64,2,4,512]{3,2,1,0:T(4,128)S(1)}, f32[64,2,4,512]{3,2,1,0:T(4,128)}, u32[]{:S(2)}) copy-start(f32[64,2,4,512]{3,2,1,0:T(4,128)} %field.1) | copy-start | bytes 3145732
  1.6 31.7 %collective-permute-start = (f32[512,128]{1,0:T(8,128)S(1)}, f32[512,128]{1,0:T(8,128)S(1)}, u32[]{:S(2)}, u32[]{:S(2)}) collective-permute-start(f32[512,128]{1,0:T(8,128)S(1)} %get-tuple-element.24), channel_id=1, source_target_pairs={{0,24},{8,16},{16,8},{24,0},{1,25},{9,17},{17,9},{25,1},{2,26},{10... | collective-permute-start | bytes 786440 | tf_op jit(solution)/shard_map/ppermute | solution.py:314
  3.0 30.4 %collective-permute-start.1 = (f32[512,128]{1,0:T(8,128)S(1)}, f32[512,128]{1,0:T(8,128)S(1)}, u32[]{:S(2)}, u32[]{:S(2)}) collective-permute-start(f32[512,128]{1,0:T(8,128)S(1)} %get-tuple-element.25), channel_id=1, source_target_pairs={{0,16},{8,24},{16,0},{24,8},{1,17},{9,25},{17,1},{25,9},{2,18},{10... | collective-permute-start | bytes 786440 | tf_op jit(solution)/shard_map/ppermute | solution.py:314
  4.1 29.3 %collective-permute-start.2 = (f32[512,128]{1,0:T(8,128)S(1)}, f32[512,128]{1,0:T(8,128)S(1)}, u32[]{:S(2)}, u32[]{:S(2)}) collective-permute-start(f32[512,128]{1,0:T(8,128)S(1)} %get-tuple-element.26), channel_id=1, source_target_pairs={{0,8},{8,0},{16,24},{24,16},{1,9},{9,1},{17,25},{25,17},{2,10},{10... | collective-permute-start | bytes 786440 | tf_op jit(solution)/shard_map/ppermute | solution.py:314
  5.2 7.0 %collective-permute-start.3 = (f32[16,2,4,512]{3,2,1,0:T(4,128)S(1)}, f32[16,2,4,512]{3,2,1,0:T(4,128)S(1)}, u32[]{:S(2)}, u32[]{:S(2)}) collective-permute-start(f32[16,2,4,512]{3,2,1,0:T(4,128)S(1)} %get-tuple-element.28), channel_id=1, source_target_pairs={{0,4},{4,0},{1,5},{5,1},{2,6},{6,2},{3,7},{7,3},{8,12},{12,8},{9,1... | collective-permute-start | bytes 786440 | tf_op jit(solution)/shard_map/ppermute | solution.py:309
  13.7 10.5 %collective-permute-start.4 = (f32[176,128]{1,0:T(8,128)}, f32[176,128]{1,0:T(8,128)S(1)}, u32[]{:S(2)}, u32[]{:S(2)}) collective-permute-start(f32[176,128]{1,0:T(8,128)} %get-tuple-element.34), channel_id=1, source_target_pairs={{0,8},{8,0},{16,24},{24,16},{1,9},{9,1},{17,25},{25,17},{2,10},{10... | collective-permute-start | bytes 270344 | tf_op jit(solution)/shard_map/ppermute | solution.py:314
  14.1 16.6 %collective-permute-start.5 = (f32[176,128]{1,0:T(8,128)}, f32[176,128]{1,0:T(8,128)S(1)}, u32[]{:S(2)}, u32[]{:S(2)}) collective-permute-start(f32[176,128]{1,0:T(8,128)} %get-tuple-element.35), channel_id=1, source_target_pairs={{0,16},{8,24},{16,0},{24,8},{1,17},{9,25},{17,1},{25,9},{2,18},{10... | collective-permute-start | bytes 270344 | tf_op jit(solution)/shard_map/ppermute | solution.py:314
  21.2 2.1 %copy-start.2 = (f32[8]{0:T(128)S(1)}, f32[8]{0:T(128)}, u32[]{:S(2)}) copy-start(f32[8]{0:T(128)} %get-tuple-element.62) | copy-start | bytes 100
  24.2 9.1 %collective-permute-start.6 = (f32[176,128]{1,0:T(8,128)S(1)}, f32[176,128]{1,0:T(8,128)S(1)}, u32[]{:S(2)}, u32[]{:S(2)}) collective-permute-start(f32[176,128]{1,0:T(8,128)S(1)} %get-tuple-element.36), channel_id=1, source_target_pairs={{0,24},{8,16},{16,8},{24,0},{1,25},{9,17},{17,9},{25,1},{2,26},{10... | collective-permute-start | bytes 270344 | tf_op jit(solution)/shard_map/ppermute | solution.py:314
  52.8 32.9 %all-to-all-start = ((f32[16,136,128]{2,1,0:T(8,128)}), f32[16,136,128]{2,1,0:T(8,128)S(1)}, u32[]{:S(2)}, u32[]{:S(2)}) async-start(f32[16,136,128]{2,1,0:T(8,128)} %bitcast.40), calls=%async_computation | async-start | bytes 2228224 | tf_op jit(solution)/shard_map/all_to_all | solution.py:475
